TPU v7x, 32 devices: a whole 2x2x4 slice. The times are simulated.
32 devices in a mesh: dp: 8 (over z, y), head: 4 (over x, core).
Axes of the slice: x: 2, y: 2, z: 4, core: 2. Of those that a mesh axis runs over, the one named last changes fastest.
Arguments:
- tokens: bfloat16 [16384, 512], P(('dp', 'head'))
- cotangent: bfloat16 [16384, 512], P(('dp', 'head'))
- seq_start: int32 [16384], P('dp'), may hold values from 0 to 2047, as said below
- time_bucket: int32 [16384], P('dp'), may hold values from 0 to 127
- proj_weight: float32 [512, 4, 512], P('dp', None, 'head'), may hold values from -0.25 to 0.25
- out_weight: float32 [512, 512], P('head', 'dp')
- small_params: float32 [8832], replicated, may hold values from -3 to 3
- proj_mean: float32 [512, 4, 512], P('dp', None, 'head'), may hold values from -0.0014648438 to 0.0014648438
- proj_square: float32 [512, 4, 512], P('dp', None, 'head'), may hold values from 7.5783296e-10 to 3.0313319e-09
- out_mean: float32 [512, 512], P('head', 'dp'), may hold values from -0.0014648438 to 0.0014648438
- out_square: float32 [512, 512], P('head', 'dp'), may hold values from 7.5783296e-10 to 3.0313319e-09
- small_mean: float32 [8832], replicated, may hold values from -0.00390625 to 0.00390625
- small_square: float32 [8832], replicated, may hold values from 6.8204966e-09 to 2.7281986e-08
Outputs:
- mixed: bfloat16 [16384, 512], P(('dp', 'head'))
- input_grad: float32 [16384, 512], P(('dp', 'head'))
- grad_proj: float32 [512, 4, 512], P('dp', None, 'head')
- grad_out: float32 [512, 512], P('head', 'dp')
- grad_small: float32 [8832], replicated
- grad_norm: float32 [], replicated
- new_proj: float32 [512, 4, 512], P('dp', None, 'head')
- mean_proj: float32 [512, 4, 512], P('dp', None, 'head')
- square_proj: float32 [512, 4, 512], P('dp', None, 'head')
- new_out: float32 [512, 512], P('head', 'dp')
- mean_out: float32 [512, 512], P('head', 'dp')
- square_out: float32 [512, 512], P('head', 'dp')
- new_small: float32 [8832], replicated
- mean_small: float32 [8832], replicated
- square_small: float32 [8832], replicated
Inputs may be any that keep to these rules, and one draw needn't show every extreme that they name: `seq_start`: within each aligned group of 2048 tokens, the group-local index of the first token of the token's sequence; sequences are contiguous runs and the value equals a token's own index where its sequence begins; in every group one sequence begins within the first 512 tokens and ends within the last 512, the last token of the group is a sequence of its own, the others hold at most 256 tokens.
All inputs are finite; a program needn't handle non-finite values.
Results may differ from a plain program's by a relative error of at most 0.0089.
Values may be sent and summed in bfloat16 or wider, within the bound.
No kernel may reach another device: no remote copies, remote signals or barrier semaphores. Data moves between devices by JAX's collectives and lax.ppermute only.
A program may use at most 128 MiB of HBM per device.

v0:
```python
import math

import jax
import jax.numpy as jnp
from jax import lax
from jax.sharding import PartitionSpec as P

D = 512
HEAD_DIM = 64
HD = 512
BLOCK = 512
POS = 8192
NTB = 128
STEP = 10


norm_epsilon = 1e-06
adam_epsilon = 1e-08
beta_one = 0.9
beta_two = 0.999
clip_norm = 1.0
rate_matrix = 0.05
rate_small = 0.3
decay_matrix = 0.1


def adam_step(weight, grad, first, second, factor, rate, decay):
    clipped = grad * factor
    first_new = beta_one * first + (1.0 - beta_one) * clipped
    second_new = beta_two * second + (1.0 - beta_two) * clipped * clipped
    update = (
        first_new
        / (1.0 - beta_one**STEP)
        / (jnp.sqrt(second_new / (1.0 - beta_two**STEP)) + adam_epsilon)
    )
    return (weight - rate * (update + decay * weight), first_new, second_new)


def diagonal_sums(matrix):
    row_count, col_count = matrix.shape
    flipped = matrix[:, ::-1]
    padded = jnp.pad(flipped, ((0, 0), (0, row_count)))
    flattened = padded.reshape(-1)[: row_count * (row_count + col_count - 1)]
    return jnp.sum(flattened.reshape(row_count, row_count + col_count - 1), 0)


def toeplitz_tile(vector, row_count, col_count):
    period = row_count + col_count
    extended = jnp.pad(vector, (0, 1))
    repeated = jnp.tile(extended, row_count + 1)[: row_count * (period + 1)]
    hankel = repeated.reshape(row_count, period + 1)[:, :col_count]
    return hankel[:, ::-1]


def shards(
    tokens,
    cotangent,
    seq_start,
    time_bucket,
    proj_weight,
    out_weight,
    small_params,
    proj_mean,
    proj_square,
    out_mean,
    out_square,
    small_mean,
    small_square,
):
    inputs = tokens.astype(jnp.float32)
    centred = inputs - jnp.mean(inputs, -1, keepdims=True)
    scale_in = lax.rsqrt(jnp.mean(centred * centred, -1, keepdims=True) + norm_epsilon)
    normed = centred * scale_in
    gathered = lax.all_gather(normed.astype(jnp.bfloat16), "head", axis=0, tiled=True)
    proj_low, out_low = (
        lax.all_gather(proj_weight.astype(jnp.bfloat16), "dp", axis=0, tiled=True),
        lax.all_gather(out_weight.astype(jnp.bfloat16), "dp", axis=1, tiled=True),
    )
    group_rows = gathered.shape[0]
    width_here = proj_low.shape[2]
    heads_here = width_here // HEAD_DIM
    blocks = group_rows // BLOCK
    factor_qk = 1.0 / math.sqrt(HEAD_DIM)
    projected = jnp.einsum("td,dch->tch", gathered, proj_low, preferred_element_type=jnp.float32)
    sigma = jax.nn.sigmoid(projected)
    active = projected * sigma
    gating = active[:, 0]
    shaped = active[:, 1:].astype(jnp.bfloat16).reshape(group_rows, 3, heads_here, HEAD_DIM)
    values = shaped[:, 0]
    queries = shaped[:, 1]
    keys_all = shaped[:, 2]
    bias_out = small_params[:D]
    pos_table = small_params[D : D + POS]
    time_table = small_params[D + POS :]
    extent = max(group_rows, POS) + BLOCK
    pos_padded = jnp.concatenate(
        [
            jnp.full((BLOCK - 1,), pos_table[0], jnp.float32),
            pos_table,
            jnp.full((extent - BLOCK + 1 - POS,), pos_table[POS - 1], jnp.float32),
        ]
    )
    time_vector = jnp.concatenate([time_table[1:][::-1], time_table])
    time_square = toeplitz_tile(time_vector, NTB, NTB)
    time_onehot = (time_bucket[:, None] == jnp.arange(NTB, dtype=jnp.int32)[None, :]).astype(
        jnp.float32
    )
    time_rows = jnp.dot(time_onehot, time_square, precision=lax.Precision.HIGHEST)
    time_high = lax.optimization_barrier(time_rows.astype(jnp.bfloat16))
    time_low = (time_rows - time_high.astype(jnp.float32)).astype(jnp.bfloat16)
    time_split = jnp.concatenate([time_high, time_low], axis=1)
    onehot_low = time_onehot.astype(jnp.bfloat16)
    onehot_pair = jnp.concatenate([onehot_low, onehot_low], axis=1)

    def block_scores(row_block, col_block):
        row_first = row_block * BLOCK
        col_first = col_block * BLOCK
        query_rows = lax.dynamic_slice_in_dim(queries, row_first, BLOCK, 0)
        key_rows = lax.dynamic_slice_in_dim(keys_all, col_first, BLOCK, 0)
        value_rows = lax.dynamic_slice_in_dim(values, col_first, BLOCK, 0)
        product = (
            jnp.einsum("qhd,khd->hqk", query_rows, key_rows, preferred_element_type=jnp.float32)
            * factor_qk
        )
        offset = row_first - col_first
        pos_bias = toeplitz_tile(
            lax.dynamic_slice_in_dim(pos_padded, offset, 2 * BLOCK - 1, 0), BLOCK, BLOCK
        )
        time_bias = jnp.einsum(
            "qb,kb->qk",
            lax.dynamic_slice_in_dim(time_split, row_first, BLOCK, 0),
            lax.dynamic_slice_in_dim(onehot_pair, col_first, BLOCK, 0),
            preferred_element_type=jnp.float32,
        )
        scores = product + (pos_bias + time_bias)[None]
        row_index = row_first + jnp.arange(BLOCK, dtype=jnp.int32)
        col_index = col_first + jnp.arange(BLOCK, dtype=jnp.int32)
        row_seq = lax.dynamic_slice_in_dim(seq_start, row_first, BLOCK, 0)
        col_seq = lax.dynamic_slice_in_dim(seq_start, col_first, BLOCK, 0)
        mask = (row_seq[:, None] == col_seq[None, :]) & (col_index[None, :] <= row_index[:, None])
        return (scores, mask[None], query_rows, key_rows, value_rows)

    def forward_block(row_block):

        def forward_inner(col_block, total):
            scores, mask, query_rows, key_rows, value_rows = block_scores(row_block, col_block)
            weights = jnp.where(mask, scores * jax.nn.sigmoid(scores), 0.0).astype(jnp.bfloat16)
            return total + jnp.einsum(
                "hqk,khd->qhd", weights, value_rows, preferred_element_type=jnp.float32
            )

        return lax.fori_loop(
            0, row_block + 1, forward_inner, jnp.zeros((BLOCK, heads_here, HEAD_DIM), jnp.float32)
        )

    attn = lax.map(forward_block, jnp.arange(blocks, dtype=jnp.int32)).reshape(
        group_rows, width_here
    )
    head_total = lax.psum(jnp.sum(attn, -1), "head")
    centre_mid = attn - (head_total / HD)[:, None]
    spread = lax.psum(jnp.sum(centre_mid * centre_mid, -1), "head")
    variance = spread / HD
    scale_mid = lax.rsqrt(variance + norm_epsilon)[:, None]
    attn_normed = centre_mid * scale_mid
    gated = (attn_normed * gating).astype(jnp.bfloat16)
    grad_result = cotangent.astype(jnp.float32)
    piece = gated
    branch = lax.psum_scatter(
        jnp.dot(piece, out_low, preferred_element_type=jnp.float32),
        "head",
        scatter_dimension=0,
        tiled=True,
    )
    result = branch + bias_out + inputs
    cotangent_all = lax.all_gather(cotangent, "head", axis=0, tiled=True)
    weight_out_grad = jnp.einsum(
        "th,td->hd", gated, cotangent_all, preferred_element_type=jnp.float32
    )
    grad_gated = jnp.einsum("td,hd->th", cotangent_all, out_low, preferred_element_type=jnp.float32)
    mixed = result.astype(jnp.bfloat16)
    grad_gating = grad_gated * attn_normed
    grad_normed_mid = grad_gated * gating
    back_sums = lax.psum(
        (jnp.sum(grad_normed_mid, -1), jnp.sum(grad_normed_mid * attn_normed, -1)), "head"
    )
    attn_grad = scale_mid * (
        grad_normed_mid - (back_sums[0] / HD)[:, None] - attn_normed * (back_sums[1] / HD)[:, None]
    )
    attn_grad = attn_grad.astype(jnp.bfloat16).reshape(group_rows, heads_here, HEAD_DIM)

    def backward_block(carry, row_block):

        def backward_inner(col_block, state):
            query_grad, time_part, key_grad, value_grad, pos_extent = state
            scores, mask, query_rows, key_rows, value_rows = block_scores(row_block, col_block)
            col_first = col_block * BLOCK
            sig_scores = jax.nn.sigmoid(scores)
            weights = jnp.where(mask, scores * sig_scores, 0.0).astype(jnp.bfloat16)
            back_rows = lax.dynamic_slice_in_dim(attn_grad, row_block * BLOCK, BLOCK, 0)
            value_add = jnp.einsum(
                "hqk,qhd->khd", weights, back_rows, preferred_element_type=jnp.float32
            )
            value_grad = lax.dynamic_update_slice_in_dim(
                value_grad,
                lax.dynamic_slice_in_dim(value_grad, col_first, BLOCK, 0) + value_add,
                col_first,
                0,
            )
            weight_grad = jnp.einsum(
                "qhd,khd->hqk", back_rows, value_rows, preferred_element_type=jnp.float32
            )
            score_grad = jnp.where(
                mask, weight_grad * sig_scores * (1.0 + scores * (1.0 - sig_scores)), 0.0
            ).astype(jnp.bfloat16)
            query_grad = (
                query_grad
                + jnp.einsum(
                    "hqk,khd->qhd", score_grad, key_rows, preferred_element_type=jnp.float32
                )
                * factor_qk
            )
            key_add = (
                jnp.einsum(
                    "hqk,qhd->khd", score_grad, query_rows, preferred_element_type=jnp.float32
                )
                * factor_qk
            )
            key_grad = lax.dynamic_update_slice_in_dim(
                key_grad,
                lax.dynamic_slice_in_dim(key_grad, col_first, BLOCK, 0) + key_add,
                col_first,
                0,
            )
            summed = jnp.sum(score_grad.astype(jnp.float32), 0)
            diagonal = diagonal_sums(summed)
            offset = (row_block - col_block) * BLOCK
            pos_extent = lax.dynamic_update_slice_in_dim(
                pos_extent,
                lax.dynamic_slice_in_dim(pos_extent, offset, 2 * BLOCK - 1, 0) + diagonal,
                offset,
                0,
            )
            col_onehot = lax.dynamic_slice_in_dim(onehot_low, col_first, BLOCK, 0)
            time_part = time_part + jnp.einsum(
                "hqk,kb->qb", score_grad, col_onehot, preferred_element_type=jnp.float32
            )
            return (query_grad, time_part, key_grad, value_grad, pos_extent)

        key_grad, value_grad, pos_extent = carry
        start_state = (
            jnp.zeros((BLOCK, heads_here, HEAD_DIM), jnp.float32),
            jnp.zeros((BLOCK, NTB), jnp.float32),
            key_grad,
            value_grad,
            pos_extent,
        )
        query_grad, time_part, key_grad, value_grad, pos_extent = lax.fori_loop(
            0, row_block + 1, backward_inner, start_state
        )
        return ((key_grad, value_grad, pos_extent), (query_grad, time_part))

    zero_rows = jnp.zeros((group_rows, heads_here, HEAD_DIM), jnp.float32)
    start_carry = (zero_rows, zero_rows, jnp.zeros((extent,), jnp.float32))
    (key_grad, value_grad, pos_extent), (query_blocks, time_blocks) = lax.scan(
        backward_block, start_carry, jnp.arange(blocks, dtype=jnp.int32)
    )
    time_columns = time_blocks.reshape(group_rows, NTB)
    time_matrix = jnp.einsum(
        "ta,tb->ab", time_onehot, time_columns, precision=lax.Precision.HIGHEST
    )
    time_diagonal = diagonal_sums(time_matrix)
    time_grad = time_diagonal[NTB - 1 :] + jnp.concatenate(
        [jnp.zeros((1,), jnp.float32), time_diagonal[: NTB - 1][::-1]]
    )
    pos_grad = jnp.concatenate(
        [pos_extent[BLOCK - 1 : BLOCK + POS - 2], jnp.sum(pos_extent[BLOCK + POS - 2 :])[None]]
    )
    grad_stack = jnp.stack(
        [
            grad_gating,
            value_grad.reshape(group_rows, width_here),
            query_blocks.reshape(group_rows, width_here),
            key_grad.reshape(group_rows, width_here),
        ],
        axis=1,
    )
    proj_back = (grad_stack * sigma * (1.0 + projected * (1.0 - sigma))).astype(jnp.bfloat16)
    weight_proj_grad = jnp.einsum(
        "td,tch->dch", gathered, proj_back, preferred_element_type=jnp.float32
    )
    piece = proj_back
    normed_grad = lax.psum_scatter(
        jnp.einsum("tch,dch->td", piece, proj_low, preferred_element_type=jnp.float32).astype(
            jnp.bfloat16
        ),
        "head",
        scatter_dimension=0,
        tiled=True,
    ).astype(jnp.float32)
    input_grad = grad_result + scale_in * (
        normed_grad
        - jnp.mean(normed_grad, -1, keepdims=True)
        - normed * jnp.mean(normed_grad * normed, -1, keepdims=True)
    )
    grad_proj, grad_out = (
        lax.psum_scatter(weight_proj_grad, "dp", scatter_dimension=0, tiled=True),
        lax.psum_scatter(weight_out_grad, "dp", scatter_dimension=1, tiled=True),
    )
    small_local = jnp.concatenate([jnp.sum(grad_result, 0), pos_grad, time_grad])
    grad_small = lax.psum(small_local, ("dp", "head"))
    sharded_squares = jnp.sum(grad_proj * grad_proj) + jnp.sum(grad_out * grad_out)
    total = lax.psum(sharded_squares, ("dp", "head")) + jnp.sum(grad_small * grad_small)
    grad_norm = jnp.sqrt(total)
    factor = jnp.minimum(1.0, clip_norm / (grad_norm + 1e-06))
    new_proj, mean_proj, square_proj = adam_step(
        proj_weight, grad_proj, proj_mean, proj_square, factor, rate_matrix, decay_matrix
    )
    new_out, mean_out, square_out = adam_step(
        out_weight, grad_out, out_mean, out_square, factor, rate_matrix, decay_matrix
    )
    new_small, mean_small, square_small = adam_step(
        small_params, grad_small, small_mean, small_square, factor, rate_small, 0.0
    )
    return (
        mixed,
        input_grad,
        grad_proj,
        grad_out,
        grad_small,
        grad_norm,
        new_proj,
        mean_proj,
        square_proj,
        new_out,
        mean_out,
        square_out,
        new_small,
        mean_small,
        square_small,
    )


def solution(mesh):
    in_specs = (
        P(("dp", "head"), None),
        P(("dp", "head"), None),
        P("dp"),
        P("dp"),
        P("dp", None, "head"),
        P("head", "dp"),
        P(),
        P("dp", None, "head"),
        P("dp", None, "head"),
        P("head", "dp"),
        P("head", "dp"),
        P(),
        P(),
    )
    out_specs = (
        P(("dp", "head"), None),
        P(("dp", "head"), None),
        P("dp", None, "head"),
        P("head", "dp"),
        P(),
        P(),
        P("dp", None, "head"),
        P("dp", None, "head"),
        P("dp", None, "head"),
        P("head", "dp"),
        P("head", "dp"),
        P("head", "dp"),
        P(),
        P(),
        P(),
    )
    return jax.shard_map(shards, mesh=mesh, in_specs=in_specs, out_specs=out_specs, check_vma=False)
```

profile of v0, /device:TPU:0, one launch (start us, length us, event | category | flops | bytes accessed | tf_op | source)
XLA Modules:
  0.0 876.4 jit_solution(9794177068898441048)
XLA Ops:
  14.0 33.1 %all_gather.13 = bf16[512,4,128]{2,0,1:T(8,128)(2,1)S(1)} all-gather(bf16[64,4,128]{2,0,1:T(8,128)(2,1)S(1)} %copy.180), channel_id=1, replica_groups=mesh['dp'=8,'head'=4] {'dp'}, dimensions={0}, use_global_device_ids=true | all-gather | bytes 589824 | tf_op jit(solution)/shard_map/all_gather | solution.py:76
  53.3 32.5 %all_gather.14 = bf16[128,512]{0,1:T(8,128)(2,1)} all-gather(bf16[128,64]{0,1:T(8,128)(2,1)S(1)} %convert_element_type.100), channel_id=1, replica_groups=mesh['dp'=8,'head'=4] {'dp'}, dimensions={1}, use_global_device_ids=true | all-gather | bytes 147456 | tf_op jit(solution)/shard_map/all_gather | solution.py:77
  87.8 5.5 fusion.48
  95.9 142.1 %while.87 = (s32[]{:T(128)}, f32[4,512,2,64]{1,3,2,0:T(8,128)}, s32[4]{0:T(128)S(1)}, s32[2048]{0:T(1024)S(1)}, bf16[2048,2,64]{0,2,1:T(8,128)(2,1)}, /*index=5*...) while((s32[]{:T(128)}, f32[4,512,2,64]{1,3,2,0:T(8,128)}, ...), condition=%wide.region_5.6_spmd, body=%wide.region_2.5_spmd.sunk | while | flops 273744896 | bytes 26666800 | solution.py:156
  101.1 11.4 %while.90 = (s32[]{:T(128)}, f32[512,2,64]{0,2,1:T(8,128)}, s32[]{:T(128)}, bf16[2048,2,64]{0,2,1:T(8,128)(2,1)}, s32[512]{0:T(512)S(1)}, /*index=5*/s32[2048]{0...) while((s32[]{:T(128)}, f32[512,2,64]{0,2,1:T(8,128)}, ...), condition=%wide.region_4.4_spmd, body=%wide.region_3.3_spmd.sunk | while | flops 273744896 | bytes 25089384 | solution.py:152
  103.8 3.2 reshape.261
  119.5 22.9 %while.90 = (s32[]{:T(128)}, f32[512,2,64]{0,2,1:T(8,128)}, s32[]{:T(128)}, bf16[2048,2,64]{0,2,1:T(8,128)(2,1)}, s32[512]{0:T(512)S(1)}, /*index=5*/s32[2048]{0...) while((s32[]{:T(128)}, f32[512,2,64]{0,2,1:T(8,128)}, ...), condition=%wide.region_4.4_spmd, body=%wide.region_3.3_spmd.sunk | while | flops 273744896 | bytes 25089384 | solution.py:152
  122.2 3.2 reshape.261
  133.6 3.2 reshape.261
  149.3 34.3 %while.90 = (s32[]{:T(128)}, f32[512,2,64]{0,2,1:T(8,128)}, s32[]{:T(128)}, bf16[2048,2,64]{0,2,1:T(8,128)(2,1)}, s32[512]{0:T(512)S(1)}, /*index=5*/s32[2048]{0...) while((s32[]{:T(128)}, f32[512,2,64]{0,2,1:T(8,128)}, ...), condition=%wide.region_4.4_spmd, body=%wide.region_3.3_spmd.sunk | while | flops 273744896 | bytes 25089384 | solution.py:152
  152.0 3.2 reshape.261
  163.4 3.2 reshape.261
  174.9 3.2 reshape.261
  190.6 45.7 %while.90 = (s32[]{:T(128)}, f32[512,2,64]{0,2,1:T(8,128)}, s32[]{:T(128)}, bf16[2048,2,64]{0,2,1:T(8,128)(2,1)}, s32[512]{0:T(512)S(1)}, /*index=5*/s32[2048]{0...) while((s32[]{:T(128)}, f32[512,2,64]{0,2,1:T(8,128)}, ...), condition=%wide.region_4.4_spmd, body=%wide.region_3.3_spmd.sunk | while | flops 273744896 | bytes 25089384 | solution.py:152
  193.2 3.2 reshape.261
  204.7 3.2 reshape.261
  216.1 3.2 reshape.261
  227.5 3.2 reshape.261
  240.5 5.8 psum.42
  246.4 6.7 psum.43
  253.2 2.7 fusion.71
  255.9 10.6 %all-reduce.6 = (f32[2048]{0:T(1024)S(1)}, f32[2048]{0:T(1024)S(1)}) all-reduce(f32[2048]{0:T(1024)S(1)} %get-tuple-element.1056, f32[2048]{0:T(1024)S(1)} %get-tuple-element.1055), channel_id=1, replica_groups=mesh['dp'=8,'head'=4] {'head'}, use_global_device_ids=true, to_apply=%region_14.15 | all-reduce | flops 4096 | bytes 32768 | tf_op jit(solution)/shard_map/psum | solution.py:183
  266.5 2.9 multiply_convert_fusion
  272.2 332.7 %while.89 = (s32[]{:T(128)}, f32[2048,2,64]{0,2,1:T(8,128)}, f32[2048,2,64]{0,2,1:T(8,128)}, f32[8704]{0:T(1024)}, f32[4,512,2,64]{1,0,3,2:T(4,128)}, /*index=5*...) while((s32[]{:T(128)}, f32[2048,2,64]{0,2,1:T(8,128)}, ...), condition=%wide.region_20.21_spmd.clone, body=%wide.region_15.20_spmd.clone.sunk | while | flops 550896128 | bytes 66399368 | solution.py:264
  280.7 26.2 %while.91 = (s32[]{:T(128)}, f32[512,2,64]{0,2,1:T(8,128)}, f32[512,128]{1,0:T(8,128)}, f32[2048,2,64]{0,2,1:T(8,128)}, f32[2048,2,64]{0,2,1:T(8,128)}, /*index=...) while((s32[]{:T(128)}, f32[512,2,64]{0,2,1:T(8,128)}, ...), condition=%wide.region_19.19_spmd, body=%wide.region_16.18_spmd.sunk | while | flops 550109696 | bytes 62716512 | solution.py:257
  283.4 3.2 reshape.259
  302.3 3.0 reshape.260
  308.2 6.1 dynamic_update_slice.53
  324.5 52.5 %while.91 = (s32[]{:T(128)}, f32[512,2,64]{0,2,1:T(8,128)}, f32[512,128]{1,0:T(8,128)}, f32[2048,2,64]{0,2,1:T(8,128)}, f32[2048,2,64]{0,2,1:T(8,128)}, /*index=...) while((s32[]{:T(128)}, f32[512,2,64]{0,2,1:T(8,128)}, ...), condition=%wide.region_19.19_spmd, body=%wide.region_16.18_spmd.sunk | while | flops 550109696 | bytes 62716512 | solution.py:257
  327.2 3.2 reshape.259
  346.1 3.0 reshape.260
  353.4 3.2 reshape.259
  366.2 2.6 fusion.142
  372.4 3.0 reshape.260
  378.2 6.1 dynamic_update_slice.53
  394.6 78.7 %while.91 = (s32[]{:T(128)}, f32[512,2,64]{0,2,1:T(8,128)}, f32[512,128]{1,0:T(8,128)}, f32[2048,2,64]{0,2,1:T(8,128)}, f32[2048,2,64]{0,2,1:T(8,128)}, /*index=...) while((s32[]{:T(128)}, f32[512,2,64]{0,2,1:T(8,128)}, ...), condition=%wide.region_19.19_spmd, body=%wide.region_16.18_spmd.sunk | while | flops 550109696 | bytes 62716512 | solution.py:257
  397.3 3.2 reshape.259
  416.2 3.0 reshape.260
  423.5 3.2 reshape.259
  442.4 3.0 reshape.260
  449.7 3.2 reshape.259
  468.7 3.0 reshape.260
  474.5 6.1 dynamic_update_slice.53
  490.9 105.0 %while.91 = (s32[]{:T(128)}, f32[512,2,64]{0,2,1:T(8,128)}, f32[512,128]{1,0:T(8,128)}, f32[2048,2,64]{0,2,1:T(8,128)}, f32[2048,2,64]{0,2,1:T(8,128)}, /*index=...) while((s32[]{:T(128)}, f32[512,2,64]{0,2,1:T(8,128)}, ...), condition=%wide.region_19.19_spmd, body=%wide.region_16.18_spmd.sunk | while | flops 550109696 | bytes 62716512 | solution.py:257
  493.6 3.2 reshape.259
  512.5 3.0 reshape.260
  519.8 3.2 reshape.259
  538.7 3.0 reshape.260
  546.1 3.2 reshape.259
  565.0 3.0 reshape.260
  572.3 3.2 reshape.259
  591.2 3.0 reshape.260
  597.1 6.1 dynamic_update_slice.53
  604.9 3.1 stack_reshape.10
  608.0 2.8 fusion.79
  610.8 4.1 fusion.47
  617.3 2.7 bitcast_convert_fusion
  621.0 2.8 fusion.78
  628.5 43.9 %reduce-scatter.11.cloned.1.call-done = f32[128,64]{0,1:T(8,128)} async-done(((f32[128,512]{0,1:T(8,128)}), f32[128,64]{0,1:T(8,128)}) %reduce-scatter.11.cloned.1.call-update) | async-done | bytes 32784 | tf_op jit(solution)/shard_map/reduce_scatter | solution.py:307
  673.7 65.3 %reduce-scatter.9.cloned.1.call-done = f32[64,4,128]{2,0,1:T(8,128)} async-done(((f32[512,4,128]{2,0,1:T(8,128)}), f32[64,4,128]{2,0,1:T(8,128)}) %reduce-scatter.9.cloned.1.call-update) | async-done | bytes 131088 | tf_op jit(solution)/shard_map/reduce_scatter | solution.py:306
  743.6 28.5 %reduce-scatter.7.cloned.1.call-done = bf16[512,512]{1,0:T(8,128)(2,1)} async-done(((bf16[2048,512]{1,0:T(8,128)(2,1)}), bf16[512,512]{1,0:T(8,128)(2,1)}) %reduce-scatter.7.cloned.1.call-update) | async-done | bytes 524304 | tf_op jit(solution)/shard_map/reduce_scatter | solution.py:292
  773.8 45.2 %reduce-scatter.5.cloned.1.call-done = f32[512,512]{1,0:T(8,128)} async-done(((f32[2048,512]{1,0:T(8,128)}), f32[512,512]{1,0:T(8,128)}) %reduce-scatter.5.cloned.1.call-update) | async-done | bytes 1048592 | tf_op jit(solution)/shard_map/reduce_scatter | solution.py:168
  819.0 3.0 convert_reduce_fusion.3
  822.8 39.8 %all-reduce.5 = (f32[8832]{0:T(1024)S(1)}, f32[]{:T(128)}) all-reduce(f32[8832]{0:T(1024)S(1)} %concatenate.23, f32[]{:T(128)S(6)} %add.383), channel_id=1, replica_groups=mesh['dp'=8,'head'=4] {'dp','head'}, use_global_device_ids=true, to_apply=%region_29.30 | all-reduce | flops 8833 | bytes 70664 | tf_op jit(solution)/shard_map/psum | solution.py:310
  (765 shorter events, 376.2 us)
Async XLA Ops:
  7.2 6.1 copy-start.28
  7.2 6.8 copy-start.23
  7.2 80.6 %all-gather.3.cloned.1.call-start = ((), (), s32[]{:S(2)}) async-start(), calls=%async_computation.4 | async-start | bytes 2621440 | tf_op jit(solution)/shard_map/all_gather | solution.py:74
  12.5 240.7 %all-gather.5.cloned.1.call-start = ((), (), s32[]{:S(2)}) async-start(), calls=%async_computation.6 | async-start | bytes 2621440 | tf_op jit(solution)/shard_map/all_gather | solution.py:175
  13.2 659.1 %reduce-scatter.11.cloned.1.call-start = ((), (), s32[]{:S(2)}) async-start(), calls=%async_computation.9 | async-start | bytes 294912 | tf_op jit(solution)/shard_map/reduce_scatter | solution.py:307
  47.1 40.7 %copy-start.25 = (bf16[512,4,128]{2,0,1:T(8,128)(2,1)}, bf16[512,4,128]{2,0,1:T(8,128)(2,1)S(1)}, u32[]{:S(2)}) copy-start(bf16[512,4,128]{2,0,1:T(8,128)(2,1)S(1)} %all_gather.13) | copy-start | bytes 1572868
  50.8 2.4 copy-start.32
  93.3 2.5 copy-start.15
  238.0 2.4 copy-start.11
  240.0 13.2 %copy-start.19 = (bf16[128,512]{0,1:T(8,128)(2,1)S(1)}, bf16[128,512]{0,1:T(8,128)(2,1)}, u32[]{:S(2)}) copy-start(bf16[128,512]{0,1:T(8,128)(2,1)} %all_gather.14) | copy-start | bytes 393220
  289.9 2.7 copy-start.2
  292.5 6.2 copy-start.1
  293.9 4.8 copy-start.3
  333.7 2.7 copy-start.2
  336.4 6.2 copy-start.1
  337.7 4.8 copy-start.3
  359.9 2.7 copy-start.2
  362.6 6.2 copy-start.1
  364.0 4.8 copy-start.3
  403.8 2.7 copy-start.2
  406.4 6.2 copy-start.1
  407.8 4.8 copy-start.3
  430.0 2.7 copy-start.2
  432.7 6.2 copy-start.1
  434.0 4.8 copy-start.3
  456.2 2.7 copy-start.2
  458.9 6.2 copy-start.1
  460.3 4.8 copy-start.3
  500.1 2.7 copy-start.2
  502.7 6.2 copy-start.1
  504.1 4.8 copy-start.3
  526.3 2.7 copy-start.2
  529.0 6.2 copy-start.1
  530.4 4.8 copy-start.3
  552.6 2.7 copy-start.2
  555.2 6.2 copy-start.1
  556.6 4.8 copy-start.3
  578.8 2.7 copy-start.2
  581.4 6.2 copy-start.1
  582.8 4.8 copy-start.3
  604.9 3.1 copy-start.12
  608.0 2.8 copy-start.7
  610.7 128.3 %reduce-scatter.9.cloned.1.call-start = ((), (), s32[]{:S(2)}) async-start(), calls=%async_computation.8 | async-start | bytes 1179648 | tf_op jit(solution)/shard_map/reduce_scatter | solution.py:306
  610.8 4.1 copy-start.43
  614.9 2.4 copy-start.26
  617.2 154.8 %reduce-scatter.7.cloned.1.call-start = ((), (), s32[]{:S(2)}) async-start(), calls=%async_computation.7 | async-start | bytes 2621440 | tf_op jit(solution)/shard_map/reduce_scatter | solution.py:292
  620.0 199.0 %reduce-scatter.5.cloned.1.call-start = ((), (), s32[]{:S(2)}) async-start(), calls=%async_computation.5 | async-start | bytes 5242880 | tf_op jit(solution)/shard_map/reduce_scatter | solution.py:168
  623.8 148.3 %copy-start.10 = (bf16[512,512]{1,0:T(8,128)(2,1)S(1)}, bf16[512,512]{1,0:T(8,128)(2,1)}, u32[]{:S(2)}) copy-start(bf16[512,512]{1,0:T(8,128)(2,1)} %param.21) | copy-start | bytes 1572868
  623.8 148.2 %copy-start.36 = (f32[512]{0:T(512)S(1)}, f32[512]{0:T(512)}, u32[]{:S(2)}) copy-start(f32[512]{0:T(512)} %copy-done.35) | copy-start | bytes 6148
  623.8 148.2 %copy-start.40 = (f32[512]{0:T(512)S(1)}, f32[512]{0:T(512)}, u32[]{:S(2)}) copy-start(f32[512]{0:T(512)} %copy-done.39) | copy-start | bytes 6148
  623.8 195.1 %copy-start.16 = (bf16[512,512]{1,0:T(8,128)(2,1)S(1)}, bf16[512,512]{1,0:T(8,128)(2,1)}, u32[]{:S(2)}) copy-start(bf16[512,512]{1,0:T(8,128)(2,1)} %param.22) | copy-start | bytes 1572868
  623.9 195.1 %slice-start = ((f32[8832]{0:T(1024)}), f32[512]{0:T(512)S(1)}, s32[]{:S(2)}) async-start(f32[8832]{0:T(1024)} %param.27), calls=%async_computation.10 | async-start | bytes 4096 | tf_op jit(solution)/shard_map/slice | solution.py:92
  773.7 91.0 %copy-start.18 = (f32[64,4,128]{2,0,1:T(8,128)S(1)}, f32[64,4,128]{2,0,1:T(8,128)}, u32[]{:S(2)}) copy-start(f32[64,4,128]{2,0,1:T(8,128)} %reduce-scatter.9.cloned.1.call-done) | copy-start | bytes 393220
  773.7 91.0 %copy-start.24 = (f32[64,4,128]{2,1,0:T(4,128)S(1)}, f32[64,4,128]{2,1,0:T(4,128)}, u32[]{:S(2)}) copy-start(f32[64,4,128]{2,1,0:T(4,128)} %param.25) | copy-start | bytes 393220
  773.7 91.0 %copy-start.30 = (f32[64,4,128]{2,1,0:T(4,128)S(1)}, f32[64,4,128]{2,1,0:T(4,128)}, u32[]{:S(2)}) copy-start(f32[64,4,128]{2,1,0:T(4,128)} %param.28) | copy-start | bytes 393220
  773.7 91.0 %copy-start.31 = (f32[64,4,128]{2,1,0:T(4,128)S(1)}, f32[64,4,128]{2,1,0:T(4,128)}, u32[]{:S(2)}) copy-start(f32[64,4,128]{2,1,0:T(4,128)} %param.29) | copy-start | bytes 393220
  773.7 93.3 %copy-start.29 = (f32[8832]{0:T(1024)S(1)}, f32[8832]{0:T(1024)}, u32[]{:S(2)}) copy-start(f32[8832]{0:T(1024)} %param.27) | copy-start | bytes 105988
  773.7 93.3 %copy-start.37 = (f32[8832]{0:T(1024)S(1)}, f32[8832]{0:T(1024)}, u32[]{:S(2)}) copy-start(f32[8832]{0:T(1024)} %param.32) | copy-start | bytes 105988
  773.8 93.3 %copy-start.38 = (f32[8832]{0:T(1024)S(1)}, f32[8832]{0:T(1024)}, u32[]{:S(2)}) copy-start(f32[8832]{0:T(1024)} %param.33) | copy-start | bytes 105988
  822.0 45.7 %copy-start.33 = (f32[128,64]{0,1:T(8,128)S(1)}, f32[128,64]{0,1:T(8,128)}, u32[]{:S(2)}) copy-start(f32[128,64]{0,1:T(8,128)} %param.26) | copy-start | bytes 98308
  822.0 45.7 %copy-start.34 = (f32[128,64]{0,1:T(8,128)S(1)}, f32[128,64]{0,1:T(8,128)}, u32[]{:S(2)}) copy-start(f32[128,64]{0,1:T(8,128)} %reduce-scatter.11.cloned.1.call-done) | copy-start | bytes 98308
  822.0 45.7 %copy-start.41 = (f32[128,64]{0,1:T(8,128)S(1)}, f32[128,64]{0,1:T(8,128)}, u32[]{:S(2)}) copy-start(f32[128,64]{0,1:T(8,128)} %param.30) | copy-start | bytes 98308
  822.0 45.7 %copy-start.42 = (f32[128,64]{0,1:T(8,128)S(1)}, f32[128,64]{0,1:T(8,128)}, u32[]{:S(2)}) copy-start(f32[128,64]{0,1:T(8,128)} %param.31) | copy-start | bytes 98308
  862.7 5.7 copy-start.27
  (77 other events, 121.9 us)
Sparse Core Ops, SparseCore 0:
  12.6 25.2 all-gather.2
  39.5 22.5 all-gather.4
  610.9 61.4 reduce-scatter.10
  676.2 62.7 reduce-scatter.8
  741.6 30.4 reduce-scatter.6
  774.4 44.4 reduce-scatter.4
where the time goes:
time: 883 us; the launch traced here: 876 us
  local copies, waits for them, and re-layouts  308 us (35%)
  waiting for transfers between devices  184 us (21%)
  matrix products  162 us (18%)
  blocking collectives  129 us (15%)
  other arithmetic  54.5 us (6%)
  loops' own time  20.3 us (2%)
  between operations  18.5 us (2%)
    reduce_scatter x1, waiting for transfers between devices, shards(): lax.psum_scatter(weight_proj_grad, 'dp', scatter_dimension=0, tiled=True)  65.3 us
    reshape x21, local copies, waits for them, and re-layouts, toeplitz_tile(): hankel = repeated.reshape(row_count, period + 1)[:, :col_count]  64 us
    reduce_scatter x1, waiting for transfers between devices, shards(): lax.psum_scatter(jnp.dot(piece, out_low, preferred_element_type=jnp.float...  45.2 us
    reduce_scatter x1, waiting for transfers between devices, shards(): lax.psum_scatter(weight_out_grad, 'dp', scatter_dimension=1, tiled=True)  43.9 us
    psum x1, blocking collectives, shards(): grad_small = lax.psum(small_local, ('dp', 'head'))  39.8 us
    while x250, local copies, waits for them, and re-layouts  38.3 us
    another operation x42, local copies, waits for them, and re-layouts, toeplitz_tile(): repeated = jnp.tile(extended, row_count + 1)[:row_count * (period + 1)]  37.5 us
    dynamic_update_slice x12, local copies, waits for them, and re-layouts, shards(): lax.map(forward_block, jnp.arange(blocks, dtype=jnp.int32))  36.1 us
  transfers between devices with their start and end apart: 6, of which 4 were waited for; matrix products, arithmetic and copies ran while one was open for 19% of the time, Pallas kernels for 0%

commit v1 on v0

v1 whole, which is shorter than its diff:
```python
import functools
import math

import jax
import jax.numpy as jnp
from jax import lax
from jax.experimental import pallas as pl
from jax.experimental.pallas import tpu as pltpu
from jax.sharding import PartitionSpec as P

D = 512
HEAD_DIM = 64
HD = 512
POS = 8192
NTB = 128
STEP = 10
TILE = 256
NEG = -1e9

norm_epsilon = 1e-06
adam_epsilon = 1e-08
beta_one = 0.9
beta_two = 0.999
clip_norm = 1.0
rate_matrix = 0.05
rate_small = 0.3
decay_matrix = 0.1

f32 = jnp.float32
bf16 = jnp.bfloat16
VMEM = pl.BlockSpec(memory_space=pltpu.VMEM)
SMEM = pl.BlockSpec(memory_space=pltpu.SMEM)
ANY = pl.BlockSpec(memory_space=pl.ANY)


def adam_step(weight, grad, first, second, factor, rate, decay):
    clipped = grad * factor
    first_new = beta_one * first + (1.0 - beta_one) * clipped
    second_new = beta_two * second + (1.0 - beta_two) * clipped * clipped
    update = (
        first_new
        / (1.0 - beta_one**STEP)
        / (jnp.sqrt(second_new / (1.0 - beta_two**STEP)) + adam_epsilon)
    )
    return (weight - rate * (update + decay * weight), first_new, second_new)


def swap(x, axis, k):
    n = lax.axis_size(axis)
    return lax.ppermute(x, axis, [(i, i ^ k) for i in range(n)])


def gather_head(x):
    n = lax.axis_size("head")
    pieces = [None] * n
    pieces[0] = x
    for k in range(2, n, 2):
        pieces[k] = swap(x, "head", k)
    pieces[1] = swap(x, "head", 1)
    for k in range(2, n, 2):
        pieces[k + 1] = swap(pieces[k], "head", 1)
    return pieces


def gather_dp(x):
    n = lax.axis_size("dp")
    arrays, offsets = [x], [[0]]
    k = n // 2
    while k:
        arrays.append(swap(jnp.concatenate(arrays, 0) if len(arrays) > 1 else x, "dp", k))
        offsets.append([o ^ k for group in offsets for o in group])
        k //= 2
    return arrays, offsets


def scatter_dp(x):
    n = lax.axis_size("dp")
    me = lax.axis_index("dp")
    low = 2 ** ((n.bit_length() - 1) // 2)
    high = n // low
    parts = x.reshape((high, low) + x.shape[1:])
    here = me % low
    total = lax.dynamic_index_in_dim(parts, here, 1, False).astype(f32)
    for k in range(1, low):
        sent = lax.dynamic_index_in_dim(parts, here ^ k, 1, False)
        total = total + swap(sent, "dp", k).astype(f32)
    row = me // low
    narrow = total.astype(bf16)
    mine = lax.dynamic_index_in_dim(total, row, 0, False)
    for k in range(1, high):
        sent = lax.dynamic_index_in_dim(narrow, row ^ k, 0, False)
        mine = mine + swap(sent, "dp", k * low).astype(f32)
    return mine


def scatter_head(x):
    n = lax.axis_size("head")
    me = lax.axis_index("head")
    core, chip = me % 2, me // 2
    parts = x.reshape(n // 2, 2, x.shape[0] // n, x.shape[1])
    total = lax.dynamic_index_in_dim(parts, core, 1, False).astype(f32)
    sent = lax.dynamic_index_in_dim(parts, 1 - core, 1, False)
    total = total + swap(sent, "head", 1).astype(f32)
    narrow = total.astype(bf16)
    mine = lax.dynamic_index_in_dim(total, chip, 0, False)
    for k in range(1, n // 2):
        sent = lax.dynamic_index_in_dim(narrow, chip ^ k, 0, False)
        mine = mine + swap(sent, "head", 2 * k).astype(f32)
    return mine


def sum_all(x):
    for axis in ("head", "dp"):
        k = 1
        while k < lax.axis_size(axis):
            x = x + swap(x, axis, k)
            k *= 2
    return x


def dot(a, b):
    return lax.dot_general(a, b, (((1,), (0,)), ((), ())), preferred_element_type=f32)


def dot_nt(a, b):
    return lax.dot_general(a, b, (((1,), (1,)), ((), ())), preferred_element_type=f32)


def flip(a):
    return jnp.transpose(a.astype(f32))


def lanes(i):
    return pl.ds(pl.multiple_of(i * TILE, TILE), TILE)


def by_head(block, heads):
    zero = jnp.zeros((HEAD_DIM, block.shape[1]), block.dtype)
    return jnp.concatenate(
        [
            jnp.concatenate(
                [block[g * HEAD_DIM : (g + 1) * HEAD_DIM] if g == h else zero for g in range(heads)], axis=0
            )
            for h in range(heads)
        ],
        axis=1,
    )


def diagonals(x):
    rows, cols = x.shape
    z = jnp.concatenate([x, jnp.zeros((rows, cols), f32)], axis=1)
    total = z[:8]
    for q in range(1, rows // 8):
        total = total + pltpu.roll(z[8 * q : 8 * q + 8], 2 * cols - 8 * q, 1)
    g = total[0:1]
    for r in range(1, 8):
        g = g + pltpu.roll(total, 2 * cols - r, 1)[r : r + 1]
    return g


def copy_pieces(pieces, target, sems, me):
    copies = [
        pltpu.make_async_copy(piece, target.at[me ^ k], sems.at[k]) for k, piece in enumerate(pieces)
    ]
    for copy in copies:
        copy.start()
    return copies


def forward_kernel(heads, n_head, offsets, me_ref, first_ref, *refs):
    refs = list(refs)
    take = lambda count: [refs.pop(0) for _ in range(count)]
    x_pieces, cot_pieces, w_pieces = take(n_head), take(n_head), take(len(offsets))
    tb_ref, ss_ref, small_ref = take(3)
    attn_ref, d_ref, gate_ref, gg_ref, stat_ref = take(5)
    kx_ref, kxt_ref, qxt_ref, v_ref, qm_ref, pos_ref, wt_ref = take(7)
    x_ref, cot_ref, w_ref, vt_ref, acc_ref, x_sem, cot_sem, w_sem = refs
    nb, width = attn_ref.shape[0], attn_ref.shape[1]
    per = x_ref.shape[1] // TILE
    copies = copy_pieces(x_pieces, x_ref, x_sem, me_ref[0]) + copy_pieces(cot_pieces, cot_ref, cot_sem, me_ref[0])
    count = 0
    for piece, group in zip(w_pieces, offsets):
        rows = piece.shape[0] // len(group)
        for at, offset in enumerate(group):
            start = pl.multiple_of((me_ref[1] ^ offset) * rows, 16)
            copy = pltpu.make_async_copy(
                piece.at[pl.ds(at * rows, rows)], w_ref.at[pl.ds(start, rows)], w_sem.at[count]
            )
            copy.start()
            copies.append(copy)
            count += 1

    for d in range(nb):
        here = small_ref[:, D + d * TILE : D + (d + 1) * TILE]
        before = here if d == 0 else small_ref[:, D + (d - 1) * TILE : D + d * TILE]
        row = jnp.concatenate([here, before], axis=1) * 0.5
        tile = pltpu.roll(
            jnp.broadcast_to(row, (TILE, 2 * TILE)), 0, 1, stride=1, stride_axis=0
        )[:, :TILE]
        if d == 0:
            b = lax.broadcasted_iota(jnp.int32, (TILE, TILE), 0)
            a = lax.broadcasted_iota(jnp.int32, (TILE, TILE), 1)
            tile = jnp.where(b <= a, tile, NEG)
        pos_ref[d] = tile
    table = small_ref[:, D + POS : D + POS + NTB]
    row = jnp.concatenate([table, table], axis=1)
    upper = pltpu.roll(jnp.broadcast_to(row, (NTB, 2 * NTB)), 0, 1, stride=1, stride_axis=0)[:, :NTB]
    a = lax.broadcasted_iota(jnp.int32, (NTB, NTB), 0)
    b = lax.broadcasted_iota(jnp.int32, (NTB, NTB), 1)
    upper = jnp.where(b >= a, upper, 0.0)
    square = (jnp.where(b > a, upper, jnp.transpose(upper)) * 0.5).astype(bf16)

    for copy in copies:
        copy.wait()
    wt_ref[...] = flip(w_ref[...]).astype(bf16)

    def project(i, _):
        rows = lanes(i % per)
        p = dot_nt(wt_ref[: 4 * width], x_ref[i // per, rows, :])
        sg = 0.5 + 0.5 * jnp.tanh(0.5 * p)
        act = p * sg
        d_ref[i] = sg + act * (1.0 - sg)
        gate_ref[i] = act[:width]
        gg_ref[i] = dot_nt(wt_ref[4 * width :], cot_ref[i // per, rows, :])
        vt = act[width : 2 * width]
        vt_ref[i] = vt.astype(bf16)
        v_ref[i] = flip(vt).astype(bf16)
        qt = act[2 * width : 3 * width].astype(bf16)
        kt = act[3 * width :]
        onehot = (lax.broadcasted_iota(jnp.int32, (NTB, TILE), 0) == tb_ref[:, lanes(i)]).astype(f32)
        low = onehot.astype(bf16)
        kxt_ref[i, :NTB] = low
        kxt_ref[i, NTB:] = kt.astype(bf16)
        kx_ref[i, :, :NTB] = flip(onehot).astype(bf16)
        kx_ref[i, :, NTB:] = flip(kt).astype(bf16)
        trow = dot(square, low).astype(bf16)
        qs = (qt.astype(f32) * (0.5 / math.sqrt(HEAD_DIM))).astype(bf16)
        qxt_ref[i, :NTB] = jnp.concatenate([trow] * heads, axis=1)
        qxt_ref[i, NTB:] = by_head(qs, heads)
        q = flip(qt).astype(bf16)
        lane = lax.broadcasted_iota(jnp.int32, (TILE, width), 1) // HEAD_DIM
        for h in range(heads):
            qm_ref[i, h * TILE : (h + 1) * TILE, :] = jnp.where(lane == h, q, jnp.zeros_like(q))
        return 0

    lax.fori_loop(0, nb, project, 0)
    key_index = lax.broadcasted_iota(jnp.int32, (TILE, TILE), 0)

    def rows(i, _):
        acc_ref[...] = jnp.zeros_like(acc_ref)
        start = ss_ref[:, lanes(i)]

        def cols(j, _):
            s = dot(kx_ref[j], qxt_ref[i]) + jnp.concatenate([pos_ref[i - j]] * heads, axis=1)
            seen = (key_index + j * TILE) >= start
            s = jnp.where(jnp.concatenate([seen] * heads, axis=1), s, NEG)
            w = (s + s * jnp.tanh(s)).astype(bf16)
            acc_ref[...] += dot(vt_ref[j], w)
            return 0

        lax.fori_loop(first_ref[i], i + 1, cols, 0)
        at = jnp.concatenate(
            [
                acc_ref[h * HEAD_DIM : (h + 1) * HEAD_DIM, h * TILE : (h + 1) * TILE]
                for h in range(heads)
            ],
            axis=0,
        )
        attn_ref[i] = at
        mean = jnp.sum(at, axis=0, keepdims=True) / width
        centred = at - mean
        grad = gg_ref[i] * gate_ref[i]
        stat_ref[i] = jnp.concatenate(
            [
                mean,
                jnp.sum(centred * centred, axis=0, keepdims=True),
                jnp.sum(grad, axis=0, keepdims=True),
                jnp.sum(grad * centred, axis=0, keepdims=True),
            ],
            axis=0,
        )
        return 0

    lax.fori_loop(0, nb, rows, 0)


def middle_kernel(heads, n_head, me_ref, *refs):
    refs = list(refs)
    take = lambda count: [refs.pop(0) for _ in range(count)]
    x_pieces, cot_pieces, stats = take(n_head), take(n_head), take(n_head)
    attn_ref, d_ref, gate_ref, gg_ref, wt_ref = take(5)
    dat_ref, gu_ref, branch_ref, wg_ref = take(4)
    x_ref, cot_ref, ow_ref, acc_ref, x_sem, cot_sem = refs
    nb, width = attn_ref.shape[0], attn_ref.shape[1]
    per = x_ref.shape[1] // TILE
    copies = copy_pieces(x_pieces, x_ref, x_sem, me_ref[0]) + copy_pieces(cot_pieces, cot_ref, cot_sem, me_ref[0])
    ow_ref[...] = wt_ref[4 * width :]
    acc_ref[...] = jnp.zeros_like(acc_ref)
    for copy in copies:
        copy.wait()

    def rows(i, _):
        parts = [s[i] for s in stats]
        mean = sum(p[0:1] for p in parts) / n_head
        spread = sum(p[1:2] + width * (p[0:1] - mean) * (p[0:1] - mean) for p in parts)
        scale = lax.rsqrt(spread / HD + norm_epsilon)
        first = sum(p[2:3] for p in parts) / HD
        second = scale * sum(p[3:4] + (p[0:1] - mean) * p[2:3] for p in parts) / HD
        normed = (attn_ref[i] - mean) * scale
        gate, gg = gate_ref[i], gg_ref[i]
        gated = normed * gate
        dat_ref[i] = scale * (gg * gate - first - normed * second)
        gu = (gg * normed * d_ref[i]).astype(bf16)
        gu_ref[i] = gu
        at = lanes(i % per)
        branch_ref[pl.ds(pl.multiple_of(i * TILE, TILE), TILE), :] = dot(
            flip(gated.astype(bf16)).astype(bf16), ow_ref[...]
        ).astype(bf16)
        acc_ref[:width] += dot(gu, x_ref[i // per, at, :])
        acc_ref[width:] += dot(gated.astype(bf16), cot_ref[i // per, at, :])
        return 0

    lax.fori_loop(0, nb, rows, 0)
    wg_ref[...] = flip(acc_ref[...]).astype(bf16)


def backward_kernel(heads, n_head, me_ref, first_ref, *refs):
    refs = list(refs)
    take = lambda count: [refs.pop(0) for _ in range(count)]
    x_pieces = take(n_head)
    wt_ref, d_ref, kx_ref, kxt_ref, qxt_ref, v_ref, qm_ref, pos_ref, dat_ref, gu_ref, ss_ref = take(11)
    wg_ref, gn_ref, pg_ref, tg_ref = take(4)
    x_ref, dax_ref, daxt_ref, accv_ref, acck_ref, accq_ref, posg_ref, m2_ref, gp_ref, acc_ref, x_sem = refs
    nb, width = dat_ref.shape[0], dat_ref.shape[1]
    per = x_ref.shape[1] // TILE
    copies = copy_pieces(x_pieces, x_ref, x_sem, me_ref[0])
    accv_ref[...] = jnp.zeros_like(accv_ref)
    acck_ref[...] = jnp.zeros_like(acck_ref)
    posg_ref[...] = jnp.zeros_like(posg_ref)
    m2_ref[...] = jnp.zeros_like(m2_ref)
    lane = lax.broadcasted_iota(jnp.int32, (TILE, width), 1) // HEAD_DIM
    key_index = lax.broadcasted_iota(jnp.int32, (TILE, TILE), 0)
    factor = 1.0 / math.sqrt(HEAD_DIM)

    def rows(i, _):
        grad = dat_ref[i]
        daxt_ref[...] = by_head((grad * 0.5).astype(bf16), heads)
        natural = flip(grad).astype(bf16)
        for h in range(heads):
            dax_ref[h * TILE : (h + 1) * TILE, :] = jnp.where(lane == h, natural, jnp.zeros_like(natural))
        accq_ref[...] = jnp.zeros_like(accq_ref)
        start = ss_ref[:, lanes(i)]

        def cols(j, _):
            s = dot(kx_ref[j], qxt_ref[i]) + jnp.concatenate([pos_ref[i - j]] * heads, axis=1)
            seen = (key_index + j * TILE) >= start
            s = jnp.where(jnp.concatenate([seen] * heads, axis=1), s, NEG)
            t = jnp.tanh(s)
            u = 1.0 + t
            w = s * u
            ds = dot(v_ref[j], daxt_ref[...]) * (u + w * (1.0 - t))
            low = ds.astype(bf16)
            accv_ref[j] += dot(w.astype(bf16), dax_ref[...])
            acck_ref[j] += dot(low, qm_ref[i])
            accq_ref[...] += dot(kxt_ref[j], low)
            posg_ref[i - j] += sum(ds[:, h * TILE : (h + 1) * TILE] for h in range(heads))
            return 0

        lax.fori_loop(first_ref[i], i + 1, cols, 0)
        dq = jnp.concatenate(
            [
                accq_ref[
                    NTB + h * HEAD_DIM : NTB + (h + 1) * HEAD_DIM, h * TILE : (h + 1) * TILE
                ]
                for h in range(heads)
            ],
            axis=0,
        )
        tp = sum(accq_ref[:NTB, h * TILE : (h + 1) * TILE] for h in range(heads))
        high = tp.astype(bf16)
        rest = (tp - high.astype(f32)).astype(bf16)
        onehot = kx_ref[i, :, :NTB]
        m2_ref[...] += dot(high, onehot) + dot(rest, onehot)
        gp_ref[i, :width] = gu_ref[i]
        gp_ref[i, 2 * width : 3 * width] = (dq * factor * d_ref[i, 2 * width : 3 * width]).astype(bf16)
        return 0

    lax.fori_loop(0, nb, rows, 0)
    for copy in copies:
        copy.wait()
    acc_ref[...] = jnp.zeros_like(acc_ref)

    def tail(i, _):
        gp_ref[i, width : 2 * width] = (flip(accv_ref[i]) * d_ref[i, width : 2 * width]).astype(bf16)
        gp_ref[i, 3 * width :] = (flip(acck_ref[i]) * factor * d_ref[i, 3 * width :]).astype(bf16)
        gp = gp_ref[i]
        acc_ref[...] += dot(gp[width:], x_ref[i // per, lanes(i % per), :])
        gn_ref[pl.ds(pl.multiple_of(i * TILE, TILE), TILE), :] = dot(
            flip(gp).astype(bf16), wt_ref[: 4 * width]
        ).astype(bf16)
        return 0

    lax.fori_loop(0, nb, tail, 0)
    wg_ref[...] = flip(acc_ref[...]).astype(bf16)
    pg_ref[...] = jnp.zeros_like(pg_ref)
    for d in range(nb):
        g = diagonals(posg_ref[d])
        pg_ref[:, d * TILE : (d + 1) * TILE] += g[:, :TILE]
        if d > 0:
            pg_ref[:, (d - 1) * TILE : d * TILE] += g[:, TILE:]
    m2 = m2_ref[...]
    g = diagonals(m2 + jnp.transpose(m2))[:, :NTB]
    zero = lax.broadcasted_iota(jnp.int32, (1, NTB), 1) == 0
    tg_ref[...] = jnp.where(zero, 0.5 * g, g)


def call(kernel, name, in_specs, outs, scratch):
    return pl.pallas_call(
        kernel,
        out_shape=[jax.ShapeDtypeStruct(shape, dtype) for shape, dtype in outs],
        in_specs=in_specs,
        out_specs=[VMEM] * len(outs),
        scratch_shapes=scratch,
        compiler_params=pltpu.CompilerParams(vmem_limit_bytes=60 * 2**20),
        name=name,
    )


def shards(
    tokens,
    cotangent,
    seq_start,
    time_bucket,
    proj_weight,
    out_weight,
    small_params,
    proj_mean,
    proj_square,
    out_mean,
    out_square,
    small_mean,
    small_square,
):
    n_head = lax.axis_size("head")
    n_dp = lax.axis_size("dp")
    me_head, me_dp = lax.axis_index("head"), lax.axis_index("dp")
    here = tokens.shape[0]
    group = here * n_head
    nb = group // TILE
    rows_here, _, width = proj_weight.shape
    heads = width // HEAD_DIM
    me = jnp.stack([me_head, me_dp]).astype(jnp.int32)

    inputs = tokens.astype(f32)
    centred = inputs - jnp.mean(inputs, -1, keepdims=True)
    scale_in = lax.rsqrt(jnp.mean(centred * centred, -1, keepdims=True) + norm_epsilon)
    normed = centred * scale_in
    weights = jnp.concatenate(
        [proj_weight.reshape(rows_here, 4 * width).astype(bf16), out_weight.T.astype(bf16)], axis=1
    )
    x_pieces = gather_head(normed.astype(bf16))
    w_pieces, offsets = gather_dp(weights)
    cot_pieces = gather_head(cotangent)
    first = seq_start[::TILE] // TILE
    starts = seq_start.reshape(1, group)

    big = [pltpu.VMEM((n_head, here, D), bf16)]
    sems = [pltpu.SemaphoreType.DMA((n_head,))]
    attn, dsilu, gate, grad_gated, stat, kx, kxt, qxt, v, qm, pos, wt = call(
        functools.partial(forward_kernel, heads, n_head, offsets),
        "forward",
        [SMEM] * 2 + [ANY] * (2 * n_head + len(w_pieces)) + [VMEM] * 3,
        [
            ((nb, width, TILE), f32),
            ((nb, 4 * width, TILE), f32),
            ((nb, width, TILE), f32),
            ((nb, width, TILE), f32),
            ((nb, 4, TILE), f32),
            ((nb, TILE, NTB + width), bf16),
            ((nb, NTB + width, TILE), bf16),
            ((nb, NTB + width, heads * TILE), bf16),
            ((nb, TILE, width), bf16),
            ((nb, heads * TILE, width), bf16),
            ((nb, TILE, TILE), f32),
            ((5 * width, D), bf16),
        ],
        big
        + big
        + [
            pltpu.VMEM((D, 5 * width), bf16),
            pltpu.VMEM((nb, width, TILE), bf16),
            pltpu.VMEM((width, heads * TILE), f32),
        ]
        + sems
        + sems
        + [pltpu.SemaphoreType.DMA((n_dp,))],
    )(
        me, first, *x_pieces, *cot_pieces, *w_pieces,
        time_bucket.reshape(1, group), starts, small_params.reshape(1, -1),
    )
    stats = [stat] + [swap(stat, "head", k) for k in range(1, n_head)]
    grad_attn, grad_u, branch, wg_early = call(
        functools.partial(middle_kernel, heads, n_head),
        "middle",
        [SMEM] + [ANY] * (2 * n_head) + [VMEM] * (n_head + 5),
        [
            ((nb, width, TILE), f32),
            ((nb, width, TILE), bf16),
            ((group, D), bf16),
            ((D, 2 * width), bf16),
        ],
        big + big + [pltpu.VMEM((width, D), bf16), pltpu.VMEM((2 * width, D), f32)] + sems + sems,
    )(
        me, *x_pieces, *cot_pieces, *stats, attn, dsilu[:, :width], gate, grad_gated, wt,
    )
    mixed = (scatter_head(branch) + small_params[:D] + inputs).astype(bf16)
    early = scatter_dp(wg_early.reshape(n_dp, rows_here, 2 * width))
    wg_late, grad_rows, pos_grad, time_grad = call(
        functools.partial(backward_kernel, heads, n_head),
        "backward",
        [SMEM] * 2 + [ANY] * n_head + [VMEM] * 11,
        [
            ((D, 3 * width), bf16),
            ((group, D), bf16),
            ((1, group), f32),
            ((1, NTB), f32),
        ],
        big
        + [
            pltpu.VMEM((heads * TILE, width), bf16),
            pltpu.VMEM((width, heads * TILE), bf16),
            pltpu.VMEM((nb, TILE, width), f32),
            pltpu.VMEM((nb, TILE, width), f32),
            pltpu.VMEM((NTB + width, heads * TILE), f32),
            pltpu.VMEM((nb, TILE, TILE), f32),
            pltpu.VMEM((NTB, NTB), f32),
            pltpu.VMEM((nb, 4 * width, TILE), bf16),
            pltpu.VMEM((3 * width, D), f32),
        ]
        + sems,
    )(me, first, *x_pieces, wt, dsilu, kx, kxt, qxt, v, qm, pos, grad_attn, grad_u, starts)

    grad_result = cotangent.astype(f32)
    late = scatter_dp(wg_late.reshape(n_dp, rows_here, 3 * width))
    small_local = jnp.concatenate([jnp.sum(grad_result, 0), pos_grad[0], time_grad[0]])
    small_sum = sum_all(small_local)
    grad_small = jnp.concatenate(
        [small_sum[: D + group], jnp.zeros((POS - group,), f32), small_sum[D + group :]]
    )
    normed_grad = scatter_head(grad_rows)
    input_grad = grad_result + scale_in * (
        normed_grad
        - jnp.mean(normed_grad, -1, keepdims=True)
        - normed * jnp.mean(normed_grad * normed, -1, keepdims=True)
    )
    grad_out = early[:, width:].T
    grad_proj = jnp.concatenate([early[:, :width], late], axis=1).reshape(rows_here, 4, width)
    squares = jnp.sum(early * early) + jnp.sum(late * late)
    total = sum_all(squares) + jnp.sum(small_sum * small_sum)
    grad_norm = jnp.sqrt(total)
    factor = jnp.minimum(1.0, clip_norm / (grad_norm + 1e-06))
    new_proj, mean_proj, square_proj = adam_step(
        proj_weight, grad_proj, proj_mean, proj_square, factor, rate_matrix, decay_matrix
    )
    new_out, mean_out, square_out = adam_step(
        out_weight, grad_out, out_mean, out_square, factor, rate_matrix, decay_matrix
    )
    new_small, mean_small, square_small = adam_step(
        small_params, grad_small, small_mean, small_square, factor, rate_small, 0.0
    )
    return (
        mixed,
        input_grad,
        grad_proj,
        grad_out,
        grad_small,
        grad_norm,
        new_proj,
        mean_proj,
        square_proj,
        new_out,
        mean_out,
        square_out,
        new_small,
        mean_small,
        square_small,
    )


def solution(mesh):
    in_specs = (
        P(("dp", "head"), None),
        P(("dp", "head"), None),
        P("dp"),
        P("dp"),
        P("dp", None, "head"),
        P("head", "dp"),
        P(),
        P("dp", None, "head"),
        P("dp", None, "head"),
        P("head", "dp"),
        P("head", "dp"),
        P(),
        P(),
    )
    out_specs = (
        P(("dp", "head"), None),
        P(("dp", "head"), None),
        P("dp", None, "head"),
        P("head", "dp"),
        P(),
        P(),
        P("dp", None, "head"),
        P("dp", None, "head"),
        P("dp", None, "head"),
        P("head", "dp"),
        P("head", "dp"),
        P("head", "dp"),
        P(),
        P(),
        P(),
    )
    return jax.shard_map(shards, mesh=mesh, in_specs=in_specs, out_specs=out_specs, check_vma=False)
```

time: 883 us -> 210 us (0.24)
  local copies, waits for them, and re-layouts: 308 us -> 12.5 us
  matrix products: 162 us -> 0 us
  blocking collectives: 129 us -> 0 us
  waiting for transfers between devices: 184 us -> 56.6 us
  Pallas kernels: 0 us -> 75.1 us
  starting transfers between devices: 0.24 us -> 41.6 us
  other arithmetic: 54.5 us -> 16 us
  loops' own time: 20.3 us -> 0 us
  between operations: 18.5 us -> 7.87 us
    reduce_scatter x4 -> x0, waiting for transfers between devices: 183 us -> none  [the longest x1 65.3 us: shards(): lax.psum_scatter(weight_proj_grad, 'dp', scatter_dimension=0, tiled=True)]
    dot_general x98 -> x0, matrix products: 162 us -> none  [the longest x20 25.9 us: block_scores(): jnp.einsum('qb,kb->qk', lax.dynamic_slice_in_dim(time_split, row_first, B...]
    reshape x32 -> x2, local copies, waits for them, and re-layouts: 94 us -> 1.45 us  [the longest x1 1.41 us: shards(): small_params.reshape(1, -1)]
    pallas_call x0 -> x3, Pallas kernels: none -> 75.1 us  [the longest x1 35.8 us: shards(): call(functools.partial(backward_kernel, heads, n_head), 'backward', [SMEM...]
    all_gather x2 -> x0, blocking collectives: 65.6 us -> none  [the longest x1 33.1 us: shards(): lax.all_gather(proj_weight.astype(jnp.bfloat16), 'dp', axis=0, tiled=True)]
    psum x4 -> x0, blocking collectives: 63 us -> none  [the longest x1 39.8 us: shards(): grad_small = lax.psum(small_local, ('dp', 'head'))]
    ppermute x0 -> x34, waiting for transfers between devices: none -> 56.6 us  [swap(): return lax.ppermute(x, axis, [(i, i ^ k) for i in range(n)])]
    another operation x55 -> x0, local copies, waits for them, and re-layouts: 49.2 us -> none  [the longest x42 37.5 us: toeplitz_tile(): repeated = jnp.tile(extended, row_count + 1)[:row_count * (period + 1)]]
  transfers between devices with their start and end apart: 6 -> 34, of which waited for: 4 -> 16; matrix products, arithmetic and copies ran while one was open for 19% -> 8% of each run, Pallas kernels for 0% -> 0%
where the time goes in v1:
time: 210 us
  Pallas kernels  75.1 us (36%)
  waiting for transfers between devices  56.6 us (27%)
  starting transfers between devices  41.6 us (20%)
  other arithmetic  16 us (8%)
  local copies, waits for them, and re-layouts  12.5 us (6%)
  between operations  7.87 us (4%)
    ppermute x34, waiting for transfers between devices, swap(): return lax.ppermute(x, axis, [(i, i ^ k) for i in range(n)])  56.6 us
    ppermute x34, starting transfers between devices, swap(): return lax.ppermute(x, axis, [(i, i ^ k) for i in range(n)])  41.6 us
    pallas_call x1, Pallas kernels, shards(): call(functools.partial(backward_kernel, heads, n_head), 'backward', [SMEM...  35.8 us
    pallas_call x1, Pallas kernels, shards(): call(functools.partial(forward_kernel, heads, n_head, offsets), 'forward'...  30 us
    pallas_call x1, Pallas kernels, shards(): call(functools.partial(middle_kernel, heads, n_head), 'middle', [SMEM] +...  9.32 us
  transfers between devices with their start and end apart: 34, of which 16 were waited for; matrix products, arithmetic and copies ran while one was open for 8% of the time, Pallas kernels for 0%

profile of v1, /device:TPU:0, one launch (start us, length us, event | category | flops | bytes accessed | tf_op | source)
XLA Modules:
  0.0 209.8 jit_solution(2498506849721061047)
XLA Ops:
  0.7 1.2 convert_reduce_fusion
  2.0 1.3 fusion.8
  3.3 0.6 copy-done.29
  3.9 1.2 fusion.4.refs_0_
  5.1 3.0 %collective-permute-start.1 = (bf16[512,512]{1,0:T(8,128)(2,1)S(1)}, bf16[512,512]{1,0:T(8,128)(2,1)S(1)}, u32[]{:S(2)}, u32[]{:S(2)}) collective-permute-start(bf16[512,512]{1,0:T(8,128)(2,1)S(1)} %fusion.4.refs_0_), channel_id=1, source_target_pairs={{0,2},{1,3},{2,0},{3,1},{4,6},{5,7},{6,4},{7,5},{8,10},{9,11},{10,... | collective-permute-start | bytes 1572872 | tf_op jit(solution)/shard_map/ppermute | solution.py:50
  8.3 3.1 %collective-permute-start.6 = (bf16[64,640]{1,0:T(8,128)(2,1)S(1)}, bf16[64,640]{1,0:T(8,128)(2,1)S(1)}, u32[]{:S(2)}, u32[]{:S(2)}) collective-permute-start(bf16[64,640]{1,0:T(8,128)(2,1)S(1)} %pad_maximum_fusion.3.refs_8_), channel_id=1, source_target_pairs={{0,16},{4,20},{8,24},{12,28},{16,0},{20,4},{24,8},{28,12},{1,17},{... | collective-permute-start | bytes 245768 | tf_op jit(solution)/shard_map/ppermute | solution.py:50
  11.4 3.0 %collective-permute-done.6.refs_9_ = bf16[64,640]{1,0:T(8,128)(2,1)S(1)} collective-permute-done((bf16[64,640]{1,0:T(8,128)(2,1)S(1)}, bf16[64,640]{1,0:T(8,128)(2,1)S(1)}, u32[]{:S(2)}, u32[]{:S(2)}) %collective-permute-start.6) | collective-permute-done | bytes 81952 | tf_op jit(solution)/shard_map/ppermute | solution.py:50
  14.4 0.7 pad_maximum_fusion.1
  15.1 1.4 collective-permute-start.7
  16.5 0.5 collective-permute-start.3
  17.0 3.9 %collective-permute-done.1.refs_2_ = bf16[512,512]{1,0:T(8,128)(2,1)S(1)} collective-permute-done((bf16[512,512]{1,0:T(8,128)(2,1)S(1)}, bf16[512,512]{1,0:T(8,128)(2,1)S(1)}, u32[]{:S(2)}, u32[]{:S(2)}) %collective-permute-start.1) | collective-permute-done | bytes 524320 | tf_op jit(solution)/shard_map/ppermute | solution.py:50
  20.9 10.4 %collective-permute-done.4.refs_6_ = bf16[512,512]{1,0:T(8,128)(2,1)S(1)} collective-permute-done((bf16[512,512]{1,0:T(8,128)(2,1)S(1)}, bf16[512,512]{1,0:T(8,128)(2,1)S(1)}, u32[]{:S(2)}, u32[]{:S(2)}) %collective-permute-start.4) | collective-permute-done | bytes 524320 | tf_op jit(solution)/shard_map/ppermute | solution.py:50
  31.3 1.3 slice.21
  32.6 1.4 reshape.81.refs_14_
  34.1 1.8 collective-permute-start.8
  35.9 0.6 pad_add_fusion.me_ref
  36.5 1.2 and_select_fusion.first_ref
  37.7 6.6 %collective-permute-done.8.refs_11_ = bf16[256,640]{1,0:T(8,128)(2,1)S(1)} collective-permute-done((bf16[256,640]{1,0:T(8,128)(2,1)S(1)}, bf16[256,640]{1,0:T(8,128)(2,1)S(1)}, u32[]{:S(2)}, u32[]{:S(2)}) %collective-permute-start.8) | collective-permute-done | bytes 327712 | tf_op jit(solution)/shard_map/ppermute | solution.py:50
  44.3 0.6 copy-done.15
  45.2 30.0 %forward.1 = (f32[8,128,256]{2,1,0:T(8,128)}, f32[8,512,256]{2,1,0:T(8,128)}, f32[8,128,256]{2,1,0:T(8,128)}, f32[8,128,256]{2,1,0:T(8,128)}, f32[8,4,256]{2,1,0...) custom-call(s32[2]{0:T(128)} %pad_add_fusion.me_ref, ...), custom_call_target="tpu_custom_call" | custom-call | tf_op jit(solution)/shard_map/forward/pallas_call | solution.py:470
  75.3 1.8 collective-permute-start.10
  77.1 2.3 %slice.22.refs_13_ = f32[8,128,256]{2,1,0:T(8,128)} slice(f32[8,512,256]{2,1,0:T(8,128)} %get-tuple-element.37.refs_5_), slice={[0:8], [0:128], [0:256]} | slice | bytes 2097152 | tf_op jit(solution)/shard_map/slice | solution.py:515
  79.5 1.1 collective-permute-done.11.refs_11_
  80.6 0.6 copy-done.28
  81.2 9.3 %middle.1 = (f32[8,128,256]{2,1,0:T(8,128)}, bf16[8,128,256]{2,1,0:T(8,128)(2,1)}, bf16[2048,512]{1,0:T(8,128)(2,1)}, bf16[512,256]{1,0:T(8,128)(2,1)}) custom-call(s32[2]{0:T(128)} %pad_add_fusion.me_ref, bf16[512,512]{1,0:T(8,128)(2,1)} %copy-done.1, bf16[512,512]{1,0:T(8,128)(2,1)} %copy-done.5, bf16[512,512]{1,0:T(8,128)(2,1)} %copy-done.4, ...), custom_call_target="tpu_custom_call" | custom-call | tf_op jit(solution)/shard_map/middle/pallas_call | solution.py:503
  90.5 35.8 %backward.1 = (bf16[512,384]{1,0:T(8,128)(2,1)}, bf16[2048,512]{1,0:T(8,128)(2,1)}, f32[1,2048]{1,0:T(1,128)}, f32[1,128]{1,0:T(1,128)}) custom-call(s32[2]{0:T(128)} %pad_add_fusion.me_ref, s32[8]{0:T(128)} %and_select_fusion.first_ref, bf16[512,512]{1,0:T(8,128)(2,1)} %copy-done.1, bf16[512,512]{1,0:T(8,128)(2,1)} %copy-done.5, ...), custom_call_target="tpu_custom_call" | custom-call | tf_op jit(solution)/shard_map/backward/pallas_call | solution.py:519
  126.3 2.4 %dynamic-slice_bitcast_fusion = bf16[2,512,512]{2,1,0:T(8,128)(2,1)} fusion(bf16[2,2,512,512]{3,2,1,0:T(8,128)(2,1)} %bitcast.92, s32[]{:T(128)S(6)} %select_n.81), kind=kLoop, calls=%fused_computation.22 | loop fusion | bytes 2097156 | tf_op jit(solution)/shard_map/jit(dynamic_index_in_dim)/squeeze | solution.py:102
  129.0 1.1 dynamic-slice_bitcast_fusion.1
  130.0 0.3 collective-permute-start.12
  130.3 1.6 dynamic-slice_bitcast_fusion.3
  131.9 2.1 collective-permute-start.20
  134.0 4.5 %collective-permute-done.16 = bf16[4,64,256]{2,1,0:T(8,128)(2,1)} collective-permute-done((bf16[4,64,256]{2,1,0:T(8,128)(2,1)}, bf16[4,64,256]{2,1,0:T(8,128)(2,1)}, u32[]{:S(2)}, u32[]{:S(2)}) %collective-permute-start.16) | collective-permute-done | bytes 131104 | tf_op jit(solution)/shard_map/ppermute | solution.py:50
  138.6 1.0 fusion.27
  139.6 1.9 convert_add_fusion
  141.6 0.8 collective-permute-start.15
  142.9 1.3 collective-permute-start.13
  144.2 3.7 %collective-permute-start.19 = (bf16[64,256]{1,0:T(8,128)(2,1)S(1)}, bf16[64,256]{1,0:T(8,128)(2,1)S(1)}, u32[]{:S(2)}, u32[]{:S(2)}) collective-permute-start(bf16[64,256]{1,0:T(8,128)(2,1)S(1)} %get-tuple-element.85), channel_id=1, source_target_pairs={{0,24},{4,28},{8,16},{12,20},{16,8},{20,12},{24,0},{28,4},{1,25},{... | collective-permute-start | bytes 98312 | tf_op jit(solution)/shard_map/ppermute | solution.py:50
  147.9 8.7 %collective-permute-done.15 = bf16[512,512]{1,0:T(8,128)(2,1)S(1)} collective-permute-done((bf16[512,512]{1,0:T(8,128)(2,1)S(1)}, bf16[512,512]{1,0:T(8,128)(2,1)S(1)}, u32[]{:S(2)}, u32[]{:S(2)}) %collective-permute-start.15) | collective-permute-done | bytes 524320 | tf_op jit(solution)/shard_map/ppermute | solution.py:50
  156.5 0.5 fusion.13
  157.0 8.3 %collective-permute-done.13 = bf16[512,512]{1,0:T(8,128)(2,1)S(1)} collective-permute-done((bf16[512,512]{1,0:T(8,128)(2,1)S(1)}, bf16[512,512]{1,0:T(8,128)(2,1)S(1)}, u32[]{:S(2)}, u32[]{:S(2)}) %collective-permute-start.13) | collective-permute-done | bytes 524320 | tf_op jit(solution)/shard_map/ppermute | solution.py:50
  165.3 1.7 convert_reduce_fusion.1
  167.3 1.1 collective-permute-done.24
  168.4 0.9 collective-permute-start.25
  169.3 3.7 %collective-permute-start.23 = (bf16[64,384]{1,0:T(8,128)(2,1)S(1)}, bf16[64,384]{1,0:T(8,128)(2,1)S(1)}, u32[]{:S(2)}, u32[]{:S(2)}) collective-permute-start(bf16[64,384]{1,0:T(8,128)(2,1)S(1)} %get-tuple-element.82), channel_id=1, source_target_pairs={{0,24},{4,28},{8,16},{12,20},{16,8},{20,12},{24,0},{28,4},{1,25},{... | collective-permute-start | bytes 147464 | tf_op jit(solution)/shard_map/ppermute | solution.py:50
  173.0 1.7 collective-permute-start.22
  174.7 1.6 collective-permute-start.21
  176.3 0.6 collective-permute-start.26
  176.9 0.6 multiply_reduce_fusion.1
  177.6 2.5 %collective-permute-done.26 = f32[2688]{0:T(1024)S(1)} collective-permute-done((f32[2688]{0:T(1024)S(1)}, f32[2688]{0:T(1024)S(1)}, u32[]{:S(2)}, u32[]{:S(2)}) %collective-permute-start.26) | collective-permute-done | bytes 10784 | tf_op jit(solution)/shard_map/ppermute | solution.py:50
  180.0 0.4 collective-permute-start.27
  180.5 0.6 multiply_reduce_fusion
  181.1 2.6 %collective-permute-done.27 = f32[2688]{0:T(1024)S(1)} collective-permute-done((f32[2688]{0:T(1024)S(1)}, f32[2688]{0:T(1024)S(1)}, u32[]{:S(2)}, u32[]{:S(2)}) %collective-permute-start.27) | collective-permute-done | bytes 10784 | tf_op jit(solution)/shard_map/ppermute | solution.py:50
  185.2 0.9 collective-permute-start.29
  187.0 2.2 %collective-permute-start.30 = (f32[]{:T(128)}, f32[]{:T(128)}, u32[]{:S(2)}, u32[]{:S(2)}) collective-permute-start(f32[]{:T(128)} %add.243), channel_id=1, source_target_pairs={{0,2},{1,3},{2,0},{3,1},{4,6},{5,7},{6,4},{7,5},{8,10},{9,11},{10,... | collective-permute-start | bytes 20 | tf_op jit(solution)/shard_map/ppermute | solution.py:50
  189.3 1.3 collective-permute-done.30
  191.3 2.0 collective-permute-start.31
  193.3 1.6 collective-permute-done.31
  195.5 2.9 %collective-permute-start.32 = (f32[]{:T(128)}, f32[]{:T(128)}, u32[]{:S(2)}, u32[]{:S(2)}) collective-permute-start(f32[]{:T(128)} %add.245), channel_id=1, source_target_pairs={{0,8},{4,12},{8,0},{12,4},{16,24},{20,28},{24,16},{28,20},{1,9},{5... | collective-permute-start | bytes 20 | tf_op jit(solution)/shard_map/ppermute | solution.py:50
  198.5 0.6 collective-permute-done.32
  199.8 4.2 %collective-permute-start.33 = (f32[]{:T(128)}, f32[]{:T(128)}, u32[]{:S(2)}, u32[]{:S(2)}) collective-permute-start(f32[]{:T(128)} %add.246), channel_id=1, source_target_pairs={{0,16},{4,20},{8,24},{12,28},{16,0},{20,4},{24,8},{28,12},{1,17},{... | collective-permute-start | bytes 20 | tf_op jit(solution)/shard_map/ppermute | solution.py:50
  205.0 0.6 multiply_reduce_fusion.2
  206.3 0.7 multiply_subtract_fusion.2
  207.0 0.9 multiply_subtract_fusion
  208.0 0.7 multiply_subtract_fusion.1
  (126 shorter events, 2.3 us)
Async XLA Ops:
  0.6 7.5 %copy-start.2 = (bf16[512,512]{1,0:T(8,128)(2,1)S(1)}, bf16[512,512]{1,0:T(8,128)(2,1)}, u32[]{:S(2)}) copy-start(bf16[512,512]{1,0:T(8,128)(2,1)} %refs_4_.3) | copy-start | bytes 1572868
  0.7 7.6 %copy-start.11 = (f32[64,4,128]{2,1,0:T(4,128)S(1)}, f32[64,4,128]{2,1,0:T(4,128)}, u32[]{:S(2)}) copy-start(f32[64,4,128]{2,1,0:T(4,128)} %param.17) | copy-start | bytes 393220
  0.7 7.6 %copy-start.20 = (f32[128,64]{0,1:T(8,128)S(1)}, f32[128,64]{0,1:T(8,128)}, u32[]{:S(2)}) copy-start(f32[128,64]{0,1:T(8,128)} %param.18) | copy-start | bytes 98308
  1.9 1.3 copy-start.22
  5.1 39.1 %copy-start.1 = (bf16[512,512]{1,0:T(8,128)(2,1)}, bf16[512,512]{1,0:T(8,128)(2,1)S(1)}, u32[]{:S(2)}) copy-start(bf16[512,512]{1,0:T(8,128)(2,1)S(1)} %fusion.4.refs_0_) | copy-start | bytes 1572868
  5.1 15.8 %collective-permute-start.1 = (bf16[512,512]{1,0:T(8,128)(2,1)S(1)}, bf16[512,512]{1,0:T(8,128)(2,1)S(1)}, u32[]{:S(2)}, u32[]{:S(2)}) collective-permute-start(bf16[512,512]{1,0:T(8,128)(2,1)S(1)} %fusion.4.refs_0_), channel_id=1, source_target_pairs={{0,2},{1,3},{2,0},{3,1},{4,6},{5,7},{6,4},{7,5},{8,10},{9,11},{10,... | collective-permute-start | bytes 1572872 | tf_op jit(solution)/shard_map/ppermute | solution.py:50
  8.2 23.2 %collective-permute-start.4 = (bf16[512,512]{1,0:T(8,128)(2,1)S(1)}, bf16[512,512]{1,0:T(8,128)(2,1)S(1)}, u32[]{:S(2)}, u32[]{:S(2)}) collective-permute-start(bf16[512,512]{1,0:T(8,128)(2,1)S(1)} %copy-done.2), channel_id=1, source_target_pairs={{0,2},{1,3},{2,0},{3,1},{4,6},{5,7},{6,4},{7,5},{8,10},{9,11},{10,... | collective-permute-start | bytes 1572872 | tf_op jit(solution)/shard_map/ppermute | solution.py:50
  8.3 36.0 %copy-start.16 = (bf16[64,640]{1,0:T(8,128)(2,1)}, bf16[64,640]{1,0:T(8,128)(2,1)S(1)}, u32[]{:S(2)}) copy-start(bf16[64,640]{1,0:T(8,128)(2,1)S(1)} %pad_maximum_fusion.3.refs_8_) | copy-start | bytes 245764
  8.3 6.1 %collective-permute-start.6 = (bf16[64,640]{1,0:T(8,128)(2,1)S(1)}, bf16[64,640]{1,0:T(8,128)(2,1)S(1)}, u32[]{:S(2)}, u32[]{:S(2)}) collective-permute-start(bf16[64,640]{1,0:T(8,128)(2,1)S(1)} %pad_maximum_fusion.3.refs_8_), channel_id=1, source_target_pairs={{0,16},{4,20},{8,24},{12,28},{16,0},{20,4},{24,8},{28,12},{1,17},{... | collective-permute-start | bytes 245768 | tf_op jit(solution)/shard_map/ppermute | solution.py:50
  14.4 29.9 %copy-start.9 = (bf16[64,640]{1,0:T(8,128)(2,1)}, bf16[64,640]{1,0:T(8,128)(2,1)S(1)}, u32[]{:S(2)}) copy-start(bf16[64,640]{1,0:T(8,128)(2,1)S(1)} %collective-permute-done.6.refs_9_) | copy-start | bytes 245764
  15.1 18.9 %collective-permute-start.7 = (bf16[128,640]{1,0:T(8,128)(2,1)}, bf16[128,640]{1,0:T(8,128)(2,1)S(1)}, u32[]{:S(2)}, u32[]{:S(2)}) collective-permute-start(bf16[128,640]{1,0:T(8,128)(2,1)} %pad_maximum_fusion.1), channel_id=1, source_target_pairs={{0,8},{4,12},{8,0},{12,4},{16,24},{20,28},{24,16},{28,20},{1,9},{5... | collective-permute-start | bytes 491528 | tf_op jit(solution)/shard_map/ppermute | solution.py:50
  16.5 21.1 %collective-permute-start = (bf16[512,512]{1,0:T(8,128)(2,1)S(1)}, bf16[512,512]{1,0:T(8,128)(2,1)S(1)}, u32[]{:S(2)}, u32[]{:S(2)}) collective-permute-start(bf16[512,512]{1,0:T(8,128)(2,1)S(1)} %fusion.4.refs_0_), channel_id=1, source_target_pairs={{0,1},{1,0},{2,3},{3,2},{4,5},{5,4},{6,7},{7,6},{8,9},{9,8},{10,11... | collective-permute-start | bytes 1572872 | tf_op jit(solution)/shard_map/ppermute | solution.py:50
  16.5 21.1 %collective-permute-start.3 = (bf16[512,512]{1,0:T(8,128)(2,1)S(1)}, bf16[512,512]{1,0:T(8,128)(2,1)}, u32[]{:S(2)}, u32[]{:S(2)}) collective-permute-start(bf16[512,512]{1,0:T(8,128)(2,1)S(1)} %copy-done.2), channel_id=1, source_target_pairs={{0,1},{1,0},{2,3},{3,2},{4,5},{5,4},{6,7},{7,6},{8,9},{9,8},{10,11... | collective-permute-start | bytes 1572872 | tf_op jit(solution)/shard_map/ppermute | solution.py:50
  20.9 23.4 %copy-start.4 = (bf16[512,512]{1,0:T(8,128)(2,1)}, bf16[512,512]{1,0:T(8,128)(2,1)S(1)}, u32[]{:S(2)}) copy-start(bf16[512,512]{1,0:T(8,128)(2,1)S(1)} %collective-permute-done.1.refs_2_) | copy-start | bytes 1572868
  20.9 23.4 %collective-permute-start.2 = (bf16[512,512]{1,0:T(8,128)(2,1)S(1)}, bf16[512,512]{1,0:T(8,128)(2,1)S(1)}, u32[]{:S(2)}, u32[]{:S(2)}) collective-permute-start(bf16[512,512]{1,0:T(8,128)(2,1)S(1)} %collective-permute-done.1.refs_2_), channel_id=1, source_target_pairs={{0,1},{1,0},{2,3},{3,2},{4,5},{5,4},{6,7},{7,6},{8,9},{9,8},{10,11... | collective-permute-start | bytes 1572872 | tf_op jit(solution)/shard_map/ppermute | solution.py:50
  31.3 13.0 %copy-start.8 = (bf16[512,512]{1,0:T(8,128)(2,1)}, bf16[512,512]{1,0:T(8,128)(2,1)S(1)}, u32[]{:S(2)}) copy-start(bf16[512,512]{1,0:T(8,128)(2,1)S(1)} %collective-permute-done.4.refs_6_) | copy-start | bytes 1572868
  31.3 13.0 %collective-permute-start.5 = (bf16[512,512]{1,0:T(8,128)(2,1)S(1)}, bf16[512,512]{1,0:T(8,128)(2,1)}, u32[]{:S(2)}, u32[]{:S(2)}) collective-permute-start(bf16[512,512]{1,0:T(8,128)(2,1)S(1)} %collective-permute-done.4.refs_6_), channel_id=1, source_target_pairs={{0,1},{1,0},{2,3},{3,2},{4,5},{5,4},{6,7},{7,6},{8,9},{9,8},{10,11... | collective-permute-start | bytes 1572872 | tf_op jit(solution)/shard_map/ppermute | solution.py:50
  34.0 10.3 %copy-start.10 = (bf16[128,640]{1,0:T(8,128)(2,1)}, bf16[128,640]{1,0:T(8,128)(2,1)S(1)}, u32[]{:S(2)}) copy-start(bf16[128,640]{1,0:T(8,128)(2,1)S(1)} %collective-permute-done.7.refs_10_) | copy-start | bytes 491524
  34.1 10.2 %collective-permute-start.8 = (bf16[256,640]{1,0:T(8,128)(2,1)S(1)}, bf16[256,640]{1,0:T(8,128)(2,1)S(1)}, u32[]{:S(2)}, u32[]{:S(2)}) collective-permute-start(bf16[256,640]{1,0:T(8,128)(2,1)S(1)} %pad_maximum_fusion), channel_id=1, source_target_pairs={{0,4},{4,0},{8,12},{12,8},{16,20},{20,16},{24,28},{28,24},{1,5},{5... | collective-permute-start | bytes 983048 | tf_op jit(solution)/shard_map/ppermute | solution.py:50
  37.7 6.7 %copy-start.5 = (bf16[512,512]{1,0:T(8,128)(2,1)}, bf16[512,512]{1,0:T(8,128)(2,1)S(1)}, u32[]{:S(2)}) copy-start(bf16[512,512]{1,0:T(8,128)(2,1)S(1)} %collective-permute-done.refs_1_) | copy-start | bytes 1572868
  75.2 4.3 %collective-permute-start.9 = (f32[8,4,256]{2,1,0:T(4,128)}, f32[8,4,256]{2,1,0:T(4,128)S(1)}, u32[]{:S(2)}, u32[]{:S(2)}) collective-permute-start(f32[8,4,256]{2,1,0:T(4,128)} %get-tuple-element.35.refs_8_), channel_id=1, source_target_pairs={{0,1},{1,0},{2,3},{3,2},{4,5},{5,4},{6,7},{7,6},{8,9},{9,8},{10,11... | collective-permute-start | bytes 98312 | tf_op jit(solution)/shard_map/ppermute | solution.py:50
  75.3 4.2 %collective-permute-start.10 = (f32[8,4,256]{2,1,0:T(4,128)}, f32[8,4,256]{2,1,0:T(4,128)S(1)}, u32[]{:S(2)}, u32[]{:S(2)}) collective-permute-start(f32[8,4,256]{2,1,0:T(4,128)} %get-tuple-element.35.refs_8_), channel_id=1, source_target_pairs={{0,2},{1,3},{2,0},{3,1},{4,6},{5,7},{6,4},{7,5},{8,10},{9,11},{10,... | collective-permute-start | bytes 98312 | tf_op jit(solution)/shard_map/ppermute | solution.py:50
  77.0 3.6 %collective-permute-start.11 = (f32[8,4,256]{2,1,0:T(4,128)}, f32[8,4,256]{2,1,0:T(4,128)S(1)}, u32[]{:S(2)}, u32[]{:S(2)}) collective-permute-start(f32[8,4,256]{2,1,0:T(4,128)} %get-tuple-element.35.refs_8_), channel_id=1, source_target_pairs={{0,3},{1,2},{2,1},{3,0},{4,7},{5,6},{6,5},{7,4},{8,11},{9,10},{10,... | collective-permute-start | bytes 98312 | tf_op jit(solution)/shard_map/ppermute | solution.py:50
  126.3 2.6 %copy-start.7 = (bf16[2048,512]{1,0:T(8,128)(2,1)S(1)}, bf16[2048,512]{1,0:T(8,128)(2,1)}, u32[]{:S(2)}) copy-start(bf16[2048,512]{1,0:T(8,128)(2,1)} %get-tuple-element.41) | copy-start | bytes 6291460
  126.3 5.6 %copy-start.14 = (bf16[512,384]{1,0:T(8,128)(2,1)S(1)}, bf16[512,384]{1,0:T(8,128)(2,1)}, u32[]{:S(2)}) copy-start(bf16[512,384]{1,0:T(8,128)(2,1)} %get-tuple-element.52) | copy-start | bytes 1179652
  128.8 10.8 %collective-permute-start.14 = (bf16[2,512,512]{2,1,0:T(8,128)(2,1)}, bf16[2,512,512]{2,1,0:T(8,128)(2,1)}, u32[]{:S(2)}, u32[]{:S(2)}) collective-permute-start(bf16[2,512,512]{2,1,0:T(8,128)(2,1)} %dynamic-slice_bitcast_fusion), channel_id=1, source_target_pairs={{0,1},{1,0},{2,3},{3,2},{4,5},{5,4},{6,7},{7,6},{8,9},{9,8},{10,11... | collective-permute-start | bytes 3145736 | tf_op jit(solution)/shard_map/ppermute | solution.py:50
  130.0 12.4 %collective-permute-start.12 = (bf16[2,512,512]{2,1,0:T(8,128)(2,1)}, bf16[2,512,512]{2,1,0:T(8,128)(2,1)S(1)}, u32[]{:S(2)}, u32[]{:S(2)}) collective-permute-start(bf16[2,512,512]{2,1,0:T(8,128)(2,1)} %dynamic-slice_bitcast_fusion.1), channel_id=1, source_target_pairs={{0,1},{1,0},{2,3},{3,2},{4,5},{5,4},{6,7},{7,6},{8,9},{9,8},{10,11... | collective-permute-start | bytes 3145736 | tf_op jit(solution)/shard_map/ppermute | solution.py:50
  131.9 6.7 %collective-permute-start.16 = (bf16[4,64,256]{2,1,0:T(8,128)(2,1)}, bf16[4,64,256]{2,1,0:T(8,128)(2,1)}, u32[]{:S(2)}, u32[]{:S(2)}) collective-permute-start(bf16[4,64,256]{2,1,0:T(8,128)(2,1)} %dynamic-slice_bitcast_fusion.3), channel_id=1, source_target_pairs={{0,4},{4,0},{8,12},{12,8},{16,20},{20,16},{24,28},{28,24},{1,5},{5... | collective-permute-start | bytes 393224 | tf_op jit(solution)/shard_map/ppermute | solution.py:50
  131.9 35.3 %collective-permute-start.20 = (bf16[4,64,384]{2,1,0:T(8,128)(2,1)S(1)}, bf16[4,64,384]{2,1,0:T(8,128)(2,1)S(1)}, u32[]{:S(2)}, u32[]{:S(2)}) collective-permute-start(bf16[4,64,384]{2,1,0:T(8,128)(2,1)S(1)} %dynamic-slice_bitcast_fusion.2), channel_id=1, source_target_pairs={{0,4},{4,0},{8,12},{12,8},{16,20},{20,16},{24,28},{28,24},{1,5},{5... | collective-permute-start | bytes 589832 | tf_op jit(solution)/shard_map/ppermute | solution.py:50
  141.5 15.0 %copy-start = (bf16[512,512]{1,0:T(8,128)(2,1)S(1)}, bf16[512,512]{1,0:T(8,128)(2,1)}, u32[]{:S(2)}) copy-start(bf16[512,512]{1,0:T(8,128)(2,1)} %param.13) | copy-start | bytes 1572868
  141.6 15.0 %copy-start.23 = (f32[512]{0:T(512)S(1)}, f32[512]{0:T(512)}, u32[]{:S(2)}) copy-start(f32[512]{0:T(512)} %copy-done.22) | copy-start | bytes 6148
  141.6 15.0 %copy-start.30 = (f32[512]{0:T(512)S(1)}, f32[512]{0:T(512)}, u32[]{:S(2)}) copy-start(f32[512]{0:T(512)} %copy-done.29) | copy-start | bytes 6148
  141.6 14.9 %collective-permute-start.15 = (bf16[512,512]{1,0:T(8,128)(2,1)S(1)}, bf16[512,512]{1,0:T(8,128)(2,1)S(1)}, u32[]{:S(2)}, u32[]{:S(2)}) collective-permute-start(bf16[512,512]{1,0:T(8,128)(2,1)S(1)} %fusion.12), channel_id=1, source_target_pairs={{0,2},{1,3},{2,0},{3,1},{4,6},{5,7},{6,4},{7,5},{8,10},{9,11},{10,... | collective-permute-start | bytes 1572872 | tf_op jit(solution)/shard_map/ppermute | solution.py:50
  142.7 22.5 %copy-start.3 = (bf16[512,512]{1,0:T(8,128)(2,1)S(1)}, bf16[512,512]{1,0:T(8,128)(2,1)}, u32[]{:S(2)}) copy-start(bf16[512,512]{1,0:T(8,128)(2,1)} %refs_4_.3) | copy-start | bytes 1572868
  142.8 22.5 %slice-start = ((f32[8832]{0:T(1024)}), f32[512]{0:T(512)S(1)}, s32[]{:S(2)}) async-start(f32[8832]{0:T(1024)} %param.19), calls=%async_computation | async-start | bytes 4096 | tf_op jit(solution)/shard_map/slice | solution.py:517
  142.9 22.4 %collective-permute-start.13 = (bf16[512,512]{1,0:T(8,128)(2,1)S(1)}, bf16[512,512]{1,0:T(8,128)(2,1)S(1)}, u32[]{:S(2)}, u32[]{:S(2)}) collective-permute-start(bf16[512,512]{1,0:T(8,128)(2,1)S(1)} %fusion.11), channel_id=1, source_target_pairs={{0,2},{1,3},{2,0},{3,1},{4,6},{5,7},{6,4},{7,5},{8,10},{9,11},{10,... | collective-permute-start | bytes 1572872 | tf_op jit(solution)/shard_map/ppermute | solution.py:50
  144.2 30.6 %collective-permute-start.19 = (bf16[64,256]{1,0:T(8,128)(2,1)S(1)}, bf16[64,256]{1,0:T(8,128)(2,1)S(1)}, u32[]{:S(2)}, u32[]{:S(2)}) collective-permute-start(bf16[64,256]{1,0:T(8,128)(2,1)S(1)} %get-tuple-element.85), channel_id=1, source_target_pairs={{0,24},{4,28},{8,16},{12,20},{16,8},{20,12},{24,0},{28,4},{1,25},{... | collective-permute-start | bytes 98312 | tf_op jit(solution)/shard_map/ppermute | solution.py:50
  147.8 28.5 %collective-permute-start.18 = (bf16[64,256]{1,0:T(8,128)(2,1)S(1)}, bf16[64,256]{1,0:T(8,128)(2,1)S(1)}, u32[]{:S(2)}, u32[]{:S(2)}) collective-permute-start(bf16[64,256]{1,0:T(8,128)(2,1)S(1)} %get-tuple-element.86), channel_id=1, source_target_pairs={{0,16},{4,20},{8,24},{12,28},{16,0},{20,4},{24,8},{28,12},{1,17},{... | collective-permute-start | bytes 98312 | tf_op jit(solution)/shard_map/ppermute | solution.py:50
  156.5 20.4 %collective-permute-start.17 = (bf16[64,256]{1,0:T(8,128)(2,1)S(1)}, bf16[64,256]{1,0:T(8,128)(2,1)S(1)}, u32[]{:S(2)}, u32[]{:S(2)}) collective-permute-start(bf16[64,256]{1,0:T(8,128)(2,1)S(1)} %get-tuple-element.84), channel_id=1, source_target_pairs={{0,8},{4,12},{8,0},{12,4},{16,24},{20,28},{24,16},{28,20},{1,9},{5... | collective-permute-start | bytes 98312 | tf_op jit(solution)/shard_map/ppermute | solution.py:50
  165.3 1.8 copy-start.31
  165.3 1.8 copy-start.34
  167.0 39.3 %copy-start.21 = (f32[128,64]{0,1:T(8,128)S(1)}, f32[128,64]{0,1:T(8,128)}, u32[]{:S(2)}) copy-start(f32[128,64]{0,1:T(8,128)} %param.18) | copy-start | bytes 98308
  167.0 39.3 %copy-start.32 = (f32[128,64]{0,1:T(8,128)S(1)}, f32[128,64]{0,1:T(8,128)}, u32[]{:S(2)}) copy-start(f32[128,64]{0,1:T(8,128)} %param.22) | copy-start | bytes 98308
  167.0 39.3 %copy-start.33 = (f32[128,64]{0,1:T(8,128)S(1)}, f32[128,64]{0,1:T(8,128)}, u32[]{:S(2)}) copy-start(f32[128,64]{0,1:T(8,128)} %param.23) | copy-start | bytes 98308
  167.0 40.0 %copy-start.12 = (f32[64,4,128]{2,1,0:T(4,128)S(1)}, f32[64,4,128]{2,1,0:T(4,128)}, u32[]{:S(2)}) copy-start(f32[64,4,128]{2,1,0:T(4,128)} %param.17) | copy-start | bytes 393220
  167.0 40.0 %copy-start.18 = (f32[64,4,128]{2,1,0:T(4,128)S(1)}, f32[64,4,128]{2,1,0:T(4,128)}, u32[]{:S(2)}) copy-start(f32[64,4,128]{2,1,0:T(4,128)} %param.20) | copy-start | bytes 393220
  167.1 40.0 %copy-start.19 = (f32[64,4,128]{2,1,0:T(4,128)S(1)}, f32[64,4,128]{2,1,0:T(4,128)}, u32[]{:S(2)}) copy-start(f32[64,4,128]{2,1,0:T(4,128)} %param.21) | copy-start | bytes 393220
  167.1 40.9 %copy-start.17 = (f32[8832]{0:T(1024)S(1)}, f32[8832]{0:T(1024)}, u32[]{:S(2)}) copy-start(f32[8832]{0:T(1024)} %param.19) | copy-start | bytes 105988
  167.1 40.9 %copy-start.24 = (f32[8832]{0:T(1024)S(1)}, f32[8832]{0:T(1024)}, u32[]{:S(2)}) copy-start(f32[8832]{0:T(1024)} %param.24) | copy-start | bytes 105988
  167.1 40.9 %copy-start.25 = (f32[8832]{0:T(1024)S(1)}, f32[8832]{0:T(1024)}, u32[]{:S(2)}) copy-start(f32[8832]{0:T(1024)} %param.25) | copy-start | bytes 105988
  167.1 1.2 collective-permute-start.24
  168.4 4.6 %collective-permute-start.25 = (f32[2688]{0:T(1024)S(1)}, f32[2688]{0:T(1024)S(1)}, u32[]{:S(2)}, u32[]{:S(2)}) collective-permute-start(f32[2688]{0:T(1024)S(1)} %fusion.21), channel_id=1, source_target_pairs={{0,2},{1,3},{2,0},{3,1},{4,6},{5,7},{6,4},{7,5},{8,10},{9,11},{10,... | collective-permute-start | bytes 32264 | tf_op jit(solution)/shard_map/ppermute | solution.py:50
  169.3 11.2 %collective-permute-start.23 = (bf16[64,384]{1,0:T(8,128)(2,1)S(1)}, bf16[64,384]{1,0:T(8,128)(2,1)S(1)}, u32[]{:S(2)}, u32[]{:S(2)}) collective-permute-start(bf16[64,384]{1,0:T(8,128)(2,1)S(1)} %get-tuple-element.82), channel_id=1, source_target_pairs={{0,24},{4,28},{8,16},{12,20},{16,8},{20,12},{24,0},{28,4},{1,25},{... | collective-permute-start | bytes 147464 | tf_op jit(solution)/shard_map/ppermute | solution.py:50
  173.0 7.5 %collective-permute-start.22 = (bf16[64,384]{1,0:T(8,128)(2,1)S(1)}, bf16[64,384]{1,0:T(8,128)(2,1)S(1)}, u32[]{:S(2)}, u32[]{:S(2)}) collective-permute-start(bf16[64,384]{1,0:T(8,128)(2,1)S(1)} %get-tuple-element.83), channel_id=1, source_target_pairs={{0,16},{4,20},{8,24},{12,28},{16,0},{20,4},{24,8},{28,12},{1,17},{... | collective-permute-start | bytes 147464 | tf_op jit(solution)/shard_map/ppermute | solution.py:50
  174.7 5.7 %collective-permute-start.21 = (bf16[64,384]{1,0:T(8,128)(2,1)S(1)}, bf16[64,384]{1,0:T(8,128)(2,1)S(1)}, u32[]{:S(2)}, u32[]{:S(2)}) collective-permute-start(bf16[64,384]{1,0:T(8,128)(2,1)S(1)} %get-tuple-element.81), channel_id=1, source_target_pairs={{0,8},{4,12},{8,0},{12,4},{16,24},{20,28},{24,16},{28,20},{1,9},{5... | collective-permute-start | bytes 147464 | tf_op jit(solution)/shard_map/ppermute | solution.py:50
  176.3 3.7 %collective-permute-start.26 = (f32[2688]{0:T(1024)S(1)}, f32[2688]{0:T(1024)S(1)}, u32[]{:S(2)}, u32[]{:S(2)}) collective-permute-start(f32[2688]{0:T(1024)S(1)} %add.238), channel_id=1, source_target_pairs={{0,4},{4,0},{8,12},{12,8},{16,20},{20,16},{24,28},{28,24},{1,5},{5... | collective-permute-start | bytes 32264 | tf_op jit(solution)/shard_map/ppermute | solution.py:50
  180.0 3.7 %collective-permute-start.27 = (f32[2688]{0:T(1024)S(1)}, f32[2688]{0:T(1024)S(1)}, u32[]{:S(2)}, u32[]{:S(2)}) collective-permute-start(f32[2688]{0:T(1024)S(1)} %add.239), channel_id=1, source_target_pairs={{0,8},{4,12},{8,0},{12,4},{16,24},{20,28},{24,16},{28,20},{1,9},{5... | collective-permute-start | bytes 32264 | tf_op jit(solution)/shard_map/ppermute | solution.py:50
  183.7 21.2 %collective-permute-start.28 = (f32[2688]{0:T(1024)S(1)}, f32[2688]{0:T(1024)S(1)}, u32[]{:S(2)}, u32[]{:S(2)}) collective-permute-start(f32[2688]{0:T(1024)S(1)} %add.240), channel_id=1, source_target_pairs={{0,16},{4,20},{8,24},{12,28},{16,0},{20,4},{24,8},{28,12},{1,17},{... | collective-permute-start | bytes 32264 | tf_op jit(solution)/shard_map/ppermute | solution.py:50
  183.9 24.8 %copy-start.13 = (f32[64,4,128]{2,1,0:T(4,128)}, f32[64,4,128]{2,1,0:T(4,128)S(1)}, u32[]{:S(2)}) copy-start(f32[64,4,128]{2,1,0:T(4,128)S(1)} %reshape.84) | copy-start | bytes 393220
  185.2 1.2 collective-permute-start.29
  187.0 3.6 %collective-permute-start.30 = (f32[]{:T(128)}, f32[]{:T(128)}, u32[]{:S(2)}, u32[]{:S(2)}) collective-permute-start(f32[]{:T(128)} %add.243), channel_id=1, source_target_pairs={{0,2},{1,3},{2,0},{3,1},{4,6},{5,7},{6,4},{7,5},{8,10},{9,11},{10,... | collective-permute-start | bytes 20 | tf_op jit(solution)/shard_map/ppermute | solution.py:50
  191.3 3.6 %collective-permute-start.31 = (f32[]{:T(128)}, f32[]{:T(128)}, u32[]{:S(2)}, u32[]{:S(2)}) collective-permute-start(f32[]{:T(128)} %add.244), channel_id=1, source_target_pairs={{0,4},{4,0},{8,12},{12,8},{16,20},{20,16},{24,28},{28,24},{1,5},{5... | collective-permute-start | bytes 20 | tf_op jit(solution)/shard_map/ppermute | solution.py:50
  195.5 3.6 %collective-permute-start.32 = (f32[]{:T(128)}, f32[]{:T(128)}, u32[]{:S(2)}, u32[]{:S(2)}) collective-permute-start(f32[]{:T(128)} %add.245), channel_id=1, source_target_pairs={{0,8},{4,12},{8,0},{12,4},{16,24},{20,28},{24,16},{28,20},{1,9},{5... | collective-permute-start | bytes 20 | tf_op jit(solution)/shard_map/ppermute | solution.py:50
  199.8 4.5 %collective-permute-start.33 = (f32[]{:T(128)}, f32[]{:T(128)}, u32[]{:S(2)}, u32[]{:S(2)}) collective-permute-start(f32[]{:T(128)} %add.246), channel_id=1, source_target_pairs={{0,16},{4,20},{8,24},{12,28},{16,0},{20,4},{24,8},{28,12},{1,17},{... | collective-permute-start | bytes 20 | tf_op jit(solution)/shard_map/ppermute | solution.py:50
  (6 other events, 5.1 us)

commit v2 on v1

v2 whole, which is shorter than its diff:
```python
import functools
import math

import jax
import jax.numpy as jnp
from jax import lax
from jax.experimental import pallas as pl
from jax.experimental.pallas import tpu as pltpu
from jax.sharding import PartitionSpec as P

D = 512
HEAD_DIM = 64
HD = 512
POS = 8192
NTB = 128
STEP = 10
TILE = 256
NEG = -1e9

norm_epsilon = 1e-06
adam_epsilon = 1e-08
beta_one = 0.9
beta_two = 0.999
clip_norm = 1.0
rate_matrix = 0.05
rate_small = 0.3
decay_matrix = 0.1

f32 = jnp.float32
bf16 = jnp.bfloat16
VMEM = pl.BlockSpec(memory_space=pltpu.VMEM)
SMEM = pl.BlockSpec(memory_space=pltpu.SMEM)
ANY = pl.BlockSpec(memory_space=pl.ANY)


def adam_step(weight, grad, first, second, factor, rate, decay):
    clipped = grad * factor
    first_new = beta_one * first + (1.0 - beta_one) * clipped
    second_new = beta_two * second + (1.0 - beta_two) * clipped * clipped
    update = (
        first_new
        / (1.0 - beta_one**STEP)
        / (jnp.sqrt(second_new / (1.0 - beta_two**STEP)) + adam_epsilon)
    )
    return (weight - rate * (update + decay * weight), first_new, second_new)


def swap(x, axis, k):
    n = lax.axis_size(axis)
    return lax.ppermute(x, axis, [(i, i ^ k) for i in range(n)])


def gather_head(x):
    n = lax.axis_size("head")
    pieces = [None] * n
    pieces[0] = x
    for k in range(2, n, 2):
        pieces[k] = swap(x, "head", k)
    pieces[1] = swap(x, "head", 1)
    for k in range(2, n, 2):
        pieces[k + 1] = swap(pieces[k], "head", 1)
    return pieces


def gather_dp(x):
    n = lax.axis_size("dp")
    arrays, offsets = [x], [[0]]
    k = n // 2
    while k:
        arrays.append(swap(jnp.concatenate(arrays, 0) if len(arrays) > 1 else x, "dp", k))
        offsets.append([o ^ k for group in offsets for o in group])
        k //= 2
    return arrays, offsets


def split_dp(n):
    low = 2 ** ((n.bit_length() - 1) // 2)
    return n // low, low


def scatter_dp(parts):
    n = lax.axis_size("dp")
    high, low = split_dp(n)
    row = lax.axis_index("dp") // low
    total = parts[0].astype(f32)
    for k in range(1, low):
        total = total + swap(parts[k], "dp", k).astype(f32)
    narrow = total.astype(bf16)
    mine = lax.dynamic_index_in_dim(total, row, 0, False)
    for k in range(1, high):
        sent = lax.dynamic_index_in_dim(narrow, row ^ k, 0, False)
        mine = mine + swap(sent, "dp", k * low).astype(f32)
    return mine


def scatter_head(keep, send):
    n = lax.axis_size("head")
    chip = lax.axis_index("head") // 2
    total = keep.astype(f32) + swap(send, "head", 1).astype(f32)
    narrow = total.astype(bf16)
    mine = lax.dynamic_index_in_dim(total, chip, 0, False)
    for k in range(1, n // 2):
        sent = lax.dynamic_index_in_dim(narrow, chip ^ k, 0, False)
        mine = mine + swap(sent, "head", 2 * k).astype(f32)
    return mine


def dot(a, b):
    return lax.dot_general(a, b, (((1,), (0,)), ((), ())), preferred_element_type=f32)


def dot_nt(a, b):
    return lax.dot_general(a, b, (((1,), (1,)), ((), ())), preferred_element_type=f32)


def flip(a):
    return jnp.transpose(a.astype(f32))


def lanes(i):
    return pl.ds(pl.multiple_of(i * TILE, TILE), TILE)


def by_head(block, heads):
    zero = jnp.zeros((HEAD_DIM, block.shape[1]), block.dtype)
    return jnp.concatenate(
        [
            jnp.concatenate(
                [block[g * HEAD_DIM : (g + 1) * HEAD_DIM] if g == h else zero for g in range(heads)], axis=0
            )
            for h in range(heads)
        ],
        axis=1,
    )


def own_rows(block, heads):
    return jnp.concatenate(
        [block[h * HEAD_DIM : (h + 1) * HEAD_DIM, h * TILE : (h + 1) * TILE] for h in range(heads)], axis=0
    )


def own_lanes(block, heads):
    lane = lax.broadcasted_iota(jnp.int32, block.shape, 1) // HEAD_DIM
    return jnp.concatenate([jnp.where(lane == h, block, jnp.zeros_like(block)) for h in range(heads)], axis=0)


def diagonals(x):
    rows, cols = x.shape
    z = jnp.concatenate([x, jnp.zeros((rows, cols), f32)], axis=1)
    total = z[:8]
    for q in range(1, rows // 8):
        total = total + pltpu.roll(z[8 * q : 8 * q + 8], 2 * cols - 8 * q, 1)
    g = total[0:1]
    for r in range(1, 8):
        g = g + pltpu.roll(total, 2 * cols - r, 1)[r : r + 1]
    return g


def start_all(copies):
    for copy in copies:
        copy.start()
    return copies


def wait_all(copies):
    for copy in copies:
        copy.wait()


def piece_copies(pieces, target, sems, me):
    return [pltpu.make_async_copy(piece, target.at[me ^ k], sems.at[k]) for k, piece in enumerate(pieces)]


def row_copies(pieces, offsets, target, sems, me):
    copies = []
    for piece, group in zip(pieces, offsets):
        rows = piece.shape[0] // len(group)
        for at, offset in enumerate(group):
            start = pl.multiple_of((me ^ offset) * rows, 16)
            copies.append(
                pltpu.make_async_copy(
                    piece.at[pl.ds(at * rows, rows)], target.at[pl.ds(start, rows)], sems.at[len(copies)]
                )
            )
    return copies


def prepare_kernel(tb_ref, small_ref, pos_ref, oh_ref, oht_ref, trow_ref):
    nb = pos_ref.shape[0]
    for d in range(nb):
        here = small_ref[:, D + d * TILE : D + (d + 1) * TILE]
        before = here if d == 0 else small_ref[:, D + (d - 1) * TILE : D + d * TILE]
        row = jnp.concatenate([here, before], axis=1) * 0.5
        tile = pltpu.roll(
            jnp.broadcast_to(row, (TILE, 2 * TILE)), 0, 1, stride=1, stride_axis=0
        )[:, :TILE]
        if d == 0:
            b = lax.broadcasted_iota(jnp.int32, (TILE, TILE), 0)
            a = lax.broadcasted_iota(jnp.int32, (TILE, TILE), 1)
            tile = jnp.where(b <= a, tile, NEG)
        pos_ref[d] = tile
    table = small_ref[:, D + POS : D + POS + NTB]
    row = jnp.concatenate([table, table], axis=1)
    upper = pltpu.roll(jnp.broadcast_to(row, (NTB, 2 * NTB)), 0, 1, stride=1, stride_axis=0)[:, :NTB]
    a = lax.broadcasted_iota(jnp.int32, (NTB, NTB), 0)
    b = lax.broadcasted_iota(jnp.int32, (NTB, NTB), 1)
    upper = jnp.where(b >= a, upper, 0.0)
    square = (jnp.where(b > a, upper, jnp.transpose(upper)) * 0.5).astype(bf16)

    def block(i, _):
        onehot = (lax.broadcasted_iota(jnp.int32, (NTB, TILE), 0) == tb_ref[:, lanes(i)]).astype(f32)
        low = onehot.astype(bf16)
        oht_ref[i] = low
        oh_ref[i] = flip(onehot).astype(bf16)
        trow_ref[i] = dot(square, low).astype(bf16)
        return 0

    lax.fori_loop(0, nb, block, 0)


def forward_kernel(heads, n_head, offsets, me_ref, first_ref, *refs):
    refs = list(refs)
    take = lambda count: [refs.pop(0) for _ in range(count)]
    x_pieces, w_pieces = take(n_head), take(len(offsets))
    oh_in, oht_in, trow_in, pos_in, ss_ref = take(5)
    attn_ref = refs.pop(0)
    outs = take(8)
    staged = take(8)
    xn_ref, d_ref, kx_ref, kxt_ref, qxt_ref, v_ref, qm_ref, wt_ref = staged
    x_ref, w_ref, vt_ref, pos_ref, acc_ref, x_sem, w_sem, t_sem, out_sem = refs
    nb, width = attn_ref.shape[0], attn_ref.shape[1]
    per = x_ref.shape[1] // TILE
    needed = start_all(
        row_copies(w_pieces, offsets, w_ref, w_sem, me_ref[1]) + piece_copies(x_pieces, x_ref, x_sem, me_ref[0])
    )
    tables = start_all(
        [
            pltpu.make_async_copy(oh_in, kx_ref.at[:, :, :NTB], t_sem.at[0]),
            pltpu.make_async_copy(oht_in, kxt_ref.at[:, :NTB], t_sem.at[1]),
            pltpu.make_async_copy(pos_in, pos_ref, t_sem.at[2]),
        ]
        + [
            pltpu.make_async_copy(trow_in, qxt_ref.at[:, :NTB, h * TILE : (h + 1) * TILE], t_sem.at[3 + h])
            for h in range(heads)
        ]
    )
    wait_all(needed)
    wt_ref[...] = flip(w_ref[...]).astype(bf16)

    def project(i, _):
        x = x_ref[i // per, lanes(i % per), :].astype(f32)
        x = x - jnp.sum(x, axis=1, keepdims=True) / D
        x = (x * lax.rsqrt(jnp.sum(x * x, axis=1, keepdims=True) / D + norm_epsilon)).astype(bf16)
        xn_ref[i] = x
        p = dot_nt(wt_ref[...], x)
        sg = 0.5 + 0.5 * jnp.tanh(0.5 * p)
        act = p * sg
        d_ref[i] = sg + act * (1.0 - sg)
        vt = act[:width]
        vt_ref[i] = vt.astype(bf16)
        v_ref[i] = flip(vt).astype(bf16)
        qt = act[width : 2 * width].astype(bf16)
        kt = act[2 * width :]
        kxt_ref[i, NTB:] = kt.astype(bf16)
        kx_ref[i, :, NTB:] = flip(kt).astype(bf16)
        qs = (qt.astype(f32) * (0.5 / math.sqrt(HEAD_DIM))).astype(bf16)
        qxt_ref[i, NTB:] = by_head(qs, heads)
        qm_ref[i] = own_lanes(flip(qt).astype(bf16), heads)
        return 0

    lax.fori_loop(0, nb, project, 0)
    wait_all(tables)
    leaving = start_all(
        [pltpu.make_async_copy(a, b, out_sem.at[k]) for k, (a, b) in enumerate(zip(staged, outs))]
    )
    key_index = lax.broadcasted_iota(jnp.int32, (TILE, TILE), 0)

    def rows(i, _):
        acc_ref[...] = jnp.zeros_like(acc_ref)
        start = ss_ref[:, lanes(i)]

        def cols(j, _):
            s = dot(kx_ref[j], qxt_ref[i]) + jnp.concatenate([pos_ref[i - j]] * heads, axis=1)
            seen = (key_index + j * TILE) >= start
            s = jnp.where(jnp.concatenate([seen] * heads, axis=1), s, NEG)
            w = (s + s * jnp.tanh(s)).astype(bf16)
            acc_ref[...] += dot(vt_ref[j], w)
            return 0

        lax.fori_loop(first_ref[i], i + 1, cols, 0)
        attn_ref[i] = own_rows(acc_ref[...], heads)
        return 0

    lax.fori_loop(0, nb, rows, 0)
    wait_all(leaving)


def gate_kernel(n_head, offsets, per, me_ref, *refs):
    refs = list(refs)
    take = lambda count: [refs.pop(0) for _ in range(count)]
    cot_pieces, w_pieces = take(n_head), take(len(offsets))
    attn_ref, xn_ref = take(2)
    gate_ref, ga_ref, gd_ref, stat_ref, cot_out, wt_ref, gb_ref = take(7)
    cot_ref, w_ref, cot_sem, w_sem = refs
    i = pl.program_id(0)
    width = attn_ref.shape[1]

    @pl.when(i == 0)
    def _():
        needed = start_all(row_copies(w_pieces, offsets, w_ref, w_sem, me_ref[1]))
        copies = start_all(piece_copies(cot_pieces, cot_ref, cot_sem, me_ref[0]))
        wait_all(needed)
        wt_ref[...] = flip(w_ref[...]).astype(bf16)
        wait_all(copies)
        gb_ref[...] = jnp.sum(cot_ref[me_ref[0]].astype(f32), axis=0, keepdims=True)

    cot = cot_ref[i // per, lanes(i % per), :]
    cot_out[0] = cot
    p = dot_nt(wt_ref[:width], xn_ref[0])
    sg = 0.5 + 0.5 * jnp.tanh(0.5 * p)
    gate = p * sg
    gg = dot_nt(wt_ref[width:], cot)
    grad = gg * gate
    gate_ref[0] = gate
    ga_ref[0] = grad
    gd_ref[0] = gg * (sg + gate * (1.0 - sg))
    at = attn_ref[0]
    mean = jnp.sum(at, axis=0, keepdims=True) / width
    centred = at - mean
    stat_ref[0] = jnp.concatenate(
        [
            mean,
            jnp.sum(centred * centred, axis=0, keepdims=True),
            jnp.sum(grad, axis=0, keepdims=True),
            jnp.sum(grad * centred, axis=0, keepdims=True),
        ],
        axis=0,
    )


def send_rows(i, per, me, block_ref, keep, send, sem):
    device = i // per
    rows = lanes(i % per)
    mine = device % 2 == me % 2

    @pl.when(mine)
    def _():
        pltpu.make_async_copy(block_ref, keep.at[device // 2, rows], sem).start()

    @pl.when(jnp.logical_not(mine))
    def _():
        pltpu.make_async_copy(block_ref, send.at[device // 2, rows], sem).start()


def middle_kernel(heads, n_head, per, me_ref, *refs):
    refs = list(refs)
    take = lambda count: [refs.pop(0) for _ in range(count)]
    stats = take(n_head)
    attn_ref, gate_ref, ga_ref, gd_ref, xn_ref, cot_ref, wt_ref = take(7)
    dax_ref, daxt_ref, gun_ref, keep, send = take(5)
    parts = take(split_dp_count(refs))
    branch_ref, acc_ref, wg_ref, sem, part_sem = refs
    i = pl.program_id(0)
    nb = branch_ref.shape[0]
    width = attn_ref.shape[1]

    @pl.when(i == 0)
    def _():
        acc_ref[...] = jnp.zeros_like(acc_ref)

    st = [s[0] for s in stats]
    mean = sum(p[0:1] for p in st) / n_head
    spread = sum(p[1:2] + width * (p[0:1] - mean) * (p[0:1] - mean) for p in st)
    scale = lax.rsqrt(spread / HD + norm_epsilon)
    first = sum(p[2:3] for p in st) / HD
    second = scale * sum(p[3:4] + (p[0:1] - mean) * p[2:3] for p in st) / HD
    normed = (attn_ref[0] - mean) * scale
    gated = (normed * gate_ref[0]).astype(bf16)
    grad = scale * (ga_ref[0] - first - normed * second)
    dax_ref[0] = own_lanes(flip(grad).astype(bf16), heads)
    daxt_ref[0] = by_head((grad * 0.5).astype(bf16), heads)
    gu = (gd_ref[0] * normed).astype(bf16)
    gun_ref[0] = flip(gu).astype(bf16)
    branch_ref[i] = dot(flip(gated).astype(bf16), wt_ref[width:]).astype(bf16)
    send_rows(i, per, me_ref[0], branch_ref.at[i], keep, send, sem.at[i])
    acc_ref[:width] += dot(gu, xn_ref[0])
    acc_ref[width:] += dot(gated, cot_ref[0])

    @pl.when(i == nb - 1)
    def _():
        wg_ref[...] = flip(acc_ref[...]).astype(bf16)
        send_parts(wg_ref, parts, part_sem, me_ref[1])
        for k in range(nb):
            pltpu.make_async_copy(branch_ref.at[k], keep.at[0, pl.ds(0, TILE)], sem.at[k]).wait()


def split_dp_count(refs):
    return len(refs) - 5


def send_parts(wg_ref, parts, sem, me):
    low = len(parts)
    high = parts[0].shape[0]
    rows = parts[0].shape[1]
    for p in range(high * low):
        block = wg_ref.at[pl.ds(p * rows, rows)]
        for k in range(low):

            @pl.when((p % low) ^ (me % low) == k)
            def _():
                pltpu.make_async_copy(block, parts[k].at[p // low], sem.at[p]).start()

    for p in range(high * low):
        pltpu.make_async_copy(wg_ref.at[pl.ds(p * rows, rows)], parts[0].at[p // low], sem.at[p]).wait()


def backward_kernel(heads, n_dp, extra, me_ref, first_ref, *refs):
    refs = list(refs)
    take = lambda count: [refs.pop(0) for _ in range(count)]
    ins = take(8)
    d_in, xn_in, ss_ref, gb_ref = take(4)
    gp_out = refs.pop(0)
    parts = take(split_dp(n_dp)[1])
    held = take(8)
    kx_ref, kxt_ref, qxt_ref, v_ref, qm_ref, dax_ref, daxt_ref, pos_ref = held
    d_ref, xn_ref = take(2)
    accv_ref, acck_ref, accq_ref, posg_ref, m2_ref, gpq_ref, acc_ref, wg_ref, small_ref = take(9)
    in_sem, late_sem, part_sem = refs
    nb, width = v_ref.shape[0], v_ref.shape[2]
    for i in range(nb):
        for k in range(8):
            pltpu.make_async_copy(ins[k].at[i], held[k].at[i], in_sem.at[k, i]).start()
    late = start_all(
        [
            pltpu.make_async_copy(d_in, d_ref, late_sem.at[0]),
            pltpu.make_async_copy(xn_in, xn_ref, late_sem.at[1]),
        ]
    )
    accv_ref[...] = jnp.zeros_like(accv_ref)
    acck_ref[...] = jnp.zeros_like(acck_ref)
    posg_ref[...] = jnp.zeros_like(posg_ref)
    m2_ref[...] = jnp.zeros_like(m2_ref)
    key_index = lax.broadcasted_iota(jnp.int32, (TILE, TILE), 0)
    factor = 1.0 / math.sqrt(HEAD_DIM)

    def rows(i, _):
        for k in range(8):
            pltpu.make_async_copy(ins[k].at[i], held[k].at[i], in_sem.at[k, i]).wait()
        accq_ref[...] = jnp.zeros_like(accq_ref)
        start = ss_ref[:, lanes(i)]

        def cols(j, _):
            s = dot(kx_ref[j], qxt_ref[i]) + jnp.concatenate([pos_ref[i - j]] * heads, axis=1)
            seen = (key_index + j * TILE) >= start
            s = jnp.where(jnp.concatenate([seen] * heads, axis=1), s, NEG)
            t = jnp.tanh(s)
            u = 1.0 + t
            w = s * u
            ds = dot(v_ref[j], daxt_ref[i]) * (u + w * (1.0 - t))
            low = ds.astype(bf16)
            accv_ref[j] += dot(w.astype(bf16), dax_ref[i])
            acck_ref[j] += dot(low, qm_ref[i])
            accq_ref[...] += dot(kxt_ref[j], low)
            posg_ref[i - j] += sum(ds[:, h * TILE : (h + 1) * TILE] for h in range(heads))
            return 0

        lax.fori_loop(first_ref[i], i + 1, cols, 0)
        gpq_ref[i] = own_rows(accq_ref[NTB:], heads)
        tp = sum(accq_ref[:NTB, h * TILE : (h + 1) * TILE] for h in range(heads))
        high = tp.astype(bf16)
        rest = (tp - high.astype(f32)).astype(bf16)
        onehot = kx_ref[i, :, :NTB]
        m2_ref[...] += dot(high, onehot) + dot(rest, onehot)
        return 0

    lax.fori_loop(0, nb, rows, 0)
    wait_all(late)
    acc_ref[...] = jnp.zeros_like(acc_ref)

    def tail(i, _):
        gp = jnp.concatenate([flip(accv_ref[i]), gpq_ref[i] * factor, flip(acck_ref[i]) * factor], axis=0)
        gp = (gp * d_ref[i]).astype(bf16)
        gp_out[i] = flip(gp).astype(bf16)
        acc_ref[...] += dot(gp, xn_ref[i])
        return 0

    lax.fori_loop(0, nb, tail, 0)
    small_ref[...] = jnp.zeros_like(small_ref)
    small_ref[:, :D] = gb_ref[...]
    for d in range(nb):
        g = diagonals(posg_ref[d])
        small_ref[:, D + d * TILE : D + (d + 1) * TILE] += g[:, :TILE]
        if d > 0:
            small_ref[:, D + (d - 1) * TILE : D + d * TILE] += g[:, TILE:]
    m2 = m2_ref[...]
    g = diagonals(m2 + jnp.transpose(m2))[:, :NTB]
    zero = lax.broadcasted_iota(jnp.int32, (1, NTB), 1) == 0
    at = D + nb * TILE
    small_ref[:, at : at + NTB] = jnp.where(zero, 0.5 * g, g)
    step = D // n_dp
    grads = flip(acc_ref[...])
    for p in range(n_dp):
        here = jnp.concatenate(
            [small_ref[:, (p * extra + r) * 128 : (p * extra + r + 1) * 128] for r in range(extra)], axis=0
        )
        high = here.astype(bf16).astype(f32)
        block = jnp.concatenate([high, here - high, jnp.zeros((16 - 2 * extra, 128), f32)], axis=0)
        wg_ref[p * (step + 16) : p * (step + 16) + step] = grads[p * step : (p + 1) * step].astype(bf16)
        wg_ref[p * (step + 16) + step : (p + 1) * (step + 16)] = jnp.concatenate(
            [block, jnp.zeros((16, 3 * width - 128), f32)], axis=1
        ).astype(bf16)
    send_parts(wg_ref, parts, part_sem, me_ref[1])


def input_kernel(per, me_ref, gp_ref, gun_ref, wt_ref, wtu_ref, keep, send, rows_ref, sem):
    i = pl.program_id(0)
    nb = rows_ref.shape[0]
    width = gun_ref.shape[2]
    rows_ref[i] = (dot(gp_ref[0], wt_ref[...]) + dot(gun_ref[0], wtu_ref[:width])).astype(bf16)
    send_rows(i, per, me_ref[0], rows_ref.at[i], keep, send, sem.at[i])

    @pl.when(i == nb - 1)
    def _():
        for k in range(nb):
            pltpu.make_async_copy(rows_ref.at[k], keep.at[0, pl.ds(0, TILE)], sem.at[k]).wait()


def call(kernel, name, in_specs, outs, scratch, us, **more):
    return pl.pallas_call(
        kernel,
        out_shape=[jax.ShapeDtypeStruct(shape, dtype) for shape, dtype, _ in outs],
        in_specs=in_specs,
        out_specs=[spec for _, _, spec in outs],
        scratch_shapes=scratch,
        compiler_params=pltpu.CompilerParams(vmem_limit_bytes=60 * 2**20),
        cost_estimate=pl.CostEstimate(flops=int(us * 1e9), bytes_accessed=int(us * 3e6), transcendentals=0),
        name=name,
        **more,
    )


def block(shape):
    return pl.BlockSpec((1,) + tuple(shape[1:]), lambda i: (i,) + (0,) * (len(shape) - 1))


def shards(
    tokens,
    cotangent,
    seq_start,
    time_bucket,
    proj_weight,
    out_weight,
    small_params,
    proj_mean,
    proj_square,
    out_mean,
    out_square,
    small_mean,
    small_square,
):
    n_head = lax.axis_size("head")
    n_dp = lax.axis_size("dp")
    me_head, me_dp = lax.axis_index("head"), lax.axis_index("dp")
    here = tokens.shape[0]
    group = here * n_head
    nb = group // TILE
    per = here // TILE
    rows_here, _, width = proj_weight.shape
    heads = width // HEAD_DIM
    high, low = split_dp(n_dp)
    me = jnp.stack([me_head, me_dp]).astype(jnp.int32)
    dma = pltpu.SemaphoreType.DMA

    flat = proj_weight.reshape(rows_here, 4 * width)
    x_pieces = gather_head(tokens)
    w_pieces, offsets = gather_dp(flat[:, width:].astype(bf16))
    u_pieces, _ = gather_dp(
        jnp.concatenate([flat[:, :width].astype(bf16), out_weight.T.astype(bf16)], axis=1)
    )
    cot_pieces = gather_head(cotangent)
    first = seq_start[::TILE] // TILE
    starts = seq_start.reshape(1, group)

    pos, oh, oht, trow = call(
        prepare_kernel,
        "prepare",
        [VMEM] * 2,
        [
            ((nb, TILE, TILE), f32, VMEM),
            ((nb, TILE, NTB), bf16, VMEM),
            ((nb, NTB, TILE), bf16, VMEM),
            ((nb, NTB, TILE), bf16, VMEM),
        ],
        [],
        5,
    )(time_bucket.reshape(1, group), small_params.reshape(1, -1))

    shapes = [
        ((nb, TILE, D), bf16),
        ((nb, 3 * width, TILE), f32),
        ((nb, TILE, NTB + width), bf16),
        ((nb, NTB + width, TILE), bf16),
        ((nb, NTB + width, heads * TILE), bf16),
        ((nb, TILE, width), bf16),
        ((nb, heads * TILE, width), bf16),
        ((3 * width, D), bf16),
    ]
    attn, xn, dsilu, kx, kxt, qxt, v, qm, wt = call(
        functools.partial(forward_kernel, heads, n_head, offsets),
        "forward",
        [SMEM] * 2 + [ANY] * (n_head + len(w_pieces) + 4) + [VMEM],
        [((nb, width, TILE), f32, VMEM)] + [(shape, dtype, ANY) for shape, dtype in shapes],
        [pltpu.VMEM(shape, dtype) for shape, dtype in shapes]
        + [
            pltpu.VMEM((n_head, here, D), bf16),
            pltpu.VMEM((D, 3 * width), bf16),
            pltpu.VMEM((nb, width, TILE), bf16),
            pltpu.VMEM((nb, TILE, TILE), f32),
            pltpu.VMEM((width, heads * TILE), f32),
            dma((n_head,)),
            dma((n_dp,)),
            dma((3 + heads,)),
            dma((8,)),
        ],
        30,
    )(me, first, *x_pieces, *w_pieces, oh, oht, trow, pos, starts)

    column = ((nb, width, TILE), f32, block((nb, width, TILE)))
    stat_block = block((nb, 4, TILE))
    row_block = block((nb, TILE, D))
    whole = pl.BlockSpec((2 * width, D), lambda i: (0, 0))
    gate, ga, gd, stat, cot, wtu, gb = call(
        functools.partial(gate_kernel, n_head, offsets, per),
        "gate",
        [SMEM] + [ANY] * (n_head + len(u_pieces)) + [column[2], row_block],
        [
            column,
            column,
            column,
            ((nb, 4, TILE), f32, stat_block),
            ((nb, TILE, D), bf16, row_block),
            ((2 * width, D), bf16, whole),
            ((1, D), f32, pl.BlockSpec((1, D), lambda i: (0, 0))),
        ],
        [pltpu.VMEM((n_head, here, D), bf16), pltpu.VMEM((D, 2 * width), bf16), dma((n_head,)), dma((n_dp,))],
        5,
        grid=(nb,),
    )(me, *cot_pieces, *u_pieces, attn, xn)

    stats = [stat] + [swap(stat, "head", k) for k in range(1, n_head)]
    dax, daxt, gun, keep, send, *early_parts = call(
        functools.partial(middle_kernel, heads, n_head, per),
        "middle",
        [SMEM] + [stat_block] * n_head + [column[2]] * 4 + [row_block] * 2 + [whole],
        [
            ((nb, heads * TILE, width), bf16, block((nb, heads * TILE, width))),
            ((nb, width, heads * TILE), bf16, block((nb, width, heads * TILE))),
            ((nb, TILE, width), bf16, block((nb, TILE, width))),
            ((n_head // 2, here, D), bf16, ANY),
            ((n_head // 2, here, D), bf16, ANY),
        ]
        + [((high, rows_here, 2 * width), bf16, ANY)] * low,
        [
            pltpu.VMEM((nb, TILE, D), bf16),
            pltpu.VMEM((2 * width, D), f32),
            pltpu.VMEM((D, 2 * width), bf16),
            dma((nb,)),
            dma((n_dp,)),
        ],
        6,
        grid=(nb,),
    )(me, *stats, attn, gate, ga, gd, xn, cot, wtu)
    branch = scatter_head(keep, send)
    early = scatter_dp(early_parts)

    length = D + group + NTB
    extra = -(-length // (128 * n_dp))
    loaded = [shapes[2], shapes[3], shapes[4], shapes[5], shapes[6]] + [
        ((nb, heads * TILE, width), bf16),
        ((nb, width, heads * TILE), bf16),
        ((nb, TILE, TILE), f32),
    ]
    gp, *late_parts = call(
        functools.partial(backward_kernel, heads, n_dp, extra),
        "backward",
        [SMEM] * 2 + [ANY] * 10 + [VMEM] * 2,
        [((nb, TILE, 3 * width), bf16, VMEM)] + [((high, rows_here + 16, 3 * width), bf16, ANY)] * low,
        [pltpu.VMEM(shape, dtype) for shape, dtype in loaded]
        + [
            pltpu.VMEM(*shapes[1]),
            pltpu.VMEM(*shapes[0]),
            pltpu.VMEM((nb, TILE, width), f32),
            pltpu.VMEM((nb, TILE, width), f32),
            pltpu.VMEM((NTB + width, heads * TILE), f32),
            pltpu.VMEM((nb, TILE, TILE), f32),
            pltpu.VMEM((NTB, NTB), f32),
            pltpu.VMEM((nb, width, TILE), f32),
            pltpu.VMEM((3 * width, D), f32),
            pltpu.VMEM((n_dp * (rows_here + 16), 3 * width), bf16),
            pltpu.VMEM((1, extra * n_dp * 128), f32),
            dma((8, nb)),
            dma((2,)),
            dma((n_dp,)),
        ],
        35,
    )(me, first, kx, kxt, qxt, v, qm, dax, daxt, pos, dsilu, xn, starts, gb)

    keep, send = call(
        functools.partial(input_kernel, per),
        "input_rows",
        [
            SMEM,
            block((nb, TILE, 3 * width)),
            block((nb, TILE, width)),
            pl.BlockSpec((3 * width, D), lambda i: (0, 0)),
            whole,
        ],
        [((n_head // 2, here, D), bf16, ANY)] * 2,
        [pltpu.VMEM((nb, TILE, D), bf16), dma((nb,))],
        4,
        grid=(nb,),
    )(me, gp, gun, wt, wtu)
    late = scatter_dp(late_parts)
    normed_grad = scatter_head(keep, send)

    inputs = tokens.astype(f32)
    centred = inputs - jnp.mean(inputs, -1, keepdims=True)
    scale_in = lax.rsqrt(jnp.mean(centred * centred, -1, keepdims=True) + norm_epsilon)
    normed = centred * scale_in
    mixed = (branch + small_params[:D] + inputs).astype(bf16)
    input_grad = cotangent.astype(f32) + scale_in * (
        normed_grad
        - jnp.mean(normed_grad, -1, keepdims=True)
        - normed * jnp.mean(normed_grad * normed, -1, keepdims=True)
    )

    small_here = late[rows_here : rows_here + extra, :128] + late[rows_here + extra : rows_here + 2 * extra, :128]
    late = late[:rows_here]
    squares = jnp.sum(early * early) + jnp.sum(late * late)
    message = jnp.concatenate(
        [small_here, jnp.zeros((7 - extra, 128), f32), jnp.broadcast_to(squares, (1, 128))], axis=0
    )
    n_all = n_dp * n_head
    heard = lax.all_to_all(jnp.broadcast_to(message, (n_all, 8, 128)), ("dp", "head"), 0, 0, tiled=True)
    heard = heard.reshape(n_dp, n_head, 8, 128)
    small_sum = jnp.sum(heard[:, :, :extra], axis=1).reshape(-1)[:length]
    grad_small = jnp.concatenate(
        [small_sum[: D + group], jnp.zeros((POS - group,), f32), small_sum[D + group :]]
    )
    total = jnp.sum(heard[:, :, 7, 0]) + jnp.sum(small_sum * small_sum)
    grad_norm = jnp.sqrt(total)
    factor = jnp.minimum(1.0, clip_norm / (grad_norm + 1e-06))
    grad_out = early[:, width:].T
    grad_proj = jnp.concatenate([early[:, :width], late], axis=1).reshape(rows_here, 4, width)
    new_proj, mean_proj, square_proj = adam_step(
        proj_weight, grad_proj, proj_mean, proj_square, factor, rate_matrix, decay_matrix
    )
    new_out, mean_out, square_out = adam_step(
        out_weight, grad_out, out_mean, out_square, factor, rate_matrix, decay_matrix
    )
    new_small, mean_small, square_small = adam_step(
        small_params, grad_small, small_mean, small_square, factor, rate_small, 0.0
    )
    return (
        mixed,
        input_grad,
        grad_proj,
        grad_out,
        grad_small,
        grad_norm,
        new_proj,
        mean_proj,
        square_proj,
        new_out,
        mean_out,
        square_out,
        new_small,
        mean_small,
        square_small,
    )


def solution(mesh):
    in_specs = (
        P(("dp", "head"), None),
        P(("dp", "head"), None),
        P("dp"),
        P("dp"),
        P("dp", None, "head"),
        P("head", "dp"),
        P(),
        P("dp", None, "head"),
        P("dp", None, "head"),
        P("head", "dp"),
        P("head", "dp"),
        P(),
        P(),
    )
    out_specs = (
        P(("dp", "head"), None),
        P(("dp", "head"), None),
        P("dp", None, "head"),
        P("head", "dp"),
        P(),
        P(),
        P("dp", None, "head"),
        P("dp", None, "head"),
        P("dp", None, "head"),
        P("head", "dp"),
        P("head", "dp"),
        P("head", "dp"),
        P(),
        P(),
        P(),
    )
    return jax.shard_map(shards, mesh=mesh, in_specs=in_specs, out_specs=out_specs, check_vma=False)
```

time: 210 us -> 187 us (0.89)
  waiting for transfers between devices: 56.6 us -> 37.9 us
  Pallas kernels: 75.1 us -> 81.8 us
  local copies, waits for them, and re-layouts: 12.5 us -> 5.8 us
  between operations: 7.87 us -> 4.99 us
  starting transfers between devices: 41.6 us -> 39.1 us
    ppermute x34 -> x27, waiting for transfers between devices: 56.6 us -> 37.1 us  [swap(): return lax.ppermute(x, axis, [(i, i ^ k) for i in range(n)])]
    pallas_call x2 -> x5, Pallas kernels: 45.1 us -> 59.2 us  [the longest x1 27.8 us: shards(): call(functools.partial(backward_kernel, heads, n_dp, extra), 'backward',...]
    pallas_call x1, Pallas kernels: 30 us -> 22.6 us  [shards(): call(functools.partial(forward_kernel, heads, n_head, offsets), 'forward'...]
    ppermute x34 -> x27, starting transfers between devices: 41.6 us -> 35.8 us  [swap(): return lax.ppermute(x, axis, [(i, i ^ k) for i in range(n)])]
    squeeze x4 -> x0, local copies, waits for them, and re-layouts: 5.06 us -> none  [the longest x2 3.48 us: scatter_head(): sent = lax.dynamic_index_in_dim(parts, 1 - core, 1, False)]
    all_to_all x0 -> x1, starting transfers between devices: none -> 3.3 us  [shards(): lax.all_to_all(jnp.broadcast_to(message, (n_all, 8, 128)), ('dp', 'head')...]
    convert_element_type x4 -> x0, other arithmetic: 2.35 us -> none  [the longest x1 1.25 us: shards(): x_pieces = gather_head(normed.astype(bf16))]
    slice x3 -> x6, local copies, waits for them, and re-layouts: 2.34 us -> 0.03 us  [the longest x2 0.02 us: shards(): small_sum = jnp.sum(heard[:, :, :extra], axis=1).reshape(-1)[:length]]
  transfers between devices with their start and end apart: 34 -> 28, of which waited for: 16 -> 9; matrix products, arithmetic and copies ran while one was open for 8% -> 10% of each run, Pallas kernels for 0% -> 33%
where the time goes in v2:
time: 187 us; the launch traced here: 186 us
  Pallas kernels  81.8 us (44%)
  starting transfers between devices  39.1 us (21%)
  waiting for transfers between devices  37.9 us (20%)
  other arithmetic  16.7 us (9%)
  local copies, waits for them, and re-layouts  5.8 us (3%)
  between operations  4.99 us (3%)
    ppermute x27, waiting for transfers between devices, swap(): return lax.ppermute(x, axis, [(i, i ^ k) for i in range(n)])  37.1 us
    ppermute x27, starting transfers between devices, swap(): return lax.ppermute(x, axis, [(i, i ^ k) for i in range(n)])  35.8 us
    pallas_call x1, Pallas kernels, shards(): call(functools.partial(backward_kernel, heads, n_dp, extra), 'backward',...  27.8 us
    pallas_call x1, Pallas kernels, shards(): call(functools.partial(forward_kernel, heads, n_head, offsets), 'forward'...  22.6 us
    pallas_call x1, Pallas kernels, shards(): call(functools.partial(middle_kernel, heads, n_head, per), 'middle', [SME...  10.3 us
    pallas_call x1, Pallas kernels, shards(): call(functools.partial(gate_kernel, n_head, offsets, per), 'gate', [SMEM]...  9.53 us
    pallas_call x1, Pallas kernels, shards(): call(functools.partial(input_kernel, per), 'input_rows', [SMEM, block((nb...  7.11 us
    pallas_call x1, Pallas kernels, shards(): call(prepare_kernel, 'prepare', [VMEM] * 2, [((nb, TILE, TILE), f32, VMEM...  4.45 us
  transfers between devices with their start and end apart: 28, of which 9 were waited for; matrix products, arithmetic and copies ran while one was open for 10% of the time, Pallas kernels for 33%

profile of v2, /device:TPU:0, one launch (start us, length us, event | category | flops | bytes accessed | tf_op | source)
XLA Modules:
  0.0 186.3 jit_solution(1756971780236504235)
XLA Ops:
  0.6 3.0 %collective-permute-start.7 = (bf16[512,512]{1,0:T(8,128)(2,1)}, bf16[512,512]{1,0:T(8,128)(2,1)S(1)}, u32[]{:S(2)}, u32[]{:S(2)}) collective-permute-start(bf16[512,512]{1,0:T(8,128)(2,1)} %refs_0_.2), channel_id=1, source_target_pairs={{0,2},{1,3},{2,0},{3,1},{4,6},{5,7},{6,4},{7,5},{8,10},{9,11},{10,... | collective-permute-start | bytes 1572872 | tf_op jit(solution)/shard_map/ppermute | solution.py:50
  3.7 0.9 convert.5
  4.6 2.7 %collective-permute-start.9 = (bf16[64,384]{1,0:T(8,128)(2,1)S(1)}, bf16[64,384]{1,0:T(8,128)(2,1)S(1)}, u32[]{:S(2)}, u32[]{:S(2)}) collective-permute-start(bf16[64,384]{1,0:T(8,128)(2,1)S(1)} %slice.63.refs_4_), channel_id=1, source_target_pairs={{0,16},{4,20},{8,24},{12,28},{16,0},{20,4},{24,8},{28,12},{1,17},{... | collective-permute-start | bytes 147464 | tf_op jit(solution)/shard_map/ppermute | solution.py:50
  7.3 0.8 convert_bitcast_fusion
  8.1 0.4 collective-permute-start.3
  8.5 0.3 collective-permute-start.1
  8.7 1.2 convert_reduce_fusion
  9.9 1.4 reshape.73.small_ref
  11.4 0.8 slice.48
  12.1 0.5 and_select_fusion.first_ref
  12.7 4.4 %prepare.1 = (f32[8,256,256]{2,1,0:T(8,128)}, bf16[8,256,128]{2,1,0:T(8,128)(2,1)}, bf16[8,128,256]{2,1,0:T(8,128)(2,1)}, bf16[8,128,256]{2,1,0:T(8,128)(2,1)}) custom-call(s32[1,2048]{1,0:T(1,128)} %bitcast.63, f32[1,8832]{1,0:T(1,128)} %reshape.73.small_ref), custom_call_target="tpu_custom_call" | custom-call | flops 5000000000 | bytes 15000000 | tf_op jit(solution)/shard_map/prepare/pallas_call | solution.py:585
  17.1 0.3 fusion.8
  17.6 1.9 %collective-permute-start.10 = (bf16[128,384]{1,0:T(8,128)(2,1)S(1)}, bf16[128,384]{1,0:T(8,128)(2,1)S(1)}, u32[]{:S(2)}, u32[]{:S(2)}) collective-permute-start(bf16[128,384]{1,0:T(8,128)(2,1)S(1)} %pad_maximum_fusion.3), channel_id=1, source_target_pairs={{0,8},{4,12},{8,0},{12,4},{16,24},{20,28},{24,16},{28,20},{1,9},{5... | collective-permute-start | bytes 294920 | tf_op jit(solution)/shard_map/ppermute | solution.py:50
  19.5 0.3 collective-permute-start.4
  19.7 3.5 %collective-permute-done.10.refs_6_ = bf16[128,384]{1,0:T(8,128)(2,1)S(1)} collective-permute-done((bf16[128,384]{1,0:T(8,128)(2,1)S(1)}, bf16[128,384]{1,0:T(8,128)(2,1)S(1)}, u32[]{:S(2)}, u32[]{:S(2)}) %collective-permute-start.10) | collective-permute-done | bytes 98336 | tf_op jit(solution)/shard_map/ppermute | solution.py:50
  23.2 1.9 collective-permute-start.11
  25.1 0.6 pad_add_fusion.me_ref
  25.8 3.8 %collective-permute-done.11.refs_7_ = bf16[256,384]{1,0:T(8,128)(2,1)S(1)} collective-permute-done((bf16[256,384]{1,0:T(8,128)(2,1)S(1)}, bf16[256,384]{1,0:T(8,128)(2,1)S(1)}, u32[]{:S(2)}, u32[]{:S(2)}) %collective-permute-start.11) | collective-permute-done | bytes 196640 | tf_op jit(solution)/shard_map/ppermute | solution.py:50
  29.6 1.6 collective-permute-start.5
  31.3 0.8 copy-done.22
  32.0 0.2 copy-done.23
  32.2 22.6 %forward.1 = (f32[8,128,256]{2,1,0:T(8,128)}, bf16[8,256,512]{2,1,0:T(8,128)(2,1)}, f32[8,384,256]{2,1,0:T(8,128)}, bf16[8,256,256]{2,1,0:T(8,128)(2,1)}, bf16[8...) custom-call(s32[2]{0:T(128)} %pad_add_fusion.me_ref, ...), custom_call_target="tpu_custom_call" | custom-call | flops 30000001024 | bytes 90000000 | tf_op jit(solution)/shard_map/forward/pallas_call | solution.py:609
  54.9 0.6 copy-done.26
  55.5 0.2 copy-done.24
  55.7 9.5 %gate.1 = (f32[8,128,256]{2,1,0:T(8,128)}, f32[8,128,256]{2,1,0:T(8,128)}, f32[8,128,256]{2,1,0:T(8,128)}, f32[8,4,256]{2,1,0:T(4,128)}, bf16[8,256,512]{2,1,0:T...) custom-call(s32[2]{0:T(128)} %pad_add_fusion.me_ref, bf16[512,512]{1,0:T(8,128)(2,1)} %refs_0_.3, ...), custom_call_target="tpu_custom_call" | custom-call | flops 5000000000 | bytes 15000000 | tf_op jit(solution)/shard_map/gate/pallas_call | solution.py:633
  65.2 0.5 collective-permute-start.12
  65.7 1.5 collective-permute-start.13
  67.2 0.1 pad.4.clone
  67.3 2.5 %collective-permute-done.13.refs_2_ = f32[8,4,256]{2,1,0:T(4,128)S(1)} collective-permute-done((f32[8,4,256]{2,1,0:T(4,128)}, f32[8,4,256]{2,1,0:T(4,128)S(1)}, u32[]{:S(2)}, u32[]{:S(2)}) %collective-permute-start.13) | collective-permute-done | bytes 32800 | tf_op jit(solution)/shard_map/ppermute | solution.py:50
  69.9 1.2 collective-permute-done.14.refs_3_
  71.1 0.6 copy-done.29
  71.7 10.3 %middle.1 = (bf16[8,512,128]{2,1,0:T(8,128)(2,1)}, bf16[8,128,512]{2,1,0:T(8,128)(2,1)}, bf16[8,256,128]{2,1,0:T(8,128)(2,1)}, bf16[2,512,512]{2,1,0:T(8,128)(2,...) custom-call(s32[2]{0:T(128)} %pad_add_fusion.me_ref, ...), custom_call_target="tpu_custom_call" | custom-call | flops 6000000000 | bytes 18000000 | tf_op jit(solution)/shard_map/middle/pallas_call | solution.py:652
  82.1 1.0 collective-permute-start.19
  83.1 27.8 %backward.1 = (bf16[8,256,384]{2,1,0:T(8,128)(2,1)}, bf16[4,80,384]{2,1,0:T(8,128)(2,1)}, bf16[4,80,384]{2,1,0:T(8,128)(2,1)}) custom-call(s32[2]{0:T(128)} %pad_add_fusion.me_ref, s32[8]{0:T(128)} %and_select_fusion.first_ref, bf16[8,256,256]{2,1,0:T(8,128)(2,1)} %get-tuple-element.61.refs_0_, bf16[8,256,256]{2,1,0:T(8,128)(2,1)} %get-tuple-element.62.refs_1_, ...), custom_call_target="tpu_custom_call" | custom-call | flops 35000000512 | bytes 105000000 | tf_op jit(solution)/shard_map/backward/pallas_call | solution.py:684
  110.9 1.7 collective-permute-start.23
  112.7 6.4 %collective-permute-start.20 = (bf16[64,256]{1,0:T(8,128)(2,1)S(1)}, bf16[64,256]{1,0:T(8,128)(2,1)S(1)}, u32[]{:S(2)}, u32[]{:S(2)}) collective-permute-start(bf16[64,256]{1,0:T(8,128)(2,1)S(1)} %get-tuple-element.103), channel_id=1, source_target_pairs={{0,8},{4,12},{8,0},{12,4},{16,24},{20,28},{24,16},{28,20},{1,9},{5... | collective-permute-start | bytes 98312 | tf_op jit(solution)/shard_map/ppermute | solution.py:50
  119.1 2.9 %collective-permute-start.21 = (bf16[64,256]{1,0:T(8,128)(2,1)S(1)}, bf16[64,256]{1,0:T(8,128)(2,1)S(1)}, u32[]{:S(2)}, u32[]{:S(2)}) collective-permute-start(bf16[64,256]{1,0:T(8,128)(2,1)S(1)} %get-tuple-element.105), channel_id=1, source_target_pairs={{0,16},{4,20},{8,24},{12,28},{16,0},{20,4},{24,8},{28,12},{1,17},{... | collective-permute-start | bytes 98312 | tf_op jit(solution)/shard_map/ppermute | solution.py:50
  122.0 1.0 convert_add_fusion.3
  123.1 5.0 %collective-permute-start.24 = (bf16[80,384]{1,0:T(8,128)(2,1)S(1)}, bf16[80,384]{1,0:T(8,128)(2,1)S(1)}, u32[]{:S(2)}, u32[]{:S(2)}) collective-permute-start(bf16[80,384]{1,0:T(8,128)(2,1)S(1)} %get-tuple-element.100), channel_id=1, source_target_pairs={{0,8},{4,12},{8,0},{12,4},{16,24},{20,28},{24,16},{28,20},{1,9},{5... | collective-permute-start | bytes 184328 | tf_op jit(solution)/shard_map/ppermute | solution.py:50
  128.1 1.3 collective-permute-start.25
  129.4 1.1 collective-permute-start.26
  130.5 0.6 multiply_reduce_fusion.1
  131.1 3.2 %collective-permute-done.25 = bf16[80,384]{1,0:T(8,128)(2,1)S(1)} collective-permute-done((bf16[80,384]{1,0:T(8,128)(2,1)S(1)}, bf16[80,384]{1,0:T(8,128)(2,1)S(1)}, u32[]{:S(2)}, u32[]{:S(2)}) %collective-permute-start.25) | collective-permute-done | bytes 61472 | tf_op jit(solution)/shard_map/ppermute | solution.py:50
  134.3 1.2 collective-permute-done.26
  135.6 0.6 multiply_reduce_fusion
  137.7 0.7 broadcast_in_dim.19
  138.3 3.3 %all-to-all-start = ((f32[32,8,128]{2,1,0:T(8,128)}), f32[32,8,128]{2,1,0:T(8,128)}, u32[]{:S(2)}, u32[]{:S(2)}) async-start(f32[32,8,128]{2,1,0:T(8,128)} %broadcast_in_dim.19), calls=%async_computation | async-start | bytes 262144 | tf_op jit(solution)/shard_map/all_to_all | solution.py:745
  141.6 7.1 %input_rows.1 = (bf16[2,512,512]{2,1,0:T(8,128)(2,1)}, bf16[2,512,512]{2,1,0:T(8,128)(2,1)}) custom-call(s32[2]{0:T(128)} %pad_add_fusion.me_ref, bf16[8,256,384]{2,1,0:T(8,128)(2,1)} %get-tuple-element.70.gp_ref, bf16[8,256,128]{2,1,0:T(8,128)(2,1)} %get-tuple-element.71.gun_ref, bf16[384,512]{1,0:T(8,128)(2,1)} %get-tuple-element.72.wt_ref, ...), custom_call_target="tpu_custom_call" | custom-call | flops 4000000000 | bytes 12000000 | tf_op jit(solution)/shard_map/input_rows/pallas_call | solution.py:709
  148.8 0.1 collective-permute-start.17
  149.0 0.9 all-to-all-done
  149.8 0.9 slice_reduce_fusion
  150.8 0.6 fusion.21
  151.4 1.5 slice_reduce_fusion.1
  154.3 1.9 %multiply_subtract_fusion = (f32[64,4,128]{2,1,0:T(4,128)}, f32[64,4,128]{2,1,0:T(4,128)}, f32[64,4,128]{2,1,0:T(4,128)}) fusion(f32[64,4,128]{2,1,0:T(4,128)S(1)} %copy-done.4, f32[64,4,128]{2,1,0:T(4,128)S(1)} %reshape.75, f32[]{:T(128)S(6)} %min.3, f32[64,4,128]{2,1,0:T(4,128)} %param.20, f32[64,4,128]{2,1,0:T(4,128)} %param.21), kind=kLoop, calls=%fused_computation.30 | loop fusion | flops 524288 | bytes 917508 | tf_op jit(solution)/shard_map/sub | solution.py:45
  156.2 1.5 multiply_subtract_fusion.1
  157.7 0.3 convert_add_fusion
  158.2 0.9 collective-permute-start.18
  159.1 0.3 convert_add_fusion.1
  159.5 1.2 collective-permute-start.16
  160.8 0.7 multiply_subtract_fusion.2
  161.5 11.5 %collective-permute-done.18 = bf16[512,512]{1,0:T(8,128)(2,1)S(1)} collective-permute-done((bf16[512,512]{1,0:T(8,128)(2,1)S(1)}, bf16[512,512]{1,0:T(8,128)(2,1)S(1)}, u32[]{:S(2)}, u32[]{:S(2)}) %collective-permute-start.18) | collective-permute-done | bytes 524320 | tf_op jit(solution)/shard_map/ppermute | solution.py:50
  173.0 0.5 fusion.13
  173.5 10.0 %collective-permute-done.16 = bf16[512,512]{1,0:T(8,128)(2,1)S(1)} collective-permute-done((bf16[512,512]{1,0:T(8,128)(2,1)S(1)}, bf16[512,512]{1,0:T(8,128)(2,1)S(1)}, u32[]{:S(2)}, u32[]{:S(2)}) %collective-permute-start.16) | collective-permute-done | bytes 524320 | tf_op jit(solution)/shard_map/ppermute | solution.py:50
  183.5 1.7 fusion.7
  (111 shorter events, 1.0 us)
Async XLA Ops:
  0.6 16.8 %collective-permute-start.7 = (bf16[512,512]{1,0:T(8,128)(2,1)}, bf16[512,512]{1,0:T(8,128)(2,1)S(1)}, u32[]{:S(2)}, u32[]{:S(2)}) collective-permute-start(bf16[512,512]{1,0:T(8,128)(2,1)} %refs_0_.2), channel_id=1, source_target_pairs={{0,2},{1,3},{2,0},{3,1},{4,6},{5,7},{6,4},{7,5},{8,10},{9,11},{10,... | collective-permute-start | bytes 1572872 | tf_op jit(solution)/shard_map/ppermute | solution.py:50
  3.6 27.5 %collective-permute-start.6 = (bf16[512,512]{1,0:T(8,128)(2,1)}, bf16[512,512]{1,0:T(8,128)(2,1)S(1)}, u32[]{:S(2)}, u32[]{:S(2)}) collective-permute-start(bf16[512,512]{1,0:T(8,128)(2,1)} %refs_0_.2), channel_id=1, source_target_pairs={{0,1},{1,0},{2,3},{3,2},{4,5},{5,4},{6,7},{7,6},{8,9},{9,8},{10,11... | collective-permute-start | bytes 1572872 | tf_op jit(solution)/shard_map/ppermute | solution.py:50
  4.6 18.6 %copy-start.8 = (bf16[64,384]{1,0:T(8,128)(2,1)}, bf16[64,384]{1,0:T(8,128)(2,1)S(1)}, u32[]{:S(2)}) copy-start(bf16[64,384]{1,0:T(8,128)(2,1)S(1)} %slice.63.refs_4_) | copy-start | bytes 147460
  4.6 12.9 %collective-permute-start.9 = (bf16[64,384]{1,0:T(8,128)(2,1)S(1)}, bf16[64,384]{1,0:T(8,128)(2,1)S(1)}, u32[]{:S(2)}, u32[]{:S(2)}) collective-permute-start(bf16[64,384]{1,0:T(8,128)(2,1)S(1)} %slice.63.refs_4_), channel_id=1, source_target_pairs={{0,16},{4,20},{8,24},{12,28},{16,0},{20,4},{24,8},{28,12},{1,17},{... | collective-permute-start | bytes 147464 | tf_op jit(solution)/shard_map/ppermute | solution.py:50
  8.1 9.1 %copy-start.17 = (bf16[64,256]{1,0:T(8,128)(2,1)}, bf16[64,256]{1,0:T(8,128)(2,1)S(1)}, u32[]{:S(2)}) copy-start(bf16[64,256]{1,0:T(8,128)(2,1)S(1)} %pad_maximum_fusion.6.refs_4_) | copy-start | bytes 98308
  8.1 11.4 %collective-permute-start.3 = (bf16[64,256]{1,0:T(8,128)(2,1)S(1)}, bf16[64,256]{1,0:T(8,128)(2,1)S(1)}, u32[]{:S(2)}, u32[]{:S(2)}) collective-permute-start(bf16[64,256]{1,0:T(8,128)(2,1)S(1)} %pad_maximum_fusion.6.refs_4_), channel_id=1, source_target_pairs={{0,16},{4,20},{8,24},{12,28},{16,0},{20,4},{24,8},{28,12},{1,17},{... | collective-permute-start | bytes 98312 | tf_op jit(solution)/shard_map/ppermute | solution.py:50
  8.5 22.7 %collective-permute-start.1 = (bf16[512,512]{1,0:T(8,128)(2,1)}, bf16[512,512]{1,0:T(8,128)(2,1)S(1)}, u32[]{:S(2)}, u32[]{:S(2)}) collective-permute-start(bf16[512,512]{1,0:T(8,128)(2,1)} %refs_0_.3), channel_id=1, source_target_pairs={{0,2},{1,3},{2,0},{3,1},{4,6},{5,7},{6,4},{7,5},{8,10},{9,11},{10,... | collective-permute-start | bytes 1572872 | tf_op jit(solution)/shard_map/ppermute | solution.py:50
  12.7 4.5 %copy-start = (bf16[512,512]{1,0:T(8,128)(2,1)S(1)}, bf16[512,512]{1,0:T(8,128)(2,1)}, u32[]{:S(2)}) copy-start(bf16[512,512]{1,0:T(8,128)(2,1)} %refs_0_.2) | copy-start | bytes 1572868
  12.7 13.0 %copy-start.6 = (bf16[512,512]{1,0:T(8,128)(2,1)S(1)}, bf16[512,512]{1,0:T(8,128)(2,1)}, u32[]{:S(2)}) copy-start(bf16[512,512]{1,0:T(8,128)(2,1)} %refs_0_.3) | copy-start | bytes 1572868
  17.4 13.8 %copy-start.21 = (bf16[512,512]{1,0:T(8,128)(2,1)}, bf16[512,512]{1,0:T(8,128)(2,1)S(1)}, u32[]{:S(2)}) copy-start(bf16[512,512]{1,0:T(8,128)(2,1)S(1)} %collective-permute-done.7.refs_2_) | copy-start | bytes 1572868
  17.4 13.8 %collective-permute-start.8 = (bf16[512,512]{1,0:T(8,128)(2,1)S(1)}, bf16[512,512]{1,0:T(8,128)(2,1)S(1)}, u32[]{:S(2)}, u32[]{:S(2)}) collective-permute-start(bf16[512,512]{1,0:T(8,128)(2,1)S(1)} %collective-permute-done.7.refs_2_), channel_id=1, source_target_pairs={{0,1},{1,0},{2,3},{3,2},{4,5},{5,4},{6,7},{7,6},{8,9},{9,8},{10,11... | collective-permute-start | bytes 1572872 | tf_op jit(solution)/shard_map/ppermute | solution.py:50
  17.5 13.7 %copy-start.11 = (bf16[64,384]{1,0:T(8,128)(2,1)}, bf16[64,384]{1,0:T(8,128)(2,1)S(1)}, u32[]{:S(2)}) copy-start(bf16[64,384]{1,0:T(8,128)(2,1)S(1)} %collective-permute-done.9.refs_5_) | copy-start | bytes 147460
  17.6 5.6 %collective-permute-start.10 = (bf16[128,384]{1,0:T(8,128)(2,1)S(1)}, bf16[128,384]{1,0:T(8,128)(2,1)S(1)}, u32[]{:S(2)}, u32[]{:S(2)}) collective-permute-start(bf16[128,384]{1,0:T(8,128)(2,1)S(1)} %pad_maximum_fusion.3), channel_id=1, source_target_pairs={{0,8},{4,12},{8,0},{12,4},{16,24},{20,28},{24,16},{28,20},{1,9},{5... | collective-permute-start | bytes 294920 | tf_op jit(solution)/shard_map/ppermute | solution.py:50
  19.5 35.3 %copy-start.14 = (bf16[64,256]{1,0:T(8,128)(2,1)}, bf16[64,256]{1,0:T(8,128)(2,1)S(1)}, u32[]{:S(2)}) copy-start(bf16[64,256]{1,0:T(8,128)(2,1)S(1)} %collective-permute-done.3.refs_5_) | copy-start | bytes 98308
  19.5 6.2 %collective-permute-start.4 = (bf16[128,256]{1,0:T(8,128)(2,1)S(1)}, bf16[128,256]{1,0:T(8,128)(2,1)S(1)}, u32[]{:S(2)}, u32[]{:S(2)}) collective-permute-start(bf16[128,256]{1,0:T(8,128)(2,1)S(1)} %pad_maximum_fusion.4), channel_id=1, source_target_pairs={{0,8},{4,12},{8,0},{12,4},{16,24},{20,28},{24,16},{28,20},{1,9},{5... | collective-permute-start | bytes 196616 | tf_op jit(solution)/shard_map/ppermute | solution.py:50
  23.2 8.0 %copy-start.15 = (bf16[128,384]{1,0:T(8,128)(2,1)}, bf16[128,384]{1,0:T(8,128)(2,1)S(1)}, u32[]{:S(2)}) copy-start(bf16[128,384]{1,0:T(8,128)(2,1)S(1)} %collective-permute-done.10.refs_6_) | copy-start | bytes 294916
  23.2 6.4 %collective-permute-start.11 = (bf16[256,384]{1,0:T(8,128)(2,1)S(1)}, bf16[256,384]{1,0:T(8,128)(2,1)S(1)}, u32[]{:S(2)}, u32[]{:S(2)}) collective-permute-start(bf16[256,384]{1,0:T(8,128)(2,1)S(1)} %pad_maximum_fusion), channel_id=1, source_target_pairs={{0,4},{4,0},{8,12},{12,8},{16,20},{20,16},{24,28},{28,24},{1,5},{5... | collective-permute-start | bytes 589832 | tf_op jit(solution)/shard_map/ppermute | solution.py:50
  25.7 29.1 %copy-start.16 = (bf16[128,256]{1,0:T(8,128)(2,1)}, bf16[128,256]{1,0:T(8,128)(2,1)S(1)}, u32[]{:S(2)}) copy-start(bf16[128,256]{1,0:T(8,128)(2,1)S(1)} %collective-permute-done.4.refs_6_) | copy-start | bytes 196612
  25.7 29.2 %collective-permute-start = (bf16[512,512]{1,0:T(8,128)(2,1)S(1)}, bf16[512,512]{1,0:T(8,128)(2,1)S(1)}, u32[]{:S(2)}, u32[]{:S(2)}) collective-permute-start(bf16[512,512]{1,0:T(8,128)(2,1)S(1)} %copy-done.6), channel_id=1, source_target_pairs={{0,1},{1,0},{2,3},{3,2},{4,5},{5,4},{6,7},{7,6},{8,9},{9,8},{10,11... | collective-permute-start | bytes 1572872 | tf_op jit(solution)/shard_map/ppermute | solution.py:50
  29.6 1.7 copy-start.25
  29.6 25.2 %collective-permute-start.5 = (bf16[256,256]{1,0:T(8,128)(2,1)S(1)}, bf16[256,256]{1,0:T(8,128)(2,1)S(1)}, u32[]{:S(2)}, u32[]{:S(2)}) collective-permute-start(bf16[256,256]{1,0:T(8,128)(2,1)S(1)} %pad_maximum_fusion.1), channel_id=1, source_target_pairs={{0,4},{4,0},{8,12},{12,8},{16,20},{20,16},{24,28},{28,24},{1,5},{5... | collective-permute-start | bytes 393224 | tf_op jit(solution)/shard_map/ppermute | solution.py:50
  31.2 23.7 %copy-start.20 = (bf16[512,512]{1,0:T(8,128)(2,1)}, bf16[512,512]{1,0:T(8,128)(2,1)S(1)}, u32[]{:S(2)}) copy-start(bf16[512,512]{1,0:T(8,128)(2,1)S(1)} %collective-permute-done.1.refs_2_) | copy-start | bytes 1572868
  31.2 23.7 %collective-permute-start.2 = (bf16[512,512]{1,0:T(8,128)(2,1)S(1)}, bf16[512,512]{1,0:T(8,128)(2,1)}, u32[]{:S(2)}, u32[]{:S(2)}) collective-permute-start(bf16[512,512]{1,0:T(8,128)(2,1)S(1)} %collective-permute-done.1.refs_2_), channel_id=1, source_target_pairs={{0,1},{1,0},{2,3},{3,2},{4,5},{5,4},{6,7},{7,6},{8,9},{9,8},{10,11... | collective-permute-start | bytes 1572872 | tf_op jit(solution)/shard_map/ppermute | solution.py:50
  31.2 0.8 copy-start.22
  31.2 1.0 copy-start.23
  54.9 0.7 copy-start.26
  54.9 0.8 copy-start.24
  65.2 2.1 %collective-permute-start.12 = (f32[8,4,256]{2,1,0:T(4,128)}, f32[8,4,256]{2,1,0:T(4,128)S(1)}, u32[]{:S(2)}, u32[]{:S(2)}) collective-permute-start(f32[8,4,256]{2,1,0:T(4,128)} %get-tuple-element.53.refs_0_), channel_id=1, source_target_pairs={{0,1},{1,0},{2,3},{3,2},{4,5},{5,4},{6,7},{7,6},{8,9},{9,8},{10,11... | collective-permute-start | bytes 98312 | tf_op jit(solution)/shard_map/ppermute | solution.py:50
  65.7 4.1 %collective-permute-start.13 = (f32[8,4,256]{2,1,0:T(4,128)}, f32[8,4,256]{2,1,0:T(4,128)S(1)}, u32[]{:S(2)}, u32[]{:S(2)}) collective-permute-start(f32[8,4,256]{2,1,0:T(4,128)} %get-tuple-element.53.refs_0_), channel_id=1, source_target_pairs={{0,2},{1,3},{2,0},{3,1},{4,6},{5,7},{6,4},{7,5},{8,10},{9,11},{10,... | collective-permute-start | bytes 98312 | tf_op jit(solution)/shard_map/ppermute | solution.py:50
  67.2 3.9 %collective-permute-start.14 = (f32[8,4,256]{2,1,0:T(4,128)}, f32[8,4,256]{2,1,0:T(4,128)S(1)}, u32[]{:S(2)}, u32[]{:S(2)}) collective-permute-start(f32[8,4,256]{2,1,0:T(4,128)} %get-tuple-element.53.refs_0_), channel_id=1, source_target_pairs={{0,3},{1,2},{2,1},{3,0},{4,7},{5,6},{6,5},{7,4},{8,11},{9,10},{10,... | collective-permute-start | bytes 98312 | tf_op jit(solution)/shard_map/ppermute | solution.py:50
  67.3 3.8 %copy-start.27 = (f32[8,4,256]{2,1,0:T(4,128)}, f32[8,4,256]{2,1,0:T(4,128)S(1)}, u32[]{:S(2)}) copy-start(f32[8,4,256]{2,1,0:T(4,128)S(1)} %collective-permute-done.12.refs_1_) | copy-start | bytes 98308
  69.9 1.2 copy-start.28
  71.1 0.6 copy-start.29
  82.1 30.6 %collective-permute-start.19 = (bf16[4,64,256]{2,1,0:T(8,128)(2,1)}, bf16[4,64,256]{2,1,0:T(8,128)(2,1)S(1)}, u32[]{:S(2)}, u32[]{:S(2)}) collective-permute-start(bf16[4,64,256]{2,1,0:T(8,128)(2,1)} %get-tuple-element.76), channel_id=1, source_target_pairs={{0,4},{4,0},{8,12},{12,8},{16,20},{20,16},{24,28},{28,24},{1,5},{5... | collective-permute-start | bytes 393224 | tf_op jit(solution)/shard_map/ppermute | solution.py:50
  83.1 29.6 %copy-start.12 = (bf16[4,64,256]{2,1,0:T(8,128)(2,1)S(1)}, bf16[4,64,256]{2,1,0:T(8,128)(2,1)}, u32[]{:S(2)}) copy-start(bf16[4,64,256]{2,1,0:T(8,128)(2,1)} %get-tuple-element.75) | copy-start | bytes 393220
  110.9 11.1 %collective-permute-start.23 = (bf16[4,80,384]{2,1,0:T(8,128)(2,1)}, bf16[4,80,384]{2,1,0:T(8,128)(2,1)S(1)}, u32[]{:S(2)}, u32[]{:S(2)}) collective-permute-start(bf16[4,80,384]{2,1,0:T(8,128)(2,1)} %get-tuple-element.78), channel_id=1, source_target_pairs={{0,4},{4,0},{8,12},{12,8},{16,20},{20,16},{24,28},{28,24},{1,5},{5... | collective-permute-start | bytes 737288 | tf_op jit(solution)/shard_map/ppermute | solution.py:50
  112.7 46.4 %collective-permute-start.15 = (bf16[2,512,512]{2,1,0:T(8,128)(2,1)}, bf16[2,512,512]{2,1,0:T(8,128)(2,1)S(1)}, u32[]{:S(2)}, u32[]{:S(2)}) collective-permute-start(bf16[2,512,512]{2,1,0:T(8,128)(2,1)} %get-tuple-element.60), channel_id=1, source_target_pairs={{0,1},{1,0},{2,3},{3,2},{4,5},{5,4},{6,7},{7,6},{8,9},{9,8},{10,11... | collective-permute-start | bytes 3145736 | tf_op jit(solution)/shard_map/ppermute | solution.py:50
  112.7 15.3 %collective-permute-start.20 = (bf16[64,256]{1,0:T(8,128)(2,1)S(1)}, bf16[64,256]{1,0:T(8,128)(2,1)S(1)}, u32[]{:S(2)}, u32[]{:S(2)}) collective-permute-start(bf16[64,256]{1,0:T(8,128)(2,1)S(1)} %get-tuple-element.103), channel_id=1, source_target_pairs={{0,8},{4,12},{8,0},{12,4},{16,24},{20,28},{24,16},{28,20},{1,9},{5... | collective-permute-start | bytes 98312 | tf_op jit(solution)/shard_map/ppermute | solution.py:50
  119.1 10.3 %collective-permute-start.21 = (bf16[64,256]{1,0:T(8,128)(2,1)S(1)}, bf16[64,256]{1,0:T(8,128)(2,1)S(1)}, u32[]{:S(2)}, u32[]{:S(2)}) collective-permute-start(bf16[64,256]{1,0:T(8,128)(2,1)S(1)} %get-tuple-element.105), channel_id=1, source_target_pairs={{0,16},{4,20},{8,24},{12,28},{16,0},{20,4},{24,8},{28,12},{1,17},{... | collective-permute-start | bytes 98312 | tf_op jit(solution)/shard_map/ppermute | solution.py:50
  122.0 8.5 %collective-permute-start.22 = (bf16[64,256]{1,0:T(8,128)(2,1)S(1)}, bf16[64,256]{1,0:T(8,128)(2,1)S(1)}, u32[]{:S(2)}, u32[]{:S(2)}) collective-permute-start(bf16[64,256]{1,0:T(8,128)(2,1)S(1)} %get-tuple-element.104), channel_id=1, source_target_pairs={{0,24},{4,28},{8,16},{12,20},{16,8},{20,12},{24,0},{28,4},{1,25},{... | collective-permute-start | bytes 98312 | tf_op jit(solution)/shard_map/ppermute | solution.py:50
  123.1 8.1 %collective-permute-start.24 = (bf16[80,384]{1,0:T(8,128)(2,1)S(1)}, bf16[80,384]{1,0:T(8,128)(2,1)S(1)}, u32[]{:S(2)}, u32[]{:S(2)}) collective-permute-start(bf16[80,384]{1,0:T(8,128)(2,1)S(1)} %get-tuple-element.100), channel_id=1, source_target_pairs={{0,8},{4,12},{8,0},{12,4},{16,24},{20,28},{24,16},{28,20},{1,9},{5... | collective-permute-start | bytes 184328 | tf_op jit(solution)/shard_map/ppermute | solution.py:50
  128.1 6.3 %collective-permute-start.25 = (bf16[80,384]{1,0:T(8,128)(2,1)S(1)}, bf16[80,384]{1,0:T(8,128)(2,1)S(1)}, u32[]{:S(2)}, u32[]{:S(2)}) collective-permute-start(bf16[80,384]{1,0:T(8,128)(2,1)S(1)} %get-tuple-element.102), channel_id=1, source_target_pairs={{0,16},{4,20},{8,24},{12,28},{16,0},{20,4},{24,8},{28,12},{1,17},{... | collective-permute-start | bytes 184328 | tf_op jit(solution)/shard_map/ppermute | solution.py:50
  129.4 6.1 %collective-permute-start.26 = (bf16[80,384]{1,0:T(8,128)(2,1)S(1)}, bf16[80,384]{1,0:T(8,128)(2,1)S(1)}, u32[]{:S(2)}, u32[]{:S(2)}) collective-permute-start(bf16[80,384]{1,0:T(8,128)(2,1)S(1)} %get-tuple-element.101), channel_id=1, source_target_pairs={{0,24},{4,28},{8,16},{12,20},{16,8},{20,12},{24,0},{28,4},{1,25},{... | collective-permute-start | bytes 184328 | tf_op jit(solution)/shard_map/ppermute | solution.py:50
  131.1 17.7 %copy-start.9 = (f32[64,256]{1,0:T(8,128)}, f32[64,256]{1,0:T(8,128)S(1)}, u32[]{:S(2)}) copy-start(f32[64,256]{1,0:T(8,128)S(1)} %get-tuple-element.93) | copy-start | bytes 196612
  138.3 11.5 %all-to-all-start = ((f32[32,8,128]{2,1,0:T(8,128)}), f32[32,8,128]{2,1,0:T(8,128)}, u32[]{:S(2)}, u32[]{:S(2)}) async-start(f32[32,8,128]{2,1,0:T(8,128)} %broadcast_in_dim.19), calls=%async_computation | async-start | bytes 262144 | tf_op jit(solution)/shard_map/all_to_all | solution.py:745
  141.6 12.7 %copy-start.4 = (f32[64,4,128]{2,1,0:T(4,128)S(1)}, f32[64,4,128]{2,1,0:T(4,128)}, u32[]{:S(2)}) copy-start(f32[64,4,128]{2,1,0:T(4,128)} %param.17) | copy-start | bytes 393220
  148.8 9.0 %copy-start.3 = (bf16[2,512,512]{2,1,0:T(8,128)(2,1)S(1)}, bf16[2,512,512]{2,1,0:T(8,128)(2,1)}, u32[]{:S(2)}) copy-start(bf16[2,512,512]{2,1,0:T(8,128)(2,1)} %get-tuple-element.73) | copy-start | bytes 3145732
  148.8 8.9 %collective-permute-start.17 = (bf16[2,512,512]{2,1,0:T(8,128)(2,1)}, bf16[2,512,512]{2,1,0:T(8,128)(2,1)S(1)}, u32[]{:S(2)}, u32[]{:S(2)}) collective-permute-start(bf16[2,512,512]{2,1,0:T(8,128)(2,1)} %get-tuple-element.74), channel_id=1, source_target_pairs={{0,1},{1,0},{2,3},{3,2},{4,5},{5,4},{6,7},{7,6},{8,9},{9,8},{10,11... | collective-permute-start | bytes 3145736 | tf_op jit(solution)/shard_map/ppermute | solution.py:50
  148.9 9.1 %copy-start.5 = (f32[64,4,128]{2,1,0:T(4,128)}, f32[64,4,128]{2,1,0:T(4,128)S(1)}, u32[]{:S(2)}) copy-start(f32[64,4,128]{2,1,0:T(4,128)S(1)} %reshape.75) | copy-start | bytes 393220
  157.7 1.4 copy-start.2
  158.2 14.8 %collective-permute-start.18 = (bf16[512,512]{1,0:T(8,128)(2,1)S(1)}, bf16[512,512]{1,0:T(8,128)(2,1)S(1)}, u32[]{:S(2)}, u32[]{:S(2)}) collective-permute-start(bf16[512,512]{1,0:T(8,128)(2,1)S(1)} %fusion.12), channel_id=1, source_target_pairs={{0,2},{1,3},{2,0},{3,1},{4,6},{5,7},{6,4},{7,5},{8,10},{9,11},{10,... | collective-permute-start | bytes 1572872 | tf_op jit(solution)/shard_map/ppermute | solution.py:50
  159.1 1.7 copy-start.10
  159.1 1.7 copy-start.13
  159.1 1.7 copy-start.18
  159.1 1.7 copy-start.19
  159.1 13.9 %copy-start.1 = (bf16[512,512]{1,0:T(8,128)(2,1)S(1)}, bf16[512,512]{1,0:T(8,128)(2,1)}, u32[]{:S(2)}) copy-start(bf16[512,512]{1,0:T(8,128)(2,1)} %refs_0_.2) | copy-start | bytes 1572868
  159.4 24.1 %copy-start.7 = (bf16[512,512]{1,0:T(8,128)(2,1)S(1)}, bf16[512,512]{1,0:T(8,128)(2,1)}, u32[]{:S(2)}) copy-start(bf16[512,512]{1,0:T(8,128)(2,1)} %refs_0_.3) | copy-start | bytes 1572868
  159.4 24.1 %slice-start = ((f32[8832]{0:T(1024)}), f32[512]{0:T(512)S(1)}, s32[]{:S(2)}) async-start(f32[8832]{0:T(1024)} %param.19), calls=%async_computation.1 | async-start | bytes 4096 | tf_op jit(solution)/shard_map/slice | solution.py:731
  159.5 24.0 %collective-permute-start.16 = (bf16[512,512]{1,0:T(8,128)(2,1)S(1)}, bf16[512,512]{1,0:T(8,128)(2,1)S(1)}, u32[]{:S(2)}, u32[]{:S(2)}) collective-permute-start(bf16[512,512]{1,0:T(8,128)(2,1)S(1)} %fusion.11), channel_id=1, source_target_pairs={{0,2},{1,3},{2,0},{3,1},{4,6},{5,7},{6,4},{7,5},{8,10},{9,11},{10,... | collective-permute-start | bytes 1572872 | tf_op jit(solution)/shard_map/ppermute | solution.py:50

commit v3 on v2

v3 whole, which is shorter than its diff:
```python
import functools
import math

import jax
import jax.numpy as jnp
from jax import lax
from jax.experimental import pallas as pl
from jax.experimental.pallas import tpu as pltpu
from jax.sharding import PartitionSpec as P

D = 512
HEAD_DIM = 64
HD = 512
POS = 8192
NTB = 128
STEP = 10
TILE = 256
NEG = -1e9

norm_epsilon = 1e-06
adam_epsilon = 1e-08
beta_one = 0.9
beta_two = 0.999
clip_norm = 1.0
rate_matrix = 0.05
rate_small = 0.3
decay_matrix = 0.1

f32 = jnp.float32
bf16 = jnp.bfloat16
VMEM = pl.BlockSpec(memory_space=pltpu.VMEM)
SMEM = pl.BlockSpec(memory_space=pltpu.SMEM)


def adam_step(weight, grad, first, second, factor, rate, decay):
    clipped = grad * factor
    first_new = beta_one * first + (1.0 - beta_one) * clipped
    second_new = beta_two * second + (1.0 - beta_two) * clipped * clipped
    update = (
        first_new
        / (1.0 - beta_one**STEP)
        / (jnp.sqrt(second_new / (1.0 - beta_two**STEP)) + adam_epsilon)
    )
    return (weight - rate * (update + decay * weight), first_new, second_new)


def swap(x, axis, k):
    n = lax.axis_size(axis)
    return lax.ppermute(x, axis, [(i, i ^ k) for i in range(n)])


def gather_head(x):
    n = lax.axis_size("head")
    pieces = [x] + [None] * (n - 1)
    for k in range(2, n, 2):
        pieces[k] = swap(x, "head", k)
    pieces[1] = swap(x, "head", 1)
    for k in range(2, n, 2):
        pieces[k + 1] = swap(pieces[k], "head", 1)
    return pieces


def gather_direct(x):
    return [x] + [swap(x, "head", k) for k in range(1, lax.axis_size("head"))]


def after_all(arrays, other):
    return lax.optimization_barrier((*arrays, other))[:-1]


def after(x, *others):
    return lax.optimization_barrier((x,) + others)[0]


def gather_dp(x):
    n = lax.axis_size("dp")
    arrays, offsets, operands = [x], [[0]], []
    k = n // 2
    while k:
        operand = jnp.concatenate(arrays, 0) if len(arrays) > 1 else x
        operands.append(operand)
        arrays.append(swap(operand, "dp", k))
        offsets.append([o ^ k for group in offsets for o in group])
        k //= 2
    return arrays, offsets, operands


def split_dp(n):
    low = 2 ** ((n.bit_length() - 1) // 2)
    return n // low, low


def add_parts(own, received):
    total = own.astype(f32)
    for part in received:
        total = total + part.astype(f32)
    return total


def send_high(total):
    high, low = split_dp(lax.axis_size("dp"))
    row = lax.axis_index("dp") // low
    narrow = total.astype(bf16)
    blocks = [lax.dynamic_index_in_dim(total, row, 0, False)]
    for k in range(1, high):
        sent = lax.dynamic_index_in_dim(narrow, row ^ k, 0, False)
        blocks.append(swap(sent, "dp", k * low))
    return blocks


def scatter_core(keep, send, behind):
    return keep.astype(f32) + after(swap(send, "head", 1), behind).astype(f32)


def scatter_chip(total):
    n = lax.axis_size("head")
    chip = lax.axis_index("head") // 2
    narrow = total.astype(bf16)
    mine = lax.dynamic_index_in_dim(total, chip, 0, False)
    for k in range(1, n // 2):
        sent = lax.dynamic_index_in_dim(narrow, chip ^ k, 0, False)
        mine = mine + swap(sent, "head", 2 * k).astype(f32)
    return mine


def dot(a, b):
    return lax.dot_general(a, b, (((1,), (0,)), ((), ())), preferred_element_type=f32)


def dot_nt(a, b):
    return lax.dot_general(a, b, (((1,), (1,)), ((), ())), preferred_element_type=f32)


def flip(a):
    return jnp.transpose(a.astype(f32))


def lanes(i):
    return pl.ds(pl.multiple_of(i * TILE, TILE), TILE)


def by_head(block, heads):
    zero = jnp.zeros((HEAD_DIM, block.shape[1]), block.dtype)
    return jnp.concatenate(
        [
            jnp.concatenate(
                [block[g * HEAD_DIM : (g + 1) * HEAD_DIM] if g == h else zero for g in range(heads)], axis=0
            )
            for h in range(heads)
        ],
        axis=1,
    )


def own_rows(block, heads):
    return jnp.concatenate(
        [block[h * HEAD_DIM : (h + 1) * HEAD_DIM, h * TILE : (h + 1) * TILE] for h in range(heads)], axis=0
    )


def own_lanes(block, heads):
    lane = lax.broadcasted_iota(jnp.int32, block.shape, 1) // HEAD_DIM
    return jnp.concatenate([jnp.where(lane == h, block, jnp.zeros_like(block)) for h in range(heads)], axis=0)


def diagonals(x):
    rows, cols = x.shape
    z = jnp.concatenate([x, jnp.zeros((rows, cols), f32)], axis=1)
    total = z[:8]
    for q in range(1, rows // 8):
        total = total + pltpu.roll(z[8 * q : 8 * q + 8], 2 * cols - 8 * q, 1)
    g = total[0:1]
    for r in range(1, 8):
        g = g + pltpu.roll(total, 2 * cols - r, 1)[r : r + 1]
    return g


def cast_kernel(w_ref, o_ref, low_ref):
    width = o_ref.shape[1]
    for c in range(4):
        low_ref[:, c * width : (c + 1) * width] = w_ref[:, c, :].astype(bf16)
    low_ref[:, 4 * width :] = o_ref[...].astype(bf16)


def row_lanes(ref, first, count):
    return jnp.concatenate([ref[first + k : first + k + 1, :] for k in range(count)], axis=1)


def prepare_kernel(tb_ref, small_ref, pos_ref, oh_ref, oht_ref, trow_ref):
    nb = pos_ref.shape[0]
    for d in range(nb):
        here = row_lanes(small_ref, D // 128 + d * TILE // 128, TILE // 128)
        before = here if d == 0 else row_lanes(small_ref, D // 128 + (d - 1) * TILE // 128, TILE // 128)
        row = jnp.concatenate([here, before], axis=1) * 0.5
        tile = pltpu.roll(
            jnp.broadcast_to(row, (TILE, 2 * TILE)), 0, 1, stride=1, stride_axis=0
        )[:, :TILE]
        if d == 0:
            b = lax.broadcasted_iota(jnp.int32, (TILE, TILE), 0)
            a = lax.broadcasted_iota(jnp.int32, (TILE, TILE), 1)
            tile = jnp.where(b <= a, tile, NEG)
        pos_ref[d] = tile
    table = row_lanes(small_ref, (D + POS) // 128, NTB // 128)
    row = jnp.concatenate([table, table], axis=1)
    upper = pltpu.roll(jnp.broadcast_to(row, (NTB, 2 * NTB)), 0, 1, stride=1, stride_axis=0)[:, :NTB]
    a = lax.broadcasted_iota(jnp.int32, (NTB, NTB), 0)
    b = lax.broadcasted_iota(jnp.int32, (NTB, NTB), 1)
    upper = jnp.where(b >= a, upper, 0.0)
    square = (jnp.where(b > a, upper, jnp.transpose(upper)) * 0.5).astype(bf16)

    def block(i, _):
        onehot = (lax.broadcasted_iota(jnp.int32, (NTB, TILE), 0) == tb_ref[:, lanes(i)]).astype(f32)
        low = onehot.astype(bf16)
        oht_ref[i] = low
        oh_ref[i] = flip(onehot).astype(bf16)
        trow_ref[i] = dot(square, low).astype(bf16)
        return 0

    lax.fori_loop(0, nb, block, 0)


def forward_kernel(heads, n_head, offsets, first_ref, *refs):
    refs = list(refs)
    take = lambda count: [refs.pop(0) for _ in range(count)]
    x_pieces, w_pieces = take(n_head), take(len(offsets))
    oh_ref, oht_ref, trow_ref, pos_ref, ss_ref = take(5)
    attn_ref, xn_ref, d_ref, kx_ref, kxt_ref, qxt_ref, v_ref, qm_ref, wt_ref = take(9)
    w_ref, vt_ref, acc_ref = refs
    nb, width = attn_ref.shape[0], attn_ref.shape[1]
    per = x_pieces[0].shape[0] // TILE
    for piece, group in zip(w_pieces, offsets):
        rows = piece.shape[0] // len(group)
        for at, offset in enumerate(group):
            start = pl.multiple_of((lax.axis_index("dp") ^ offset) * rows, 16)
            w_ref[pl.ds(start, rows), :] = piece[at * rows : (at + 1) * rows, :]
    wt_ref[...] = flip(w_ref[...]).astype(bf16)

    def project(i, x):
        x = x.astype(f32)
        x = x - jnp.sum(x, axis=1, keepdims=True) / D
        x = (x * lax.rsqrt(jnp.sum(x * x, axis=1, keepdims=True) / D + norm_epsilon)).astype(bf16)
        xn_ref[i] = x
        p = dot_nt(wt_ref[width : 4 * width], x)
        sg = 0.5 + 0.5 * jnp.tanh(0.5 * p)
        act = p * sg
        d_ref[i] = sg + act * (1.0 - sg)
        vt = act[:width]
        vt_ref[i] = vt.astype(bf16)
        v_ref[i] = flip(vt).astype(bf16)
        qt = act[width : 2 * width].astype(bf16)
        kt = act[2 * width :]
        kxt_ref[i, :NTB] = oht_ref[i]
        kxt_ref[i, NTB:] = kt.astype(bf16)
        kx_ref[i, :, :NTB] = oh_ref[i]
        kx_ref[i, :, NTB:] = flip(kt).astype(bf16)
        qs = (qt.astype(f32) * (0.5 / math.sqrt(HEAD_DIM))).astype(bf16)
        qxt_ref[i, :NTB] = jnp.concatenate([trow_ref[i]] * heads, axis=1)
        qxt_ref[i, NTB:] = by_head(qs, heads)
        qm_ref[i] = own_lanes(flip(qt).astype(bf16), heads)

    for k, piece in enumerate(x_pieces):
        for r in range(per):
            project((lax.axis_index("head") ^ k) * per + r, piece[r * TILE : (r + 1) * TILE, :])
    key_index = lax.broadcasted_iota(jnp.int32, (TILE, TILE), 0)

    def rows(i, _):
        acc_ref[...] = jnp.zeros_like(acc_ref)
        start = ss_ref[:, lanes(i)]

        def cols(j, _):
            s = dot(kx_ref[j], qxt_ref[i]) + jnp.concatenate([pos_ref[i - j]] * heads, axis=1)
            seen = (key_index + j * TILE) >= start
            s = jnp.where(jnp.concatenate([seen] * heads, axis=1), s, NEG)
            w = (s + s * jnp.tanh(s)).astype(bf16)
            acc_ref[...] += dot(vt_ref[j], w)
            return 0

        lax.fori_loop(first_ref[i * TILE] // TILE, i + 1, cols, 0)
        attn_ref[i] = own_rows(acc_ref[...], heads)
        return 0

    lax.fori_loop(0, nb, rows, 0)


def gate_kernel(n_head, *refs):
    refs = list(refs)
    take = lambda count: [refs.pop(0) for _ in range(count)]
    cot_pieces = take(n_head)
    attn_ref, xn_ref, wt_ref = take(3)
    p_ref, gg_ref, stat_ref, gb_ref = refs
    width = attn_ref.shape[1]
    per = cot_pieces[0].shape[0] // TILE
    gb_ref[...] = jnp.sum(cot_pieces[0][...].astype(f32), axis=0, keepdims=True)
    for k, piece in enumerate(cot_pieces):
        for r in range(per):
            i = (lax.axis_index("head") ^ k) * per + r
            p = dot_nt(wt_ref[:width], xn_ref[i])
            gate = p * (0.5 + 0.5 * jnp.tanh(0.5 * p))
            gg = dot_nt(wt_ref[4 * width :], piece[r * TILE : (r + 1) * TILE, :])
            grad = gg * gate
            p_ref[i] = p
            gg_ref[i] = gg
            at = attn_ref[i]
            mean = jnp.sum(at, axis=0, keepdims=True) / width
            centred = at - mean
            stat_ref[i] = jnp.concatenate(
                [
                    mean,
                    jnp.sum(centred * centred, axis=0, keepdims=True),
                    jnp.sum(grad, axis=0, keepdims=True),
                    jnp.sum(grad * centred, axis=0, keepdims=True),
                ],
                axis=0,
            )


def middle_kernel(heads, n_head, *refs):
    refs = list(refs)
    take = lambda count: [refs.pop(0) for _ in range(count)]
    stats = take(n_head)
    cot_pieces = take(n_head)
    attn_ref, p_ref, gg_ref, xn_ref, wt_ref = take(5)
    branches = take(n_head)
    dax_ref, daxt_ref, gun_ref = take(3)
    parts, acc_ref, wg_ref = refs[:-2], refs[-2], refs[-1]
    width = attn_ref.shape[1]
    per = cot_pieces[0].shape[0] // TILE
    for k, piece in enumerate(cot_pieces):
        for r in range(per):
            i = (lax.axis_index("head") ^ k) * per + r
            at = slice(r * TILE, (r + 1) * TILE)
            st = [s[i] for s in stats]
            mean = sum(p[0:1] for p in st) / n_head
            spread = sum(p[1:2] + width * (p[0:1] - mean) * (p[0:1] - mean) for p in st)
            scale = lax.rsqrt(spread / HD + norm_epsilon)
            first = sum(p[2:3] for p in st) / HD
            second = scale * sum(p[3:4] + (p[0:1] - mean) * p[2:3] for p in st) / HD
            normed = (attn_ref[i] - mean) * scale
            p = p_ref[i]
            sg = 0.5 + 0.5 * jnp.tanh(0.5 * p)
            gate = p * sg
            gg = gg_ref[i]
            gated = (normed * gate).astype(bf16)
            grad = scale * (gg * gate - first - normed * second)
            dax_ref[i] = own_lanes(flip(grad).astype(bf16), heads)
            daxt_ref[i] = by_head((grad * 0.5).astype(bf16), heads)
            gu = (gg * normed * (sg + gate * (1.0 - sg))).astype(bf16)
            gun_ref[i] = flip(gu).astype(bf16)
            branches[k][at, :] = dot(flip(gated).astype(bf16), wt_ref[4 * width :]).astype(bf16)
            add_gate, add_out = dot(gu, xn_ref[i]), dot(gated, piece[at, :])
            if k + r == 0:
                acc_ref[:width] = add_gate
                acc_ref[width:] = add_out
            else:
                acc_ref[:width] += add_gate
                acc_ref[width:] += add_out
    wg_ref[...] = flip(acc_ref[...])
    send_parts(wg_ref, parts)


def send_parts(wg_ref, parts):
    low = len(parts)
    high, rows = parts[0].shape[0], parts[0].shape[1]
    me = lax.axis_index("dp") % low
    for k in range(low):
        for p in range(high):
            start = pl.multiple_of((p * low + (me ^ k)) * rows, 16)
            parts[k][p] = wg_ref[pl.ds(start, rows), :].astype(bf16)


def backward_kernel(heads, n_dp, extra, first_ref, *refs):
    refs = list(refs)
    take = lambda count: [refs.pop(0) for _ in range(count)]
    kx_ref, kxt_ref, qxt_ref, v_ref, qm_ref, dax_ref, daxt_ref, pos_ref = take(8)
    d_ref, xn_ref, ss_ref, gb_ref = take(4)
    gp_ref = refs.pop(0)
    parts = take(split_dp(n_dp)[1])
    accv_ref, acck_ref, accq_ref, posg_ref, m2_ref, gpq_ref, acc_ref, wg_ref, small_ref = refs
    nb, width = v_ref.shape[0], v_ref.shape[2]
    accv_ref[...] = jnp.zeros_like(accv_ref)
    acck_ref[...] = jnp.zeros_like(acck_ref)
    posg_ref[...] = jnp.zeros_like(posg_ref)
    m2_ref[...] = jnp.zeros_like(m2_ref)
    key_index = lax.broadcasted_iota(jnp.int32, (TILE, TILE), 0)
    factor = 1.0 / math.sqrt(HEAD_DIM)

    def rows(i, _):
        accq_ref[...] = jnp.zeros_like(accq_ref)
        start = ss_ref[:, lanes(i)]

        def cols(j, _):
            s = dot(kx_ref[j], qxt_ref[i]) + jnp.concatenate([pos_ref[i - j]] * heads, axis=1)
            seen = (key_index + j * TILE) >= start
            s = jnp.where(jnp.concatenate([seen] * heads, axis=1), s, NEG)
            t = jnp.tanh(s)
            u = 1.0 + t
            w = s * u
            ds = dot(v_ref[j], daxt_ref[i]) * (u + w * (1.0 - t))
            low = ds.astype(bf16)
            accv_ref[j] += dot(w.astype(bf16), dax_ref[i])
            acck_ref[j] += dot(low, qm_ref[i])
            accq_ref[...] += dot(kxt_ref[j], low)
            posg_ref[i - j] += sum(ds[:, h * TILE : (h + 1) * TILE] for h in range(heads))
            return 0

        lax.fori_loop(first_ref[i * TILE] // TILE, i + 1, cols, 0)
        gpq_ref[i] = own_rows(accq_ref[NTB:], heads)
        tp = sum(accq_ref[:NTB, h * TILE : (h + 1) * TILE] for h in range(heads))
        high = tp.astype(bf16)
        rest = (tp - high.astype(f32)).astype(bf16)
        onehot = kx_ref[i, :, :NTB]
        m2_ref[...] += dot(high, onehot) + dot(rest, onehot)
        return 0

    lax.fori_loop(0, nb, rows, 0)
    acc_ref[...] = jnp.zeros_like(acc_ref)

    def tail(i, _):
        gp = jnp.concatenate([flip(accv_ref[i]), gpq_ref[i] * factor, flip(acck_ref[i]) * factor], axis=0)
        gp = (gp * d_ref[i]).astype(bf16)
        gp_ref[i] = flip(gp).astype(bf16)
        acc_ref[...] += dot(gp, xn_ref[i])
        return 0

    lax.fori_loop(0, nb, tail, 0)
    small_ref[...] = jnp.zeros_like(small_ref)
    small_ref[:, :D] = gb_ref[...]
    for d in range(nb):
        g = diagonals(posg_ref[d])
        small_ref[:, D + d * TILE : D + (d + 1) * TILE] += g[:, :TILE]
        if d > 0:
            small_ref[:, D + (d - 1) * TILE : D + d * TILE] += g[:, TILE:]
    m2 = m2_ref[...]
    g = diagonals(m2 + jnp.transpose(m2))[:, :NTB]
    zero = lax.broadcasted_iota(jnp.int32, (1, NTB), 1) == 0
    at = D + nb * TILE
    small_ref[:, at : at + NTB] = jnp.where(zero, 0.5 * g, g)
    step = D // n_dp
    grads = flip(acc_ref[...])
    for p in range(n_dp):
        here = jnp.concatenate(
            [small_ref[:, (p * extra + r) * 128 : (p * extra + r + 1) * 128] for r in range(extra)], axis=0
        )
        high = here.astype(bf16).astype(f32)
        block = jnp.concatenate([high, here - high, jnp.zeros((16 - 2 * extra, 128), f32)], axis=0)
        wg_ref[p * (step + 16) : p * (step + 16) + step] = grads[p * step : (p + 1) * step]
        wg_ref[p * (step + 16) + step : (p + 1) * (step + 16)] = jnp.concatenate(
            [block, jnp.zeros((16, 3 * width - 128), f32)], axis=1
        )
    send_parts(wg_ref, parts)


def input_kernel(n_head, gp_ref, gun_ref, wt_ref, keep, send):
    width = gun_ref.shape[2]
    per = keep.shape[1] // TILE
    for k in range(n_head):
        device = lax.axis_index("head") ^ k
        target = (keep, send)[k % 2]
        for r in range(per):
            i = device * per + r
            rows = dot(gp_ref[i], wt_ref[width : 4 * width]) + dot(gun_ref[i], wt_ref[:width])
            target[device // 2, r * TILE : (r + 1) * TILE] = rows.astype(bf16)


def collect_kernel(high, extra, *refs):
    blocks, (grads_ref, message_ref) = refs[:high], refs[high:]
    total = blocks[0][...]
    for k in range(1, high):
        total = total + blocks[k][...].astype(f32)
    rows = grads_ref.shape[0]
    grads = total[:rows]
    grads_ref[...] = grads
    squares = jnp.sum(jnp.sum(grads * grads, axis=0, keepdims=True), axis=1, keepdims=True)
    message = jnp.concatenate(
        [
            total[rows : rows + extra, :128] + total[rows + extra : rows + 2 * extra, :128],
            jnp.zeros((7 - extra, 128), f32),
            jnp.broadcast_to(squares, (1, 128)),
        ],
        axis=0,
    )
    for k in range(message_ref.shape[0]):
        message_ref[k] = message


def update_kernel(n_head, extra, group, heard_ref, grads_ref, *refs):
    state, outs = refs[:9], refs[9:]
    grad_proj_ref, grad_out_ref, grad_small_ref, norm_ref = outs[:4]
    n_all = heard_ref.shape[0]
    width = grad_out_ref.shape[1]
    lead, pos_rows, used = D // 128, POS // 128, (D + group) // 128
    grad_small_ref[...] = jnp.zeros_like(grad_small_ref)
    squares = heard_ref[0, 7:8, :]
    for k in range(1, n_all):
        squares = squares + heard_ref[k, 7:8, :]
    for p in range(n_all // n_head):
        rows = heard_ref[p * n_head, :extra, :]
        for h in range(1, n_head):
            rows = rows + heard_ref[p * n_head + h, :extra, :]
        for r in range(extra):
            at = p * extra + r
            if at < used:
                grad_small_ref[at : at + 1, :] = rows[r : r + 1]
            elif at == used:
                grad_small_ref[lead + pos_rows : lead + pos_rows + 1, :] = rows[r : r + 1]
    small = grad_small_ref[...]
    total = jnp.sum(jnp.sum(small * small, axis=0, keepdims=True), axis=1, keepdims=True) + squares[:, :1]
    norm = jnp.sqrt(total)
    norm_ref[...] = norm
    factor = jnp.minimum(1.0, clip_norm / (norm + 1e-06))

    def update(get, put, grad, rate, decay):
        for k, value in enumerate(adam_step(get(0), grad, get(1), get(2), factor, rate, decay)):
            put(k, value)

    for c in range(4):
        grad = grads_ref[:, 3 * width : 4 * width] if c == 0 else grads_ref[:, (c - 1) * width : c * width]
        grad_proj_ref[:, c, :] = grad

        def put(k, value):
            outs[4 + k][:, c, :] = value

        update(lambda k: state[k][:, c, :], put, grad, rate_matrix, decay_matrix)
    grad = grads_ref[:, 4 * width :]
    grad_out_ref[...] = grad

    def put_out(k, value):
        outs[7 + k][...] = value

    update(lambda k: state[3 + k][...], put_out, grad, rate_matrix, decay_matrix)

    def put_small(k, value):
        outs[10 + k][...] = value

    update(lambda k: state[6 + k][...], put_small, small, rate_small, 0.0)


def call(kernel, name, in_specs, outs, scratch, us, room=20):
    return pl.pallas_call(
        kernel,
        out_shape=[jax.ShapeDtypeStruct(shape, dtype) for shape, dtype, _ in outs],
        in_specs=in_specs,
        out_specs=[spec for _, _, spec in outs],
        scratch_shapes=scratch,
        compiler_params=pltpu.CompilerParams(vmem_limit_bytes=room * 2**20),
        cost_estimate=pl.CostEstimate(flops=int(us * 1e9), bytes_accessed=int(us * 3e6), transcendentals=0),
        name=name,
    )


def block(shape):
    return pl.BlockSpec((1,) + tuple(shape[1:]), lambda i: (i,) + (0,) * (len(shape) - 1))


def shards(
    tokens,
    cotangent,
    seq_start,
    time_bucket,
    proj_weight,
    out_weight,
    small_params,
    proj_mean,
    proj_square,
    out_mean,
    out_square,
    small_mean,
    small_square,
):
    n_head = lax.axis_size("head")
    n_dp = lax.axis_size("dp")
    here = tokens.shape[0]
    group = here * n_head
    nb = group // TILE
    per = here // TILE
    rows_here, _, width = proj_weight.shape
    heads = width // HEAD_DIM
    high, low = split_dp(n_dp)

    (weights,) = call(
        cast_kernel, "cast", [VMEM] * 2, [((rows_here, 5 * width), bf16, VMEM)], [], 1
    )(proj_weight, out_weight.T)
    x_pieces = gather_head(tokens)
    w_pieces, offsets, operands = gather_dp(weights)
    cot_pieces = gather_direct(after(cotangent, operands[-1]))
    starts = seq_start.reshape(1, group)
    small_rows = small_params.reshape(-1, 128)
    times = time_bucket.reshape(1, group)

    pos, oh, oht, trow = call(
        prepare_kernel,
        "prepare",
        [VMEM] * 2,
        [
            ((nb, TILE, TILE), f32, VMEM),
            ((nb, TILE, NTB), bf16, VMEM),
            ((nb, NTB, TILE), bf16, VMEM),
            ((nb, NTB, TILE), bf16, VMEM),
        ],
        [],
        5,
    )(after(times, operands[1]), small_rows)

    items = [
        ((nb, width, TILE), f32),
        ((nb, TILE, D), bf16),
        ((nb, 3 * width, TILE), f32),
        ((nb, TILE, NTB + width), bf16),
        ((nb, NTB + width, TILE), bf16),
        ((nb, NTB + width, heads * TILE), bf16),
        ((nb, TILE, width), bf16),
        ((nb, heads * TILE, width), bf16),
        ((5 * width, D), bf16),
    ]
    attn, xn, dsilu, kx, kxt, qxt, v, qm, wt = call(
        functools.partial(forward_kernel, heads, n_head, offsets),
        "forward",
        [SMEM] + [VMEM] * (n_head + len(w_pieces) + 5),
        [item + (VMEM,) for item in items],
        [
            pltpu.VMEM((D, 5 * width), bf16),
            pltpu.VMEM((nb, width, TILE), bf16),
            pltpu.VMEM((width, heads * TILE), f32),
        ],
        30,
    )(seq_start, *x_pieces, *w_pieces, oh, oht, trow, pos, starts)

    column = ((nb, width, TILE), f32, VMEM)
    p_gate, gg, stat, gb = call(
        functools.partial(gate_kernel, n_head),
        "gate",
        [VMEM] * (n_head + 3),
        [column, column, ((nb, 4, TILE), f32, VMEM), ((1, D), f32, VMEM)],
        [],
        5,
    )(*cot_pieces, attn, xn, wt)

    stats = [stat] + [swap(stat, "head", k) for k in range(1, n_head)]
    out = call(
        functools.partial(middle_kernel, heads, n_head),
        "middle",
        [VMEM] * (2 * n_head + 5),
        [((here, D), bf16, VMEM)] * n_head
        + [
            ((nb, heads * TILE, width), bf16, VMEM),
            ((nb, width, heads * TILE), bf16, VMEM),
            ((nb, TILE, width), bf16, VMEM),
        ]
        + [((high, rows_here, 2 * width), bf16, VMEM)] * low,
        [pltpu.VMEM((2 * width, D), f32), pltpu.VMEM((D, 2 * width), f32)],
        6,
    )(*stats, *cot_pieces, attn, p_gate, gg, xn, wt)
    branches, (dax, daxt, gun), early_parts = out[:n_head], out[n_head : n_head + 3], out[n_head + 3 :]
    received = [swap(branches[k], "head", k) for k in range(1, n_head)]
    early_received = [swap(early_parts[k], "dp", k) for k in range(1, low)]

    length = D + group + NTB
    extra = -(-length // (128 * n_dp))
    gp, *late_parts = call(
        functools.partial(backward_kernel, heads, n_dp, extra),
        "backward",
        [SMEM] + [VMEM] * 12,
        [((nb, TILE, 3 * width), bf16, VMEM)] + [((high, rows_here + 16, 3 * width), bf16, VMEM)] * low,
        [
            pltpu.VMEM((nb, TILE, width), f32),
            pltpu.VMEM((nb, TILE, width), f32),
            pltpu.VMEM((NTB + width, heads * TILE), f32),
            pltpu.VMEM((nb, TILE, TILE), f32),
            pltpu.VMEM((NTB, NTB), f32),
            pltpu.VMEM((nb, width, TILE), f32),
            pltpu.VMEM((3 * width, D), f32),
            pltpu.VMEM((n_dp * (rows_here + 16), 3 * width), f32),
            pltpu.VMEM((1, extra * n_dp * 128), f32),
        ],
        35,
        24,
    )(seq_start, kx, kxt, qxt, v, qm, dax, daxt, pos, dsilu, xn, starts, gb)

    tied = lax.optimization_barrier((gp, *late_parts, *received, *early_received))
    gp, late_parts = tied[0], tied[1 : 1 + low]
    received, early_received = tied[1 + low : low + n_head], tied[low + n_head :]
    late_received = [swap(late_parts[k], "dp", k) for k in range(1, low)]
    early = add_parts(early_parts[0], early_received)
    keep, send = call(
        functools.partial(input_kernel, n_head),
        "input_rows",
        [VMEM] * 3,
        [((n_head // 2, here, D), bf16, VMEM)] * 2,
        [],
        4,
    )(gp, gun, wt)
    late_received = after_all(late_received, send)
    late = add_parts(late_parts[0], late_received)
    both = jnp.concatenate([late, jnp.pad(early, ((0, 0), (0, 16), (0, 0)))], axis=2)
    blocks = send_high(both)
    rows_total = scatter_core(keep, send, both)
    blocks[0] = after(blocks[0], rows_total)
    n_all = n_dp * n_head
    grads_shape = ((rows_here, 5 * width), f32)
    grads, message = call(
        functools.partial(collect_kernel, high, extra),
        "collect",
        [VMEM] * high,
        [grads_shape + (VMEM,), ((n_all, 8, 128), f32, VMEM)],
        [],
        0.1,
    )(*blocks)
    message, rows_total = lax.optimization_barrier((message, rows_total))
    heard = lax.all_to_all(message, ("dp", "head"), 0, 0, tiled=True)
    normed_grad = scatter_chip(rows_total)
    mixed = (add_parts(branches[0], after_all(received, message)) + small_params[:D] + tokens.astype(f32)).astype(bf16)

    inputs = tokens.astype(f32)
    centred = inputs - jnp.mean(inputs, -1, keepdims=True)
    scale_in = lax.rsqrt(jnp.mean(centred * centred, -1, keepdims=True) + norm_epsilon)
    normed = centred * scale_in
    input_grad = cotangent.astype(f32) + scale_in * (
        normed_grad
        - jnp.mean(normed_grad, -1, keepdims=True)
        - normed * jnp.mean(normed_grad * normed, -1, keepdims=True)
    )

    state = [proj_weight, proj_mean, proj_square, out_weight.T, out_mean.T, out_square.T]
    state += [x.reshape(-1, 128) for x in (small_params, small_mean, small_square)]
    proj_shape, out_shape, small_shape = proj_weight.shape, (rows_here, width), small_rows.shape
    shapes = [proj_shape, out_shape, small_shape, (1, 1)] + [proj_shape] * 3 + [out_shape] * 3 + [small_shape] * 3
    results = call(
        functools.partial(update_kernel, n_head, extra, group),
        "update",
        [VMEM] * (2 + len(state)),
        [(shape, f32, VMEM) for shape in shapes],
        [],
        0.1,
    )(heard, grads, *state)
    grad_proj, grad_out, grad_small, grad_norm = results[:4]
    grad_out, grad_small, grad_norm = grad_out.T, grad_small.reshape(-1), grad_norm.reshape(())
    new_proj, mean_proj, square_proj = results[4:7]
    new_out, mean_out, square_out = [x.T for x in results[7:10]]
    new_small, mean_small, square_small = [x.reshape(-1) for x in results[10:13]]
    return (
        mixed,
        input_grad,
        grad_proj,
        grad_out,
        grad_small,
        grad_norm,
        new_proj,
        mean_proj,
        square_proj,
        new_out,
        mean_out,
        square_out,
        new_small,
        mean_small,
        square_small,
    )


def solution(mesh):
    in_specs = (
        P(("dp", "head"), None),
        P(("dp", "head"), None),
        P("dp"),
        P("dp"),
        P("dp", None, "head"),
        P("head", "dp"),
        P(),
        P("dp", None, "head"),
        P("dp", None, "head"),
        P("head", "dp"),
        P("head", "dp"),
        P(),
        P(),
    )
    out_specs = (
        P(("dp", "head"), None),
        P(("dp", "head"), None),
        P("dp", None, "head"),
        P("head", "dp"),
        P(),
        P(),
        P("dp", None, "head"),
        P("dp", None, "head"),
        P("dp", None, "head"),
        P("head", "dp"),
        P("head", "dp"),
        P("head", "dp"),
        P(),
        P(),
        P(),
    )
    return jax.shard_map(shards, mesh=mesh, in_specs=in_specs, out_specs=out_specs, check_vma=False)
```

time: 187 us -> 130 us (0.70)
  Pallas kernels: 81.8 us -> 54.2 us
  starting transfers between devices: 39.1 us -> 28.3 us
  other arithmetic: 16.7 us -> 7.84 us
  between operations: 4.99 us -> 1.12 us
  waiting for transfers between devices: 37.9 us -> 34.7 us
  local copies, waits for them, and re-layouts: 5.8 us -> 3.2 us
    pallas_call x3 -> x6, Pallas kernels: 26.9 us -> 9.13 us  [the longest x1 2.75 us: shards(): call(functools.partial(input_kernel, n_head), 'input_rows', [VMEM] * 3, [...]
    ppermute x27 -> x22, starting transfers between devices: 35.8 us -> 24.8 us  [swap(): return lax.ppermute(x, axis, [(i, i ^ k) for i in range(n)])]
    ppermute x27 -> x22, waiting for transfers between devices: 37.1 us -> 26.1 us  [swap(): return lax.ppermute(x, axis, [(i, i ^ k) for i in range(n)])]
    all_to_all x1, waiting for transfers between devices: 0.88 us -> 8.58 us  [shards(): heard = lax.all_to_all(message, ('dp', 'head'), 0, 0, tiled=True)]
    pallas_call x1, Pallas kernels: 22.6 us -> 17.2 us  [shards(): call(functools.partial(forward_kernel, heads, n_head, offsets), 'forward'...]
    reduce_sum x5 -> x0, other arithmetic: 4.32 us -> none  [the longest x2 2.15 us: shards(): total = jnp.sum(heard[:, :, 7, 0]) + jnp.sum(small_sum * small_sum)]
    sub x3 -> x0, other arithmetic: 4.03 us -> none  [adam_step(): return (weight - rate * (update + decay * weight), first_new, second_new)]
    pallas_call x1, Pallas kernels: 4.45 us -> 1.91 us  [shards(): call(prepare_kernel, 'prepare', [VMEM] * 2, [((nb, TILE, TILE), f32, VMEM...]
  transfers between devices with their start and end apart: 28 -> 23, of which waited for: 9 -> 9; matrix products, arithmetic and copies ran while one was open for 10% -> 3% of each run, Pallas kernels for 33% -> 38%
where the time goes in v3:
time: 130 us; the launch traced here: 129 us
  Pallas kernels  54.2 us (42%)
  waiting for transfers between devices  34.7 us (27%)
  starting transfers between devices  28.3 us (22%)
  other arithmetic  7.84 us (6%)
  local copies, waits for them, and re-layouts  3.2 us (2%)
    ppermute x22, waiting for transfers between devices, swap(): return lax.ppermute(x, axis, [(i, i ^ k) for i in range(n)])  26.1 us
    pallas_call x1, Pallas kernels, shards(): call(functools.partial(backward_kernel, heads, n_dp, extra), 'backward',...  25.9 us
    ppermute x22, starting transfers between devices, swap(): return lax.ppermute(x, axis, [(i, i ^ k) for i in range(n)])  24.8 us
    pallas_call x1, Pallas kernels, shards(): call(functools.partial(forward_kernel, heads, n_head, offsets), 'forward'...  17.2 us
    all_to_all x1, waiting for transfers between devices, shards(): heard = lax.all_to_all(message, ('dp', 'head'), 0, 0, tiled=True)  8.58 us
    all_to_all x1, starting transfers between devices, shards(): heard = lax.all_to_all(message, ('dp', 'head'), 0, 0, tiled=True)  3.54 us
    add x1, other arithmetic, shards(): cotangent.astype(f32)  2.93 us
    pallas_call x1, Pallas kernels, shards(): call(functools.partial(input_kernel, n_head), 'input_rows', [VMEM] * 3, [...  2.75 us
  transfers between devices with their start and end apart: 23, of which 9 were waited for; matrix products, arithmetic and copies ran while one was open for 3% of the time, Pallas kernels for 38%

profile of v3, /device:TPU:0, one launch (start us, length us, event | category | flops | bytes accessed | tf_op | source)
XLA Modules:
  0.0 129.4 jit_solution(9754993981979672649)
XLA Ops:
  0.7 3.0 %collective-permute-start.6 = (bf16[512,512]{1,0:T(8,128)(2,1)}, bf16[512,512]{1,0:T(8,128)(2,1)S(1)}, u32[]{:S(2)}, u32[]{:S(2)}) collective-permute-start(bf16[512,512]{1,0:T(8,128)(2,1)} %refs_0_.2), channel_id=1, source_target_pairs={{0,2},{1,3},{2,0},{3,1},{4,6},{5,7},{6,4},{7,5},{8,10},{9,11},{10,... | collective-permute-start | bytes 1572872 | tf_op jit(solution)/shard_map/ppermute | solution.py:49
  3.7 0.9 copy-done.2
  4.6 0.8 copy-done.9
  5.3 0.1 cast.1.refs_4_
  5.5 2.7 %collective-permute-start = (bf16[64,640]{1,0:T(8,128)(2,1)S(1)}, bf16[64,640]{1,0:T(8,128)(2,1)S(1)}, u32[]{:S(2)}, u32[]{:S(2)}) collective-permute-start(bf16[64,640]{1,0:T(8,128)(2,1)S(1)} %cast.1.refs_4_), channel_id=1, source_target_pairs={{0,16},{4,20},{8,24},{12,28},{16,0},{20,4},{24,8},{28,12},{1,17},{... | collective-permute-start | bytes 245768 | tf_op jit(solution)/shard_map/ppermute | solution.py:49
  8.1 4.1 %collective-permute-done.refs_5_ = bf16[64,640]{1,0:T(8,128)(2,1)S(1)} collective-permute-done((bf16[64,640]{1,0:T(8,128)(2,1)S(1)}, bf16[64,640]{1,0:T(8,128)(2,1)S(1)}, u32[]{:S(2)}, u32[]{:S(2)}) %collective-permute-start) | collective-permute-done | bytes 81952 | tf_op jit(solution)/shard_map/ppermute | solution.py:49
  12.2 0.6 collective-permute-start.1
  12.8 0.0 collective-permute-start.5
  12.9 2.9 %collective-permute-done.6.refs_2_ = bf16[512,512]{1,0:T(8,128)(2,1)S(1)} collective-permute-done((bf16[512,512]{1,0:T(8,128)(2,1)}, bf16[512,512]{1,0:T(8,128)(2,1)S(1)}, u32[]{:S(2)}, u32[]{:S(2)}) %collective-permute-start.6) | collective-permute-done | bytes 524320 | tf_op jit(solution)/shard_map/ppermute | solution.py:49
  15.8 0.0 collective-permute-start.7
  15.8 1.8 %collective-permute-done.1.refs_6_ = bf16[128,640]{1,0:T(8,128)(2,1)S(1)} collective-permute-done((bf16[128,640]{1,0:T(8,128)(2,1)S(1)}, bf16[128,640]{1,0:T(8,128)(2,1)S(1)}, u32[]{:S(2)}, u32[]{:S(2)}) %collective-permute-start.1) | collective-permute-done | bytes 163872 | tf_op jit(solution)/shard_map/ppermute | solution.py:49
  17.7 1.6 %collective-permute-start.8 = (bf16[256,640]{1,0:T(8,128)(2,1)S(1)}, bf16[256,640]{1,0:T(8,128)(2,1)S(1)}, u32[]{:S(2)}, u32[]{:S(2)}) collective-permute-start(bf16[256,640]{1,0:T(8,128)(2,1)S(1)} %pad_maximum_fusion), channel_id=1, source_target_pairs={{0,4},{4,0},{8,12},{12,8},{16,20},{20,16},{24,28},{28,24},{1,5},{5... | collective-permute-start | bytes 983048 | tf_op jit(solution)/shard_map/ppermute | solution.py:49
  19.3 1.9 %prepare.1 = (f32[8,256,256]{2,1,0:T(8,128)S(1)}, bf16[8,256,128]{2,1,0:T(8,128)(2,1)S(1)}, bf16[8,128,256]{2,1,0:T(8,128)(2,1)S(1)}, bf16[8,128,256]{2,1,0:T(8,128)(2,1)S(1)}) custom-call(s32[1,2048]{1,0:T(1,128)S(1)} %bitcast.43, f32[69,128]{1,0:T(8,128)S(1)} %bitcast.35), custom_call_target="tpu_custom_call" | custom-call | flops 5000000000 | bytes 15000000 | tf_op jit(solution)/shard_map/prepare/pallas_call | solution.py:590
  21.2 0.1 collective-permute-start.2
  21.3 0.6 collective-permute-start.3
  21.9 1.3 collective-permute-start.4
  23.1 2.9 %collective-permute-done.8.refs_7_ = bf16[256,640]{1,0:T(8,128)(2,1)S(1)} collective-permute-done((bf16[256,640]{1,0:T(8,128)(2,1)S(1)}, bf16[256,640]{1,0:T(8,128)(2,1)S(1)}, u32[]{:S(2)}, u32[]{:S(2)}) %collective-permute-start.8) | collective-permute-done | bytes 327712 | tf_op jit(solution)/shard_map/ppermute | solution.py:49
  26.1 17.2 %forward.1 = (f32[8,128,256]{2,1,0:T(8,128)S(1)}, bf16[8,256,512]{2,1,0:T(8,128)(2,1)S(1)}, f32[8,384,256]{2,1,0:T(8,128)S(1)}, bf16[8,256,256]{2,1,0:T(8,128)(2...) custom-call(s32[2048]{0:T(1024)S(1)} %copy-done.14, ...), custom_call_target="tpu_custom_call" | custom-call | flops 30000001024 | bytes 90000000 | tf_op jit(solution)/shard_map/forward/pallas_call | solution.py:615
  43.3 0.0 collective-permute-done.2.refs_1_.refs_5_
  43.3 3.1 %collective-permute-done.4.refs_3_.refs_7_ = bf16[512,512]{1,0:T(8,128)(2,1)S(1)} collective-permute-done((bf16[512,512]{1,0:T(8,128)(2,1)S(1)}, bf16[512,512]{1,0:T(8,128)(2,1)S(1)}, u32[]{:S(2)}, u32[]{:S(2)}) %collective-permute-start.4) | collective-permute-done | bytes 524320 | tf_op jit(solution)/shard_map/ppermute | solution.py:49
  46.4 1.6 %gate.1 = (f32[8,128,256]{2,1,0:T(8,128)S(1)}, f32[8,128,256]{2,1,0:T(8,128)S(1)}, f32[8,4,256]{2,1,0:T(4,128)S(1)}, f32[1,512]{1,0:T(1,128)S(1)}) custom-call(bf16[512,512]{1,0:T(8,128)(2,1)S(1)} %copy-done.1, bf16[512,512]{1,0:T(8,128)(2,1)S(1)} %collective-permute-done.2.refs_1_.refs_5_, bf16[512,512]{1,0:T(8,128)(2,1)S(1)} %collective-permute-done.3.refs_2_.refs_6_, ...), custom_call_target="tpu_custom_call" | custom-call | flops 5000000000 | bytes 15000000 | tf_op jit(solution)/shard_map/gate/pallas_call | solution.py:629
  48.0 0.6 collective-permute-start.10
  48.6 1.1 collective-permute-start.11
  49.7 0.5 collective-permute-start.9
  50.2 2.1 %collective-permute-done.10.refs_2_ = f32[8,4,256]{2,1,0:T(4,128)S(1)} collective-permute-done((f32[8,4,256]{2,1,0:T(4,128)S(1)}, f32[8,4,256]{2,1,0:T(4,128)S(1)}, u32[]{:S(2)}, u32[]{:S(2)}) %collective-permute-start.10) | collective-permute-done | bytes 32800 | tf_op jit(solution)/shard_map/ppermute | solution.py:49
  52.3 2.1 %middle.1 = (bf16[512,512]{1,0:T(8,128)(2,1)S(1)}, bf16[512,512]{1,0:T(8,128)(2,1)S(1)}, bf16[512,512]{1,0:T(8,128)(2,1)S(1)}, bf16[512,512]{1,0:T(8,128)(2,1)S(...) custom-call(f32[8,4,256]{2,1,0:T(4,128)S(1)} %get-tuple-element.87.r, ...), custom_call_target="tpu_custom_call" | custom-call | flops 6000000000 | bytes 18000000 | tf_op jit(solution)/shard_map/middle/pallas_call | solution.py:639
  54.4 0.2 collective-permute-start.12
  54.6 1.2 collective-permute-start.13
  55.9 0.4 collective-permute-start.14
  56.3 0.5 collective-permute-start.15
  56.8 25.9 %backward.1 = (bf16[8,256,384]{2,1,0:T(8,128)(2,1)S(1)}, bf16[4,80,384]{2,1,0:T(8,128)(2,1)S(1)}, bf16[4,80,384]{2,1,0:T(8,128)(2,1)S(1)}) custom-call(s32[2048]{0:T(1024)S(1)} %copy-done.14, bf16[8,256,256]{2,1,0:T(8,128)(2,1)S(1)} %get-tuple-element.91.refs_0_, bf16[8,256,256]{2,1,0:T(8,128)(2,1)S(1)} %get-tuple-element.92.refs_1_, ...), custom_call_target="tpu_custom_call" | custom-call | flops 35000000512 | bytes 105000000 | tf_op jit(solution)/shard_map/backward/pallas_call | solution.py:659
  82.7 0.0 copy-start.22
  82.8 0.1 collective-permute-start.16
  82.9 0.5 copy-done.22
  83.4 2.7 %input_rows.1 = (bf16[2,512,512]{2,1,0:T(8,128)(2,1)S(1)}, bf16[2,512,512]{2,1,0:T(8,128)(2,1)}) custom-call(bf16[8,256,384]{2,1,0:T(8,128)(2,1)S(1)} %get-tuple-element.112.gp_ref, bf16[8,256,128]{2,1,0:T(8,128)(2,1)S(1)} %get-tuple-element.113.gun_ref, bf16[640,512]{1,0:T(8,128)(2,1)S(1)} %get-tuple-element.86.refs_6_.refs_12_.wt_ref), custom_call_target="tpu_custom_call" | custom-call | flops 4000000000 | bytes 12000000 | tf_op jit(solution)/shard_map/input_rows/pallas_call | solution.py:684
  86.2 0.2 collective-permute-start.17
  86.4 0.1 convert_reduce_fusion
  86.6 0.9 convert_add_fusion.3
  87.5 3.4 %collective-permute-done.16 = bf16[4,80,384]{2,1,0:T(8,128)(2,1)S(1)} collective-permute-done((bf16[4,80,384]{2,1,0:T(8,128)(2,1)S(1)}, bf16[4,80,384]{2,1,0:T(8,128)(2,1)S(1)}, u32[]{:S(2)}, u32[]{:S(2)}) %collective-permute-start.16) | collective-permute-done | bytes 245792 | tf_op jit(solution)/shard_map/ppermute | solution.py:49
  90.9 0.1 convert_add_fusion.2
  91.0 0.1 dynamic-slice_bitcast_fusion.1
  91.1 6.7 %collective-permute-start.18 = (bf16[80,640]{1,0:T(8,128)(2,1)S(1)}, bf16[80,640]{1,0:T(8,128)(2,1)S(1)}, u32[]{:S(2)}, u32[]{:S(2)}) collective-permute-start(bf16[80,640]{1,0:T(8,128)(2,1)S(1)} %get-tuple-element.147), channel_id=1, source_target_pairs={{0,8},{4,12},{8,0},{12,4},{16,24},{20,28},{24,16},{28,20},{1,9},{5... | collective-permute-start | bytes 307208 | tf_op jit(solution)/shard_map/ppermute | solution.py:49
  97.7 1.1 collective-permute-start.19
  98.9 1.3 %collective-permute-start.20 = (bf16[80,640]{1,0:T(8,128)(2,1)S(1)}, bf16[80,640]{1,0:T(8,128)(2,1)S(1)}, u32[]{:S(2)}, u32[]{:S(2)}) collective-permute-start(bf16[80,640]{1,0:T(8,128)(2,1)S(1)} %get-tuple-element.145), channel_id=1, source_target_pairs={{0,24},{4,28},{8,16},{12,20},{16,8},{20,12},{24,0},{28,4},{1,25},{... | collective-permute-start | bytes 307208 | tf_op jit(solution)/shard_map/ppermute | solution.py:49
  100.2 0.1 select_maximum_fusion
  100.3 1.6 %convert_add_fusion = f32[2,512,512]{2,1,0:T(8,128)S(1)} fusion(bf16[2,512,512]{2,1,0:T(8,128)(2,1)} %collective-permute-done.17, bf16[2,512,512]{2,1,0:T(8,128)(2,1)S(1)} %get-tuple-element.118), kind=kLoop, calls=%fused_computation | loop fusion | flops 1572864 | bytes 4194304 | tf_op jit(solution)/shard_map/add | solution.py:112
  101.9 0.0 copy-start.3
  101.9 0.0 copy-start.4
  101.9 0.0 copy-start.5
  101.9 0.0 copy-start.7
  101.9 0.0 copy-start.8
  101.9 0.0 copy-start.10
  102.0 0.0 copy-start.11
  102.0 0.0 copy-start.12
  102.0 5.8 %collective-permute-done.19.refs_2_ = bf16[80,640]{1,0:T(8,128)(2,1)S(1)} collective-permute-done((bf16[80,640]{1,0:T(8,128)(2,1)S(1)}, bf16[80,640]{1,0:T(8,128)(2,1)S(1)}, u32[]{:S(2)}, u32[]{:S(2)}) %collective-permute-start.19) | collective-permute-done | bytes 102432 | tf_op jit(solution)/shard_map/ppermute | solution.py:49
  107.8 0.8 collect.1
  108.6 0.9 fusion.10
  109.4 1.0 collective-permute-start.21
  110.4 3.5 %all-to-all-start = ((f32[32,8,128]{2,1,0:T(8,128)}), f32[32,8,128]{2,1,0:T(8,128)S(1)}, u32[]{:S(2)}, u32[]{:S(2)}) async-start(f32[32,8,128]{2,1,0:T(8,128)} %get-tuple-element.122), calls=%async_computation | async-start | bytes 262144 | tf_op jit(solution)/shard_map/all_to_all | solution.py:709
  114.0 0.3 fusion.8
  114.3 8.6 %all-to-all-done.heard_ref = f32[32,8,128]{2,1,0:T(8,128)S(1)} async-done(((f32[32,8,128]{2,1,0:T(8,128)}), f32[32,8,128]{2,1,0:T(8,128)S(1)}, u32[]{:S(2)}, u32[]{:S(2)}) %all-to-all-start) | async-done | bytes 131104 | tf_op jit(solution)/shard_map/all_to_all | solution.py:709
  122.9 1.7 %update.1 = (f32[64,4,128]{2,1,0:T(4,128)}, f32[64,128]{1,0:T(8,128)}, f32[69,128]{1,0:T(8,128)}, f32[1,1]{1,0:T(1,128)}, f32[64,4,128]{2,1,0:T(4,128)}, /*index...) custom-call(f32[32,8,128]{2,1,0:T(8,128)S(1)} %all-to-all-done.heard, ...), custom_call_target="tpu_custom_call" | custom-call | flops 100000000 | bytes 300000 | tf_op jit(solution)/shard_map/update/pallas_call | solution.py:727
  124.7 1.7 %fusion.11 = (f32[512]{0:T(512)S(1)}, f32[512]{0:T(512)S(1)}) fusion(bf16[512,512]{1,0:T(8,128)(2,1)S(1)} %collective-permute-done.21, f32[2,512,512]{2,1,0:T(8,128)} %copy-done.15, s32[]{:T(128)S(6)} %select_n.36, f32[512]{0:T(512)S(1)} %add_rsqrt_fusion, f32[512]{0:T(512)S(1)} %broadcast_multiply_fusion.2, bf16[512,512]{1,0:T(8,128)(2,1)S(1)} %copy-done), kind=kLoop, calls=%fused_computation.21 | loop fusion | flops 2096128 | bytes 2105348 | tf_op jit(solution)/shard_map/reduce_sum | solution.py:719
  126.4 2.9 %fusion.7 = (f32[512,512]{1,0:T(8,128)}, bf16[512,512]{1,0:T(8,128)(2,1)}) fusion(bf16[512,512]{1,0:T(8,128)(2,1)S(1)} %copy-done, bf16[512,512]{1,0:T(8,128)(2,1)S(1)} %copy-done.1, f32[512]{0:T(512)S(1)} %get-tuple-element.148, f32[512]{0:T(512)S(1)} %get-tuple-element.149, f32[512]{0:T(512)S(1)} %add_rsqrt_fusion, f32[512]{0:T(512)S(1)} %broadcast_multiply_fusion.2, ...), kind=kLoop, calls=%fused_computation.11 | loop fusion | flops 5505024 | bytes 6301700 | tf_op jit(solution)/shard_map/add | solution.py:717
  (55 shorter events, 0.2 us)
Async XLA Ops:
  0.6 12.2 %copy-start = (bf16[512,512]{1,0:T(8,128)(2,1)S(1)}, bf16[512,512]{1,0:T(8,128)(2,1)}, u32[]{:S(2)}) copy-start(bf16[512,512]{1,0:T(8,128)(2,1)} %refs_0_.2) | copy-start | bytes 1572868
  0.7 15.1 %collective-permute-start.6 = (bf16[512,512]{1,0:T(8,128)(2,1)}, bf16[512,512]{1,0:T(8,128)(2,1)S(1)}, u32[]{:S(2)}, u32[]{:S(2)}) collective-permute-start(bf16[512,512]{1,0:T(8,128)(2,1)} %refs_0_.2), channel_id=1, source_target_pairs={{0,2},{1,3},{2,0},{3,1},{4,6},{5,7},{6,4},{7,5},{8,10},{9,11},{10,... | collective-permute-start | bytes 1572872 | tf_op jit(solution)/shard_map/ppermute | solution.py:49
  3.7 0.9 copy-start.2
  4.6 0.8 copy-start.9
  5.3 13.9 %copy-start.6 = (f32[8832]{0:T(1024)S(1)}, f32[8832]{0:T(1024)}, u32[]{:S(2)}) copy-start(f32[8832]{0:T(1024)} %param.19) | copy-start | bytes 105988
  5.3 13.9 %copy-start.13 = (s32[2048]{0:T(1024)S(1)}, s32[2048]{0:T(1024)}, u32[]{:S(2)}) copy-start(s32[2048]{0:T(1024)} %param.16) | copy-start | bytes 24580
  5.5 6.8 %collective-permute-start = (bf16[64,640]{1,0:T(8,128)(2,1)S(1)}, bf16[64,640]{1,0:T(8,128)(2,1)S(1)}, u32[]{:S(2)}, u32[]{:S(2)}) collective-permute-start(bf16[64,640]{1,0:T(8,128)(2,1)S(1)} %cast.1.refs_4_), channel_id=1, source_target_pairs={{0,16},{4,20},{8,24},{12,28},{16,0},{20,4},{24,8},{28,12},{1,17},{... | collective-permute-start | bytes 245768 | tf_op jit(solution)/shard_map/ppermute | solution.py:49
  12.2 5.4 %collective-permute-start.1 = (bf16[128,640]{1,0:T(8,128)(2,1)S(1)}, bf16[128,640]{1,0:T(8,128)(2,1)S(1)}, u32[]{:S(2)}, u32[]{:S(2)}) collective-permute-start(bf16[128,640]{1,0:T(8,128)(2,1)S(1)} %pad_maximum_fusion.1), channel_id=1, source_target_pairs={{0,8},{4,12},{8,0},{12,4},{16,24},{20,28},{24,16},{28,20},{1,9},{5... | collective-permute-start | bytes 491528 | tf_op jit(solution)/shard_map/ppermute | solution.py:49
  12.8 9.0 %collective-permute-start.5 = (bf16[512,512]{1,0:T(8,128)(2,1)S(1)}, bf16[512,512]{1,0:T(8,128)(2,1)S(1)}, u32[]{:S(2)}, u32[]{:S(2)}) collective-permute-start(bf16[512,512]{1,0:T(8,128)(2,1)S(1)} %copy-done), channel_id=1, source_target_pairs={{0,1},{1,0},{2,3},{3,2},{4,5},{5,4},{6,7},{7,6},{8,9},{9,8},{10,11... | collective-permute-start | bytes 1572872 | tf_op jit(solution)/shard_map/ppermute | solution.py:49
  15.8 10.3 %collective-permute-start.7 = (bf16[512,512]{1,0:T(8,128)(2,1)S(1)}, bf16[512,512]{1,0:T(8,128)(2,1)S(1)}, u32[]{:S(2)}, u32[]{:S(2)}) collective-permute-start(bf16[512,512]{1,0:T(8,128)(2,1)S(1)} %collective-permute-done.6.refs_2_), channel_id=1, source_target_pairs={{0,1},{1,0},{2,3},{3,2},{4,5},{5,4},{6,7},{7,6},{8,9},{9,8},{10,11... | collective-permute-start | bytes 1572872 | tf_op jit(solution)/shard_map/ppermute | solution.py:49
  17.7 8.4 %collective-permute-start.8 = (bf16[256,640]{1,0:T(8,128)(2,1)S(1)}, bf16[256,640]{1,0:T(8,128)(2,1)S(1)}, u32[]{:S(2)}, u32[]{:S(2)}) collective-permute-start(bf16[256,640]{1,0:T(8,128)(2,1)S(1)} %pad_maximum_fusion), channel_id=1, source_target_pairs={{0,4},{4,0},{8,12},{12,8},{16,20},{20,16},{24,28},{28,24},{1,5},{5... | collective-permute-start | bytes 983048 | tf_op jit(solution)/shard_map/ppermute | solution.py:49
  19.3 1.9 %copy-start.1 = (bf16[512,512]{1,0:T(8,128)(2,1)S(1)}, bf16[512,512]{1,0:T(8,128)(2,1)}, u32[]{:S(2)}) copy-start(bf16[512,512]{1,0:T(8,128)(2,1)} %refs_4_) | copy-start | bytes 1572868
  19.3 6.8 %copy-start.14 = (s32[2048]{0:T(1024)S(1)}, s32[2048]{0:T(1024)}, u32[]{:S(2)}) copy-start(s32[2048]{0:T(1024)} %first_ref.3) | copy-start | bytes 24580
  21.2 22.1 %collective-permute-start.2 = (bf16[512,512]{1,0:T(8,128)(2,1)S(1)}, bf16[512,512]{1,0:T(8,128)(2,1)S(1)}, u32[]{:S(2)}, u32[]{:S(2)}) collective-permute-start(bf16[512,512]{1,0:T(8,128)(2,1)S(1)} %copy-done.1), channel_id=1, source_target_pairs={{0,1},{1,0},{2,3},{3,2},{4,5},{5,4},{6,7},{7,6},{8,9},{9,8},{10,11... | collective-permute-start | bytes 1572872 | tf_op jit(solution)/shard_map/ppermute | solution.py:49
  21.3 22.1 %collective-permute-start.3 = (bf16[512,512]{1,0:T(8,128)(2,1)S(1)}, bf16[512,512]{1,0:T(8,128)(2,1)S(1)}, u32[]{:S(2)}, u32[]{:S(2)}) collective-permute-start(bf16[512,512]{1,0:T(8,128)(2,1)S(1)} %copy-done.1), channel_id=1, source_target_pairs={{0,2},{1,3},{2,0},{3,1},{4,6},{5,7},{6,4},{7,5},{8,10},{9,11},{10,... | collective-permute-start | bytes 1572872 | tf_op jit(solution)/shard_map/ppermute | solution.py:49
  21.9 24.5 %collective-permute-start.4 = (bf16[512,512]{1,0:T(8,128)(2,1)S(1)}, bf16[512,512]{1,0:T(8,128)(2,1)S(1)}, u32[]{:S(2)}, u32[]{:S(2)}) collective-permute-start(bf16[512,512]{1,0:T(8,128)(2,1)S(1)} %copy-done.1), channel_id=1, source_target_pairs={{0,3},{1,2},{2,1},{3,0},{4,7},{5,6},{6,5},{7,4},{8,11},{9,10},{10,... | collective-permute-start | bytes 1572872 | tf_op jit(solution)/shard_map/ppermute | solution.py:49
  48.0 4.3 %collective-permute-start.10 = (f32[8,4,256]{2,1,0:T(4,128)S(1)}, f32[8,4,256]{2,1,0:T(4,128)S(1)}, u32[]{:S(2)}, u32[]{:S(2)}) collective-permute-start(f32[8,4,256]{2,1,0:T(4,128)S(1)} %get-tuple-element.87.refs_0_), channel_id=1, source_target_pairs={{0,2},{1,3},{2,0},{3,1},{4,6},{5,7},{6,4},{7,5},{8,10},{9,11},{10,... | collective-permute-start | bytes 98312 | tf_op jit(solution)/shard_map/ppermute | solution.py:49
  48.6 3.7 %collective-permute-start.11 = (f32[8,4,256]{2,1,0:T(4,128)S(1)}, f32[8,4,256]{2,1,0:T(4,128)S(1)}, u32[]{:S(2)}, u32[]{:S(2)}) collective-permute-start(f32[8,4,256]{2,1,0:T(4,128)S(1)} %get-tuple-element.87.refs_0_), channel_id=1, source_target_pairs={{0,3},{1,2},{2,1},{3,0},{4,7},{5,6},{6,5},{7,4},{8,11},{9,10},{10,... | collective-permute-start | bytes 98312 | tf_op jit(solution)/shard_map/ppermute | solution.py:49
  49.7 2.6 %collective-permute-start.9 = (f32[8,4,256]{2,1,0:T(4,128)S(1)}, f32[8,4,256]{2,1,0:T(4,128)S(1)}, u32[]{:S(2)}, u32[]{:S(2)}) collective-permute-start(f32[8,4,256]{2,1,0:T(4,128)S(1)} %get-tuple-element.87.refs_0_), channel_id=1, source_target_pairs={{0,1},{1,0},{2,3},{3,2},{4,5},{5,4},{6,7},{7,6},{8,9},{9,8},{10,11... | collective-permute-start | bytes 98312 | tf_op jit(solution)/shard_map/ppermute | solution.py:49
  54.4 28.4 %collective-permute-start.12 = (bf16[512,512]{1,0:T(8,128)(2,1)S(1)}, bf16[512,512]{1,0:T(8,128)(2,1)S(1)}, u32[]{:S(2)}, u32[]{:S(2)}) collective-permute-start(bf16[512,512]{1,0:T(8,128)(2,1)S(1)} %get-tuple-element.103), channel_id=1, source_target_pairs={{0,1},{1,0},{2,3},{3,2},{4,5},{5,4},{6,7},{7,6},{8,9},{9,8},{10,11... | collective-permute-start | bytes 1572872 | tf_op jit(solution)/shard_map/ppermute | solution.py:49
  54.6 28.1 %collective-permute-start.13 = (bf16[512,512]{1,0:T(8,128)(2,1)S(1)}, bf16[512,512]{1,0:T(8,128)(2,1)S(1)}, u32[]{:S(2)}, u32[]{:S(2)}) collective-permute-start(bf16[512,512]{1,0:T(8,128)(2,1)S(1)} %get-tuple-element.104), channel_id=1, source_target_pairs={{0,2},{1,3},{2,0},{3,1},{4,6},{5,7},{6,4},{7,5},{8,10},{9,11},{10,... | collective-permute-start | bytes 1572872 | tf_op jit(solution)/shard_map/ppermute | solution.py:49
  55.9 26.9 %collective-permute-start.14 = (bf16[512,512]{1,0:T(8,128)(2,1)S(1)}, bf16[512,512]{1,0:T(8,128)(2,1)S(1)}, u32[]{:S(2)}, u32[]{:S(2)}) collective-permute-start(bf16[512,512]{1,0:T(8,128)(2,1)S(1)} %get-tuple-element.105), channel_id=1, source_target_pairs={{0,3},{1,2},{2,1},{3,0},{4,7},{5,6},{6,5},{7,4},{8,11},{9,10},{10,... | collective-permute-start | bytes 1572872 | tf_op jit(solution)/shard_map/ppermute | solution.py:49
  56.3 26.4 %collective-permute-start.15 = (bf16[4,64,256]{2,1,0:T(8,128)(2,1)S(1)}, bf16[4,64,256]{2,1,0:T(8,128)(2,1)S(1)}, u32[]{:S(2)}, u32[]{:S(2)}) collective-permute-start(bf16[4,64,256]{2,1,0:T(8,128)(2,1)S(1)} %get-tuple-element.106), channel_id=1, source_target_pairs={{0,4},{4,0},{8,12},{12,8},{16,20},{20,16},{24,28},{28,24},{1,5},{5... | collective-permute-start | bytes 393224 | tf_op jit(solution)/shard_map/ppermute | solution.py:49
  82.7 0.7 copy-start.22
  82.8 3.4 %copy-start.17 = (bf16[512,512]{1,0:T(8,128)(2,1)}, bf16[512,512]{1,0:T(8,128)(2,1)S(1)}, u32[]{:S(2)}) copy-start(bf16[512,512]{1,0:T(8,128)(2,1)S(1)} %collective-permute-done.12) | copy-start | bytes 1572868
  82.8 3.4 %copy-start.19 = (bf16[512,512]{1,0:T(8,128)(2,1)}, bf16[512,512]{1,0:T(8,128)(2,1)S(1)}, u32[]{:S(2)}) copy-start(bf16[512,512]{1,0:T(8,128)(2,1)S(1)} %collective-permute-done.13) | copy-start | bytes 1572868
  82.8 3.4 %copy-start.21 = (bf16[512,512]{1,0:T(8,128)(2,1)}, bf16[512,512]{1,0:T(8,128)(2,1)S(1)}, u32[]{:S(2)}) copy-start(bf16[512,512]{1,0:T(8,128)(2,1)S(1)} %collective-permute-done.14) | copy-start | bytes 1572868
  82.8 8.1 %collective-permute-start.16 = (bf16[4,80,384]{2,1,0:T(8,128)(2,1)S(1)}, bf16[4,80,384]{2,1,0:T(8,128)(2,1)S(1)}, u32[]{:S(2)}, u32[]{:S(2)}) collective-permute-start(bf16[4,80,384]{2,1,0:T(8,128)(2,1)S(1)} %get-tuple-element.111), channel_id=1, source_target_pairs={{0,4},{4,0},{8,12},{12,8},{16,20},{20,16},{24,28},{28,24},{1,5},{5... | collective-permute-start | bytes 737288 | tf_op jit(solution)/shard_map/ppermute | solution.py:49
  86.2 14.1 %collective-permute-start.17 = (bf16[2,512,512]{2,1,0:T(8,128)(2,1)}, bf16[2,512,512]{2,1,0:T(8,128)(2,1)}, u32[]{:S(2)}, u32[]{:S(2)}) collective-permute-start(bf16[2,512,512]{2,1,0:T(8,128)(2,1)} %get-tuple-element.114), channel_id=1, source_target_pairs={{0,1},{1,0},{2,3},{3,2},{4,5},{5,4},{6,7},{7,6},{8,9},{9,8},{10,11... | collective-permute-start | bytes 3145736 | tf_op jit(solution)/shard_map/ppermute | solution.py:49
  91.1 10.9 %collective-permute-start.18 = (bf16[80,640]{1,0:T(8,128)(2,1)S(1)}, bf16[80,640]{1,0:T(8,128)(2,1)S(1)}, u32[]{:S(2)}, u32[]{:S(2)}) collective-permute-start(bf16[80,640]{1,0:T(8,128)(2,1)S(1)} %get-tuple-element.147), channel_id=1, source_target_pairs={{0,8},{4,12},{8,0},{12,4},{16,24},{20,28},{24,16},{28,20},{1,9},{5... | collective-permute-start | bytes 307208 | tf_op jit(solution)/shard_map/ppermute | solution.py:49
  97.7 10.0 %collective-permute-start.19 = (bf16[80,640]{1,0:T(8,128)(2,1)S(1)}, bf16[80,640]{1,0:T(8,128)(2,1)S(1)}, u32[]{:S(2)}, u32[]{:S(2)}) collective-permute-start(bf16[80,640]{1,0:T(8,128)(2,1)S(1)} %get-tuple-element.146), channel_id=1, source_target_pairs={{0,16},{4,20},{8,24},{12,28},{16,0},{20,4},{24,8},{28,12},{1,17},{... | collective-permute-start | bytes 307208 | tf_op jit(solution)/shard_map/ppermute | solution.py:49
  98.9 8.9 %collective-permute-start.20 = (bf16[80,640]{1,0:T(8,128)(2,1)S(1)}, bf16[80,640]{1,0:T(8,128)(2,1)S(1)}, u32[]{:S(2)}, u32[]{:S(2)}) collective-permute-start(bf16[80,640]{1,0:T(8,128)(2,1)S(1)} %get-tuple-element.145), channel_id=1, source_target_pairs={{0,24},{4,28},{8,16},{12,20},{16,8},{20,12},{24,0},{28,4},{1,25},{... | collective-permute-start | bytes 307208 | tf_op jit(solution)/shard_map/ppermute | solution.py:49
  101.9 6.7 %copy-start.15 = (f32[2,512,512]{2,1,0:T(8,128)}, f32[2,512,512]{2,1,0:T(8,128)S(1)}, u32[]{:S(2)}) copy-start(f32[2,512,512]{2,1,0:T(8,128)S(1)} %convert_add_fusion) | copy-start | bytes 6291460
  101.9 21.0 %copy-start.3 = (f32[64,4,128]{2,1,0:T(4,128)S(1)}, f32[64,4,128]{2,1,0:T(4,128)}, u32[]{:S(2)}) copy-start(f32[64,4,128]{2,1,0:T(4,128)} %refs_0_.4) | copy-start | bytes 393220
  101.9 21.0 %copy-start.4 = (f32[64,4,128]{2,1,0:T(4,128)S(1)}, f32[64,4,128]{2,1,0:T(4,128)}, u32[]{:S(2)}) copy-start(f32[64,4,128]{2,1,0:T(4,128)} %refs_1_.1) | copy-start | bytes 393220
  101.9 21.0 %copy-start.5 = (f32[64,4,128]{2,1,0:T(4,128)S(1)}, f32[64,4,128]{2,1,0:T(4,128)}, u32[]{:S(2)}) copy-start(f32[64,4,128]{2,1,0:T(4,128)} %refs_2_.1) | copy-start | bytes 393220
  101.9 21.0 %copy-start.7 = (f32[8832]{0:T(1024)S(1)}, f32[8832]{0:T(1024)}, u32[]{:S(2)}) copy-start(f32[8832]{0:T(1024)} %param.24) | copy-start | bytes 105988
  101.9 21.0 %copy-start.8 = (f32[8832]{0:T(1024)S(1)}, f32[8832]{0:T(1024)}, u32[]{:S(2)}) copy-start(f32[8832]{0:T(1024)} %param.25) | copy-start | bytes 105988
  101.9 21.0 %copy-start.10 = (f32[128,64]{0,1:T(8,128)S(1)}, f32[128,64]{0,1:T(8,128)}, u32[]{:S(2)}) copy-start(f32[128,64]{0,1:T(8,128)} %param.18) | copy-start | bytes 98308
  102.0 21.0 %copy-start.11 = (f32[128,64]{0,1:T(8,128)S(1)}, f32[128,64]{0,1:T(8,128)}, u32[]{:S(2)}) copy-start(f32[128,64]{0,1:T(8,128)} %param.22) | copy-start | bytes 98308
  102.0 21.0 %copy-start.12 = (f32[128,64]{0,1:T(8,128)S(1)}, f32[128,64]{0,1:T(8,128)}, u32[]{:S(2)}) copy-start(f32[128,64]{0,1:T(8,128)} %param.23) | copy-start | bytes 98308
  109.4 17.0 %copy-start.18 = (bf16[512,512]{1,0:T(8,128)(2,1)S(1)}, bf16[512,512]{1,0:T(8,128)(2,1)}, u32[]{:S(2)}) copy-start(bf16[512,512]{1,0:T(8,128)(2,1)} %copy-done.17) | copy-start | bytes 1572868
  109.4 15.2 %collective-permute-start.21 = (bf16[512,512]{1,0:T(8,128)(2,1)}, bf16[512,512]{1,0:T(8,128)(2,1)S(1)}, u32[]{:S(2)}, u32[]{:S(2)}) collective-permute-start(bf16[512,512]{1,0:T(8,128)(2,1)} %fusion.10), channel_id=1, source_target_pairs={{0,2},{1,3},{2,0},{3,1},{4,6},{5,7},{6,4},{7,5},{8,10},{9,11},{10,... | collective-permute-start | bytes 1572872 | tf_op jit(solution)/shard_map/ppermute | solution.py:49
  110.4 12.5 %all-to-all-start = ((f32[32,8,128]{2,1,0:T(8,128)}), f32[32,8,128]{2,1,0:T(8,128)S(1)}, u32[]{:S(2)}, u32[]{:S(2)}) async-start(f32[32,8,128]{2,1,0:T(8,128)} %get-tuple-element.122), calls=%async_computation | async-start | bytes 262144 | tf_op jit(solution)/shard_map/all_to_all | solution.py:709
  122.9 3.6 %copy-start.16 = (f32[2,512,512]{2,1,0:T(8,128)S(1)}, f32[2,512,512]{2,1,0:T(8,128)}, u32[]{:S(2)}) copy-start(f32[2,512,512]{2,1,0:T(8,128)} %copy-done.15) | copy-start | bytes 6291460
  122.9 3.6 %copy-start.20 = (bf16[512,512]{1,0:T(8,128)(2,1)S(1)}, bf16[512,512]{1,0:T(8,128)(2,1)}, u32[]{:S(2)}) copy-start(bf16[512,512]{1,0:T(8,128)(2,1)} %copy-done.19) | copy-start | bytes 1572868

commit v4 on v3

--- a/solution.py
+++ b/solution.py
@@ -16,6 +16,7 @@
 STEP = 10
 TILE = 256
 NEG = -1e9
+ROOM = 24
 
 norm_epsilon = 1e-06
 adam_epsilon = 1e-08
@@ -29,7 +30,6 @@
 f32 = jnp.float32
 bf16 = jnp.bfloat16
 VMEM = pl.BlockSpec(memory_space=pltpu.VMEM)
-SMEM = pl.BlockSpec(memory_space=pltpu.SMEM)
 
 
 def adam_step(weight, grad, first, second, factor, rate, decay):
@@ -49,23 +49,20 @@
     return lax.ppermute(x, axis, [(i, i ^ k) for i in range(n)])
 
 
-def gather_head(x):
-    n = lax.axis_size("head")
-    pieces = [x] + [None] * (n - 1)
-    for k in range(2, n, 2):
-        pieces[k] = swap(x, "head", k)
-    pieces[1] = swap(x, "head", 1)
-    for k in range(2, n, 2):
-        pieces[k + 1] = swap(pieces[k], "head", 1)
+def gather_chips(x):
+    return [swap(x, "head", k) for k in range(2, lax.axis_size("head"), 2)]
+
+
+def gather_cores(x, others):
+    pieces = [x, swap(x, "head", 1)]
+    for other in others:
+        pieces += [other, swap(other, "head", 1)]
     return pieces
 
 
-def gather_direct(x):
-    return [x] + [swap(x, "head", k) for k in range(1, lax.axis_size("head"))]
-
-
-def after_all(arrays, other):
-    return lax.optimization_barrier((*arrays, other))[:-1]
+def after_all(arrays, *others):
+    arrays = tuple(arrays)
+    return lax.optimization_barrier(arrays + others)[: len(arrays)]
 
 
 def after(x, *others):
@@ -90,37 +87,18 @@
     return n // low, low
 
 
-def add_parts(own, received):
-    total = own.astype(f32)
-    for part in received:
-        total = total + part.astype(f32)
-    return total
-
-
-def send_high(total):
-    high, low = split_dp(lax.axis_size("dp"))
-    row = lax.axis_index("dp") // low
-    narrow = total.astype(bf16)
-    blocks = [lax.dynamic_index_in_dim(total, row, 0, False)]
-    for k in range(1, high):
-        sent = lax.dynamic_index_in_dim(narrow, row ^ k, 0, False)
-        blocks.append(swap(sent, "dp", k * low))
-    return blocks
-
-
-def scatter_core(keep, send, behind):
-    return keep.astype(f32) + after(swap(send, "head", 1), behind).astype(f32)
-
-
-def scatter_chip(total):
-    n = lax.axis_size("head")
-    chip = lax.axis_index("head") // 2
-    narrow = total.astype(bf16)
-    mine = lax.dynamic_index_in_dim(total, chip, 0, False)
-    for k in range(1, n // 2):
-        sent = lax.dynamic_index_in_dim(narrow, chip ^ k, 0, False)
-        mine = mine + swap(sent, "head", 2 * k).astype(f32)
-    return mine
+def scatter_high(own, received, us):
+    high, rows, columns = own.shape
+    low = 1 + len(received)
+    mine, *leaving = call(
+        fold_kernel,
+        "fold",
+        [VMEM] * low,
+        [((rows, columns), f32, VMEM)] + [((rows, columns), bf16, VMEM)] * (high - 1),
+        [],
+        us,
+    )(own, *received)
+    return [mine] + [swap(sent, "dp", (k + 1) * low) for k, sent in enumerate(leaving)]
 
 
 def dot(a, b):
@@ -152,6 +130,10 @@
     )
 
 
+def query_columns(qs, trow, heads):
+    return jnp.concatenate([jnp.concatenate([trow] * heads, axis=1), by_head(qs, heads)], axis=0)
+
+
 def own_rows(block, heads):
     return jnp.concatenate(
         [block[h * HEAD_DIM : (h + 1) * HEAD_DIM, h * TILE : (h + 1) * TILE] for h in range(heads)], axis=0
@@ -161,6 +143,14 @@
 def own_lanes(block, heads):
     lane = lax.broadcasted_iota(jnp.int32, block.shape, 1) // HEAD_DIM
     return jnp.concatenate([jnp.where(lane == h, block, jnp.zeros_like(block)) for h in range(heads)], axis=0)
+
+
+def masked(product, bias, start, j, heads):
+    key = j * TILE + lax.broadcasted_iota(jnp.int32, (TILE, TILE), 0)
+    seen = key >= start
+    return jnp.where(
+        jnp.concatenate([seen] * heads, axis=1), product + jnp.concatenate([bias] * heads, axis=1), NEG
+    )
 
 
 def diagonals(x):
@@ -219,15 +209,19 @@
     lax.fori_loop(0, nb, block, 0)
 
 
-def forward_kernel(heads, n_head, offsets, first_ref, *refs):
-    refs = list(refs)
-    take = lambda count: [refs.pop(0) for _ in range(count)]
-    x_pieces, w_pieces = take(n_head), take(len(offsets))
-    oh_ref, oht_ref, trow_ref, pos_ref, ss_ref = take(5)
-    attn_ref, xn_ref, d_ref, kx_ref, kxt_ref, qxt_ref, v_ref, qm_ref, wt_ref = take(9)
-    w_ref, vt_ref, acc_ref = refs
-    nb, width = attn_ref.shape[0], attn_ref.shape[1]
+def normalize_kernel(*refs):
+    x_pieces, xn_ref = refs[:-1], refs[-1]
     per = x_pieces[0].shape[0] // TILE
+    for k, piece in enumerate(x_pieces):
+        for r in range(per):
+            x = piece[r * TILE : (r + 1) * TILE, :].astype(f32)
+            x = x - jnp.sum(x, axis=1, keepdims=True) / D
+            x = x * lax.rsqrt(jnp.sum(x * x, axis=1, keepdims=True) / D + norm_epsilon)
+            xn_ref[(lax.axis_index("head") ^ k) * per + r] = x.astype(bf16)
+
+
+def assemble_kernel(offsets, *refs):
+    w_pieces, (wt_ref, w_ref) = refs[:-2], refs[-2:]
     for piece, group in zip(w_pieces, offsets):
         rows = piece.shape[0] // len(group)
         for at, offset in enumerate(group):
@@ -235,15 +229,20 @@
             w_ref[pl.ds(start, rows), :] = piece[at * rows : (at + 1) * rows, :]
     wt_ref[...] = flip(w_ref[...]).astype(bf16)
 
-    def project(i, x):
-        x = x.astype(f32)
-        x = x - jnp.sum(x, axis=1, keepdims=True) / D
-        x = (x * lax.rsqrt(jnp.sum(x * x, axis=1, keepdims=True) / D + norm_epsilon)).astype(bf16)
-        xn_ref[i] = x
+
+def project_kernel(heads, *refs):
+    refs = list(refs)
+    take = lambda count: [refs.pop(0) for _ in range(count)]
+    xn_ref, wt_ref, oh_ref, oht_ref = take(4)
+    d_ref, kx_ref, kxt_ref, qs_ref, q_ref, v_ref, vt_ref = refs
+    width = v_ref.shape[2]
+
+    def project(i):
+        x = xn_ref[i]
         p = dot_nt(wt_ref[width : 4 * width], x)
         sg = 0.5 + 0.5 * jnp.tanh(0.5 * p)
         act = p * sg
-        d_ref[i] = sg + act * (1.0 - sg)
+        d_ref[i] = (sg + act * (1.0 - sg)).astype(bf16)
         vt = act[:width]
         vt_ref[i] = vt.astype(bf16)
         v_ref[i] = flip(vt).astype(bf16)
@@ -254,32 +253,29 @@
         kx_ref[i, :, :NTB] = oh_ref[i]
         kx_ref[i, :, NTB:] = flip(kt).astype(bf16)
         qs = (qt.astype(f32) * (0.5 / math.sqrt(HEAD_DIM))).astype(bf16)
-        qxt_ref[i, :NTB] = jnp.concatenate([trow_ref[i]] * heads, axis=1)
-        qxt_ref[i, NTB:] = by_head(qs, heads)
-        qm_ref[i] = own_lanes(flip(qt).astype(bf16), heads)
-
-    for k, piece in enumerate(x_pieces):
-        for r in range(per):
-            project((lax.axis_index("head") ^ k) * per + r, piece[r * TILE : (r + 1) * TILE, :])
-    key_index = lax.broadcasted_iota(jnp.int32, (TILE, TILE), 0)
-
-    def rows(i, _):
-        acc_ref[...] = jnp.zeros_like(acc_ref)
-        start = ss_ref[:, lanes(i)]
-
-        def cols(j, _):
-            s = dot(kx_ref[j], qxt_ref[i]) + jnp.concatenate([pos_ref[i - j]] * heads, axis=1)
-            seen = (key_index + j * TILE) >= start
-            s = jnp.where(jnp.concatenate([seen] * heads, axis=1), s, NEG)
-            w = (s + s * jnp.tanh(s)).astype(bf16)
-            acc_ref[...] += dot(vt_ref[j], w)
-            return 0
-
-        lax.fori_loop(first_ref[i * TILE] // TILE, i + 1, cols, 0)
-        attn_ref[i] = own_rows(acc_ref[...], heads)
-        return 0
-
-    lax.fori_loop(0, nb, rows, 0)
+        qs_ref[i] = qs
+        q_ref[i] = flip(qt).astype(bf16)
+
+    for i in range(xn_ref.shape[0]):
+        project(i)
+
+def attend_kernel(heads, first, last, *refs):
+    if first:
+        before_ref, refs = refs[0], refs[1:]
+    kx_ref, qs_ref, trow_ref, vt_ref, pos_ref, ss_ref, attn_ref = refs
+    if first:
+        attn_ref[:first] = before_ref[...]
+    for i in range(first, last):
+        queries = query_columns(qs_ref[i], trow_ref[i], heads)
+        scores = [dot(kx_ref[j], queries) for j in range(i + 1)]
+        weights = []
+        for j in range(i + 1):
+            h = masked(scores[j], pos_ref[i - j], ss_ref[:, i * TILE : (i + 1) * TILE], j, heads)
+            weights.append((h + h * jnp.tanh(h)).astype(bf16))
+        total = dot(vt_ref[0], weights[0])
+        for j in range(1, i + 1):
+            total = total + dot(vt_ref[j], weights[j])
+        attn_ref[i] = own_rows(total, heads)
 
 
 def gate_kernel(n_head, *refs):
@@ -314,14 +310,14 @@
             )
 
 
-def middle_kernel(heads, n_head, *refs):
+def middle_kernel(n_head, *refs):
     refs = list(refs)
     take = lambda count: [refs.pop(0) for _ in range(count)]
     stats = take(n_head)
     cot_pieces = take(n_head)
     attn_ref, p_ref, gg_ref, xn_ref, wt_ref = take(5)
     branches = take(n_head)
-    dax_ref, daxt_ref, gun_ref = take(3)
+    da_ref, dat_ref, gun_ref = take(3)
     parts, acc_ref, wg_ref = refs[:-2], refs[-2], refs[-1]
     width = attn_ref.shape[1]
     per = cot_pieces[0].shape[0] // TILE
@@ -342,8 +338,8 @@
             gg = gg_ref[i]
             gated = (normed * gate).astype(bf16)
             grad = scale * (gg * gate - first - normed * second)
-            dax_ref[i] = own_lanes(flip(grad).astype(bf16), heads)
-            daxt_ref[i] = by_head((grad * 0.5).astype(bf16), heads)
+            da_ref[i] = flip(grad).astype(bf16)
+            dat_ref[i] = (grad * 0.5).astype(bf16)
             gu = (gg * normed * (sg + gate * (1.0 - sg))).astype(bf16)
             gun_ref[i] = flip(gu).astype(bf16)
             branches[k][at, :] = dot(flip(gated).astype(bf16), wt_ref[4 * width :]).astype(bf16)
@@ -368,55 +364,65 @@
             parts[k][p] = wg_ref[pl.ds(start, rows), :].astype(bf16)
 
 
-def backward_kernel(heads, n_dp, extra, first_ref, *refs):
+def backward_kernel(heads, n_dp, extra, *refs):
     refs = list(refs)
     take = lambda count: [refs.pop(0) for _ in range(count)]
-    kx_ref, kxt_ref, qxt_ref, v_ref, qm_ref, dax_ref, daxt_ref, pos_ref = take(8)
+    kx_ref, kxt_ref, qs_ref, trow_ref, q_ref, v_ref, da_ref, dat_ref, pos_ref = take(9)
     d_ref, xn_ref, ss_ref, gb_ref = take(4)
     gp_ref = refs.pop(0)
     parts = take(split_dp(n_dp)[1])
-    accv_ref, acck_ref, accq_ref, posg_ref, m2_ref, gpq_ref, acc_ref, wg_ref, small_ref = refs
+    accv_ref, acck_ref, posg_ref, gpq_ref, acc_ref, wg_ref, small_ref = refs
     nb, width = v_ref.shape[0], v_ref.shape[2]
-    accv_ref[...] = jnp.zeros_like(accv_ref)
-    acck_ref[...] = jnp.zeros_like(acck_ref)
-    posg_ref[...] = jnp.zeros_like(posg_ref)
-    m2_ref[...] = jnp.zeros_like(m2_ref)
-    key_index = lax.broadcasted_iota(jnp.int32, (TILE, TILE), 0)
     factor = 1.0 / math.sqrt(HEAD_DIM)
-
-    def rows(i, _):
-        accq_ref[...] = jnp.zeros_like(accq_ref)
-        start = ss_ref[:, lanes(i)]
-
-        def cols(j, _):
-            s = dot(kx_ref[j], qxt_ref[i]) + jnp.concatenate([pos_ref[i - j]] * heads, axis=1)
-            seen = (key_index + j * TILE) >= start
-            s = jnp.where(jnp.concatenate([seen] * heads, axis=1), s, NEG)
-            t = jnp.tanh(s)
-            u = 1.0 + t
-            w = s * u
-            ds = dot(v_ref[j], daxt_ref[i]) * (u + w * (1.0 - t))
-            low = ds.astype(bf16)
-            accv_ref[j] += dot(w.astype(bf16), dax_ref[i])
-            acck_ref[j] += dot(low, qm_ref[i])
-            accq_ref[...] += dot(kxt_ref[j], low)
-            posg_ref[i - j] += sum(ds[:, h * TILE : (h + 1) * TILE] for h in range(heads))
-            return 0
-
-        lax.fori_loop(first_ref[i * TILE] // TILE, i + 1, cols, 0)
-        gpq_ref[i] = own_rows(accq_ref[NTB:], heads)
-        tp = sum(accq_ref[:NTB, h * TILE : (h + 1) * TILE] for h in range(heads))
-        high = tp.astype(bf16)
-        rest = (tp - high.astype(f32)).astype(bf16)
-        onehot = kx_ref[i, :, :NTB]
-        m2_ref[...] += dot(high, onehot) + dot(rest, onehot)
-        return 0
-
-    lax.fori_loop(0, nb, rows, 0)
+    tiles = [(i, j) for i in range(nb) for j in range(i + 1)]
+    products, weights, grads = {}, {}, {}
+    dq = None
+
+    def add(ref, at, value, first):
+        ref[at] = value if first else ref[at] + value
+
+    for t in range(len(tiles) + 2):
+        if t < len(tiles):
+            i, j = tiles[t]
+            if j == 0:
+                queries = query_columns(qs_ref[i], trow_ref[i], heads)
+                backs = by_head(dat_ref[i], heads)
+            products[t] = dot(kx_ref[j], queries), dot(v_ref[j], backs)
+        if 0 <= t - 1 < len(tiles):
+            i, j = tiles[t - 1]
+            product, back = products.pop(t - 1)
+            h = masked(product, pos_ref[i - j], ss_ref[:, i * TILE : (i + 1) * TILE], j, heads)
+            th = jnp.tanh(h)
+            u = 1.0 + th
+            w = h * u
+            ds = back * (u + w * (1.0 - th))
+            weights[t - 1], grads[t - 1] = w.astype(bf16), ds.astype(bf16)
+            add(posg_ref, i - j, sum(ds[:, g * TILE : (g + 1) * TILE] for g in range(heads)), j == 0)
+        if t >= 2:
+            i, j = tiles[t - 2]
+            low = grads.pop(t - 2)
+            if j == 0:
+                da = own_lanes(da_ref[i], heads)
+                times = jnp.concatenate([kx_ref[i, :, :NTB]] * heads, axis=0)
+                q = jnp.concatenate([times, own_lanes(q_ref[i], heads)], axis=1)
+            add(accv_ref, j, dot(weights.pop(t - 2), da), i == j)
+            add(acck_ref, j, dot(low, q), i == j)
+            more = dot(kxt_ref[j, NTB:], low)
+            dq = more if j == 0 else dq + more
+            if i == j:
+                gpq_ref[i] = own_rows(dq, heads)
+    m2 = None
+    for j in range(nb):
+        part = acck_ref[j, :, :NTB]
+        high = part.astype(bf16)
+        rest = (part - high.astype(f32)).astype(bf16)
+        onehot = kxt_ref[j, :NTB]
+        part = dot(onehot, high) + dot(onehot, rest)
+        m2 = part if j == 0 else m2 + part
     acc_ref[...] = jnp.zeros_like(acc_ref)
 
     def tail(i, _):
-        gp = jnp.concatenate([flip(accv_ref[i]), gpq_ref[i] * factor, flip(acck_ref[i]) * factor], axis=0)
+        gp = jnp.concatenate([flip(accv_ref[i]), gpq_ref[i] * factor, flip(acck_ref[i, :, NTB:]) * factor], axis=0)
         gp = (gp * d_ref[i]).astype(bf16)
         gp_ref[i] = flip(gp).astype(bf16)
         acc_ref[...] += dot(gp, xn_ref[i])
@@ -430,7 +436,6 @@
         small_ref[:, D + d * TILE : D + (d + 1) * TILE] += g[:, :TILE]
         if d > 0:
             small_ref[:, D + (d - 1) * TILE : D + d * TILE] += g[:, TILE:]
-    m2 = m2_ref[...]
     g = diagonals(m2 + jnp.transpose(m2))[:, :NTB]
     zero = lax.broadcasted_iota(jnp.int32, (1, NTB), 1) == 0
     at = D + nb * TILE
@@ -462,13 +467,54 @@
             target[device // 2, r * TILE : (r + 1) * TILE] = rows.astype(bf16)
 
 
+def fold_kernel(*refs):
+    low = sum(len(ref.shape) == 3 for ref in refs)
+    row = lax.axis_index("dp") // low
+    for k, out in enumerate(refs[low:]):
+        total = refs[0][row ^ k].astype(f32)
+        for ref in refs[1:low]:
+            total = total + ref[row ^ k].astype(f32)
+        out[...] = total.astype(out.dtype)
+
+
+def mix_kernel(tokens_ref, bias_ref, *refs):
+    total = tokens_ref[...].astype(f32) + row_lanes(bias_ref, 0, D // 128)
+    for ref in refs[:-1]:
+        total = total + ref[...].astype(f32)
+    refs[-1][...] = total.astype(bf16)
+
+
+def finish_kernel(tokens_ref, cot_ref, mine_ref, *refs):
+    x = tokens_ref[...].astype(f32)
+    x = x - jnp.sum(x, axis=1, keepdims=True) / D
+    scale = lax.rsqrt(jnp.sum(x * x, axis=1, keepdims=True) / D + norm_epsilon)
+    x = x * scale
+    grad = mine_ref[...]
+    for ref in refs[:-1]:
+        grad = grad + ref[...].astype(f32)
+    mean = jnp.sum(grad, axis=1, keepdims=True) / D
+    along = jnp.sum(grad * x, axis=1, keepdims=True) / D
+    refs[-1][...] = cot_ref[...].astype(f32) + scale * (grad - mean - x * along)
+
+
+def rows_kernel(chips, keep_ref, crossed_ref, mine_ref, *leaving):
+    chip = lax.axis_index("head") // 2
+    for k in range(chips):
+        total = keep_ref[chip ^ k].astype(f32) + crossed_ref[chip ^ k].astype(f32)
+        if k == 0:
+            mine_ref[...] = total
+        else:
+            leaving[k - 1][...] = total.astype(bf16)
+
+
 def collect_kernel(high, extra, *refs):
-    blocks, (grads_ref, message_ref) = refs[:high], refs[high:]
-    total = blocks[0][...]
+    late_blocks, early_blocks, (grads_ref, message_ref) = refs[:high], refs[high : 2 * high], refs[2 * high :]
+    rows = grads_ref.shape[0]
+    total, early = late_blocks[0][...], early_blocks[0][...]
     for k in range(1, high):
-        total = total + blocks[k][...].astype(f32)
-    rows = grads_ref.shape[0]
-    grads = total[:rows]
+        total = total + late_blocks[k][...].astype(f32)
+        early = early + early_blocks[k][...].astype(f32)
+    grads = jnp.concatenate([total[:rows], early], axis=1)
     grads_ref[...] = grads
     squares = jnp.sum(jnp.sum(grads * grads, axis=0, keepdims=True), axis=1, keepdims=True)
     message = jnp.concatenate(
@@ -580,9 +626,9 @@
     (weights,) = call(
         cast_kernel, "cast", [VMEM] * 2, [((rows_here, 5 * width), bf16, VMEM)], [], 1
     )(proj_weight, out_weight.T)
-    x_pieces = gather_head(tokens)
+    x_pieces = gather_cores(tokens, gather_chips(after(tokens, weights)))
     w_pieces, offsets, operands = gather_dp(weights)
-    cot_pieces = gather_direct(after(cotangent, operands[-1]))
+    cot_chips = gather_chips(after(cotangent, weights))
     starts = seq_start.reshape(1, group)
     small_rows = small_params.reshape(-1, 128)
     times = time_bucket.reshape(1, group)
@@ -602,28 +648,48 @@
     )(after(times, operands[1]), small_rows)
 
     items = [
-        ((nb, width, TILE), f32),
-        ((nb, TILE, D), bf16),
-        ((nb, 3 * width, TILE), f32),
+        ((nb, 3 * width, TILE), bf16),
         ((nb, TILE, NTB + width), bf16),
         ((nb, NTB + width, TILE), bf16),
-        ((nb, NTB + width, heads * TILE), bf16),
+        ((nb, width, TILE), bf16),
         ((nb, TILE, width), bf16),
-        ((nb, heads * TILE, width), bf16),
-        ((5 * width, D), bf16),
+        ((nb, TILE, width), bf16),
+        ((nb, width, TILE), bf16),
     ]
-    attn, xn, dsilu, kx, kxt, qxt, v, qm, wt = call(
-        functools.partial(forward_kernel, heads, n_head, offsets),
-        "forward",
-        [SMEM] + [VMEM] * (n_head + len(w_pieces) + 5),
+    (xn,) = call(normalize_kernel, "normalize", [VMEM] * n_head, [((nb, TILE, D), bf16, VMEM)], [], 1)(*x_pieces)
+    (wt,) = call(
+        functools.partial(assemble_kernel, offsets),
+        "assemble",
+        [VMEM] * len(w_pieces),
+        [((5 * width, D), bf16, VMEM)],
+        [pltpu.VMEM((D, 5 * width), bf16)],
+        5,
+    )(*w_pieces)
+    dsilu, kx, kxt, qs, q, v, vt = call(
+        functools.partial(project_kernel, heads),
+        "project",
+        [VMEM] * 4,
         [item + (VMEM,) for item in items],
-        [
-            pltpu.VMEM((D, 5 * width), bf16),
-            pltpu.VMEM((nb, width, TILE), bf16),
-            pltpu.VMEM((width, heads * TILE), f32),
-        ],
-        30,
-    )(seq_start, *x_pieces, *w_pieces, oh, oht, trow, pos, starts)
+        [],
+        5,
+    )(xn, wt, oh, oht)
+
+    def attend(first, last, *before):
+        (attn,) = call(
+            functools.partial(attend_kernel, heads, first, last),
+            "attend",
+            [VMEM] * (len(before) + 6),
+            [((last, width, TILE), f32, VMEM)],
+            [],
+            8,
+        )(*before, kx, qs, trow, vt, pos, starts)
+        return attn
+
+    split = nb - nb // 4
+    attn = attend(0, split)
+    cot_chips = after_all(cot_chips, attn)
+    attn = attend(split, nb, after(attn, *cot_chips))
+    cot_pieces = gather_cores(cotangent, cot_chips)
 
     column = ((nb, width, TILE), f32, VMEM)
     p_gate, gg, stat, gb = call(
@@ -637,20 +703,20 @@
 
     stats = [stat] + [swap(stat, "head", k) for k in range(1, n_head)]
     out = call(
-        functools.partial(middle_kernel, heads, n_head),
+        functools.partial(middle_kernel, n_head),
         "middle",
         [VMEM] * (2 * n_head + 5),
         [((here, D), bf16, VMEM)] * n_head
         + [
-            ((nb, heads * TILE, width), bf16, VMEM),
-            ((nb, width, heads * TILE), bf16, VMEM),
+            ((nb, TILE, width), bf16, VMEM),
+            ((nb, width, TILE), bf16, VMEM),
             ((nb, TILE, width), bf16, VMEM),
         ]
         + [((high, rows_here, 2 * width), bf16, VMEM)] * low,
         [pltpu.VMEM((2 * width, D), f32), pltpu.VMEM((D, 2 * width), f32)],
         6,
     )(*stats, *cot_pieces, attn, p_gate, gg, xn, wt)
-    branches, (dax, daxt, gun), early_parts = out[:n_head], out[n_head : n_head + 3], out[n_head + 3 :]
+    branches, (da, dat, gun), early_parts = out[:n_head], out[n_head : n_head + 3], out[n_head + 3 :]
     received = [swap(branches[k], "head", k) for k in range(1, n_head)]
     early_received = [swap(early_parts[k], "dp", k) for k in range(1, low)]
 
@@ -659,28 +725,25 @@
     gp, *late_parts = call(
         functools.partial(backward_kernel, heads, n_dp, extra),
         "backward",
-        [SMEM] + [VMEM] * 12,
+        [VMEM] * 13,
         [((nb, TILE, 3 * width), bf16, VMEM)] + [((high, rows_here + 16, 3 * width), bf16, VMEM)] * low,
         [
             pltpu.VMEM((nb, TILE, width), f32),
-            pltpu.VMEM((nb, TILE, width), f32),
-            pltpu.VMEM((NTB + width, heads * TILE), f32),
+            pltpu.VMEM((nb, TILE, NTB + width), f32),
             pltpu.VMEM((nb, TILE, TILE), f32),
-            pltpu.VMEM((NTB, NTB), f32),
             pltpu.VMEM((nb, width, TILE), f32),
             pltpu.VMEM((3 * width, D), f32),
             pltpu.VMEM((n_dp * (rows_here + 16), 3 * width), f32),
             pltpu.VMEM((1, extra * n_dp * 128), f32),
         ],
         35,
-        24,
-    )(seq_start, kx, kxt, qxt, v, qm, dax, daxt, pos, dsilu, xn, starts, gb)
+        ROOM,
+    )(kx, kxt, qs, trow, q, v, da, dat, pos, dsilu, xn, starts, gb)
 
     tied = lax.optimization_barrier((gp, *late_parts, *received, *early_received))
     gp, late_parts = tied[0], tied[1 : 1 + low]
     received, early_received = tied[1 + low : low + n_head], tied[low + n_head :]
     late_received = [swap(late_parts[k], "dp", k) for k in range(1, low)]
-    early = add_parts(early_parts[0], early_received)
     keep, send = call(
         functools.partial(input_kernel, n_head),
         "input_rows",
@@ -689,37 +752,40 @@
         [],
         4,
     )(gp, gun, wt)
+    early_blocks = scatter_high(after(early_parts[0], send), early_received, 1)
     late_received = after_all(late_received, send)
-    late = add_parts(late_parts[0], late_received)
-    both = jnp.concatenate([late, jnp.pad(early, ((0, 0), (0, 16), (0, 0)))], axis=2)
-    blocks = send_high(both)
-    rows_total = scatter_core(keep, send, both)
-    blocks[0] = after(blocks[0], rows_total)
+    late_blocks = scatter_high(late_parts[0], late_received, 6)
+    late_blocks[0] = after(late_blocks[0], *early_blocks)
+    chips = n_head // 2
+    crossed = swap(after(send, late_blocks[0]), "head", 1)
+    mine, *leaving = call(
+        functools.partial(rows_kernel, chips),
+        "rows",
+        [VMEM] * 2,
+        [((here, D), f32, VMEM)] + [((here, D), bf16, VMEM)] * (chips - 1),
+        [],
+        0.1,
+    )(keep, crossed)
+    arrived = [swap(leaving[k - 1], "head", 2 * k) for k in range(1, chips)]
     n_all = n_dp * n_head
     grads_shape = ((rows_here, 5 * width), f32)
     grads, message = call(
         functools.partial(collect_kernel, high, extra),
         "collect",
-        [VMEM] * high,
+        [VMEM] * (2 * high),
         [grads_shape + (VMEM,), ((n_all, 8, 128), f32, VMEM)],
         [],
-        0.1,
-    )(*blocks)
-    message, rows_total = lax.optimization_barrier((message, rows_total))
+        10,
+    )(*late_blocks, *early_blocks)
+    message = after(message, *leaving)
     heard = lax.all_to_all(message, ("dp", "head"), 0, 0, tiled=True)
-    normed_grad = scatter_chip(rows_total)
-    mixed = (add_parts(branches[0], after_all(received, message)) + small_params[:D] + tokens.astype(f32)).astype(bf16)
-
-    inputs = tokens.astype(f32)
-    centred = inputs - jnp.mean(inputs, -1, keepdims=True)
-    scale_in = lax.rsqrt(jnp.mean(centred * centred, -1, keepdims=True) + norm_epsilon)
-    normed = centred * scale_in
-    input_grad = cotangent.astype(f32) + scale_in * (
-        normed_grad
-        - jnp.mean(normed_grad, -1, keepdims=True)
-        - normed * jnp.mean(normed_grad * normed, -1, keepdims=True)
-    )
-
+    (mixed,) = call(
+        mix_kernel, "mix", [VMEM] * (2 + n_head), [((here, D), bf16, VMEM)], [], 1
+    )(after(tokens, message), small_rows, branches[0], *received)
+    (input_grad,) = call(
+        finish_kernel, "finish", [VMEM] * (2 + chips), [((here, D), f32, VMEM)], [], 1
+    )(after(tokens, mixed), cotangent, mine, *arrived)
+    heard = after(heard, input_grad)
     state = [proj_weight, proj_mean, proj_square, out_weight.T, out_mean.T, out_square.T]
     state += [x.reshape(-1, 128) for x in (small_params, small_mean, small_square)]
     proj_shape, out_shape, small_shape = proj_weight.shape, (rows_here, width), small_rows.shape

time: 130 us -> 109 us (0.84)
  Pallas kernels: 54.2 us -> 45 us
  waiting for transfers between devices: 34.7 us -> 26.9 us
  other arithmetic: 7.84 us -> 0.04 us
  starting transfers between devices: 28.3 us -> 30.6 us
  local copies, waits for them, and re-layouts: 3.2 us -> 4.91 us
    all_to_all x1, waiting for transfers between devices: 8.58 us -> 0.01 us  [shards(): heard = lax.all_to_all(message, ('dp', 'head'), 0, 0, tiled=True)]
    pallas_call x1, Pallas kernels: 25.9 us -> 19.8 us  [shards(): call(functools.partial(backward_kernel, heads, n_dp, extra), 'backward',...]
    add x4 -> x0, other arithmetic: 5.51 us -> none  [the longest x1 2.93 us: shards(): cotangent.astype(f32)]
    unnamed x46 -> x42, local copies, waits for them, and re-layouts: 2.27 us -> 4.91 us
    reduce_sum x3 -> x0, other arithmetic: 2.17 us -> none  [the longest x1 1.73 us: shards(): jnp.mean(normed_grad, -1, keepdims=True)]
    pallas_call x2 -> x11, Pallas kernels: 19.4 us -> 17.3 us  [the longest x2 6.74 us: attend(): call(functools.partial(attend_kernel, heads, first, last), 'attend', [VME...]
    ppermute x22 -> x25, starting transfers between devices: 24.8 us -> 26.2 us  [swap(): return lax.ppermute(x, axis, [(i, i ^ k) for i in range(n)])]
    ppermute x22 -> x25, waiting for transfers between devices: 26.1 us -> 26.9 us  [swap(): return lax.ppermute(x, axis, [(i, i ^ k) for i in range(n)])]
  transfers between devices with their start and end apart: 23 -> 26, of which waited for: 9 -> 11; matrix products, arithmetic and copies ran while one was open for 3% -> 0% of each run, Pallas kernels for 38% -> 36%
where the time goes in v4:
time: 109 us
  Pallas kernels  45 us (41%)
  starting transfers between devices  30.6 us (28%)
  waiting for transfers between devices  26.9 us (25%)
  local copies, waits for them, and re-layouts  4.91 us (5%)
  between operations  1.11 us (1%)
    ppermute x25, waiting for transfers between devices, swap(): return lax.ppermute(x, axis, [(i, i ^ k) for i in range(n)])  26.9 us
    ppermute x25, starting transfers between devices, swap(): return lax.ppermute(x, axis, [(i, i ^ k) for i in range(n)])  26.2 us
    pallas_call x1, Pallas kernels, shards(): call(functools.partial(backward_kernel, heads, n_dp, extra), 'backward',...  19.8 us
    pallas_call x2, Pallas kernels, attend(): call(functools.partial(attend_kernel, heads, first, last), 'attend', [VME...  6.74 us
    unnamed x42, local copies, waits for them, and re-layouts  4.91 us
    all_to_all x1, starting transfers between devices, shards(): heard = lax.all_to_all(message, ('dp', 'head'), 0, 0, tiled=True)  4.37 us
    pallas_call x1, Pallas kernels, shards(): call(finish_kernel, 'finish', [VMEM] * (2 + chips), [((here, D), f32, VME...  2.73 us
  transfers between devices with their start and end apart: 26, of which 11 were waited for; matrix products, arithmetic and copies ran while one was open for 0% of the time, Pallas kernels for 36%

profile of v4, /device:TPU:0, one launch (start us, length us, event | category | flops | bytes accessed | tf_op | source)
XLA Modules:
  0.0 108.5 jit_solution(15538489893116670502)
XLA Ops:
  0.7 0.0 copy-start.1
  0.7 1.0 copy-done.1
  1.6 0.8 copy-done.8
  2.4 0.1 cast.1.refs_0_
  2.5 3.0 %collective-permute-start.1 = (bf16[512,512]{1,0:T(8,128)(2,1)S(1)}, bf16[512,512]{1,0:T(8,128)(2,1)S(1)}, u32[]{:S(2)}, u32[]{:S(2)}) collective-permute-start(bf16[512,512]{1,0:T(8,128)(2,1)S(1)} %copy-done), channel_id=1, source_target_pairs={{0,2},{1,3},{2,0},{3,1},{4,6},{5,7},{6,4},{7,5},{8,10},{9,11},{10,... | collective-permute-start | bytes 1572872 | tf_op jit(solution)/shard_map/ppermute | solution.py:49
  5.5 2.6 %collective-permute-start.3 = (bf16[64,640]{1,0:T(8,128)(2,1)S(1)}, bf16[64,640]{1,0:T(8,128)(2,1)S(1)}, u32[]{:S(2)}, u32[]{:S(2)}) collective-permute-start(bf16[64,640]{1,0:T(8,128)(2,1)S(1)} %cast.1.refs_0_), channel_id=1, source_target_pairs={{0,16},{4,20},{8,24},{12,28},{16,0},{20,4},{24,8},{28,12},{1,17},{... | collective-permute-start | bytes 245768 | tf_op jit(solution)/shard_map/ppermute | solution.py:49
  8.1 4.1 %collective-permute-done.3.refs_1_ = bf16[64,640]{1,0:T(8,128)(2,1)S(1)} collective-permute-done((bf16[64,640]{1,0:T(8,128)(2,1)S(1)}, bf16[64,640]{1,0:T(8,128)(2,1)S(1)}, u32[]{:S(2)}, u32[]{:S(2)}) %collective-permute-start.3) | collective-permute-done | bytes 81952 | tf_op jit(solution)/shard_map/ppermute | solution.py:49
  12.3 0.6 collective-permute-start.4
  12.9 0.5 collective-permute-start.6
  13.4 0.5 collective-permute-start.7
  13.9 3.7 %collective-permute-done.4.refs_2_ = bf16[128,640]{1,0:T(8,128)(2,1)S(1)} collective-permute-done((bf16[128,640]{1,0:T(8,128)(2,1)S(1)}, bf16[128,640]{1,0:T(8,128)(2,1)S(1)}, u32[]{:S(2)}, u32[]{:S(2)}) %collective-permute-start.4) | collective-permute-done | bytes 163872 | tf_op jit(solution)/shard_map/ppermute | solution.py:49
  17.7 1.6 %collective-permute-start.5 = (bf16[256,640]{1,0:T(8,128)(2,1)S(1)}, bf16[256,640]{1,0:T(8,128)(2,1)S(1)}, u32[]{:S(2)}, u32[]{:S(2)}) collective-permute-start(bf16[256,640]{1,0:T(8,128)(2,1)S(1)} %pad_maximum_fusion), channel_id=1, source_target_pairs={{0,4},{4,0},{8,12},{12,8},{16,20},{20,16},{24,28},{28,24},{1,5},{5... | collective-permute-start | bytes 983048 | tf_op jit(solution)/shard_map/ppermute | solution.py:49
  19.3 0.0 collective-permute-done.1.refs_2_
  19.3 1.9 %prepare.1 = (f32[8,256,256]{2,1,0:T(8,128)S(1)}, bf16[8,256,128]{2,1,0:T(8,128)(2,1)S(1)}, bf16[8,128,256]{2,1,0:T(8,128)(2,1)S(1)}, bf16[8,128,256]{2,1,0:T(8,128)(2,1)S(1)}) custom-call(s32[1,2048]{1,0:T(1,128)S(1)} %bitcast.26, f32[69,128]{1,0:T(8,128)S(1)} %bitcast.17), custom_call_target="tpu_custom_call" | custom-call | flops 5000000000 | bytes 15000000 | tf_op jit(solution)/shard_map/prepare/pallas_call | solution.py:636
  21.2 3.6 %collective-permute-done.5.refs_3_ = bf16[256,640]{1,0:T(8,128)(2,1)S(1)} collective-permute-done((bf16[256,640]{1,0:T(8,128)(2,1)S(1)}, bf16[256,640]{1,0:T(8,128)(2,1)S(1)}, u32[]{:S(2)}, u32[]{:S(2)}) %collective-permute-start.5) | collective-permute-done | bytes 327712 | tf_op jit(solution)/shard_map/ppermute | solution.py:49
  24.8 0.3 assemble.1.refs_1_.refs_6_.refs_12_.wt_ref
  25.1 1.3 %normalize.1.refs_0_.refs_5_.refs_11_.refs_10_ = bf16[8,256,512]{2,1,0:T(8,128)(2,1)S(1)} custom-call(bf16[512,512]{1,0:T(8,128)(2,1)S(1)} %copy-done, bf16[512,512]{1,0:T(8,128)(2,1)S(1)} %collective-permute-done.refs_1_, bf16[512,512]{1,0:T(8,128)(2,1)S(1)} %collective-permute-done.1.refs_2_, bf16[512,512]{1,0:T(8,128)(2,1)S(1)} %collective-permute-done.2.refs_3_), custom_call_target="tpu_custom_call" | custom-call | flops 1000000000 | bytes 3000000 | tf_op jit(solution)/shard_map/normalize/pallas_call | solution.py:659
  26.4 0.0 copy-start.18
  26.4 1.8 %project.1 = (bf16[8,384,256]{2,1,0:T(8,128)(2,1)S(1)}, bf16[8,256,256]{2,1,0:T(8,128)(2,1)S(1)}, bf16[8,256,256]{2,1,0:T(8,128)(2,1)S(1)}, bf16[8,128,256]{2,1,...) custom-call(bf16[8,256,512]{2,1,0:T(8,128)(2,1)S(1)} %normalize.1.re, ...), custom_call_target="tpu_custom_call" | custom-call | flops 5000000000 | bytes 15000000 | tf_op jit(solution)/shard_map/project/pallas_call | solution.py:668
  28.3 3.9 %attend.2.refs_0_ = f32[6,128,256]{2,1,0:T(8,128)S(1)} custom-call(bf16[8,256,256]{2,1,0:T(8,128)(2,1)S(1)} %get-tuple-element.93.refs_0_.refs_1_, bf16[8,128,256]{2,1,0:T(8,128)(2,1)S(1)} %get-tuple-element.95.refs_1_.refs_2_, bf16[8,128,256]{2,1,0:T(8,128)(2,1)S(1)} %get-tuple-element.96.refs_2_.refs_3_, ...), custom_call_target="tpu_custom_call" | custom-call | flops 8000000000 | bytes 24000000 | tf_op jit(solution)/shard_map/attend/pallas_call | solution.py:678
  32.2 0.1 collective-permute-start.8
  32.3 2.8 %attend.3.refs_4_.refs_8_ = f32[8,128,256]{2,1,0:T(8,128)S(1)} custom-call(f32[6,128,256]{2,1,0:T(8,128)S(1)} %attend.2.refs_0_, bf16[8,256,256]{2,1,0:T(8,128)(2,1)S(1)} %get-tuple-element.93.refs_0_.refs_1_, bf16[8,128,256]{2,1,0:T(8,128)(2,1)S(1)} %get-tuple-element.95.refs_1_.refs_2_, bf16[8,128,256]{2,1,0:T(8,128)(2,1)S(1)} %get-tuple-element.96.refs_2_.refs_3_, ...), custom_call_target="tpu_custom_call" | custom-call | flops 8000000000 | bytes 24000000 | tf_op jit(solution)/shard_map/attend/pallas_call | solution.py:678
  35.2 1.6 %gate.1 = (f32[8,128,256]{2,1,0:T(8,128)S(1)}, f32[8,128,256]{2,1,0:T(8,128)S(1)}, f32[8,4,256]{2,1,0:T(4,128)S(1)}, f32[1,512]{1,0:T(1,128)S(1)}) custom-call(bf16[512,512]{1,0:T(8,128)(2,1)S(1)} %copy-done.12, bf16[512,512]{1,0:T(8,128)(2,1)S(1)} %collective-permute-done.6.refs_1_.refs_5_, bf16[512,512]{1,0:T(8,128)(2,1)S(1)} %collective-permute-done.7.refs_2_.refs_6_, ...), custom_call_target="tpu_custom_call" | custom-call | flops 5000000000 | bytes 15000000 | tf_op jit(solution)/shard_map/gate/pallas_call | solution.py:695
  36.8 0.7 collective-permute-start.11
  37.5 1.5 %collective-permute-start.10 = (f32[8,4,256]{2,1,0:T(4,128)S(1)}, f32[8,4,256]{2,1,0:T(4,128)S(1)}, u32[]{:S(2)}, u32[]{:S(2)}) collective-permute-start(f32[8,4,256]{2,1,0:T(4,128)S(1)} %get-tuple-element.104.refs_0_), channel_id=1, source_target_pairs={{0,2},{1,3},{2,0},{3,1},{4,6},{5,7},{6,4},{7,5},{8,10},{9,11},{10,... | collective-permute-start | bytes 98312 | tf_op jit(solution)/shard_map/ppermute | solution.py:49
  39.0 1.2 %collective-permute-done.11.refs_3_ = f32[8,4,256]{2,1,0:T(4,128)S(1)} collective-permute-done((f32[8,4,256]{2,1,0:T(4,128)S(1)}, f32[8,4,256]{2,1,0:T(4,128)S(1)}, u32[]{:S(2)}, u32[]{:S(2)}) %collective-permute-start.11) | collective-permute-done | bytes 32800 | tf_op jit(solution)/shard_map/ppermute | solution.py:49
  40.2 1.2 %collective-permute-done.10.refs_2_ = f32[8,4,256]{2,1,0:T(4,128)S(1)} collective-permute-done((f32[8,4,256]{2,1,0:T(4,128)S(1)}, f32[8,4,256]{2,1,0:T(4,128)S(1)}, u32[]{:S(2)}, u32[]{:S(2)}) %collective-permute-start.10) | collective-permute-done | bytes 32800 | tf_op jit(solution)/shard_map/ppermute | solution.py:49
  41.4 2.1 %middle.1 = (bf16[512,512]{1,0:T(8,128)(2,1)S(1)}, bf16[512,512]{1,0:T(8,128)(2,1)S(1)}, bf16[512,512]{1,0:T(8,128)(2,1)S(1)}, bf16[512,512]{1,0:T(8,128)(2,1)S(...) custom-call(f32[8,4,256]{2,1,0:T(4,128)S(1)} %get-tuple-element.104., ...), custom_call_target="tpu_custom_call" | custom-call | flops 6000000000 | bytes 18000000 | tf_op jit(solution)/shard_map/middle/pallas_call | solution.py:705
  43.5 0.0 copy-start.19
  43.5 1.6 %collective-permute-start.15 = (bf16[4,64,256]{2,1,0:T(8,128)(2,1)S(1)}, bf16[4,64,256]{2,1,0:T(8,128)(2,1)S(1)}, u32[]{:S(2)}, u32[]{:S(2)}) collective-permute-start(bf16[4,64,256]{2,1,0:T(8,128)(2,1)S(1)} %get-tuple-element.117), channel_id=1, source_target_pairs={{0,4},{4,0},{8,12},{12,8},{16,20},{20,16},{24,28},{28,24},{1,5},{5... | collective-permute-start | bytes 393224 | tf_op jit(solution)/shard_map/ppermute | solution.py:49
  45.1 1.5 %collective-permute-start.13 = (bf16[512,512]{1,0:T(8,128)(2,1)S(1)}, bf16[512,512]{1,0:T(8,128)(2,1)S(1)}, u32[]{:S(2)}, u32[]{:S(2)}) collective-permute-start(bf16[512,512]{1,0:T(8,128)(2,1)S(1)} %get-tuple-element.115), channel_id=1, source_target_pairs={{0,2},{1,3},{2,0},{3,1},{4,6},{5,7},{6,4},{7,5},{8,10},{9,11},{10,... | collective-permute-start | bytes 1572872 | tf_op jit(solution)/shard_map/ppermute | solution.py:49
  46.6 0.4 collective-permute-start.14
  47.0 19.8 %backward.1 = (bf16[8,256,384]{2,1,0:T(8,128)(2,1)S(1)}, bf16[4,80,384]{2,1,0:T(8,128)(2,1)S(1)}, bf16[4,80,384]{2,1,0:T(8,128)(2,1)S(1)}) custom-call(bf16[8,256,256]{2,1,0:T(8,128)(2,1)S(1)} %get-tuple-element.93.refs_0_.refs_1_, bf16[8,256,256]{2,1,0:T(8,128)(2,1)S(1)} %get-tuple-element.94.refs_1_, ...), custom_call_target="tpu_custom_call" | custom-call | flops 35000000512 | bytes 105000000 | tf_op jit(solution)/shard_map/backward/pallas_call | solution.py:725
  66.8 0.0 copy-start.13
  66.8 3.5 %collective-permute-done.14.refs_3_ = bf16[512,512]{1,0:T(8,128)(2,1)S(1)} collective-permute-done((bf16[512,512]{1,0:T(8,128)(2,1)S(1)}, bf16[512,512]{1,0:T(8,128)(2,1)S(1)}, u32[]{:S(2)}, u32[]{:S(2)}) %collective-permute-start.14) | collective-permute-done | bytes 524320 | tf_op jit(solution)/shard_map/ppermute | solution.py:49
  70.3 0.5 collective-permute-start.16
  70.8 1.8 %input_rows.1 = (bf16[2,512,512]{2,1,0:T(8,128)(2,1)S(1)}, bf16[2,512,512]{2,1,0:T(8,128)(2,1)S(1)}) custom-call(bf16[8,256,384]{2,1,0:T(8,128)(2,1)S(1)} %get-tuple-element.120.gp_ref, bf16[8,256,128]{2,1,0:T(8,128)(2,1)S(1)} %get-tuple-element.121.gun_ref, bf16[640,512]{1,0:T(8,128)(2,1)S(1)} %assemble.1.refs_1_.refs_6_.refs_12_.wt_ref), custom_call_target="tpu_custom_call" | custom-call | flops 4000000000 | bytes 12000000 | tf_op jit(solution)/shard_map/input_rows/pallas_call | solution.py:747
  72.6 0.1 fold.3
  72.7 1.5 %collective-permute-start.17 = (bf16[64,256]{1,0:T(8,128)(2,1)S(1)}, bf16[64,256]{1,0:T(8,128)(2,1)S(1)}, u32[]{:S(2)}, u32[]{:S(2)}) collective-permute-start(bf16[64,256]{1,0:T(8,128)(2,1)S(1)} %get-tuple-element.129), channel_id=1, source_target_pairs={{0,8},{4,12},{8,0},{12,4},{16,24},{20,28},{24,16},{28,20},{1,9},{5... | collective-permute-start | bytes 98312 | tf_op jit(solution)/shard_map/ppermute | solution.py:49
  74.2 3.7 %collective-permute-start.18 = (bf16[64,256]{1,0:T(8,128)(2,1)S(1)}, bf16[64,256]{1,0:T(8,128)(2,1)S(1)}, u32[]{:S(2)}, u32[]{:S(2)}) collective-permute-start(bf16[64,256]{1,0:T(8,128)(2,1)S(1)} %get-tuple-element.130), channel_id=1, source_target_pairs={{0,16},{4,20},{8,24},{12,28},{16,0},{20,4},{24,8},{28,12},{1,17},{... | collective-permute-start | bytes 98312 | tf_op jit(solution)/shard_map/ppermute | solution.py:49
  77.9 0.0 collective-permute-start.19
  78.0 0.4 collective-permute-done.16.refs_1_
  78.4 0.1 fold.2
  78.5 1.4 %collective-permute-done.18.refs_6_ = bf16[64,256]{1,0:T(8,128)(2,1)S(1)} collective-permute-done((bf16[64,256]{1,0:T(8,128)(2,1)S(1)}, bf16[64,256]{1,0:T(8,128)(2,1)S(1)}, u32[]{:S(2)}, u32[]{:S(2)}) %collective-permute-start.18) | collective-permute-done | bytes 32800 | tf_op jit(solution)/shard_map/ppermute | solution.py:49
  79.8 3.8 %collective-permute-done.19.refs_7_ = bf16[64,256]{1,0:T(8,128)(2,1)S(1)} collective-permute-done((bf16[64,256]{1,0:T(8,128)(2,1)S(1)}, bf16[64,256]{1,0:T(8,128)(2,1)S(1)}, u32[]{:S(2)}, u32[]{:S(2)}) %collective-permute-start.19) | collective-permute-done | bytes 32800 | tf_op jit(solution)/shard_map/ppermute | solution.py:49
  83.7 1.0 collective-permute-start.21
  84.6 3.4 %collective-permute-start.22 = (bf16[80,384]{1,0:T(8,128)(2,1)S(1)}, bf16[80,384]{1,0:T(8,128)(2,1)S(1)}, u32[]{:S(2)}, u32[]{:S(2)}) collective-permute-start(bf16[80,384]{1,0:T(8,128)(2,1)S(1)} %get-tuple-element.135), channel_id=1, source_target_pairs={{0,24},{4,28},{8,16},{12,20},{16,8},{20,12},{24,0},{28,4},{1,25},{... | collective-permute-start | bytes 184328 | tf_op jit(solution)/shard_map/ppermute | solution.py:49
  88.0 1.0 rows.1
  89.0 1.5 %collective-permute-start.24 = (bf16[512,512]{1,0:T(8,128)(2,1)}, bf16[512,512]{1,0:T(8,128)(2,1)}, u32[]{:S(2)}, u32[]{:S(2)}) collective-permute-start(bf16[512,512]{1,0:T(8,128)(2,1)} %get-tuple-element.139), channel_id=1, source_target_pairs={{0,2},{1,3},{2,0},{3,1},{4,6},{5,7},{6,4},{7,5},{8,10},{9,11},{10,... | collective-permute-start | bytes 1572872 | tf_op jit(solution)/shard_map/ppermute | solution.py:49
  90.5 1.5 %collective-permute-done.21.refs_2_ = bf16[80,384]{1,0:T(8,128)(2,1)S(1)} collective-permute-done((bf16[80,384]{1,0:T(8,128)(2,1)S(1)}, bf16[80,384]{1,0:T(8,128)(2,1)S(1)}, u32[]{:S(2)}, u32[]{:S(2)}) %collective-permute-start.21) | collective-permute-done | bytes 61472 | tf_op jit(solution)/shard_map/ppermute | solution.py:49
  92.0 0.8 collect.1
  92.8 4.4 %all-to-all-start = ((f32[32,8,128]{2,1,0:T(8,128)}), f32[32,8,128]{2,1,0:T(8,128)S(1)}, u32[]{:S(2)}, u32[]{:S(2)}) async-start(f32[32,8,128]{2,1,0:T(8,128)} %get-tuple-element.140), calls=%async_computation | async-start | bytes 262144 | tf_op jit(solution)/shard_map/all_to_all | solution.py:781
  97.2 0.0 copy-start.14
  97.2 1.0 copy-done.14
  98.2 1.0 copy-done.16
  99.3 1.0 copy-done.20
  100.3 1.2 %mix.1 = bf16[512,512]{1,0:T(8,128)(2,1)} custom-call(bf16[512,512]{1,0:T(8,128)(2,1)S(1)} %copy-done, f32[69,128]{1,0:T(8,128)S(1)} %bitcast.18, bf16[512,512]{1,0:T(8,128)(2,1)S(1)} %copy-done.20, bf16[512,512]{1,0:T(8,128)(2,1)S(1)} %collective-permute-done.12.refs_1_, bf16[512,512]{1,0:T(8,128)(2,1)S(1)} %copy-done.14, bf16[512,512]{1,0:T(8,128)(2,1)S(1)} %copy-done.16), custom_call_target="tpu_custom_call" | custom-call | flops 1000000000 | bytes 3000000 | tf_op jit(solution)/shard_map/mix/pallas_call | solution.py:782
  101.5 0.0 copy-start.7
  101.5 0.0 copy-start.9
  101.5 0.0 copy-start.10
  101.5 0.0 copy-start.11
  101.5 2.4 %collective-permute-done.24.refs_0_ = bf16[512,512]{1,0:T(8,128)(2,1)} collective-permute-done((bf16[512,512]{1,0:T(8,128)(2,1)}, bf16[512,512]{1,0:T(8,128)(2,1)}, u32[]{:S(2)}, u32[]{:S(2)}) %collective-permute-start.24) | collective-permute-done | bytes 524320 | tf_op jit(solution)/shard_map/ppermute | solution.py:49
  103.9 2.7 %finish.1 = f32[512,512]{1,0:T(8,128)} custom-call(bf16[512,512]{1,0:T(8,128)(2,1)S(1)} %copy-done, bf16[512,512]{1,0:T(8,128)(2,1)S(1)} %copy-done.12, f32[512,512]{1,0:T(8,128)S(1)} %get-tuple-element.147.mine_ref, bf16[512,512]{1,0:T(8,128)(2,1)} %collective-permute-done.24.refs_0_), custom_call_target="tpu_custom_call" | custom-call | flops 1000000000 | bytes 3000000 | tf_op jit(solution)/shard_map/finish/pallas_call | solution.py:785
  106.7 1.7 %update.1 = (f32[64,4,128]{2,1,0:T(4,128)}, f32[64,128]{1,0:T(8,128)}, f32[69,128]{1,0:T(8,128)}, f32[1,1]{1,0:T(1,128)}, f32[64,4,128]{2,1,0:T(4,128)}, /*index...) custom-call(f32[32,8,128]{2,1,0:T(8,128)S(1)} %all-to-all-done.heard, ...), custom_call_target="tpu_custom_call" | custom-call | flops 100000000 | bytes 300000 | tf_op jit(solution)/shard_map/update/pallas_call | solution.py:793
  (50 shorter events, 0.1 us)
Async XLA Ops:
  0.6 1.9 %copy-start = (bf16[512,512]{1,0:T(8,128)(2,1)S(1)}, bf16[512,512]{1,0:T(8,128)(2,1)}, u32[]{:S(2)}) copy-start(bf16[512,512]{1,0:T(8,128)(2,1)} %tokens_ref.1) | copy-start | bytes 1572868
  0.7 1.0 copy-start.1
  1.6 0.8 copy-start.8
  2.4 10.5 %copy-start.12 = (bf16[512,512]{1,0:T(8,128)(2,1)S(1)}, bf16[512,512]{1,0:T(8,128)(2,1)}, u32[]{:S(2)}) copy-start(bf16[512,512]{1,0:T(8,128)(2,1)} %cot_ref.1) | copy-start | bytes 1572868
  2.4 16.9 %copy-start.5 = (f32[8832]{0:T(1024)S(1)}, f32[8832]{0:T(1024)}, u32[]{:S(2)}) copy-start(f32[8832]{0:T(1024)} %param.19) | copy-start | bytes 105988
  2.4 16.9 %copy-start.17 = (s32[2048]{0:T(1024)S(1)}, s32[2048]{0:T(1024)}, u32[]{:S(2)}) copy-start(s32[2048]{0:T(1024)} %param.16) | copy-start | bytes 24580
  2.5 16.7 %collective-permute-start.1 = (bf16[512,512]{1,0:T(8,128)(2,1)S(1)}, bf16[512,512]{1,0:T(8,128)(2,1)S(1)}, u32[]{:S(2)}, u32[]{:S(2)}) collective-permute-start(bf16[512,512]{1,0:T(8,128)(2,1)S(1)} %copy-done), channel_id=1, source_target_pairs={{0,2},{1,3},{2,0},{3,1},{4,6},{5,7},{6,4},{7,5},{8,10},{9,11},{10,... | collective-permute-start | bytes 1572872 | tf_op jit(solution)/shard_map/ppermute | solution.py:49
  5.5 6.7 %collective-permute-start.3 = (bf16[64,640]{1,0:T(8,128)(2,1)S(1)}, bf16[64,640]{1,0:T(8,128)(2,1)S(1)}, u32[]{:S(2)}, u32[]{:S(2)}) collective-permute-start(bf16[64,640]{1,0:T(8,128)(2,1)S(1)} %cast.1.refs_0_), channel_id=1, source_target_pairs={{0,16},{4,20},{8,24},{12,28},{16,0},{20,4},{24,8},{28,12},{1,17},{... | collective-permute-start | bytes 245768 | tf_op jit(solution)/shard_map/ppermute | solution.py:49
  12.3 5.4 %collective-permute-start.4 = (bf16[128,640]{1,0:T(8,128)(2,1)S(1)}, bf16[128,640]{1,0:T(8,128)(2,1)S(1)}, u32[]{:S(2)}, u32[]{:S(2)}) collective-permute-start(bf16[128,640]{1,0:T(8,128)(2,1)S(1)} %pad_maximum_fusion.1), channel_id=1, source_target_pairs={{0,8},{4,12},{8,0},{12,4},{16,24},{20,28},{24,16},{28,20},{1,9},{5... | collective-permute-start | bytes 491528 | tf_op jit(solution)/shard_map/ppermute | solution.py:49
  12.9 12.3 %collective-permute-start = (bf16[512,512]{1,0:T(8,128)(2,1)S(1)}, bf16[512,512]{1,0:T(8,128)(2,1)S(1)}, u32[]{:S(2)}, u32[]{:S(2)}) collective-permute-start(bf16[512,512]{1,0:T(8,128)(2,1)S(1)} %copy-done), channel_id=1, source_target_pairs={{0,1},{1,0},{2,3},{3,2},{4,5},{5,4},{6,7},{7,6},{8,9},{9,8},{10,11... | collective-permute-start | bytes 1572872 | tf_op jit(solution)/shard_map/ppermute | solution.py:49
  12.9 22.3 %collective-permute-start.6 = (bf16[512,512]{1,0:T(8,128)(2,1)S(1)}, bf16[512,512]{1,0:T(8,128)(2,1)S(1)}, u32[]{:S(2)}, u32[]{:S(2)}) collective-permute-start(bf16[512,512]{1,0:T(8,128)(2,1)S(1)} %copy-done.12), channel_id=1, source_target_pairs={{0,1},{1,0},{2,3},{3,2},{4,5},{5,4},{6,7},{7,6},{8,9},{9,8},{10,11... | collective-permute-start | bytes 1572872 | tf_op jit(solution)/shard_map/ppermute | solution.py:49
  13.4 18.9 %collective-permute-start.7 = (bf16[512,512]{1,0:T(8,128)(2,1)S(1)}, bf16[512,512]{1,0:T(8,128)(2,1)S(1)}, u32[]{:S(2)}, u32[]{:S(2)}) collective-permute-start(bf16[512,512]{1,0:T(8,128)(2,1)S(1)} %copy-done.12), channel_id=1, source_target_pairs={{0,2},{1,3},{2,0},{3,1},{4,6},{5,7},{6,4},{7,5},{8,10},{9,11},{10,... | collective-permute-start | bytes 1572872 | tf_op jit(solution)/shard_map/ppermute | solution.py:49
  17.7 7.1 %collective-permute-start.5 = (bf16[256,640]{1,0:T(8,128)(2,1)S(1)}, bf16[256,640]{1,0:T(8,128)(2,1)S(1)}, u32[]{:S(2)}, u32[]{:S(2)}) collective-permute-start(bf16[256,640]{1,0:T(8,128)(2,1)S(1)} %pad_maximum_fusion), channel_id=1, source_target_pairs={{0,4},{4,0},{8,12},{12,8},{16,20},{20,16},{24,28},{28,24},{1,5},{5... | collective-permute-start | bytes 983048 | tf_op jit(solution)/shard_map/ppermute | solution.py:49
  19.3 5.9 %collective-permute-start.2 = (bf16[512,512]{1,0:T(8,128)(2,1)S(1)}, bf16[512,512]{1,0:T(8,128)(2,1)S(1)}, u32[]{:S(2)}, u32[]{:S(2)}) collective-permute-start(bf16[512,512]{1,0:T(8,128)(2,1)S(1)} %collective-permute-done.1.refs_2_), channel_id=1, source_target_pairs={{0,1},{1,0},{2,3},{3,2},{4,5},{5,4},{6,7},{7,6},{8,9},{9,8},{10,11... | collective-permute-start | bytes 1572872 | tf_op jit(solution)/shard_map/ppermute | solution.py:49
  26.4 1.9 %copy-start.18 = (s32[2048]{0:T(1024)S(1)}, s32[2048]{0:T(1024)}, u32[]{:S(2)}) copy-start(s32[2048]{0:T(1024)} %param.15) | copy-start | bytes 24580
  32.2 2.9 %collective-permute-start.8 = (bf16[512,512]{1,0:T(8,128)(2,1)S(1)}, bf16[512,512]{1,0:T(8,128)(2,1)S(1)}, u32[]{:S(2)}, u32[]{:S(2)}) collective-permute-start(bf16[512,512]{1,0:T(8,128)(2,1)S(1)} %collective-permute-done.7.refs_2_.refs_6_), channel_id=1, source_target_pairs={{0,1},{1,0},{2,3},{3,2},{4,5},{5,4},{6,7},{7,6},{8,9},{9,8},{10,11... | collective-permute-start | bytes 1572872 | tf_op jit(solution)/shard_map/ppermute | solution.py:49
  36.8 3.4 %collective-permute-start.11 = (f32[8,4,256]{2,1,0:T(4,128)S(1)}, f32[8,4,256]{2,1,0:T(4,128)S(1)}, u32[]{:S(2)}, u32[]{:S(2)}) collective-permute-start(f32[8,4,256]{2,1,0:T(4,128)S(1)} %get-tuple-element.104.refs_0_), channel_id=1, source_target_pairs={{0,3},{1,2},{2,1},{3,0},{4,7},{5,6},{6,5},{7,4},{8,11},{9,10},{10,... | collective-permute-start | bytes 98312 | tf_op jit(solution)/shard_map/ppermute | solution.py:49
  37.5 3.9 %collective-permute-start.10 = (f32[8,4,256]{2,1,0:T(4,128)S(1)}, f32[8,4,256]{2,1,0:T(4,128)S(1)}, u32[]{:S(2)}, u32[]{:S(2)}) collective-permute-start(f32[8,4,256]{2,1,0:T(4,128)S(1)} %get-tuple-element.104.refs_0_), channel_id=1, source_target_pairs={{0,2},{1,3},{2,0},{3,1},{4,6},{5,7},{6,4},{7,5},{8,10},{9,11},{10,... | collective-permute-start | bytes 98312 | tf_op jit(solution)/shard_map/ppermute | solution.py:49
  39.0 2.4 %collective-permute-start.9 = (f32[8,4,256]{2,1,0:T(4,128)S(1)}, f32[8,4,256]{2,1,0:T(4,128)S(1)}, u32[]{:S(2)}, u32[]{:S(2)}) collective-permute-start(f32[8,4,256]{2,1,0:T(4,128)S(1)} %get-tuple-element.104.refs_0_), channel_id=1, source_target_pairs={{0,1},{1,0},{2,3},{3,2},{4,5},{5,4},{6,7},{7,6},{8,9},{9,8},{10,11... | collective-permute-start | bytes 98312 | tf_op jit(solution)/shard_map/ppermute | solution.py:49
  43.5 23.2 %copy-start.19 = (bf16[512,512]{1,0:T(8,128)(2,1)}, bf16[512,512]{1,0:T(8,128)(2,1)S(1)}, u32[]{:S(2)}) copy-start(bf16[512,512]{1,0:T(8,128)(2,1)S(1)} %get-tuple-element.142.refs_0_) | copy-start | bytes 1572868
  43.5 23.2 %collective-permute-start.15 = (bf16[4,64,256]{2,1,0:T(8,128)(2,1)S(1)}, bf16[4,64,256]{2,1,0:T(8,128)(2,1)S(1)}, u32[]{:S(2)}, u32[]{:S(2)}) collective-permute-start(bf16[4,64,256]{2,1,0:T(8,128)(2,1)S(1)} %get-tuple-element.117), channel_id=1, source_target_pairs={{0,4},{4,0},{8,12},{12,8},{16,20},{20,16},{24,28},{28,24},{1,5},{5... | collective-permute-start | bytes 393224 | tf_op jit(solution)/shard_map/ppermute | solution.py:49
  45.1 21.6 %collective-permute-start.12 = (bf16[512,512]{1,0:T(8,128)(2,1)S(1)}, bf16[512,512]{1,0:T(8,128)(2,1)S(1)}, u32[]{:S(2)}, u32[]{:S(2)}) collective-permute-start(bf16[512,512]{1,0:T(8,128)(2,1)S(1)} %get-tuple-element.114), channel_id=1, source_target_pairs={{0,1},{1,0},{2,3},{3,2},{4,5},{5,4},{6,7},{7,6},{8,9},{9,8},{10,11... | collective-permute-start | bytes 1572872 | tf_op jit(solution)/shard_map/ppermute | solution.py:49
  45.1 21.7 %collective-permute-start.13 = (bf16[512,512]{1,0:T(8,128)(2,1)S(1)}, bf16[512,512]{1,0:T(8,128)(2,1)S(1)}, u32[]{:S(2)}, u32[]{:S(2)}) collective-permute-start(bf16[512,512]{1,0:T(8,128)(2,1)S(1)} %get-tuple-element.115), channel_id=1, source_target_pairs={{0,2},{1,3},{2,0},{3,1},{4,6},{5,7},{6,4},{7,5},{8,10},{9,11},{10,... | collective-permute-start | bytes 1572872 | tf_op jit(solution)/shard_map/ppermute | solution.py:49
  46.6 23.7 %collective-permute-start.14 = (bf16[512,512]{1,0:T(8,128)(2,1)S(1)}, bf16[512,512]{1,0:T(8,128)(2,1)S(1)}, u32[]{:S(2)}, u32[]{:S(2)}) collective-permute-start(bf16[512,512]{1,0:T(8,128)(2,1)S(1)} %get-tuple-element.116), channel_id=1, source_target_pairs={{0,3},{1,2},{2,1},{3,0},{4,7},{5,6},{6,5},{7,4},{8,11},{9,10},{10,... | collective-permute-start | bytes 1572872 | tf_op jit(solution)/shard_map/ppermute | solution.py:49
  66.8 5.8 %copy-start.13 = (bf16[512,512]{1,0:T(8,128)(2,1)}, bf16[512,512]{1,0:T(8,128)(2,1)S(1)}, u32[]{:S(2)}) copy-start(bf16[512,512]{1,0:T(8,128)(2,1)S(1)} %collective-permute-done.13.refs_2_) | copy-start | bytes 1572868
  70.3 2.3 %copy-start.15 = (bf16[512,512]{1,0:T(8,128)(2,1)}, bf16[512,512]{1,0:T(8,128)(2,1)S(1)}, u32[]{:S(2)}) copy-start(bf16[512,512]{1,0:T(8,128)(2,1)S(1)} %collective-permute-done.14.refs_3_) | copy-start | bytes 1572868
  70.3 8.1 %collective-permute-start.16 = (bf16[4,80,384]{2,1,0:T(8,128)(2,1)S(1)}, bf16[4,80,384]{2,1,0:T(8,128)(2,1)S(1)}, u32[]{:S(2)}, u32[]{:S(2)}) collective-permute-start(bf16[4,80,384]{2,1,0:T(8,128)(2,1)S(1)} %get-tuple-element.119), channel_id=1, source_target_pairs={{0,4},{4,0},{8,12},{12,8},{16,20},{20,16},{24,28},{28,24},{1,5},{5... | collective-permute-start | bytes 737288 | tf_op jit(solution)/shard_map/ppermute | solution.py:49
  72.7 5.8 %collective-permute-start.17 = (bf16[64,256]{1,0:T(8,128)(2,1)S(1)}, bf16[64,256]{1,0:T(8,128)(2,1)S(1)}, u32[]{:S(2)}, u32[]{:S(2)}) collective-permute-start(bf16[64,256]{1,0:T(8,128)(2,1)S(1)} %get-tuple-element.129), channel_id=1, source_target_pairs={{0,8},{4,12},{8,0},{12,4},{16,24},{20,28},{24,16},{28,20},{1,9},{5... | collective-permute-start | bytes 98312 | tf_op jit(solution)/shard_map/ppermute | solution.py:49
  74.2 5.6 %collective-permute-start.18 = (bf16[64,256]{1,0:T(8,128)(2,1)S(1)}, bf16[64,256]{1,0:T(8,128)(2,1)S(1)}, u32[]{:S(2)}, u32[]{:S(2)}) collective-permute-start(bf16[64,256]{1,0:T(8,128)(2,1)S(1)} %get-tuple-element.130), channel_id=1, source_target_pairs={{0,16},{4,20},{8,24},{12,28},{16,0},{20,4},{24,8},{28,12},{1,17},{... | collective-permute-start | bytes 98312 | tf_op jit(solution)/shard_map/ppermute | solution.py:49
  77.9 5.7 %collective-permute-start.19 = (bf16[64,256]{1,0:T(8,128)(2,1)S(1)}, bf16[64,256]{1,0:T(8,128)(2,1)S(1)}, u32[]{:S(2)}, u32[]{:S(2)}) collective-permute-start(bf16[64,256]{1,0:T(8,128)(2,1)S(1)} %get-tuple-element.131), channel_id=1, source_target_pairs={{0,24},{4,28},{8,16},{12,20},{16,8},{20,12},{24,0},{28,4},{1,25},{... | collective-permute-start | bytes 98312 | tf_op jit(solution)/shard_map/ppermute | solution.py:49
  83.6 4.4 %collective-permute-start.23 = (bf16[2,512,512]{2,1,0:T(8,128)(2,1)S(1)}, bf16[2,512,512]{2,1,0:T(8,128)(2,1)S(1)}, u32[]{:S(2)}, u32[]{:S(2)}) collective-permute-start(bf16[2,512,512]{2,1,0:T(8,128)(2,1)S(1)} %get-tuple-element.138), channel_id=1, source_target_pairs={{0,1},{1,0},{2,3},{3,2},{4,5},{5,4},{6,7},{7,6},{8,9},{9,8},{10,11... | collective-permute-start | bytes 3145736 | tf_op jit(solution)/shard_map/ppermute | solution.py:49
  83.6 6.9 %collective-permute-start.20 = (bf16[80,384]{1,0:T(8,128)(2,1)S(1)}, bf16[80,384]{1,0:T(8,128)(2,1)S(1)}, u32[]{:S(2)}, u32[]{:S(2)}) collective-permute-start(bf16[80,384]{1,0:T(8,128)(2,1)S(1)} %get-tuple-element.133), channel_id=1, source_target_pairs={{0,8},{4,12},{8,0},{12,4},{16,24},{20,28},{24,16},{28,20},{1,9},{5... | collective-permute-start | bytes 184328 | tf_op jit(solution)/shard_map/ppermute | solution.py:49
  83.7 8.3 %collective-permute-start.21 = (bf16[80,384]{1,0:T(8,128)(2,1)S(1)}, bf16[80,384]{1,0:T(8,128)(2,1)S(1)}, u32[]{:S(2)}, u32[]{:S(2)}) collective-permute-start(bf16[80,384]{1,0:T(8,128)(2,1)S(1)} %get-tuple-element.134), channel_id=1, source_target_pairs={{0,16},{4,20},{8,24},{12,28},{16,0},{20,4},{24,8},{28,12},{1,17},{... | collective-permute-start | bytes 184328 | tf_op jit(solution)/shard_map/ppermute | solution.py:49
  84.6 7.3 %collective-permute-start.22 = (bf16[80,384]{1,0:T(8,128)(2,1)S(1)}, bf16[80,384]{1,0:T(8,128)(2,1)S(1)}, u32[]{:S(2)}, u32[]{:S(2)}) collective-permute-start(bf16[80,384]{1,0:T(8,128)(2,1)S(1)} %get-tuple-element.135), channel_id=1, source_target_pairs={{0,24},{4,28},{8,16},{12,20},{16,8},{20,12},{24,0},{28,4},{1,25},{... | collective-permute-start | bytes 184328 | tf_op jit(solution)/shard_map/ppermute | solution.py:49
  89.0 14.9 %collective-permute-start.24 = (bf16[512,512]{1,0:T(8,128)(2,1)}, bf16[512,512]{1,0:T(8,128)(2,1)}, u32[]{:S(2)}, u32[]{:S(2)}) collective-permute-start(bf16[512,512]{1,0:T(8,128)(2,1)} %get-tuple-element.139), channel_id=1, source_target_pairs={{0,2},{1,3},{2,0},{3,1},{4,6},{5,7},{6,4},{7,5},{8,10},{9,11},{10,... | collective-permute-start | bytes 1572872 | tf_op jit(solution)/shard_map/ppermute | solution.py:49
  92.8 13.9 %all-to-all-start = ((f32[32,8,128]{2,1,0:T(8,128)}), f32[32,8,128]{2,1,0:T(8,128)S(1)}, u32[]{:S(2)}, u32[]{:S(2)}) async-start(f32[32,8,128]{2,1,0:T(8,128)} %get-tuple-element.140), calls=%async_computation | async-start | bytes 262144 | tf_op jit(solution)/shard_map/all_to_all | solution.py:781
  97.2 1.0 copy-start.14
  98.2 1.0 copy-start.16
  99.3 1.0 copy-start.20
  101.5 5.2 %copy-start.2 = (f32[64,4,128]{2,1,0:T(4,128)S(1)}, f32[64,4,128]{2,1,0:T(4,128)}, u32[]{:S(2)}) copy-start(f32[64,4,128]{2,1,0:T(4,128)} %refs_0_.5) | copy-start | bytes 393220
  101.5 5.2 %copy-start.3 = (f32[64,4,128]{2,1,0:T(4,128)S(1)}, f32[64,4,128]{2,1,0:T(4,128)}, u32[]{:S(2)}) copy-start(f32[64,4,128]{2,1,0:T(4,128)} %refs_1_.1) | copy-start | bytes 393220
  101.5 5.2 %copy-start.4 = (f32[64,4,128]{2,1,0:T(4,128)S(1)}, f32[64,4,128]{2,1,0:T(4,128)}, u32[]{:S(2)}) copy-start(f32[64,4,128]{2,1,0:T(4,128)} %refs_2_.1) | copy-start | bytes 393220
  101.5 5.2 %copy-start.6 = (f32[8832]{0:T(1024)S(1)}, f32[8832]{0:T(1024)}, u32[]{:S(2)}) copy-start(f32[8832]{0:T(1024)} %param.24) | copy-start | bytes 105988
  101.5 5.2 %copy-start.7 = (f32[8832]{0:T(1024)S(1)}, f32[8832]{0:T(1024)}, u32[]{:S(2)}) copy-start(f32[8832]{0:T(1024)} %param.25) | copy-start | bytes 105988
  101.5 5.2 %copy-start.9 = (f32[128,64]{0,1:T(8,128)S(1)}, f32[128,64]{0,1:T(8,128)}, u32[]{:S(2)}) copy-start(f32[128,64]{0,1:T(8,128)} %param.18) | copy-start | bytes 98308
  101.5 5.2 %copy-start.10 = (f32[128,64]{0,1:T(8,128)S(1)}, f32[128,64]{0,1:T(8,128)}, u32[]{:S(2)}) copy-start(f32[128,64]{0,1:T(8,128)} %param.22) | copy-start | bytes 98308
  101.5 5.2 %copy-start.11 = (f32[128,64]{0,1:T(8,128)S(1)}, f32[128,64]{0,1:T(8,128)}, u32[]{:S(2)}) copy-start(f32[128,64]{0,1:T(8,128)} %param.23) | copy-start | bytes 98308

commit v5 on v4

--- a/solution.py
+++ b/solution.py
@@ -74,12 +74,17 @@
     arrays, offsets, operands = [x], [[0]], []
     k = n // 2
     while k:
-        operand = jnp.concatenate(arrays, 0) if len(arrays) > 1 else x
+        operand = join(arrays) if len(arrays) > 1 else x
         operands.append(operand)
         arrays.append(swap(operand, "dp", k))
         offsets.append([o ^ k for group in offsets for o in group])
         k //= 2
     return arrays, offsets, operands
+
+
+def join(arrays, us=2):
+    shape = (sum(x.shape[0] for x in arrays), arrays[0].shape[1])
+    return call(join_kernel, "join", [VMEM] * len(arrays), [(shape, arrays[0].dtype, VMEM)], [], us)(*arrays)[0]
 
 
 def split_dp(n):
@@ -101,6 +106,18 @@
     return [mine] + [swap(sent, "dp", (k + 1) * low) for k, sent in enumerate(leaving)]
 
 
+def fold_cores(keep, crossed):
+    chips, rows, columns = keep.shape
+    return call(
+        functools.partial(rows_kernel, chips),
+        "rows",
+        [VMEM] * 2,
+        [((rows, columns), f32, VMEM)] + [((rows, columns), bf16, VMEM)] * (chips - 1),
+        [],
+        0.1,
+    )(keep, crossed)
+
+
 def dot(a, b):
     return lax.dot_general(a, b, (((1,), (0,)), ((), ())), preferred_element_type=f32)
 
@@ -165,7 +182,12 @@
     return g
 
 
-def cast_kernel(w_ref, o_ref, low_ref):
+def cast_kernel(w_in, o_in, low_ref, w_ref, o_ref, sems):
+    copies = [pltpu.make_async_copy(w_in, w_ref, sems.at[0]), pltpu.make_async_copy(o_in, o_ref, sems.at[1])]
+    for copy in copies:
+        copy.start()
+    for copy in copies:
+        copy.wait()
     width = o_ref.shape[1]
     for c in range(4):
         low_ref[:, c * width : (c + 1) * width] = w_ref[:, c, :].astype(bf16)
@@ -173,23 +195,25 @@
 
 
 def row_lanes(ref, first, count):
-    return jnp.concatenate([ref[first + k : first + k + 1, :] for k in range(count)], axis=1)
+    return jnp.concatenate([ref[pl.ds(first + k, 1), :] for k in range(count)], axis=1)
 
 
 def prepare_kernel(tb_ref, small_ref, pos_ref, oh_ref, oht_ref, trow_ref):
     nb = pos_ref.shape[0]
-    for d in range(nb):
-        here = row_lanes(small_ref, D // 128 + d * TILE // 128, TILE // 128)
-        before = here if d == 0 else row_lanes(small_ref, D // 128 + (d - 1) * TILE // 128, TILE // 128)
-        row = jnp.concatenate([here, before], axis=1) * 0.5
-        tile = pltpu.roll(
-            jnp.broadcast_to(row, (TILE, 2 * TILE)), 0, 1, stride=1, stride_axis=0
+    step = TILE // 128
+
+    def tile(d, _):
+        first = D // 128 + d * step
+        row = jnp.concatenate([row_lanes(small_ref, first, step), row_lanes(small_ref, first - step, step)], axis=1)
+        pos_ref[d] = pltpu.roll(
+            jnp.broadcast_to(row * 0.5, (TILE, 2 * TILE)), 0, 1, stride=1, stride_axis=0
         )[:, :TILE]
-        if d == 0:
-            b = lax.broadcasted_iota(jnp.int32, (TILE, TILE), 0)
-            a = lax.broadcasted_iota(jnp.int32, (TILE, TILE), 1)
-            tile = jnp.where(b <= a, tile, NEG)
-        pos_ref[d] = tile
+        return 0
+
+    lax.fori_loop(0, nb, tile, 0)
+    b = lax.broadcasted_iota(jnp.int32, (TILE, TILE), 0)
+    a = lax.broadcasted_iota(jnp.int32, (TILE, TILE), 1)
+    pos_ref[0] = jnp.where(b <= a, pos_ref[0], NEG)
     table = row_lanes(small_ref, (D + POS) // 128, NTB // 128)
     row = jnp.concatenate([table, table], axis=1)
     upper = pltpu.roll(jnp.broadcast_to(row, (NTB, 2 * NTB)), 0, 1, stride=1, stride_axis=0)[:, :NTB]
@@ -207,6 +231,13 @@
         return 0
 
     lax.fori_loop(0, nb, block, 0)
+
+
+def join_kernel(*refs):
+    at = 0
+    for ref in refs[:-1]:
+        refs[-1][at : at + ref.shape[0]] = ref[...]
+        at += ref.shape[0]
 
 
 def normalize_kernel(*refs):
@@ -310,13 +341,39 @@
             )
 
 
+def standardized(i, n_head, stats, attn_ref):
+    width = attn_ref.shape[1]
+    st = [s[i] for s in stats]
+    mean = sum(p[0:1] for p in st) / n_head
+    spread = sum(p[1:2] + width * (p[0:1] - mean) * (p[0:1] - mean) for p in st)
+    scale = lax.rsqrt(spread / HD + norm_epsilon)
+    first = sum(p[2:3] for p in st) / HD
+    second = scale * sum(p[3:4] + (p[0:1] - mean) * p[2:3] for p in st) / HD
+    return (attn_ref[i] - mean) * scale, scale, first, second
+
+
+def branch_kernel(n_head, *refs):
+    stats, (attn_ref, p_ref, wt_ref, keep, send) = refs[:n_head], refs[n_head:]
+    width = attn_ref.shape[1]
+    per = keep.shape[1] // TILE
+    for k in range(n_head):
+        device = lax.axis_index("head") ^ k
+        for r in range(per):
+            i = device * per + r
+            normed = standardized(i, n_head, stats, attn_ref)[0]
+            p = p_ref[i]
+            gated = (normed * (p * (0.5 + 0.5 * jnp.tanh(0.5 * p)))).astype(bf16)
+            (keep, send)[k % 2][device // 2, r * TILE : (r + 1) * TILE] = dot(
+                flip(gated).astype(bf16), wt_ref[4 * width :]
+            ).astype(bf16)
+
+
 def middle_kernel(n_head, *refs):
     refs = list(refs)
     take = lambda count: [refs.pop(0) for _ in range(count)]
     stats = take(n_head)
     cot_pieces = take(n_head)
-    attn_ref, p_ref, gg_ref, xn_ref, wt_ref = take(5)
-    branches = take(n_head)
+    attn_ref, p_ref, gg_ref, xn_ref = take(4)
     da_ref, dat_ref, gun_ref = take(3)
     parts, acc_ref, wg_ref = refs[:-2], refs[-2], refs[-1]
     width = attn_ref.shape[1]
@@ -324,14 +381,7 @@
     for k, piece in enumerate(cot_pieces):
         for r in range(per):
             i = (lax.axis_index("head") ^ k) * per + r
-            at = slice(r * TILE, (r + 1) * TILE)
-            st = [s[i] for s in stats]
-            mean = sum(p[0:1] for p in st) / n_head
-            spread = sum(p[1:2] + width * (p[0:1] - mean) * (p[0:1] - mean) for p in st)
-            scale = lax.rsqrt(spread / HD + norm_epsilon)
-            first = sum(p[2:3] for p in st) / HD
-            second = scale * sum(p[3:4] + (p[0:1] - mean) * p[2:3] for p in st) / HD
-            normed = (attn_ref[i] - mean) * scale
+            normed, scale, first, second = standardized(i, n_head, stats, attn_ref)
             p = p_ref[i]
             sg = 0.5 + 0.5 * jnp.tanh(0.5 * p)
             gate = p * sg
@@ -342,8 +392,7 @@
             dat_ref[i] = (grad * 0.5).astype(bf16)
             gu = (gg * normed * (sg + gate * (1.0 - sg))).astype(bf16)
             gun_ref[i] = flip(gu).astype(bf16)
-            branches[k][at, :] = dot(flip(gated).astype(bf16), wt_ref[4 * width :]).astype(bf16)
-            add_gate, add_out = dot(gu, xn_ref[i]), dot(gated, piece[at, :])
+            add_gate, add_out = dot(gu, xn_ref[i]), dot(gated, piece[r * TILE : (r + 1) * TILE, :])
             if k + r == 0:
                 acc_ref[:width] = add_gate
                 acc_ref[width:] = add_out
@@ -371,12 +420,14 @@
     d_ref, xn_ref, ss_ref, gb_ref = take(4)
     gp_ref = refs.pop(0)
     parts = take(split_dp(n_dp)[1])
-    accv_ref, acck_ref, posg_ref, gpq_ref, acc_ref, wg_ref, small_ref = refs
+    accv_ref, acck_ref, posg_ref, acc_ref, wg_ref, small_ref = refs
     nb, width = v_ref.shape[0], v_ref.shape[2]
     factor = 1.0 / math.sqrt(HEAD_DIM)
-    tiles = [(i, j) for i in range(nb) for j in range(i + 1)]
+    tiles = [(i, j) for i in reversed(range(nb)) for j in range(i + 1)]
     products, weights, grads = {}, {}, {}
-    dq = None
+    dq = m2 = None
+    small_ref[...] = jnp.zeros_like(small_ref)
+    small_ref[:, :D] = gb_ref[...]
 
     def add(ref, at, value, first):
         ref[at] = value if first else ref[at] + value
@@ -397,7 +448,7 @@
             w = h * u
             ds = back * (u + w * (1.0 - th))
             weights[t - 1], grads[t - 1] = w.astype(bf16), ds.astype(bf16)
-            add(posg_ref, i - j, sum(ds[:, g * TILE : (g + 1) * TILE] for g in range(heads)), j == 0)
+            add(posg_ref, i - j, sum(ds[:, g * TILE : (g + 1) * TILE] for g in range(heads)), i == nb - 1)
         if t >= 2:
             i, j = tiles[t - 2]
             low = grads.pop(t - 2)
@@ -405,37 +456,28 @@
                 da = own_lanes(da_ref[i], heads)
                 times = jnp.concatenate([kx_ref[i, :, :NTB]] * heads, axis=0)
                 q = jnp.concatenate([times, own_lanes(q_ref[i], heads)], axis=1)
-            add(accv_ref, j, dot(weights.pop(t - 2), da), i == j)
-            add(acck_ref, j, dot(low, q), i == j)
+            add(accv_ref, j, dot(weights.pop(t - 2), da), i == nb - 1)
+            add(acck_ref, j, dot(low, q), i == nb - 1)
             more = dot(kxt_ref[j, NTB:], low)
             dq = more if j == 0 else dq + more
             if i == j:
-                gpq_ref[i] = own_rows(dq, heads)
-    m2 = None
-    for j in range(nb):
-        part = acck_ref[j, :, :NTB]
-        high = part.astype(bf16)
-        rest = (part - high.astype(f32)).astype(bf16)
-        onehot = kxt_ref[j, :NTB]
-        part = dot(onehot, high) + dot(onehot, rest)
-        m2 = part if j == 0 else m2 + part
-    acc_ref[...] = jnp.zeros_like(acc_ref)
-
-    def tail(i, _):
-        gp = jnp.concatenate([flip(accv_ref[i]), gpq_ref[i] * factor, flip(acck_ref[i, :, NTB:]) * factor], axis=0)
-        gp = (gp * d_ref[i]).astype(bf16)
-        gp_ref[i] = flip(gp).astype(bf16)
-        acc_ref[...] += dot(gp, xn_ref[i])
-        return 0
-
-    lax.fori_loop(0, nb, tail, 0)
-    small_ref[...] = jnp.zeros_like(small_ref)
-    small_ref[:, :D] = gb_ref[...]
-    for d in range(nb):
-        g = diagonals(posg_ref[d])
-        small_ref[:, D + d * TILE : D + (d + 1) * TILE] += g[:, :TILE]
-        if d > 0:
-            small_ref[:, D + (d - 1) * TILE : D + d * TILE] += g[:, TILE:]
+                gp = jnp.concatenate(
+                    [flip(accv_ref[i]), own_rows(dq, heads) * factor, flip(acck_ref[i, :, NTB:]) * factor], axis=0
+                )
+                gp = (gp * d_ref[i]).astype(bf16)
+                gp_ref[i] = flip(gp).astype(bf16)
+                more = dot(gp, xn_ref[i])
+                acc_ref[...] = more if i == nb - 1 else acc_ref[...] + more
+                part = acck_ref[i, :, :NTB]
+                high = part.astype(bf16)
+                rest = (part - high.astype(f32)).astype(bf16)
+                onehot = kxt_ref[i, :NTB]
+                part = dot(onehot, high) + dot(onehot, rest)
+                m2 = part if i == nb - 1 else m2 + part
+                g = diagonals(posg_ref[i])
+                small_ref[:, D + i * TILE : D + (i + 1) * TILE] += g[:, :TILE]
+                if i > 0:
+                    small_ref[:, D + (i - 1) * TILE : D + i * TILE] += g[:, TILE:]
     g = diagonals(m2 + jnp.transpose(m2))[:, :NTB]
     zero = lax.broadcasted_iota(jnp.int32, (1, NTB), 1) == 0
     at = D + nb * TILE
@@ -477,6 +519,13 @@
         out[...] = total.astype(out.dtype)
 
 
+def sum_kernel(*refs):
+    total = refs[0][...]
+    for ref in refs[1:-1]:
+        total = total + ref[...].astype(f32)
+    refs[-1][...] = total
+
+
 def mix_kernel(tokens_ref, bias_ref, *refs):
     total = tokens_ref[...].astype(f32) + row_lanes(bias_ref, 0, D // 128)
     for ref in refs[:-1]:
@@ -508,12 +557,11 @@
 
 
 def collect_kernel(high, extra, *refs):
-    late_blocks, early_blocks, (grads_ref, message_ref) = refs[:high], refs[high : 2 * high], refs[2 * high :]
+    late_blocks, (early_ref, grads_ref, message_ref) = refs[:high], refs[high:]
     rows = grads_ref.shape[0]
-    total, early = late_blocks[0][...], early_blocks[0][...]
+    total, early = late_blocks[0][...], early_ref[...]
     for k in range(1, high):
         total = total + late_blocks[k][...].astype(f32)
-        early = early + early_blocks[k][...].astype(f32)
     grads = jnp.concatenate([total[:rows], early], axis=1)
     grads_ref[...] = grads
     squares = jnp.sum(jnp.sum(grads * grads, axis=0, keepdims=True), axis=1, keepdims=True)
@@ -624,7 +672,16 @@
     high, low = split_dp(n_dp)
 
     (weights,) = call(
-        cast_kernel, "cast", [VMEM] * 2, [((rows_here, 5 * width), bf16, VMEM)], [], 1
+        cast_kernel,
+        "cast",
+        [pl.BlockSpec(memory_space=pl.ANY)] * 2,
+        [((rows_here, 5 * width), bf16, VMEM)],
+        [
+            pltpu.VMEM(proj_weight.shape, f32),
+            pltpu.VMEM((rows_here, width), f32),
+            pltpu.SemaphoreType.DMA((2,)),
+        ],
+        1,
     )(proj_weight, out_weight.T)
     x_pieces = gather_cores(tokens, gather_chips(after(tokens, weights)))
     w_pieces, offsets, operands = gather_dp(weights)
@@ -657,6 +714,7 @@
         ((nb, width, TILE), bf16),
     ]
     (xn,) = call(normalize_kernel, "normalize", [VMEM] * n_head, [((nb, TILE, D), bf16, VMEM)], [], 1)(*x_pieces)
+    w_pieces[-1] = after(join(w_pieces[-1:], 4), xn)
     (wt,) = call(
         functools.partial(assemble_kernel, offsets),
         "assemble",
@@ -702,12 +760,17 @@
     )(*cot_pieces, attn, xn, wt)
 
     stats = [stat] + [swap(stat, "head", k) for k in range(1, n_head)]
-    out = call(
+    chips = n_head // 2
+    split_shape = ((chips, here, D), bf16, VMEM)
+    keep, send = call(
+        functools.partial(branch_kernel, n_head), "branch", [VMEM] * (n_head + 3), [split_shape] * 2, [], 1
+    )(*stats, attn, p_gate, wt)
+    crossed = swap(send, "head", 1)
+    da, dat, gun, *early_parts = call(
         functools.partial(middle_kernel, n_head),
         "middle",
-        [VMEM] * (2 * n_head + 5),
-        [((here, D), bf16, VMEM)] * n_head
-        + [
+        [VMEM] * (2 * n_head + 4),
+        [
             ((nb, TILE, width), bf16, VMEM),
             ((nb, width, TILE), bf16, VMEM),
             ((nb, TILE, width), bf16, VMEM),
@@ -715,9 +778,9 @@
         + [((high, rows_here, 2 * width), bf16, VMEM)] * low,
         [pltpu.VMEM((2 * width, D), f32), pltpu.VMEM((D, 2 * width), f32)],
         6,
-    )(*stats, *cot_pieces, attn, p_gate, gg, xn, wt)
-    branches, (da, dat, gun), early_parts = out[:n_head], out[n_head : n_head + 3], out[n_head + 3 :]
-    received = [swap(branches[k], "head", k) for k in range(1, n_head)]
+    )(*stats, *cot_pieces, attn, p_gate, gg, xn)
+    branch, *leaving = fold_cores(keep, crossed)
+    received = [swap(sent, "head", 2 * (k + 1)) for k, sent in enumerate(leaving)]
     early_received = [swap(early_parts[k], "dp", k) for k in range(1, low)]
 
     length = D + group + NTB
@@ -731,7 +794,6 @@
             pltpu.VMEM((nb, TILE, width), f32),
             pltpu.VMEM((nb, TILE, NTB + width), f32),
             pltpu.VMEM((nb, TILE, TILE), f32),
-            pltpu.VMEM((nb, width, TILE), f32),
             pltpu.VMEM((3 * width, D), f32),
             pltpu.VMEM((n_dp * (rows_here + 16), 3 * width), f32),
             pltpu.VMEM((1, extra * n_dp * 128), f32),
@@ -740,9 +802,9 @@
         ROOM,
     )(kx, kxt, qs, trow, q, v, da, dat, pos, dsilu, xn, starts, gb)
 
-    tied = lax.optimization_barrier((gp, *late_parts, *received, *early_received))
+    tied = lax.optimization_barrier((gp, *late_parts, *early_received, *received))
     gp, late_parts = tied[0], tied[1 : 1 + low]
-    received, early_received = tied[1 + low : low + n_head], tied[low + n_head :]
+    early_received, received = tied[1 + low : 2 * low], tied[2 * low :]
     late_received = [swap(late_parts[k], "dp", k) for k in range(1, low)]
     keep, send = call(
         functools.partial(input_kernel, n_head),
@@ -753,35 +815,29 @@
         4,
     )(gp, gun, wt)
     early_blocks = scatter_high(after(early_parts[0], send), early_received, 1)
-    late_received = after_all(late_received, send)
-    late_blocks = scatter_high(late_parts[0], late_received, 6)
-    late_blocks[0] = after(late_blocks[0], *early_blocks)
-    chips = n_head // 2
-    crossed = swap(after(send, late_blocks[0]), "head", 1)
-    mine, *leaving = call(
-        functools.partial(rows_kernel, chips),
-        "rows",
-        [VMEM] * 2,
-        [((here, D), f32, VMEM)] + [((here, D), bf16, VMEM)] * (chips - 1),
-        [],
-        0.1,
-    )(keep, crossed)
+    crossed = swap(send, "head", 1)
+    late_received = after_all(late_received, send, crossed)
+    late_blocks = scatter_high(late_parts[0], late_received, 0.1)
+    (early,) = call(
+        sum_kernel, "sum", [VMEM] * high, [((rows_here, 2 * width), f32, VMEM)], [], 14
+    )(*early_blocks)
+    mine, *leaving = fold_cores(keep, after(crossed, late_blocks[0]))
     arrived = [swap(leaving[k - 1], "head", 2 * k) for k in range(1, chips)]
     n_all = n_dp * n_head
     grads_shape = ((rows_here, 5 * width), f32)
     grads, message = call(
         functools.partial(collect_kernel, high, extra),
         "collect",
-        [VMEM] * (2 * high),
+        [VMEM] * (high + 1),
         [grads_shape + (VMEM,), ((n_all, 8, 128), f32, VMEM)],
         [],
         10,
-    )(*late_blocks, *early_blocks)
+    )(*late_blocks, early)
     message = after(message, *leaving)
     heard = lax.all_to_all(message, ("dp", "head"), 0, 0, tiled=True)
     (mixed,) = call(
-        mix_kernel, "mix", [VMEM] * (2 + n_head), [((here, D), bf16, VMEM)], [], 1
-    )(after(tokens, message), small_rows, branches[0], *received)
+        mix_kernel, "mix", [VMEM] * (2 + chips), [((here, D), bf16, VMEM)], [], 1
+    )(after(tokens, message), small_rows, branch, *received)
     (input_grad,) = call(
         finish_kernel, "finish", [VMEM] * (2 + chips), [((here, D), f32, VMEM)], [], 1
     )(after(tokens, mixed), cotangent, mine, *arrived)

time: 109 us -> 102 us (0.936)
  waiting for transfers between devices: 26.9 us -> 20.1 us
  starting transfers between devices: 30.6 us -> 31.8 us
    ppermute x25 -> x24, waiting for transfers between devices: 26.9 us -> 20.1 us  [swap(): return lax.ppermute(x, axis, [(i, i ^ k) for i in range(n)])]
    ppermute x25 -> x24, starting transfers between devices: 26.2 us -> 28.7 us  [swap(): return lax.ppermute(x, axis, [(i, i ^ k) for i in range(n)])]
    all_to_all x1, starting transfers between devices: 4.37 us -> 3.14 us  [shards(): heard = lax.all_to_all(message, ('dp', 'head'), 0, 0, tiled=True)]
    pallas_call x1, Pallas kernels: 19.8 us -> 18.5 us  [shards(): call(functools.partial(backward_kernel, heads, n_dp, extra), 'backward',...]
    pallas_call x3 -> x9, Pallas kernels: 2.27 us -> 3.43 us  [the longest x2 1.19 us: fold_cores(): call(functools.partial(rows_kernel, chips), 'rows', [VMEM] * 2, [((rows,...]
    unnamed x42 -> x36, local copies, waits for them, and re-layouts: 4.91 us -> 3.86 us
  transfers between devices with their start and end apart: 26 -> 25, of which waited for: 11 -> 9; matrix products, arithmetic and copies ran while one was open for 0% -> 0% of each run, Pallas kernels for 36% -> 38%
where the time goes in v5:
time: 102 us
  Pallas kernels  44.9 us (44%)
  starting transfers between devices  31.8 us (31%)
  waiting for transfers between devices  20.1 us (20%)
  local copies, waits for them, and re-layouts  3.86 us (4%)
  between operations  1.11 us (1%)
    ppermute x24, starting transfers between devices, swap(): return lax.ppermute(x, axis, [(i, i ^ k) for i in range(n)])  28.7 us
    ppermute x24, waiting for transfers between devices, swap(): return lax.ppermute(x, axis, [(i, i ^ k) for i in range(n)])  20.1 us
    pallas_call x1, Pallas kernels, shards(): call(functools.partial(backward_kernel, heads, n_dp, extra), 'backward',...  18.5 us
    pallas_call x2, Pallas kernels, attend(): call(functools.partial(attend_kernel, heads, first, last), 'attend', [VME...  6.66 us
    unnamed x36, local copies, waits for them, and re-layouts  3.86 us
    all_to_all x1, starting transfers between devices, shards(): heard = lax.all_to_all(message, ('dp', 'head'), 0, 0, tiled=True)  3.14 us
    pallas_call x1, Pallas kernels, shards(): call(finish_kernel, 'finish', [VMEM] * (2 + chips), [((here, D), f32, VME...  2.74 us
    pallas_call x1, Pallas kernels, shards(): call(prepare_kernel, 'prepare', [VMEM] * 2, [((nb, TILE, TILE), f32, VMEM...  2.49 us
  transfers between devices with their start and end apart: 25, of which 9 were waited for; matrix products, arithmetic and copies ran while one was open for 0% of the time, Pallas kernels for 38%

profile of v5, /device:TPU:0, one launch (start us, length us, event | category | flops | bytes accessed | tf_op | source)
XLA Modules:
  0.0 101.8 jit_solution(12213698069470289784)
XLA Ops:
  0.7 0.0 copy-start.1
  0.7 1.0 copy-done.1
  1.6 0.8 copy-done.8
  2.4 0.3 cast.1.refs_0_
  2.7 0.0 copy-start.12
  2.7 4.1 %collective-permute-start.3 = (bf16[64,640]{1,0:T(8,128)(2,1)S(1)}, bf16[64,640]{1,0:T(8,128)(2,1)S(1)}, u32[]{:S(2)}, u32[]{:S(2)}) collective-permute-start(bf16[64,640]{1,0:T(8,128)(2,1)S(1)} %cast.1.refs_0_), channel_id=1, source_target_pairs={{0,16},{4,20},{8,24},{12,28},{16,0},{20,4},{24,8},{28,12},{1,17},{... | collective-permute-start | bytes 245768 | tf_op jit(solution)/shard_map/ppermute | solution.py:49
  6.8 1.5 %collective-permute-start.1 = (bf16[512,512]{1,0:T(8,128)(2,1)S(1)}, bf16[512,512]{1,0:T(8,128)(2,1)S(1)}, u32[]{:S(2)}, u32[]{:S(2)}) collective-permute-start(bf16[512,512]{1,0:T(8,128)(2,1)S(1)} %copy-done), channel_id=1, source_target_pairs={{0,2},{1,3},{2,0},{3,1},{4,6},{5,7},{6,4},{7,5},{8,10},{9,11},{10,... | collective-permute-start | bytes 1572872 | tf_op jit(solution)/shard_map/ppermute | solution.py:49
  8.3 2.7 %collective-permute-done.3.refs_1_ = bf16[64,640]{1,0:T(8,128)(2,1)S(1)} collective-permute-done((bf16[64,640]{1,0:T(8,128)(2,1)S(1)}, bf16[64,640]{1,0:T(8,128)(2,1)S(1)}, u32[]{:S(2)}, u32[]{:S(2)}) %collective-permute-start.3) | collective-permute-done | bytes 81952 | tf_op jit(solution)/shard_map/ppermute | solution.py:49
  11.0 0.8 collective-permute-start.4
  11.8 0.5 collective-permute-start.6
  12.3 1.5 %collective-permute-start.7 = (bf16[512,512]{1,0:T(8,128)(2,1)S(1)}, bf16[512,512]{1,0:T(8,128)(2,1)S(1)}, u32[]{:S(2)}, u32[]{:S(2)}) collective-permute-start(bf16[512,512]{1,0:T(8,128)(2,1)S(1)} %copy-done.12), channel_id=1, source_target_pairs={{0,2},{1,3},{2,0},{3,1},{4,6},{5,7},{6,4},{7,5},{8,10},{9,11},{10,... | collective-permute-start | bytes 1572872 | tf_op jit(solution)/shard_map/ppermute | solution.py:49
  13.8 2.6 %collective-permute-done.4.refs_2_ = bf16[128,640]{1,0:T(8,128)(2,1)S(1)} collective-permute-done((bf16[128,640]{1,0:T(8,128)(2,1)S(1)}, bf16[128,640]{1,0:T(8,128)(2,1)S(1)}, u32[]{:S(2)}, u32[]{:S(2)}) %collective-permute-start.4) | collective-permute-done | bytes 163872 | tf_op jit(solution)/shard_map/ppermute | solution.py:49
  16.5 1.8 %collective-permute-start.5 = (bf16[256,640]{1,0:T(8,128)(2,1)S(1)}, bf16[256,640]{1,0:T(8,128)(2,1)S(1)}, u32[]{:S(2)}, u32[]{:S(2)}) collective-permute-start(bf16[256,640]{1,0:T(8,128)(2,1)S(1)} %join.4), channel_id=1, source_target_pairs={{0,4},{4,0},{8,12},{12,8},{16,20},{20,16},{24,28},{28,24},{1,5},{5... | collective-permute-start | bytes 983048 | tf_op jit(solution)/shard_map/ppermute | solution.py:49
  18.2 3.4 %collective-permute-done.1.refs_2_ = bf16[512,512]{1,0:T(8,128)(2,1)S(1)} collective-permute-done((bf16[512,512]{1,0:T(8,128)(2,1)S(1)}, bf16[512,512]{1,0:T(8,128)(2,1)S(1)}, u32[]{:S(2)}, u32[]{:S(2)}) %collective-permute-start.1) | collective-permute-done | bytes 524320 | tf_op jit(solution)/shard_map/ppermute | solution.py:49
  21.7 2.5 %prepare.1 = (f32[8,256,256]{2,1,0:T(8,128)S(1)}, bf16[8,256,128]{2,1,0:T(8,128)(2,1)S(1)}, bf16[8,128,256]{2,1,0:T(8,128)(2,1)S(1)}, bf16[8,128,256]{2,1,0:T(8,128)(2,1)S(1)}) custom-call(s32[1,2048]{1,0:T(1,128)S(1)} %bitcast.26, f32[69,128]{1,0:T(8,128)S(1)} %bitcast.17), custom_call_target="tpu_custom_call" | custom-call | flops 5000000000 | bytes 15000000 | tf_op jit(solution)/shard_map/prepare/pallas_call | solution.py:693
  24.3 1.3 %normalize.1.refs_0_.refs_5_.refs_11_.refs_10_ = bf16[8,256,512]{2,1,0:T(8,128)(2,1)S(1)} custom-call(bf16[512,512]{1,0:T(8,128)(2,1)S(1)} %copy-done, bf16[512,512]{1,0:T(8,128)(2,1)S(1)} %collective-permute-done.refs_1_, bf16[512,512]{1,0:T(8,128)(2,1)S(1)} %collective-permute-done.1.refs_2_, bf16[512,512]{1,0:T(8,128)(2,1)S(1)} %collective-permute-done.2.refs_3_), custom_call_target="tpu_custom_call" | custom-call | flops 1000000000 | bytes 3000000 | tf_op jit(solution)/shard_map/normalize/pallas_call | solution.py:716
  25.5 0.3 assemble.1.refs_1_.refs_6_.wt_ref
  25.9 0.0 copy-start.17
  25.9 1.8 %project.1 = (bf16[8,384,256]{2,1,0:T(8,128)(2,1)S(1)}, bf16[8,256,256]{2,1,0:T(8,128)(2,1)S(1)}, bf16[8,256,256]{2,1,0:T(8,128)(2,1)S(1)}, bf16[8,128,256]{2,1,...) custom-call(bf16[8,256,512]{2,1,0:T(8,128)(2,1)S(1)} %normalize.1.re, ...), custom_call_target="tpu_custom_call" | custom-call | flops 5000000000 | bytes 15000000 | tf_op jit(solution)/shard_map/project/pallas_call | solution.py:726
  27.7 3.9 %attend.2.refs_0_ = f32[6,128,256]{2,1,0:T(8,128)S(1)} custom-call(bf16[8,256,256]{2,1,0:T(8,128)(2,1)S(1)} %get-tuple-element.92.refs_0_.refs_1_, bf16[8,128,256]{2,1,0:T(8,128)(2,1)S(1)} %get-tuple-element.94.refs_1_.refs_2_, bf16[8,128,256]{2,1,0:T(8,128)(2,1)S(1)} %get-tuple-element.95.refs_2_.refs_3_, ...), custom_call_target="tpu_custom_call" | custom-call | flops 8000000000 | bytes 24000000 | tf_op jit(solution)/shard_map/attend/pallas_call | solution.py:736
  31.6 0.6 collective-permute-start.8
  32.2 2.8 %attend.3.refs_4_.refs_8_ = f32[8,128,256]{2,1,0:T(8,128)S(1)} custom-call(f32[6,128,256]{2,1,0:T(8,128)S(1)} %attend.2.refs_0_, bf16[8,256,256]{2,1,0:T(8,128)(2,1)S(1)} %get-tuple-element.92.refs_0_.refs_1_, bf16[8,128,256]{2,1,0:T(8,128)(2,1)S(1)} %get-tuple-element.94.refs_1_.refs_2_, bf16[8,128,256]{2,1,0:T(8,128)(2,1)S(1)} %get-tuple-element.95.refs_2_.refs_3_, ...), custom_call_target="tpu_custom_call" | custom-call | flops 8000000000 | bytes 24000000 | tf_op jit(solution)/shard_map/attend/pallas_call | solution.py:736
  35.0 1.6 %gate.1 = (f32[8,128,256]{2,1,0:T(8,128)S(1)}, f32[8,128,256]{2,1,0:T(8,128)S(1)}, f32[8,4,256]{2,1,0:T(4,128)S(1)}, f32[1,512]{1,0:T(1,128)S(1)}) custom-call(bf16[512,512]{1,0:T(8,128)(2,1)S(1)} %copy-done.12, bf16[512,512]{1,0:T(8,128)(2,1)S(1)} %collective-permute-done.6.refs_1_.refs_5_, bf16[512,512]{1,0:T(8,128)(2,1)S(1)} %collective-permute-done.7.refs_2_.refs_6_, ...), custom_call_target="tpu_custom_call" | custom-call | flops 5000000000 | bytes 15000000 | tf_op jit(solution)/shard_map/gate/pallas_call | solution.py:753
  36.6 1.2 %collective-permute-start.11 = (f32[8,4,256]{2,1,0:T(4,128)S(1)}, f32[8,4,256]{2,1,0:T(4,128)S(1)}, u32[]{:S(2)}, u32[]{:S(2)}) collective-permute-start(f32[8,4,256]{2,1,0:T(4,128)S(1)} %get-tuple-element.103.refs_0_), channel_id=1, source_target_pairs={{0,3},{1,2},{2,1},{3,0},{4,7},{5,6},{6,5},{7,4},{8,11},{9,10},{10,... | collective-permute-start | bytes 98312 | tf_op jit(solution)/shard_map/ppermute | solution.py:49
  37.8 0.5 collective-permute-start.10
  38.3 0.2 collective-permute-start.9
  38.5 1.6 %collective-permute-done.11.refs_3_ = f32[8,4,256]{2,1,0:T(4,128)S(1)} collective-permute-done((f32[8,4,256]{2,1,0:T(4,128)S(1)}, f32[8,4,256]{2,1,0:T(4,128)S(1)}, u32[]{:S(2)}, u32[]{:S(2)}) %collective-permute-start.11) | collective-permute-done | bytes 32800 | tf_op jit(solution)/shard_map/ppermute | solution.py:49
  40.2 1.5 %collective-permute-done.10.refs_2_ = f32[8,4,256]{2,1,0:T(4,128)S(1)} collective-permute-done((f32[8,4,256]{2,1,0:T(4,128)S(1)}, f32[8,4,256]{2,1,0:T(4,128)S(1)}, u32[]{:S(2)}, u32[]{:S(2)}) %collective-permute-start.10) | collective-permute-done | bytes 32800 | tf_op jit(solution)/shard_map/ppermute | solution.py:49
  41.7 0.8 branch.1
  42.5 0.1 collective-permute-start.13
  42.6 1.7 %middle.1 = (bf16[8,256,128]{2,1,0:T(8,128)(2,1)S(1)}, bf16[8,128,256]{2,1,0:T(8,128)(2,1)S(1)}, bf16[8,256,128]{2,1,0:T(8,128)(2,1)S(1)}, bf16[4,64,256]{2,1,0:T(8,128)(2,1)S(1)}, bf16[4,64,256]{2,1,0:T(8,128)(2,1)S(1)}) custom-call(f32[8,4,256]{2,1,0:T(4,128)S(1)} %get-tuple-element.103.refs_0_, f32[8,4,256]{2,1,0:T(4,128)S(1)} %collective-permute-done.9.refs_1_, ...), custom_call_target="tpu_custom_call" | custom-call | flops 6000000000 | bytes 18000000 | tf_op jit(solution)/shard_map/middle/pallas_call | solution.py:769
  44.3 1.6 %collective-permute-start.12 = (bf16[4,64,256]{2,1,0:T(8,128)(2,1)S(1)}, bf16[4,64,256]{2,1,0:T(8,128)(2,1)S(1)}, u32[]{:S(2)}, u32[]{:S(2)}) collective-permute-start(bf16[4,64,256]{2,1,0:T(8,128)(2,1)S(1)} %get-tuple-element.113), channel_id=1, source_target_pairs={{0,4},{4,0},{8,12},{12,8},{16,20},{20,16},{24,28},{28,24},{1,5},{5... | collective-permute-start | bytes 393224 | tf_op jit(solution)/shard_map/ppermute | solution.py:49
  45.9 0.2 rows.2
  46.1 0.9 collective-permute-start.14
  47.0 18.5 %backward.1 = (bf16[8,256,384]{2,1,0:T(8,128)(2,1)S(1)}, bf16[4,80,384]{2,1,0:T(8,128)(2,1)S(1)}, bf16[4,80,384]{2,1,0:T(8,128)(2,1)S(1)}) custom-call(bf16[8,256,256]{2,1,0:T(8,128)(2,1)S(1)} %get-tuple-element.92.refs_0_.refs_1_, bf16[8,256,256]{2,1,0:T(8,128)(2,1)S(1)} %get-tuple-element.93.refs_1_, ...), custom_call_target="tpu_custom_call" | custom-call | flops 35000000512 | bytes 105000000 | tf_op jit(solution)/shard_map/backward/pallas_call | solution.py:788
  65.6 0.0 copy-start.14
  65.6 1.8 %input_rows.1 = (bf16[2,512,512]{2,1,0:T(8,128)(2,1)S(1)}, bf16[2,512,512]{2,1,0:T(8,128)(2,1)S(1)}) custom-call(bf16[8,256,384]{2,1,0:T(8,128)(2,1)S(1)} %get-tuple-element.119.gp_ref, bf16[8,256,128]{2,1,0:T(8,128)(2,1)S(1)} %get-tuple-element.120.gun_ref, bf16[640,512]{1,0:T(8,128)(2,1)S(1)} %assemble.1.refs_1_.refs_6_.wt_ref), custom_call_target="tpu_custom_call" | custom-call | flops 4000000000 | bytes 12000000 | tf_op jit(solution)/shard_map/input_rows/pallas_call | solution.py:809
  67.4 0.1 collective-permute-start.16
  67.5 1.0 collective-permute-start.15
  68.5 2.0 %collective-permute-start.20 = (bf16[64,256]{1,0:T(8,128)(2,1)S(1)}, bf16[64,256]{1,0:T(8,128)(2,1)S(1)}, u32[]{:S(2)}, u32[]{:S(2)}) collective-permute-start(bf16[64,256]{1,0:T(8,128)(2,1)S(1)} %get-tuple-element.131), channel_id=1, source_target_pairs={{0,8},{4,12},{8,0},{12,4},{16,24},{20,28},{24,16},{28,20},{1,9},{5... | collective-permute-start | bytes 98312 | tf_op jit(solution)/shard_map/ppermute | solution.py:49
  70.5 3.4 %collective-permute-start.21 = (bf16[64,256]{1,0:T(8,128)(2,1)S(1)}, bf16[64,256]{1,0:T(8,128)(2,1)S(1)}, u32[]{:S(2)}, u32[]{:S(2)}) collective-permute-start(bf16[64,256]{1,0:T(8,128)(2,1)S(1)} %get-tuple-element.132), channel_id=1, source_target_pairs={{0,16},{4,20},{8,24},{12,28},{16,0},{20,4},{24,8},{28,12},{1,17},{... | collective-permute-start | bytes 98312 | tf_op jit(solution)/shard_map/ppermute | solution.py:49
  73.9 0.0 collective-permute-start.22
  73.9 1.9 %collective-permute-done.15.refs_1_ = bf16[4,80,384]{2,1,0:T(8,128)(2,1)S(1)} collective-permute-done((bf16[4,80,384]{2,1,0:T(8,128)(2,1)S(1)}, bf16[4,80,384]{2,1,0:T(8,128)(2,1)S(1)}, u32[]{:S(2)}, u32[]{:S(2)}) %collective-permute-start.15) | collective-permute-done | bytes 245792 | tf_op jit(solution)/shard_map/ppermute | solution.py:49
  75.8 0.1 fold.2
  75.9 2.0 %collective-permute-start.17 = (bf16[80,384]{1,0:T(8,128)(2,1)S(1)}, bf16[80,384]{1,0:T(8,128)(2,1)S(1)}, u32[]{:S(2)}, u32[]{:S(2)}) collective-permute-start(bf16[80,384]{1,0:T(8,128)(2,1)S(1)} %get-tuple-element.124), channel_id=1, source_target_pairs={{0,8},{4,12},{8,0},{12,4},{16,24},{20,28},{24,16},{28,20},{1,9},{5... | collective-permute-start | bytes 184328 | tf_op jit(solution)/shard_map/ppermute | solution.py:49
  77.9 3.4 %collective-permute-start.18 = (bf16[80,384]{1,0:T(8,128)(2,1)S(1)}, bf16[80,384]{1,0:T(8,128)(2,1)S(1)}, u32[]{:S(2)}, u32[]{:S(2)}) collective-permute-start(bf16[80,384]{1,0:T(8,128)(2,1)S(1)} %get-tuple-element.125), channel_id=1, source_target_pairs={{0,16},{4,20},{8,24},{12,28},{16,0},{20,4},{24,8},{28,12},{1,17},{... | collective-permute-start | bytes 184328 | tf_op jit(solution)/shard_map/ppermute | solution.py:49
  81.3 0.0 collective-permute-start.19
  81.4 1.0 rows.3
  82.4 1.5 %collective-permute-start.23 = (bf16[512,512]{1,0:T(8,128)(2,1)}, bf16[512,512]{1,0:T(8,128)(2,1)}, u32[]{:S(2)}, u32[]{:S(2)}) collective-permute-start(bf16[512,512]{1,0:T(8,128)(2,1)} %get-tuple-element.137), channel_id=1, source_target_pairs={{0,2},{1,3},{2,0},{3,1},{4,6},{5,7},{6,4},{7,5},{8,10},{9,11},{10,... | collective-permute-start | bytes 1572872 | tf_op jit(solution)/shard_map/ppermute | solution.py:49
  83.8 0.9 collective-permute-done.18.refs_2_
  84.7 2.6 %collective-permute-done.19.refs_3_ = bf16[80,384]{1,0:T(8,128)(2,1)S(1)} collective-permute-done((bf16[80,384]{1,0:T(8,128)(2,1)S(1)}, bf16[80,384]{1,0:T(8,128)(2,1)S(1)}, u32[]{:S(2)}, u32[]{:S(2)}) %collective-permute-start.19) | collective-permute-done | bytes 61472 | tf_op jit(solution)/shard_map/ppermute | solution.py:49
  87.3 0.8 collect.1
  88.1 3.1 %all-to-all-start = ((f32[32,8,128]{2,1,0:T(8,128)}), f32[32,8,128]{2,1,0:T(8,128)S(1)}, u32[]{:S(2)}, u32[]{:S(2)}) async-start(f32[32,8,128]{2,1,0:T(8,128)} %get-tuple-element.138), calls=%async_computation | async-start | bytes 262144 | tf_op jit(solution)/shard_map/all_to_all | solution.py:837
  91.3 0.0 copy-start.15
  91.3 1.0 %copy-done.15 = bf16[512,512]{1,0:T(8,128)(2,1)S(1)} copy-done((bf16[512,512]{1,0:T(8,128)(2,1)S(1)}, bf16[512,512]{1,0:T(8,128)(2,1)}, u32[]{:S(2)}) %copy-start.15) | copy-done | bytes 524312
  92.3 1.0 mix.1
  93.3 0.0 copy-start.7
  93.4 0.0 copy-start.9
  93.4 0.0 copy-start.10
  93.4 0.0 copy-start.11
  93.4 2.7 %collective-permute-done.23.refs_0_ = bf16[512,512]{1,0:T(8,128)(2,1)} collective-permute-done((bf16[512,512]{1,0:T(8,128)(2,1)}, bf16[512,512]{1,0:T(8,128)(2,1)}, u32[]{:S(2)}, u32[]{:S(2)}) %collective-permute-start.23) | collective-permute-done | bytes 524320 | tf_op jit(solution)/shard_map/ppermute | solution.py:49
  96.1 1.0 %copy-done.13 = bf16[512,512]{1,0:T(8,128)(2,1)S(1)} copy-done((bf16[512,512]{1,0:T(8,128)(2,1)S(1)}, bf16[512,512]{1,0:T(8,128)(2,1)}, u32[]{:S(2)}) %copy-start.13) | copy-done | bytes 524312
  97.2 2.7 %finish.1 = f32[512,512]{1,0:T(8,128)} custom-call(bf16[512,512]{1,0:T(8,128)(2,1)S(1)} %copy-done, bf16[512,512]{1,0:T(8,128)(2,1)S(1)} %copy-done.13, f32[512,512]{1,0:T(8,128)S(1)} %get-tuple-element.143.mine_ref, bf16[512,512]{1,0:T(8,128)(2,1)} %collective-permute-done.23.refs_0_), custom_call_target="tpu_custom_call" | custom-call | flops 1000000000 | bytes 3000000 | tf_op jit(solution)/shard_map/finish/pallas_call | solution.py:841
  100.0 1.7 %update.1 = (f32[64,4,128]{2,1,0:T(4,128)}, f32[64,128]{1,0:T(8,128)}, f32[69,128]{1,0:T(8,128)}, f32[1,1]{1,0:T(1,128)}, f32[64,4,128]{2,1,0:T(4,128)}, /*index...) custom-call(f32[32,8,128]{2,1,0:T(8,128)S(1)} %all-to-all-done.heard, ...), custom_call_target="tpu_custom_call" | custom-call | flops 100000000 | bytes 300000 | tf_op jit(solution)/shard_map/update/pallas_call | solution.py:849
  (46 shorter events, 0.2 us)
Async XLA Ops:
  0.6 6.2 %copy-start = (bf16[512,512]{1,0:T(8,128)(2,1)S(1)}, bf16[512,512]{1,0:T(8,128)(2,1)}, u32[]{:S(2)}) copy-start(bf16[512,512]{1,0:T(8,128)(2,1)} %tokens_ref.1) | copy-start | bytes 1572868
  0.7 1.0 copy-start.1
  1.6 0.8 copy-start.8
  2.7 9.1 %copy-start.12 = (bf16[512,512]{1,0:T(8,128)(2,1)S(1)}, bf16[512,512]{1,0:T(8,128)(2,1)}, u32[]{:S(2)}) copy-start(bf16[512,512]{1,0:T(8,128)(2,1)} %cot_ref.1) | copy-start | bytes 1572868
  2.7 8.3 %collective-permute-start.3 = (bf16[64,640]{1,0:T(8,128)(2,1)S(1)}, bf16[64,640]{1,0:T(8,128)(2,1)S(1)}, u32[]{:S(2)}, u32[]{:S(2)}) collective-permute-start(bf16[64,640]{1,0:T(8,128)(2,1)S(1)} %cast.1.refs_0_), channel_id=1, source_target_pairs={{0,16},{4,20},{8,24},{12,28},{16,0},{20,4},{24,8},{28,12},{1,17},{... | collective-permute-start | bytes 245768 | tf_op jit(solution)/shard_map/ppermute | solution.py:49
  6.8 14.8 %collective-permute-start.1 = (bf16[512,512]{1,0:T(8,128)(2,1)S(1)}, bf16[512,512]{1,0:T(8,128)(2,1)S(1)}, u32[]{:S(2)}, u32[]{:S(2)}) collective-permute-start(bf16[512,512]{1,0:T(8,128)(2,1)S(1)} %copy-done), channel_id=1, source_target_pairs={{0,2},{1,3},{2,0},{3,1},{4,6},{5,7},{6,4},{7,5},{8,10},{9,11},{10,... | collective-permute-start | bytes 1572872 | tf_op jit(solution)/shard_map/ppermute | solution.py:49
  11.0 5.4 %collective-permute-start.4 = (bf16[128,640]{1,0:T(8,128)(2,1)S(1)}, bf16[128,640]{1,0:T(8,128)(2,1)S(1)}, u32[]{:S(2)}, u32[]{:S(2)}) collective-permute-start(bf16[128,640]{1,0:T(8,128)(2,1)S(1)} %join.3), channel_id=1, source_target_pairs={{0,8},{4,12},{8,0},{12,4},{16,24},{20,28},{24,16},{28,20},{1,9},{5... | collective-permute-start | bytes 491528 | tf_op jit(solution)/shard_map/ppermute | solution.py:49
  11.8 12.4 %collective-permute-start = (bf16[512,512]{1,0:T(8,128)(2,1)S(1)}, bf16[512,512]{1,0:T(8,128)(2,1)S(1)}, u32[]{:S(2)}, u32[]{:S(2)}) collective-permute-start(bf16[512,512]{1,0:T(8,128)(2,1)S(1)} %copy-done), channel_id=1, source_target_pairs={{0,1},{1,0},{2,3},{3,2},{4,5},{5,4},{6,7},{7,6},{8,9},{9,8},{10,11... | collective-permute-start | bytes 1572872 | tf_op jit(solution)/shard_map/ppermute | solution.py:49
  11.8 23.1 %collective-permute-start.6 = (bf16[512,512]{1,0:T(8,128)(2,1)S(1)}, bf16[512,512]{1,0:T(8,128)(2,1)S(1)}, u32[]{:S(2)}, u32[]{:S(2)}) collective-permute-start(bf16[512,512]{1,0:T(8,128)(2,1)S(1)} %copy-done.12), channel_id=1, source_target_pairs={{0,1},{1,0},{2,3},{3,2},{4,5},{5,4},{6,7},{7,6},{8,9},{9,8},{10,11... | collective-permute-start | bytes 1572872 | tf_op jit(solution)/shard_map/ppermute | solution.py:49
  12.3 19.3 %collective-permute-start.7 = (bf16[512,512]{1,0:T(8,128)(2,1)S(1)}, bf16[512,512]{1,0:T(8,128)(2,1)S(1)}, u32[]{:S(2)}, u32[]{:S(2)}) collective-permute-start(bf16[512,512]{1,0:T(8,128)(2,1)S(1)} %copy-done.12), channel_id=1, source_target_pairs={{0,2},{1,3},{2,0},{3,1},{4,6},{5,7},{6,4},{7,5},{8,10},{9,11},{10,... | collective-permute-start | bytes 1572872 | tf_op jit(solution)/shard_map/ppermute | solution.py:49
  13.8 7.8 %copy-start.5 = (f32[8832]{0:T(1024)S(1)}, f32[8832]{0:T(1024)}, u32[]{:S(2)}) copy-start(f32[8832]{0:T(1024)} %param.19) | copy-start | bytes 105988
  13.8 7.8 %copy-start.16 = (s32[2048]{0:T(1024)S(1)}, s32[2048]{0:T(1024)}, u32[]{:S(2)}) copy-start(s32[2048]{0:T(1024)} %param.16) | copy-start | bytes 24580
  16.5 7.7 %collective-permute-start.5 = (bf16[256,640]{1,0:T(8,128)(2,1)S(1)}, bf16[256,640]{1,0:T(8,128)(2,1)S(1)}, u32[]{:S(2)}, u32[]{:S(2)}) collective-permute-start(bf16[256,640]{1,0:T(8,128)(2,1)S(1)} %join.4), channel_id=1, source_target_pairs={{0,4},{4,0},{8,12},{12,8},{16,20},{20,16},{24,28},{28,24},{1,5},{5... | collective-permute-start | bytes 983048 | tf_op jit(solution)/shard_map/ppermute | solution.py:49
  21.7 2.6 %collective-permute-start.2 = (bf16[512,512]{1,0:T(8,128)(2,1)S(1)}, bf16[512,512]{1,0:T(8,128)(2,1)S(1)}, u32[]{:S(2)}, u32[]{:S(2)}) collective-permute-start(bf16[512,512]{1,0:T(8,128)(2,1)S(1)} %collective-permute-done.1.refs_2_), channel_id=1, source_target_pairs={{0,1},{1,0},{2,3},{3,2},{4,5},{5,4},{6,7},{7,6},{8,9},{9,8},{10,11... | collective-permute-start | bytes 1572872 | tf_op jit(solution)/shard_map/ppermute | solution.py:49
  25.9 1.8 %copy-start.17 = (s32[2048]{0:T(1024)S(1)}, s32[2048]{0:T(1024)}, u32[]{:S(2)}) copy-start(s32[2048]{0:T(1024)} %param.15) | copy-start | bytes 24580
  31.6 3.4 %collective-permute-start.8 = (bf16[512,512]{1,0:T(8,128)(2,1)S(1)}, bf16[512,512]{1,0:T(8,128)(2,1)S(1)}, u32[]{:S(2)}, u32[]{:S(2)}) collective-permute-start(bf16[512,512]{1,0:T(8,128)(2,1)S(1)} %collective-permute-done.7.refs_2_.refs_6_), channel_id=1, source_target_pairs={{0,1},{1,0},{2,3},{3,2},{4,5},{5,4},{6,7},{7,6},{8,9},{9,8},{10,11... | collective-permute-start | bytes 1572872 | tf_op jit(solution)/shard_map/ppermute | solution.py:49
  36.6 3.6 %collective-permute-start.11 = (f32[8,4,256]{2,1,0:T(4,128)S(1)}, f32[8,4,256]{2,1,0:T(4,128)S(1)}, u32[]{:S(2)}, u32[]{:S(2)}) collective-permute-start(f32[8,4,256]{2,1,0:T(4,128)S(1)} %get-tuple-element.103.refs_0_), channel_id=1, source_target_pairs={{0,3},{1,2},{2,1},{3,0},{4,7},{5,6},{6,5},{7,4},{8,11},{9,10},{10,... | collective-permute-start | bytes 98312 | tf_op jit(solution)/shard_map/ppermute | solution.py:49
  37.8 3.9 %collective-permute-start.10 = (f32[8,4,256]{2,1,0:T(4,128)S(1)}, f32[8,4,256]{2,1,0:T(4,128)S(1)}, u32[]{:S(2)}, u32[]{:S(2)}) collective-permute-start(f32[8,4,256]{2,1,0:T(4,128)S(1)} %get-tuple-element.103.refs_0_), channel_id=1, source_target_pairs={{0,2},{1,3},{2,0},{3,1},{4,6},{5,7},{6,4},{7,5},{8,10},{9,11},{10,... | collective-permute-start | bytes 98312 | tf_op jit(solution)/shard_map/ppermute | solution.py:49
  38.3 3.4 %collective-permute-start.9 = (f32[8,4,256]{2,1,0:T(4,128)S(1)}, f32[8,4,256]{2,1,0:T(4,128)S(1)}, u32[]{:S(2)}, u32[]{:S(2)}) collective-permute-start(f32[8,4,256]{2,1,0:T(4,128)S(1)} %get-tuple-element.103.refs_0_), channel_id=1, source_target_pairs={{0,1},{1,0},{2,3},{3,2},{4,5},{5,4},{6,7},{7,6},{8,9},{9,8},{10,11... | collective-permute-start | bytes 98312 | tf_op jit(solution)/shard_map/ppermute | solution.py:49
  42.5 3.3 %collective-permute-start.13 = (bf16[2,512,512]{2,1,0:T(8,128)(2,1)S(1)}, bf16[2,512,512]{2,1,0:T(8,128)(2,1)S(1)}, u32[]{:S(2)}, u32[]{:S(2)}) collective-permute-start(bf16[2,512,512]{2,1,0:T(8,128)(2,1)S(1)} %get-tuple-element.115), channel_id=1, source_target_pairs={{0,1},{1,0},{2,3},{3,2},{4,5},{5,4},{6,7},{7,6},{8,9},{9,8},{10,11... | collective-permute-start | bytes 3145736 | tf_op jit(solution)/shard_map/ppermute | solution.py:49
  44.3 21.3 %collective-permute-start.12 = (bf16[4,64,256]{2,1,0:T(8,128)(2,1)S(1)}, bf16[4,64,256]{2,1,0:T(8,128)(2,1)S(1)}, u32[]{:S(2)}, u32[]{:S(2)}) collective-permute-start(bf16[4,64,256]{2,1,0:T(8,128)(2,1)S(1)} %get-tuple-element.113), channel_id=1, source_target_pairs={{0,4},{4,0},{8,12},{12,8},{16,20},{20,16},{24,28},{28,24},{1,5},{5... | collective-permute-start | bytes 393224 | tf_op jit(solution)/shard_map/ppermute | solution.py:49
  46.1 19.5 %collective-permute-start.14 = (bf16[512,512]{1,0:T(8,128)(2,1)S(1)}, bf16[512,512]{1,0:T(8,128)(2,1)S(1)}, u32[]{:S(2)}, u32[]{:S(2)}) collective-permute-start(bf16[512,512]{1,0:T(8,128)(2,1)S(1)} %get-tuple-element.116), channel_id=1, source_target_pairs={{0,2},{1,3},{2,0},{3,1},{4,6},{5,7},{6,4},{7,5},{8,10},{9,11},{10,... | collective-permute-start | bytes 1572872 | tf_op jit(solution)/shard_map/ppermute | solution.py:49
  65.6 1.8 %copy-start.14 = (bf16[512,512]{1,0:T(8,128)(2,1)}, bf16[512,512]{1,0:T(8,128)(2,1)S(1)}, u32[]{:S(2)}) copy-start(bf16[512,512]{1,0:T(8,128)(2,1)S(1)} %collective-permute-done.14.refs_1_) | copy-start | bytes 1572868
  67.4 8.5 %collective-permute-start.16 = (bf16[2,512,512]{2,1,0:T(8,128)(2,1)S(1)}, bf16[2,512,512]{2,1,0:T(8,128)(2,1)S(1)}, u32[]{:S(2)}, u32[]{:S(2)}) collective-permute-start(bf16[2,512,512]{2,1,0:T(8,128)(2,1)S(1)} %get-tuple-element.121), channel_id=1, source_target_pairs={{0,1},{1,0},{2,3},{3,2},{4,5},{5,4},{6,7},{7,6},{8,9},{9,8},{10,11... | collective-permute-start | bytes 3145736 | tf_op jit(solution)/shard_map/ppermute | solution.py:49
  67.5 8.4 %collective-permute-start.15 = (bf16[4,80,384]{2,1,0:T(8,128)(2,1)S(1)}, bf16[4,80,384]{2,1,0:T(8,128)(2,1)S(1)}, u32[]{:S(2)}, u32[]{:S(2)}) collective-permute-start(bf16[4,80,384]{2,1,0:T(8,128)(2,1)S(1)} %get-tuple-element.118), channel_id=1, source_target_pairs={{0,4},{4,0},{8,12},{12,8},{16,20},{20,16},{24,28},{28,24},{1,5},{5... | collective-permute-start | bytes 737288 | tf_op jit(solution)/shard_map/ppermute | solution.py:49
  68.5 12.8 %collective-permute-start.20 = (bf16[64,256]{1,0:T(8,128)(2,1)S(1)}, bf16[64,256]{1,0:T(8,128)(2,1)S(1)}, u32[]{:S(2)}, u32[]{:S(2)}) collective-permute-start(bf16[64,256]{1,0:T(8,128)(2,1)S(1)} %get-tuple-element.131), channel_id=1, source_target_pairs={{0,8},{4,12},{8,0},{12,4},{16,24},{20,28},{24,16},{28,20},{1,9},{5... | collective-permute-start | bytes 98312 | tf_op jit(solution)/shard_map/ppermute | solution.py:49
  70.5 10.9 %collective-permute-start.21 = (bf16[64,256]{1,0:T(8,128)(2,1)S(1)}, bf16[64,256]{1,0:T(8,128)(2,1)S(1)}, u32[]{:S(2)}, u32[]{:S(2)}) collective-permute-start(bf16[64,256]{1,0:T(8,128)(2,1)S(1)} %get-tuple-element.132), channel_id=1, source_target_pairs={{0,16},{4,20},{8,24},{12,28},{16,0},{20,4},{24,8},{28,12},{1,17},{... | collective-permute-start | bytes 98312 | tf_op jit(solution)/shard_map/ppermute | solution.py:49
  73.9 7.5 %collective-permute-start.22 = (bf16[64,256]{1,0:T(8,128)(2,1)S(1)}, bf16[64,256]{1,0:T(8,128)(2,1)S(1)}, u32[]{:S(2)}, u32[]{:S(2)}) collective-permute-start(bf16[64,256]{1,0:T(8,128)(2,1)S(1)} %get-tuple-element.133), channel_id=1, source_target_pairs={{0,24},{4,28},{8,16},{12,20},{16,8},{20,12},{24,0},{28,4},{1,25},{... | collective-permute-start | bytes 98312 | tf_op jit(solution)/shard_map/ppermute | solution.py:49
  75.9 7.9 %collective-permute-start.17 = (bf16[80,384]{1,0:T(8,128)(2,1)S(1)}, bf16[80,384]{1,0:T(8,128)(2,1)S(1)}, u32[]{:S(2)}, u32[]{:S(2)}) collective-permute-start(bf16[80,384]{1,0:T(8,128)(2,1)S(1)} %get-tuple-element.124), channel_id=1, source_target_pairs={{0,8},{4,12},{8,0},{12,4},{16,24},{20,28},{24,16},{28,20},{1,9},{5... | collective-permute-start | bytes 184328 | tf_op jit(solution)/shard_map/ppermute | solution.py:49
  77.9 6.8 %collective-permute-start.18 = (bf16[80,384]{1,0:T(8,128)(2,1)S(1)}, bf16[80,384]{1,0:T(8,128)(2,1)S(1)}, u32[]{:S(2)}, u32[]{:S(2)}) collective-permute-start(bf16[80,384]{1,0:T(8,128)(2,1)S(1)} %get-tuple-element.125), channel_id=1, source_target_pairs={{0,16},{4,20},{8,24},{12,28},{16,0},{20,4},{24,8},{28,12},{1,17},{... | collective-permute-start | bytes 184328 | tf_op jit(solution)/shard_map/ppermute | solution.py:49
  81.3 6.0 %collective-permute-start.19 = (bf16[80,384]{1,0:T(8,128)(2,1)S(1)}, bf16[80,384]{1,0:T(8,128)(2,1)S(1)}, u32[]{:S(2)}, u32[]{:S(2)}) collective-permute-start(bf16[80,384]{1,0:T(8,128)(2,1)S(1)} %get-tuple-element.126), channel_id=1, source_target_pairs={{0,24},{4,28},{8,16},{12,20},{16,8},{20,12},{24,0},{28,4},{1,25},{... | collective-permute-start | bytes 184328 | tf_op jit(solution)/shard_map/ppermute | solution.py:49
  82.4 13.8 %collective-permute-start.23 = (bf16[512,512]{1,0:T(8,128)(2,1)}, bf16[512,512]{1,0:T(8,128)(2,1)}, u32[]{:S(2)}, u32[]{:S(2)}) collective-permute-start(bf16[512,512]{1,0:T(8,128)(2,1)} %get-tuple-element.137), channel_id=1, source_target_pairs={{0,2},{1,3},{2,0},{3,1},{4,6},{5,7},{6,4},{7,5},{8,10},{9,11},{10,... | collective-permute-start | bytes 1572872 | tf_op jit(solution)/shard_map/ppermute | solution.py:49
  88.1 11.8 %all-to-all-start = ((f32[32,8,128]{2,1,0:T(8,128)}), f32[32,8,128]{2,1,0:T(8,128)S(1)}, u32[]{:S(2)}, u32[]{:S(2)}) async-start(f32[32,8,128]{2,1,0:T(8,128)} %get-tuple-element.138), calls=%async_computation | async-start | bytes 262144 | tf_op jit(solution)/shard_map/all_to_all | solution.py:837
  91.3 1.0 %copy-start.15 = (bf16[512,512]{1,0:T(8,128)(2,1)S(1)}, bf16[512,512]{1,0:T(8,128)(2,1)}, u32[]{:S(2)}) copy-start(bf16[512,512]{1,0:T(8,128)(2,1)} %copy-done.14) | copy-start | bytes 1572868
  93.3 6.6 %copy-start.2 = (f32[64,4,128]{2,1,0:T(4,128)S(1)}, f32[64,4,128]{2,1,0:T(4,128)}, u32[]{:S(2)}) copy-start(f32[64,4,128]{2,1,0:T(4,128)} %refs_0_.5) | copy-start | bytes 393220
  93.3 6.6 %copy-start.3 = (f32[64,4,128]{2,1,0:T(4,128)S(1)}, f32[64,4,128]{2,1,0:T(4,128)}, u32[]{:S(2)}) copy-start(f32[64,4,128]{2,1,0:T(4,128)} %refs_1_.1) | copy-start | bytes 393220
  93.3 6.6 %copy-start.4 = (f32[64,4,128]{2,1,0:T(4,128)S(1)}, f32[64,4,128]{2,1,0:T(4,128)}, u32[]{:S(2)}) copy-start(f32[64,4,128]{2,1,0:T(4,128)} %refs_2_.1) | copy-start | bytes 393220
  93.3 6.6 %copy-start.6 = (f32[8832]{0:T(1024)S(1)}, f32[8832]{0:T(1024)}, u32[]{:S(2)}) copy-start(f32[8832]{0:T(1024)} %param.24) | copy-start | bytes 105988
  93.3 6.6 %copy-start.7 = (f32[8832]{0:T(1024)S(1)}, f32[8832]{0:T(1024)}, u32[]{:S(2)}) copy-start(f32[8832]{0:T(1024)} %param.25) | copy-start | bytes 105988
  93.4 6.6 %copy-start.9 = (f32[128,64]{0,1:T(8,128)S(1)}, f32[128,64]{0,1:T(8,128)}, u32[]{:S(2)}) copy-start(f32[128,64]{0,1:T(8,128)} %param.18) | copy-start | bytes 98308
  93.4 6.6 %copy-start.10 = (f32[128,64]{0,1:T(8,128)S(1)}, f32[128,64]{0,1:T(8,128)}, u32[]{:S(2)}) copy-start(f32[128,64]{0,1:T(8,128)} %param.22) | copy-start | bytes 98308
  93.4 6.6 %copy-start.11 = (f32[128,64]{0,1:T(8,128)S(1)}, f32[128,64]{0,1:T(8,128)}, u32[]{:S(2)}) copy-start(f32[128,64]{0,1:T(8,128)} %param.23) | copy-start | bytes 98308
  96.1 1.0 %copy-start.13 = (bf16[512,512]{1,0:T(8,128)(2,1)S(1)}, bf16[512,512]{1,0:T(8,128)(2,1)}, u32[]{:S(2)}) copy-start(bf16[512,512]{1,0:T(8,128)(2,1)} %cot_ref.1) | copy-start | bytes 1572868

commit v6 on v5

--- a/solution.py
+++ b/solution.py
@@ -16,7 +16,10 @@
 STEP = 10
 TILE = 256
 NEG = -1e9
-ROOM = 24
+ROOM = 16
+KEPT_TILES = 72
+VALUES = 12
+BACKWARD = 2
 
 norm_epsilon = 1e-06
 adam_epsilon = 1e-08
@@ -92,7 +95,7 @@
     return n // low, low
 
 
-def scatter_high(own, received, us):
+def scatter_high(own, received, us, *behind):
     high, rows, columns = own.shape
     low = 1 + len(received)
     mine, *leaving = call(
@@ -103,7 +106,9 @@
         [],
         us,
     )(own, *received)
-    return [mine] + [swap(sent, "dp", (k + 1) * low) for k, sent in enumerate(leaving)]
+    leaving = after_all(leaving, *behind)
+    order = sorted(range(1, high), key=lambda k: k != high // 2)
+    return [mine] + [swap(leaving[k - 1], "dp", k * low) for k in order]
 
 
 def fold_cores(keep, crossed):
@@ -290,10 +295,25 @@
     for i in range(xn_ref.shape[0]):
         project(i)
 
-def attend_kernel(heads, first, last, *refs):
+def tile_at(refs, i, j):
+    at = i * (i + 1) // 2 + j
+    for ref in refs:
+        if at < ref.shape[0]:
+            return ref[at]
+        at -= ref.shape[0]
+
+
+def weights_and_slope(h):
+    th = jnp.tanh(h)
+    u = 1.0 + th
+    w = h * u
+    return w, u + w * (1.0 - th)
+
+
+def attend_kernel(heads, first, last, kept, *refs):
     if first:
         before_ref, refs = refs[0], refs[1:]
-    kx_ref, qs_ref, trow_ref, vt_ref, pos_ref, ss_ref, attn_ref = refs
+    kx_ref, qs_ref, trow_ref, vt_ref, pos_ref, ss_ref, attn_ref = refs[:7]
     if first:
         attn_ref[:first] = before_ref[...]
     for i in range(first, last):
@@ -302,7 +322,12 @@
         weights = []
         for j in range(i + 1):
             h = masked(scores[j], pos_ref[i - j], ss_ref[:, i * TILE : (i + 1) * TILE], j, heads)
-            weights.append((h + h * jnp.tanh(h)).astype(bf16))
+            w, slope = weights_and_slope(h)
+            weights.append(w.astype(bf16))
+            if kept:
+                at = (i * (i + 1) - first * (first + 1)) // 2 + j
+                refs[7][at] = weights[j]
+                refs[8][at] = slope.astype(bf16)
         total = dot(vt_ref[0], weights[0])
         for j in range(1, i + 1):
             total = total + dot(vt_ref[j], weights[j])
@@ -375,7 +400,7 @@
     cot_pieces = take(n_head)
     attn_ref, p_ref, gg_ref, xn_ref = take(4)
     da_ref, dat_ref, gun_ref = take(3)
-    parts, acc_ref, wg_ref = refs[:-2], refs[-2], refs[-1]
+    (acc_ref,) = refs
     width = attn_ref.shape[1]
     per = cot_pieces[0].shape[0] // TILE
     for k, piece in enumerate(cot_pieces):
@@ -399,8 +424,6 @@
             else:
                 acc_ref[:width] += add_gate
                 acc_ref[width:] += add_out
-    wg_ref[...] = flip(acc_ref[...])
-    send_parts(wg_ref, parts)
 
 
 def send_parts(wg_ref, parts):
@@ -413,18 +436,52 @@
             parts[k][p] = wg_ref[pl.ds(start, rows), :].astype(bf16)
 
 
-def backward_kernel(heads, n_dp, extra, *refs):
+def values_kernel(heads, kept, *refs):
     refs = list(refs)
     take = lambda count: [refs.pop(0) for _ in range(count)]
-    kx_ref, kxt_ref, qs_ref, trow_ref, q_ref, v_ref, da_ref, dat_ref, pos_ref = take(9)
-    d_ref, xn_ref, ss_ref, gb_ref = take(4)
+    held = take(2 if kept else 5)
+    da_ref, d_ref, xn_ref, acc_in = take(4)
+    gpv_ref = refs.pop(0)
+    parts, wg_ref = refs[:-1], refs[-1]
+    nb, width = da_ref.shape[0], da_ref.shape[2]
+    das = [own_lanes(da_ref[i], heads) for i in range(nb)]
+    queries = None if kept else [query_columns(held[1][i], held[2][i], heads) for i in range(nb)]
+    acc = None
+    for j in range(nb):
+        if kept:
+            tiles = [tile_at(held, i, j) for i in range(j, nb)]
+        else:
+            kx_ref, _, _, pos_ref, ss_ref = held
+            tiles = [
+                weights_and_slope(
+                    masked(
+                        dot(kx_ref[j], queries[i]), pos_ref[i - j], ss_ref[:, i * TILE : (i + 1) * TILE], j, heads
+                    )
+                )[0].astype(bf16)
+                for i in range(j, nb)
+            ]
+        total = dot(jnp.concatenate(tiles, axis=1), jnp.concatenate(das[j:], axis=0))
+        gv = (flip(total) * d_ref[j, :width]).astype(bf16)
+        gpv_ref[j] = flip(gv).astype(bf16)
+        more = dot(gv, xn_ref[j])
+        acc = more if j == 0 else acc + more
+    wg_ref[...] = flip(jnp.concatenate([acc_in[...], acc], axis=0))
+    send_parts(wg_ref, parts)
+
+
+def backward_kernel(heads, n_dp, extra, kept, *refs):
+    refs = list(refs)
+    take = lambda count: [refs.pop(0) for _ in range(count)]
+    held = take(2 if kept else 4)
+    kx_ref, kxt_ref, q_ref, v_ref, dat_ref = take(5)
+    d_ref, xn_ref, gb_ref = take(3)
     gp_ref = refs.pop(0)
     parts = take(split_dp(n_dp)[1])
-    accv_ref, acck_ref, posg_ref, acc_ref, wg_ref, small_ref = refs
+    acck_ref, posg_ref, acc_ref, wg_ref, small_ref = refs
     nb, width = v_ref.shape[0], v_ref.shape[2]
     factor = 1.0 / math.sqrt(HEAD_DIM)
     tiles = [(i, j) for i in reversed(range(nb)) for j in range(i + 1)]
-    products, weights, grads = {}, {}, {}
+    products, grads = {}, {}
     dq = m2 = None
     small_ref[...] = jnp.zeros_like(small_ref)
     small_ref[:, :D] = gb_ref[...]
@@ -436,35 +493,32 @@
         if t < len(tiles):
             i, j = tiles[t]
             if j == 0:
-                queries = query_columns(qs_ref[i], trow_ref[i], heads)
                 backs = by_head(dat_ref[i], heads)
-            products[t] = dot(kx_ref[j], queries), dot(v_ref[j], backs)
+                queries = None if kept else query_columns(held[0][i], held[1][i], heads)
+            products[t] = dot(v_ref[j], backs), None if kept else dot(kx_ref[j], queries)
         if 0 <= t - 1 < len(tiles):
             i, j = tiles[t - 1]
-            product, back = products.pop(t - 1)
-            h = masked(product, pos_ref[i - j], ss_ref[:, i * TILE : (i + 1) * TILE], j, heads)
-            th = jnp.tanh(h)
-            u = 1.0 + th
-            w = h * u
-            ds = back * (u + w * (1.0 - th))
-            weights[t - 1], grads[t - 1] = w.astype(bf16), ds.astype(bf16)
+            back, product = products.pop(t - 1)
+            if kept:
+                slope = tile_at(held, i, j).astype(f32)
+            else:
+                start = held[3][:, i * TILE : (i + 1) * TILE]
+                slope = weights_and_slope(masked(product, held[2][i - j], start, j, heads))[1]
+            ds = back * slope
+            grads[t - 1] = ds.astype(bf16)
             add(posg_ref, i - j, sum(ds[:, g * TILE : (g + 1) * TILE] for g in range(heads)), i == nb - 1)
         if t >= 2:
             i, j = tiles[t - 2]
             low = grads.pop(t - 2)
             if j == 0:
-                da = own_lanes(da_ref[i], heads)
                 times = jnp.concatenate([kx_ref[i, :, :NTB]] * heads, axis=0)
                 q = jnp.concatenate([times, own_lanes(q_ref[i], heads)], axis=1)
-            add(accv_ref, j, dot(weights.pop(t - 2), da), i == nb - 1)
             add(acck_ref, j, dot(low, q), i == nb - 1)
             more = dot(kxt_ref[j, NTB:], low)
             dq = more if j == 0 else dq + more
             if i == j:
-                gp = jnp.concatenate(
-                    [flip(accv_ref[i]), own_rows(dq, heads) * factor, flip(acck_ref[i, :, NTB:]) * factor], axis=0
-                )
-                gp = (gp * d_ref[i]).astype(bf16)
+                gp = jnp.concatenate([own_rows(dq, heads), flip(acck_ref[i, :, NTB:])], axis=0)
+                gp = (gp * factor * d_ref[i, width:]).astype(bf16)
                 gp_ref[i] = flip(gp).astype(bf16)
                 more = dot(gp, xn_ref[i])
                 acc_ref[...] = more if i == nb - 1 else acc_ref[...] + more
@@ -491,13 +545,13 @@
         high = here.astype(bf16).astype(f32)
         block = jnp.concatenate([high, here - high, jnp.zeros((16 - 2 * extra, 128), f32)], axis=0)
         wg_ref[p * (step + 16) : p * (step + 16) + step] = grads[p * step : (p + 1) * step]
-        wg_ref[p * (step + 16) + step : (p + 1) * (step + 16)] = jnp.concatenate(
-            [block, jnp.zeros((16, 3 * width - 128), f32)], axis=1
-        )
+        if 2 * width > 128:
+            block = jnp.concatenate([block, jnp.zeros((16, 2 * width - 128), f32)], axis=1)
+        wg_ref[p * (step + 16) + step : (p + 1) * (step + 16)] = block
     send_parts(wg_ref, parts)
 
 
-def input_kernel(n_head, gp_ref, gun_ref, wt_ref, keep, send):
+def input_kernel(n_head, gp_ref, gun_ref, gpv_ref, wt_ref, keep, send):
     width = gun_ref.shape[2]
     per = keep.shape[1] // TILE
     for k in range(n_head):
@@ -505,7 +559,8 @@
         target = (keep, send)[k % 2]
         for r in range(per):
             i = device * per + r
-            rows = dot(gp_ref[i], wt_ref[width : 4 * width]) + dot(gun_ref[i], wt_ref[:width])
+            rows = dot(jnp.concatenate([gun_ref[i], gpv_ref[i]], axis=1), wt_ref[: 2 * width])
+            rows = rows + dot(gp_ref[i], wt_ref[2 * width : 4 * width])
             target[device // 2, r * TILE : (r + 1) * TILE] = rows.astype(bf16)
 
 
@@ -608,14 +663,15 @@
             put(k, value)
 
     for c in range(4):
-        grad = grads_ref[:, 3 * width : 4 * width] if c == 0 else grads_ref[:, (c - 1) * width : c * width]
+        at = (2, 4, 0, 1)[c] * width
+        grad = grads_ref[:, at : at + width]
         grad_proj_ref[:, c, :] = grad
 
         def put(k, value):
             outs[4 + k][:, c, :] = value
 
         update(lambda k: state[k][:, c, :], put, grad, rate_matrix, decay_matrix)
-    grad = grads_ref[:, 4 * width :]
+    grad = grads_ref[:, 3 * width : 4 * width]
     grad_out_ref[...] = grad
 
     def put_out(k, value):
@@ -629,14 +685,14 @@
     update(lambda k: state[6 + k][...], put_small, small, rate_small, 0.0)
 
 
-def call(kernel, name, in_specs, outs, scratch, us, room=20):
+def call(kernel, name, in_specs, outs, scratch, us, room=16):
     return pl.pallas_call(
         kernel,
         out_shape=[jax.ShapeDtypeStruct(shape, dtype) for shape, dtype, _ in outs],
         in_specs=in_specs,
         out_specs=[spec for _, _, spec in outs],
         scratch_shapes=scratch,
-        compiler_params=pltpu.CompilerParams(vmem_limit_bytes=room * 2**20),
+        compiler_params=pltpu.CompilerParams(vmem_limit_bytes=room * 2**20 * max(1, lax.axis_size("head") // 4)),
         cost_estimate=pl.CostEstimate(flops=int(us * 1e9), bytes_accessed=int(us * 3e6), transcendentals=0),
         name=name,
     )
@@ -732,21 +788,24 @@
         5,
     )(xn, wt, oh, oht)
 
+    kept = nb * (nb + 1) // 2 * heads <= KEPT_TILES
+
     def attend(first, last, *before):
-        (attn,) = call(
-            functools.partial(attend_kernel, heads, first, last),
+        count = (last * (last + 1) - first * (first + 1)) // 2
+        return call(
+            functools.partial(attend_kernel, heads, first, last, kept),
             "attend",
             [VMEM] * (len(before) + 6),
-            [((last, width, TILE), f32, VMEM)],
+            [((last, width, TILE), f32, VMEM)] + [((count, TILE, heads * TILE), bf16, VMEM)] * (2 * kept),
             [],
             8,
         )(*before, kx, qs, trow, vt, pos, starts)
-        return attn
 
     split = nb - nb // 4
-    attn = attend(0, split)
+    attn, *kept_first = attend(0, split)
     cot_chips = after_all(cot_chips, attn)
-    attn = attend(split, nb, after(attn, *cot_chips))
+    attn, *kept_last = attend(split, nb, after(attn, *cot_chips))
+    kept_weights, kept_slopes = zip(kept_first, kept_last) if kept else ((), ())
     cot_pieces = gather_cores(cotangent, cot_chips)
 
     column = ((nb, width, TILE), f32, VMEM)
@@ -766,7 +825,7 @@
         functools.partial(branch_kernel, n_head), "branch", [VMEM] * (n_head + 3), [split_shape] * 2, [], 1
     )(*stats, attn, p_gate, wt)
     crossed = swap(send, "head", 1)
-    da, dat, gun, *early_parts = call(
+    da, dat, gun, wg_sum = call(
         functools.partial(middle_kernel, n_head),
         "middle",
         [VMEM] * (2 * n_head + 4),
@@ -774,33 +833,42 @@
             ((nb, TILE, width), bf16, VMEM),
             ((nb, width, TILE), bf16, VMEM),
             ((nb, TILE, width), bf16, VMEM),
-        ]
-        + [((high, rows_here, 2 * width), bf16, VMEM)] * low,
-        [pltpu.VMEM((2 * width, D), f32), pltpu.VMEM((D, 2 * width), f32)],
+            ((2 * width, D), f32, VMEM),
+        ],
+        [],
         6,
     )(*stats, *cot_pieces, attn, p_gate, gg, xn)
     branch, *leaving = fold_cores(keep, crossed)
     received = [swap(sent, "head", 2 * (k + 1)) for k, sent in enumerate(leaving)]
+    held = kept_weights if kept else (kx, qs, trow, pos, starts)
+    gpv, *early_parts = call(
+        functools.partial(values_kernel, heads, kept),
+        "values",
+        [VMEM] * (len(held) + 4),
+        [((nb, TILE, width), bf16, VMEM)] + [((high, rows_here, 3 * width), bf16, VMEM)] * low,
+        [pltpu.VMEM((D, 3 * width), f32)],
+        VALUES,
+    )(*held, da, dsilu, xn, wg_sum)
     early_received = [swap(early_parts[k], "dp", k) for k in range(1, low)]
 
     length = D + group + NTB
     extra = -(-length // (128 * n_dp))
+    held = kept_slopes if kept else (qs, trow, pos, starts)
     gp, *late_parts = call(
-        functools.partial(backward_kernel, heads, n_dp, extra),
+        functools.partial(backward_kernel, heads, n_dp, extra, kept),
         "backward",
-        [VMEM] * 13,
-        [((nb, TILE, 3 * width), bf16, VMEM)] + [((high, rows_here + 16, 3 * width), bf16, VMEM)] * low,
+        [VMEM] * (len(held) + 8),
+        [((nb, TILE, 2 * width), bf16, VMEM)] + [((high, rows_here + 16, 2 * width), bf16, VMEM)] * low,
         [
-            pltpu.VMEM((nb, TILE, width), f32),
             pltpu.VMEM((nb, TILE, NTB + width), f32),
             pltpu.VMEM((nb, TILE, TILE), f32),
-            pltpu.VMEM((3 * width, D), f32),
-            pltpu.VMEM((n_dp * (rows_here + 16), 3 * width), f32),
+            pltpu.VMEM((2 * width, D), f32),
+            pltpu.VMEM((n_dp * (rows_here + 16), 2 * width), f32),
             pltpu.VMEM((1, extra * n_dp * 128), f32),
         ],
-        35,
+        BACKWARD,
         ROOM,
-    )(kx, kxt, qs, trow, q, v, da, dat, pos, dsilu, xn, starts, gb)
+    )(*held, kx, kxt, q, v, dat, dsilu, xn, gb)
 
     tied = lax.optimization_barrier((gp, *late_parts, *early_received, *received))
     gp, late_parts = tied[0], tied[1 : 1 + low]
@@ -809,17 +877,16 @@
     keep, send = call(
         functools.partial(input_kernel, n_head),
         "input_rows",
-        [VMEM] * 3,
+        [VMEM] * 4,
         [((n_head // 2, here, D), bf16, VMEM)] * 2,
         [],
         4,
-    )(gp, gun, wt)
+    )(gp, gun, gpv, wt)
     early_blocks = scatter_high(after(early_parts[0], send), early_received, 1)
     crossed = swap(send, "head", 1)
-    late_received = after_all(late_received, send, crossed)
-    late_blocks = scatter_high(late_parts[0], late_received, 0.1)
+    late_blocks = scatter_high(late_parts[0], late_received, 12, send, crossed)
     (early,) = call(
-        sum_kernel, "sum", [VMEM] * high, [((rows_here, 2 * width), f32, VMEM)], [], 14
+        sum_kernel, "sum", [VMEM] * high, [((rows_here, 3 * width), f32, VMEM)], [], 14
     )(*early_blocks)
     mine, *leaving = fold_cores(keep, after(crossed, late_blocks[0]))
     arrived = [swap(leaving[k - 1], "head", 2 * k) for k in range(1, chips)]
@@ -837,10 +904,10 @@
     heard = lax.all_to_all(message, ("dp", "head"), 0, 0, tiled=True)
     (mixed,) = call(
         mix_kernel, "mix", [VMEM] * (2 + chips), [((here, D), bf16, VMEM)], [], 1
-    )(after(tokens, message), small_rows, branch, *received)
+    )(tokens, small_rows, after(branch, message), *received)
     (input_grad,) = call(
         finish_kernel, "finish", [VMEM] * (2 + chips), [((here, D), f32, VMEM)], [], 1
-    )(after(tokens, mixed), cotangent, mine, *arrived)
+    )(tokens, cotangent, mine, *arrived)
     heard = after(heard, input_grad)
     state = [proj_weight, proj_mean, proj_square, out_weight.T, out_mean.T, out_square.T]
     state += [x.reshape(-1, 128) for x in (small_params, small_mean, small_square)]

time: 102 us -> 100 us (0.980)
  Pallas kernels: 44.9 us -> 42.8 us
    pallas_call x5 -> x6, Pallas kernels: 27 us -> 25.1 us  [the longest x1 10.6 us: shards(): call(functools.partial(backward_kernel, heads, n_dp, extra, kept), 'backw...]
  transfers between devices with their start and end apart: 25 -> 25, of which waited for: 9 -> 8; matrix products, arithmetic and copies ran while one was open for 0% -> 0% of each run, Pallas kernels for 38% -> 38%
where the time goes in v6:
time: 100 us
  Pallas kernels  42.8 us (43%)
  starting transfers between devices  32.8 us (33%)
  waiting for transfers between devices  19.4 us (19%)
  local copies, waits for them, and re-layouts  3.81 us (4%)
  between operations  1.13 us (1%)
    ppermute x24, starting transfers between devices, swap(): return lax.ppermute(x, axis, [(i, i ^ k) for i in range(n)])  29.2 us
    ppermute x24, waiting for transfers between devices, swap(): return lax.ppermute(x, axis, [(i, i ^ k) for i in range(n)])  19.4 us
    pallas_call x1, Pallas kernels, shards(): call(functools.partial(backward_kernel, heads, n_dp, extra, kept), 'backw...  10.6 us
    pallas_call x2, Pallas kernels, attend(): call(functools.partial(attend_kernel, heads, first, last, kept), 'attend'...  8.87 us
    pallas_call x1, Pallas kernels, shards(): call(functools.partial(values_kernel, heads, kept), 'values', [VMEM] * (l...  4.32 us
    unnamed x36, local copies, waits for them, and re-layouts  3.81 us
    all_to_all x1, starting transfers between devices, shards(): heard = lax.all_to_all(message, ('dp', 'head'), 0, 0, tiled=True)  3.59 us
    pallas_call x1, Pallas kernels, shards(): call(finish_kernel, 'finish', [VMEM] * (2 + chips), [((here, D), f32, VME...  2.73 us
  transfers between devices with their start and end apart: 25, of which 8 were waited for; matrix products, arithmetic and copies ran while one was open for 0% of the time, Pallas kernels for 38%

profile of v6, /device:TPU:0, one launch (start us, length us, event | category | flops | bytes accessed | tf_op | source)
XLA Modules:
  0.0 100.0 jit_solution(13323396106227954558)
XLA Ops:
  0.6 0.0 copy-start.1
  0.7 0.9 copy-done.1
  1.6 0.8 copy-done.8
  2.3 0.3 cast.1.refs_0_
  2.6 0.0 copy-start
  2.7 0.0 copy-start.12
  2.7 4.1 %collective-permute-start.5 = (bf16[64,640]{1,0:T(8,128)(2,1)S(1)}, bf16[64,640]{1,0:T(8,128)(2,1)S(1)}, u32[]{:S(2)}, u32[]{:S(2)}) collective-permute-start(bf16[64,640]{1,0:T(8,128)(2,1)S(1)} %cast.1.refs_0_), channel_id=1, source_target_pairs={{0,16},{4,20},{8,24},{12,28},{16,0},{20,4},{24,8},{28,12},{1,17},{... | collective-permute-start | bytes 245768 | tf_op jit(solution)/shard_map/ppermute | solution.py:52
  6.8 1.5 %collective-permute-start.3 = (bf16[512,512]{1,0:T(8,128)(2,1)}, bf16[512,512]{1,0:T(8,128)(2,1)S(1)}, u32[]{:S(2)}, u32[]{:S(2)}) collective-permute-start(bf16[512,512]{1,0:T(8,128)(2,1)} %tokens_ref.3), channel_id=1, source_target_pairs={{0,2},{1,3},{2,0},{3,1},{4,6},{5,7},{6,4},{7,5},{8,10},{9,11},{10,... | collective-permute-start | bytes 1572872 | tf_op jit(solution)/shard_map/ppermute | solution.py:52
  8.3 2.7 %collective-permute-done.5.refs_1_ = bf16[64,640]{1,0:T(8,128)(2,1)S(1)} collective-permute-done((bf16[64,640]{1,0:T(8,128)(2,1)S(1)}, bf16[64,640]{1,0:T(8,128)(2,1)S(1)}, u32[]{:S(2)}, u32[]{:S(2)}) %collective-permute-start.5) | collective-permute-done | bytes 81952 | tf_op jit(solution)/shard_map/ppermute | solution.py:52
  11.0 0.0 copy-start.5
  11.0 0.0 copy-start.16
  11.0 0.8 collective-permute-start.6
  11.8 0.5 collective-permute-start
  12.3 1.5 %collective-permute-start.1 = (bf16[512,512]{1,0:T(8,128)(2,1)S(1)}, bf16[512,512]{1,0:T(8,128)(2,1)S(1)}, u32[]{:S(2)}, u32[]{:S(2)}) collective-permute-start(bf16[512,512]{1,0:T(8,128)(2,1)S(1)} %copy-done.12), channel_id=1, source_target_pairs={{0,2},{1,3},{2,0},{3,1},{4,6},{5,7},{6,4},{7,5},{8,10},{9,11},{10,... | collective-permute-start | bytes 1572872 | tf_op jit(solution)/shard_map/ppermute | solution.py:52
  13.8 2.6 %collective-permute-done.6.refs_2_ = bf16[128,640]{1,0:T(8,128)(2,1)S(1)} collective-permute-done((bf16[128,640]{1,0:T(8,128)(2,1)S(1)}, bf16[128,640]{1,0:T(8,128)(2,1)S(1)}, u32[]{:S(2)}, u32[]{:S(2)}) %collective-permute-start.6) | collective-permute-done | bytes 163872 | tf_op jit(solution)/shard_map/ppermute | solution.py:52
  16.4 1.8 %collective-permute-start.7 = (bf16[256,640]{1,0:T(8,128)(2,1)S(1)}, bf16[256,640]{1,0:T(8,128)(2,1)S(1)}, u32[]{:S(2)}, u32[]{:S(2)}) collective-permute-start(bf16[256,640]{1,0:T(8,128)(2,1)S(1)} %join.4), channel_id=1, source_target_pairs={{0,4},{4,0},{8,12},{12,8},{16,20},{20,16},{24,28},{28,24},{1,5},{5... | collective-permute-start | bytes 983048 | tf_op jit(solution)/shard_map/ppermute | solution.py:52
  18.2 3.6 %collective-permute-done.3.refs_2_ = bf16[512,512]{1,0:T(8,128)(2,1)S(1)} collective-permute-done((bf16[512,512]{1,0:T(8,128)(2,1)}, bf16[512,512]{1,0:T(8,128)(2,1)S(1)}, u32[]{:S(2)}, u32[]{:S(2)}) %collective-permute-start.3) | collective-permute-done | bytes 524320 | tf_op jit(solution)/shard_map/ppermute | solution.py:52
  21.8 2.5 %prepare.1 = (f32[8,256,256]{2,1,0:T(8,128)S(1)}, bf16[8,256,128]{2,1,0:T(8,128)(2,1)S(1)}, bf16[8,128,256]{2,1,0:T(8,128)(2,1)S(1)}, bf16[8,128,256]{2,1,0:T(8,128)(2,1)S(1)}) custom-call(s32[1,2048]{1,0:T(1,128)S(1)} %bitcast.26, f32[69,128]{1,0:T(8,128)S(1)} %bitcast.17), custom_call_target="tpu_custom_call" | custom-call | flops 5000000000 | bytes 15000000 | tf_op jit(solution)/shard_map/prepare/pallas_call | solution.py:749
  24.4 1.3 %normalize.1.refs_0_.refs_5_.refs_11_.refs_8_.refs_4_ = bf16[8,256,512]{2,1,0:T(8,128)(2,1)S(1)} custom-call(bf16[512,512]{1,0:T(8,128)(2,1)S(1)} %copy-done, bf16[512,512]{1,0:T(8,128)(2,1)S(1)} %collective-permute-done.2.refs_1_, bf16[512,512]{1,0:T(8,128)(2,1)S(1)} %collective-permute-done.3.refs_2_, bf16[512,512]{1,0:T(8,128)(2,1)S(1)} %collective-permute-done.4.refs_3_), custom_call_target="tpu_custom_call" | custom-call | flops 1000000000 | bytes 3000000 | tf_op jit(solution)/shard_map/normalize/pallas_call | solution.py:772
  25.7 0.3 assemble.1.refs_1_.refs_6_.wt_ref
  26.0 0.0 copy-start.17
  26.0 1.8 %project.1 = (bf16[8,384,256]{2,1,0:T(8,128)(2,1)S(1)}, bf16[8,256,256]{2,1,0:T(8,128)(2,1)S(1)}, bf16[8,256,256]{2,1,0:T(8,128)(2,1)S(1)}, bf16[8,128,256]{2,1,...) custom-call(bf16[8,256,512]{2,1,0:T(8,128)(2,1)S(1)} %normalize.1.re, ...), custom_call_target="tpu_custom_call" | custom-call | flops 5000000000 | bytes 15000000 | tf_op jit(solution)/shard_map/project/pallas_call | solution.py:782
  27.9 5.3 %attend.2 = (f32[6,128,256]{2,1,0:T(8,128)S(1)}, bf16[21,256,512]{2,1,0:T(8,128)(2,1)S(1)}, bf16[21,256,512]{2,1,0:T(8,128)(2,1)S(1)}) custom-call(bf16[8,256,256]{2,1,0:T(8,128)(2,1)S(1)} %get-tuple-element.105.refs_0_.refs_1_.refs_2_, bf16[8,128,256]{2,1,0:T(8,128)(2,1)S(1)} %get-tuple-element.106.refs_1_.refs_2_, ...), custom_call_target="tpu_custom_call" | custom-call | flops 8000000000 | bytes 24000000 | tf_op jit(solution)/shard_map/attend/pallas_call | solution.py:795
  33.2 0.6 collective-permute-start.8
  33.7 3.6 %attend.3 = (f32[8,128,256]{2,1,0:T(8,128)S(1)}, bf16[15,256,512]{2,1,0:T(8,128)(2,1)S(1)}, bf16[15,256,512]{2,1,0:T(8,128)(2,1)S(1)}) custom-call(f32[6,128,256]{2,1,0:T(8,128)S(1)} %get-tuple-element.112.refs_0_, bf16[8,256,256]{2,1,0:T(8,128)(2,1)S(1)} %get-tuple-element.105.refs_0_.refs_1_.refs_2_, ...), custom_call_target="tpu_custom_call" | custom-call | flops 8000000000 | bytes 24000000 | tf_op jit(solution)/shard_map/attend/pallas_call | solution.py:795
  37.3 1.8 %gate.1 = (f32[8,128,256]{2,1,0:T(8,128)S(1)}, f32[8,128,256]{2,1,0:T(8,128)S(1)}, f32[8,4,256]{2,1,0:T(4,128)S(1)}, f32[1,512]{1,0:T(1,128)S(1)}) custom-call(bf16[512,512]{1,0:T(8,128)(2,1)S(1)} %copy-done.12, bf16[512,512]{1,0:T(8,128)(2,1)S(1)} %collective-permute-done.refs_1_.refs_5_, bf16[512,512]{1,0:T(8,128)(2,1)S(1)} %collective-permute-done.1.refs_2_.refs_6_, ...), custom_call_target="tpu_custom_call" | custom-call | flops 5000000000 | bytes 15000000 | tf_op jit(solution)/shard_map/gate/pallas_call | solution.py:812
  39.1 1.6 %collective-permute-start.10 = (f32[8,4,256]{2,1,0:T(4,128)S(1)}, f32[8,4,256]{2,1,0:T(4,128)S(1)}, u32[]{:S(2)}, u32[]{:S(2)}) collective-permute-start(f32[8,4,256]{2,1,0:T(4,128)S(1)} %get-tuple-element.114.refs_0_), channel_id=1, source_target_pairs={{0,2},{1,3},{2,0},{3,1},{4,6},{5,7},{6,4},{7,5},{8,10},{9,11},{10,... | collective-permute-start | bytes 98312 | tf_op jit(solution)/shard_map/ppermute | solution.py:52
  40.7 0.6 collective-permute-start.9
  41.3 1.8 %collective-permute-done.10.refs_2_ = f32[8,4,256]{2,1,0:T(4,128)S(1)} collective-permute-done((f32[8,4,256]{2,1,0:T(4,128)S(1)}, f32[8,4,256]{2,1,0:T(4,128)S(1)}, u32[]{:S(2)}, u32[]{:S(2)}) %collective-permute-start.10) | collective-permute-done | bytes 32800 | tf_op jit(solution)/shard_map/ppermute | solution.py:52
  43.1 1.2 %collective-permute-done.11.refs_3_ = f32[8,4,256]{2,1,0:T(4,128)S(1)} collective-permute-done((f32[8,4,256]{2,1,0:T(4,128)S(1)}, f32[8,4,256]{2,1,0:T(4,128)S(1)}, u32[]{:S(2)}, u32[]{:S(2)}) %collective-permute-start.11) | collective-permute-done | bytes 32800 | tf_op jit(solution)/shard_map/ppermute | solution.py:52
  44.3 0.8 branch.1
  45.1 0.1 collective-permute-start.12
  45.2 1.3 %middle.1 = (bf16[8,256,128]{2,1,0:T(8,128)(2,1)S(1)}, bf16[8,128,256]{2,1,0:T(8,128)(2,1)S(1)}, bf16[8,256,128]{2,1,0:T(8,128)(2,1)S(1)}, f32[256,512]{1,0:T(8,128)S(1)}) custom-call(f32[8,4,256]{2,1,0:T(4,128)S(1)} %get-tuple-element.114.refs_0_, f32[8,4,256]{2,1,0:T(4,128)S(1)} %collective-permute-done.9.refs_1_, ...), custom_call_target="tpu_custom_call" | custom-call | flops 6000000000 | bytes 18000000 | tf_op jit(solution)/shard_map/middle/pallas_call | solution.py:828
  46.6 1.3 %collective-permute-done.12.crossed_ref = bf16[2,512,512]{2,1,0:T(8,128)(2,1)S(1)} collective-permute-done((bf16[2,512,512]{2,1,0:T(8,128)(2,1)S(1)}, bf16[2,512,512]{2,1,0:T(8,128)(2,1)S(1)}, u32[]{:S(2)}, u32[]{:S(2)}) %collective-permute-start.12) | collective-permute-done | bytes 1048608 | tf_op jit(solution)/shard_map/ppermute | solution.py:52
  47.8 0.2 rows.2
  48.1 0.7 collective-permute-start.14
  48.8 4.3 %values.1 = (bf16[8,256,128]{2,1,0:T(8,128)(2,1)S(1)}, bf16[4,64,384]{2,1,0:T(8,128)(2,1)S(1)}, bf16[4,64,384]{2,1,0:T(8,128)(2,1)S(1)}) custom-call(bf16[21,256,512]{2,1,0:T(8,128)(2,1)S(1)} %get-tuple-element.131.refs_0_, bf16[15,256,512]{2,1,0:T(8,128)(2,1)S(1)} %get-tuple-element.132.refs_1_, bf16[8,256,128]{2,1,0:T(8,128)(2,1)S(1)} %get-tuple-element.133.refs_2_, ...), custom_call_target="tpu_custom_call" | custom-call | flops 12000000000 | bytes 36000000 | tf_op jit(solution)/shard_map/values/pallas_call | solution.py:844
  53.1 1.6 %collective-permute-start.13 = (bf16[4,64,384]{2,1,0:T(8,128)(2,1)S(1)}, bf16[4,64,384]{2,1,0:T(8,128)(2,1)S(1)}, u32[]{:S(2)}, u32[]{:S(2)}) collective-permute-start(bf16[4,64,384]{2,1,0:T(8,128)(2,1)S(1)} %get-tuple-element.135), channel_id=1, source_target_pairs={{0,4},{4,0},{8,12},{12,8},{16,20},{20,16},{24,28},{28,24},{1,5},{5... | collective-permute-start | bytes 589832 | tf_op jit(solution)/shard_map/ppermute | solution.py:52
  54.7 10.6 %backward.1 = (bf16[8,256,256]{2,1,0:T(8,128)(2,1)S(1)}, bf16[4,80,256]{2,1,0:T(8,128)(2,1)S(1)}, bf16[4,80,256]{2,1,0:T(8,128)(2,1)S(1)}) custom-call(bf16[21,256,512]{2,1,0:T(8,128)(2,1)S(1)} %get-tuple-element.119.refs_0_, bf16[15,256,512]{2,1,0:T(8,128)(2,1)S(1)} %get-tuple-element.120.refs_1_, ...), custom_call_target="tpu_custom_call" | custom-call | flops 2000000000 | bytes 6000000 | tf_op jit(solution)/shard_map/backward/pallas_call | solution.py:857
  65.3 0.0 copy-start.14
  65.3 0.6 collective-permute-start.15
  65.9 1.3 %input_rows.1 = (bf16[2,512,512]{2,1,0:T(8,128)(2,1)S(1)}, bf16[2,512,512]{2,1,0:T(8,128)(2,1)S(1)}) custom-call(bf16[8,256,256]{2,1,0:T(8,128)(2,1)S(1)} %get-tuple-element.143.gp_ref, bf16[8,256,128]{2,1,0:T(8,128)(2,1)S(1)} %get-tuple-element.144.gun_ref, bf16[8,256,128]{2,1,0:T(8,128)(2,1)S(1)} %get-tuple-element.145.gpv_ref, ...), custom_call_target="tpu_custom_call" | custom-call | flops 4000000000 | bytes 12000000 | tf_op jit(solution)/shard_map/input_rows/pallas_call | solution.py:877
  67.2 0.1 collective-permute-start.16
  67.2 0.1 fold.3
  67.3 3.7 %collective-permute-start.20 = (bf16[64,384]{1,0:T(8,128)(2,1)S(1)}, bf16[64,384]{1,0:T(8,128)(2,1)S(1)}, u32[]{:S(2)}, u32[]{:S(2)}) collective-permute-start(bf16[64,384]{1,0:T(8,128)(2,1)S(1)} %get-tuple-element.157), channel_id=1, source_target_pairs={{0,16},{4,20},{8,24},{12,28},{16,0},{20,4},{24,8},{28,12},{1,17},{... | collective-permute-start | bytes 147464 | tf_op jit(solution)/shard_map/ppermute | solution.py:52
  71.0 1.4 %collective-permute-start.21 = (bf16[64,384]{1,0:T(8,128)(2,1)S(1)}, bf16[64,384]{1,0:T(8,128)(2,1)S(1)}, u32[]{:S(2)}, u32[]{:S(2)}) collective-permute-start(bf16[64,384]{1,0:T(8,128)(2,1)S(1)} %get-tuple-element.158), channel_id=1, source_target_pairs={{0,8},{4,12},{8,0},{12,4},{16,24},{20,28},{24,16},{28,20},{1,9},{5... | collective-permute-start | bytes 147464 | tf_op jit(solution)/shard_map/ppermute | solution.py:52
  72.4 0.1 collective-permute-start.22
  72.6 2.2 %collective-permute-start.17 = (bf16[80,256]{1,0:T(8,128)(2,1)S(1)}, bf16[80,256]{1,0:T(8,128)(2,1)S(1)}, u32[]{:S(2)}, u32[]{:S(2)}) collective-permute-start(bf16[80,256]{1,0:T(8,128)(2,1)S(1)} %get-tuple-element.147), channel_id=1, source_target_pairs={{0,16},{4,20},{8,24},{12,28},{16,0},{20,4},{24,8},{28,12},{1,17},{... | collective-permute-start | bytes 122888 | tf_op jit(solution)/shard_map/ppermute | solution.py:52
  74.8 2.1 %collective-permute-start.18 = (bf16[80,256]{1,0:T(8,128)(2,1)S(1)}, bf16[80,256]{1,0:T(8,128)(2,1)S(1)}, u32[]{:S(2)}, u32[]{:S(2)}) collective-permute-start(bf16[80,256]{1,0:T(8,128)(2,1)S(1)} %get-tuple-element.148), channel_id=1, source_target_pairs={{0,8},{4,12},{8,0},{12,4},{16,24},{20,28},{24,16},{28,20},{1,9},{5... | collective-permute-start | bytes 122888 | tf_op jit(solution)/shard_map/ppermute | solution.py:52
  76.9 2.7 %collective-permute-start.19 = (bf16[80,256]{1,0:T(8,128)(2,1)S(1)}, bf16[80,256]{1,0:T(8,128)(2,1)S(1)}, u32[]{:S(2)}, u32[]{:S(2)}) collective-permute-start(bf16[80,256]{1,0:T(8,128)(2,1)S(1)} %get-tuple-element.149), channel_id=1, source_target_pairs={{0,24},{4,28},{8,16},{12,20},{16,8},{20,12},{24,0},{28,4},{1,25},{... | collective-permute-start | bytes 122888 | tf_op jit(solution)/shard_map/ppermute | solution.py:52
  79.6 1.0 rows.3
  80.5 1.1 %collective-permute-start.23 = (bf16[512,512]{1,0:T(8,128)(2,1)}, bf16[512,512]{1,0:T(8,128)(2,1)}, u32[]{:S(2)}, u32[]{:S(2)}) collective-permute-start(bf16[512,512]{1,0:T(8,128)(2,1)} %get-tuple-element.163), channel_id=1, source_target_pairs={{0,2},{1,3},{2,0},{3,1},{4,6},{5,7},{6,4},{7,5},{8,10},{9,11},{10,... | collective-permute-start | bytes 1572872 | tf_op jit(solution)/shard_map/ppermute | solution.py:52
  81.7 1.0 %collective-permute-done.19.refs_3_ = bf16[80,256]{1,0:T(8,128)(2,1)S(1)} collective-permute-done((bf16[80,256]{1,0:T(8,128)(2,1)S(1)}, bf16[80,256]{1,0:T(8,128)(2,1)S(1)}, u32[]{:S(2)}, u32[]{:S(2)}) %collective-permute-start.19) | collective-permute-done | bytes 40992 | tf_op jit(solution)/shard_map/ppermute | solution.py:52
  82.7 0.8 collect.1
  83.5 0.0 copy-start.10
  83.5 0.0 copy-start.11
  83.5 3.6 %all-to-all-start = ((f32[32,8,128]{2,1,0:T(8,128)}), f32[32,8,128]{2,1,0:T(8,128)S(1)}, u32[]{:S(2)}, u32[]{:S(2)}) async-start(f32[32,8,128]{2,1,0:T(8,128)} %get-tuple-element.164), calls=%async_computation | async-start | bytes 262144 | tf_op jit(solution)/shard_map/all_to_all | solution.py:904
  87.1 0.0 copy-start.15
  87.2 1.0 %copy-done.15 = bf16[512,512]{1,0:T(8,128)(2,1)S(1)} copy-done((bf16[512,512]{1,0:T(8,128)(2,1)S(1)}, bf16[512,512]{1,0:T(8,128)(2,1)}, u32[]{:S(2)}) %copy-start.15) | copy-done | bytes 524312
  88.2 1.0 mix.1
  89.2 5.1 %collective-permute-done.23.refs_0_ = bf16[512,512]{1,0:T(8,128)(2,1)} collective-permute-done((bf16[512,512]{1,0:T(8,128)(2,1)}, bf16[512,512]{1,0:T(8,128)(2,1)}, u32[]{:S(2)}, u32[]{:S(2)}) %collective-permute-start.23) | collective-permute-done | bytes 524320 | tf_op jit(solution)/shard_map/ppermute | solution.py:52
  94.3 1.0 %copy-done.13 = bf16[512,512]{1,0:T(8,128)(2,1)S(1)} copy-done((bf16[512,512]{1,0:T(8,128)(2,1)S(1)}, bf16[512,512]{1,0:T(8,128)(2,1)}, u32[]{:S(2)}) %copy-start.13) | copy-done | bytes 524312
  95.4 2.7 %finish.1 = f32[512,512]{1,0:T(8,128)} custom-call(bf16[512,512]{1,0:T(8,128)(2,1)S(1)} %copy-done, bf16[512,512]{1,0:T(8,128)(2,1)S(1)} %copy-done.13, f32[512,512]{1,0:T(8,128)S(1)} %get-tuple-element.167.mine_ref, bf16[512,512]{1,0:T(8,128)(2,1)} %collective-permute-done.23.refs_0_), custom_call_target="tpu_custom_call" | custom-call | flops 1000000000 | bytes 3000000 | tf_op jit(solution)/shard_map/finish/pallas_call | solution.py:908
  98.2 1.7 %update.1 = (f32[64,4,128]{2,1,0:T(4,128)}, f32[64,128]{1,0:T(8,128)}, f32[69,128]{1,0:T(8,128)}, f32[1,1]{1,0:T(1,128)}, f32[64,4,128]{2,1,0:T(4,128)}, /*index...) custom-call(f32[32,8,128]{2,1,0:T(8,128)S(1)} %all-to-all-done.heard, ...), custom_call_target="tpu_custom_call" | custom-call | flops 100000000 | bytes 300000 | tf_op jit(solution)/shard_map/update/pallas_call | solution.py:916
  (47 shorter events, 0.2 us)
Async XLA Ops:
  0.6 0.9 copy-start.1
  1.6 0.8 copy-start.8
  2.6 9.2 %copy-start = (bf16[512,512]{1,0:T(8,128)(2,1)S(1)}, bf16[512,512]{1,0:T(8,128)(2,1)}, u32[]{:S(2)}) copy-start(bf16[512,512]{1,0:T(8,128)(2,1)} %tokens_ref.3) | copy-start | bytes 1572868
  2.7 9.2 %copy-start.12 = (bf16[512,512]{1,0:T(8,128)(2,1)S(1)}, bf16[512,512]{1,0:T(8,128)(2,1)}, u32[]{:S(2)}) copy-start(bf16[512,512]{1,0:T(8,128)(2,1)} %cot_ref.1) | copy-start | bytes 1572868
  2.7 8.3 %collective-permute-start.5 = (bf16[64,640]{1,0:T(8,128)(2,1)S(1)}, bf16[64,640]{1,0:T(8,128)(2,1)S(1)}, u32[]{:S(2)}, u32[]{:S(2)}) collective-permute-start(bf16[64,640]{1,0:T(8,128)(2,1)S(1)} %cast.1.refs_0_), channel_id=1, source_target_pairs={{0,16},{4,20},{8,24},{12,28},{16,0},{20,4},{24,8},{28,12},{1,17},{... | collective-permute-start | bytes 245768 | tf_op jit(solution)/shard_map/ppermute | solution.py:52
  6.8 15.1 %collective-permute-start.3 = (bf16[512,512]{1,0:T(8,128)(2,1)}, bf16[512,512]{1,0:T(8,128)(2,1)S(1)}, u32[]{:S(2)}, u32[]{:S(2)}) collective-permute-start(bf16[512,512]{1,0:T(8,128)(2,1)} %tokens_ref.3), channel_id=1, source_target_pairs={{0,2},{1,3},{2,0},{3,1},{4,6},{5,7},{6,4},{7,5},{8,10},{9,11},{10,... | collective-permute-start | bytes 1572872 | tf_op jit(solution)/shard_map/ppermute | solution.py:52
  11.0 10.8 %copy-start.5 = (f32[8832]{0:T(1024)S(1)}, f32[8832]{0:T(1024)}, u32[]{:S(2)}) copy-start(f32[8832]{0:T(1024)} %param.19) | copy-start | bytes 105988
  11.0 10.8 %copy-start.16 = (s32[2048]{0:T(1024)S(1)}, s32[2048]{0:T(1024)}, u32[]{:S(2)}) copy-start(s32[2048]{0:T(1024)} %param.16) | copy-start | bytes 24580
  11.0 5.4 %collective-permute-start.6 = (bf16[128,640]{1,0:T(8,128)(2,1)S(1)}, bf16[128,640]{1,0:T(8,128)(2,1)S(1)}, u32[]{:S(2)}, u32[]{:S(2)}) collective-permute-start(bf16[128,640]{1,0:T(8,128)(2,1)S(1)} %join.3), channel_id=1, source_target_pairs={{0,8},{4,12},{8,0},{12,4},{16,24},{20,28},{24,16},{28,20},{1,9},{5... | collective-permute-start | bytes 491528 | tf_op jit(solution)/shard_map/ppermute | solution.py:52
  11.8 12.6 %collective-permute-start.2 = (bf16[512,512]{1,0:T(8,128)(2,1)S(1)}, bf16[512,512]{1,0:T(8,128)(2,1)S(1)}, u32[]{:S(2)}, u32[]{:S(2)}) collective-permute-start(bf16[512,512]{1,0:T(8,128)(2,1)S(1)} %copy-done), channel_id=1, source_target_pairs={{0,1},{1,0},{2,3},{3,2},{4,5},{5,4},{6,7},{7,6},{8,9},{9,8},{10,11... | collective-permute-start | bytes 1572872 | tf_op jit(solution)/shard_map/ppermute | solution.py:52
  11.8 25.5 %collective-permute-start = (bf16[512,512]{1,0:T(8,128)(2,1)S(1)}, bf16[512,512]{1,0:T(8,128)(2,1)S(1)}, u32[]{:S(2)}, u32[]{:S(2)}) collective-permute-start(bf16[512,512]{1,0:T(8,128)(2,1)S(1)} %copy-done.12), channel_id=1, source_target_pairs={{0,1},{1,0},{2,3},{3,2},{4,5},{5,4},{6,7},{7,6},{8,9},{9,8},{10,11... | collective-permute-start | bytes 1572872 | tf_op jit(solution)/shard_map/ppermute | solution.py:52
  12.3 20.8 %collective-permute-start.1 = (bf16[512,512]{1,0:T(8,128)(2,1)S(1)}, bf16[512,512]{1,0:T(8,128)(2,1)S(1)}, u32[]{:S(2)}, u32[]{:S(2)}) collective-permute-start(bf16[512,512]{1,0:T(8,128)(2,1)S(1)} %copy-done.12), channel_id=1, source_target_pairs={{0,2},{1,3},{2,0},{3,1},{4,6},{5,7},{6,4},{7,5},{8,10},{9,11},{10,... | collective-permute-start | bytes 1572872 | tf_op jit(solution)/shard_map/ppermute | solution.py:52
  16.4 7.9 %collective-permute-start.7 = (bf16[256,640]{1,0:T(8,128)(2,1)S(1)}, bf16[256,640]{1,0:T(8,128)(2,1)S(1)}, u32[]{:S(2)}, u32[]{:S(2)}) collective-permute-start(bf16[256,640]{1,0:T(8,128)(2,1)S(1)} %join.4), channel_id=1, source_target_pairs={{0,4},{4,0},{8,12},{12,8},{16,20},{20,16},{24,28},{28,24},{1,5},{5... | collective-permute-start | bytes 983048 | tf_op jit(solution)/shard_map/ppermute | solution.py:52
  21.8 2.6 %collective-permute-start.4 = (bf16[512,512]{1,0:T(8,128)(2,1)S(1)}, bf16[512,512]{1,0:T(8,128)(2,1)S(1)}, u32[]{:S(2)}, u32[]{:S(2)}) collective-permute-start(bf16[512,512]{1,0:T(8,128)(2,1)S(1)} %collective-permute-done.3.refs_2_), channel_id=1, source_target_pairs={{0,1},{1,0},{2,3},{3,2},{4,5},{5,4},{6,7},{7,6},{8,9},{9,8},{10,11... | collective-permute-start | bytes 1572872 | tf_op jit(solution)/shard_map/ppermute | solution.py:52
  26.0 1.8 %copy-start.17 = (s32[2048]{0:T(1024)S(1)}, s32[2048]{0:T(1024)}, u32[]{:S(2)}) copy-start(s32[2048]{0:T(1024)} %param.15) | copy-start | bytes 24580
  33.2 4.2 %collective-permute-start.8 = (bf16[512,512]{1,0:T(8,128)(2,1)S(1)}, bf16[512,512]{1,0:T(8,128)(2,1)S(1)}, u32[]{:S(2)}, u32[]{:S(2)}) collective-permute-start(bf16[512,512]{1,0:T(8,128)(2,1)S(1)} %collective-permute-done.1.refs_2_.refs_6_), channel_id=1, source_target_pairs={{0,1},{1,0},{2,3},{3,2},{4,5},{5,4},{6,7},{7,6},{8,9},{9,8},{10,11... | collective-permute-start | bytes 1572872 | tf_op jit(solution)/shard_map/ppermute | solution.py:52
  39.1 4.0 %collective-permute-start.10 = (f32[8,4,256]{2,1,0:T(4,128)S(1)}, f32[8,4,256]{2,1,0:T(4,128)S(1)}, u32[]{:S(2)}, u32[]{:S(2)}) collective-permute-start(f32[8,4,256]{2,1,0:T(4,128)S(1)} %get-tuple-element.114.refs_0_), channel_id=1, source_target_pairs={{0,2},{1,3},{2,0},{3,1},{4,6},{5,7},{6,4},{7,5},{8,10},{9,11},{10,... | collective-permute-start | bytes 98312 | tf_op jit(solution)/shard_map/ppermute | solution.py:52
  40.7 3.6 %collective-permute-start.11 = (f32[8,4,256]{2,1,0:T(4,128)S(1)}, f32[8,4,256]{2,1,0:T(4,128)S(1)}, u32[]{:S(2)}, u32[]{:S(2)}) collective-permute-start(f32[8,4,256]{2,1,0:T(4,128)S(1)} %get-tuple-element.114.refs_0_), channel_id=1, source_target_pairs={{0,3},{1,2},{2,1},{3,0},{4,7},{5,6},{6,5},{7,4},{8,11},{9,10},{10,... | collective-permute-start | bytes 98312 | tf_op jit(solution)/shard_map/ppermute | solution.py:52
  40.7 3.6 %collective-permute-start.9 = (f32[8,4,256]{2,1,0:T(4,128)S(1)}, f32[8,4,256]{2,1,0:T(4,128)S(1)}, u32[]{:S(2)}, u32[]{:S(2)}) collective-permute-start(f32[8,4,256]{2,1,0:T(4,128)S(1)} %get-tuple-element.114.refs_0_), channel_id=1, source_target_pairs={{0,1},{1,0},{2,3},{3,2},{4,5},{5,4},{6,7},{7,6},{8,9},{9,8},{10,11... | collective-permute-start | bytes 98312 | tf_op jit(solution)/shard_map/ppermute | solution.py:52
  45.1 2.7 %collective-permute-start.12 = (bf16[2,512,512]{2,1,0:T(8,128)(2,1)S(1)}, bf16[2,512,512]{2,1,0:T(8,128)(2,1)S(1)}, u32[]{:S(2)}, u32[]{:S(2)}) collective-permute-start(bf16[2,512,512]{2,1,0:T(8,128)(2,1)S(1)} %get-tuple-element.117), channel_id=1, source_target_pairs={{0,1},{1,0},{2,3},{3,2},{4,5},{5,4},{6,7},{7,6},{8,9},{9,8},{10,11... | collective-permute-start | bytes 3145736 | tf_op jit(solution)/shard_map/ppermute | solution.py:52
  48.1 17.2 %collective-permute-start.14 = (bf16[512,512]{1,0:T(8,128)(2,1)S(1)}, bf16[512,512]{1,0:T(8,128)(2,1)S(1)}, u32[]{:S(2)}, u32[]{:S(2)}) collective-permute-start(bf16[512,512]{1,0:T(8,128)(2,1)S(1)} %get-tuple-element.136), channel_id=1, source_target_pairs={{0,2},{1,3},{2,0},{3,1},{4,6},{5,7},{6,4},{7,5},{8,10},{9,11},{10,... | collective-permute-start | bytes 1572872 | tf_op jit(solution)/shard_map/ppermute | solution.py:52
  53.1 12.2 %collective-permute-start.13 = (bf16[4,64,384]{2,1,0:T(8,128)(2,1)S(1)}, bf16[4,64,384]{2,1,0:T(8,128)(2,1)S(1)}, u32[]{:S(2)}, u32[]{:S(2)}) collective-permute-start(bf16[4,64,384]{2,1,0:T(8,128)(2,1)S(1)} %get-tuple-element.135), channel_id=1, source_target_pairs={{0,4},{4,0},{8,12},{12,8},{16,20},{20,16},{24,28},{28,24},{1,5},{5... | collective-permute-start | bytes 589832 | tf_op jit(solution)/shard_map/ppermute | solution.py:52
  65.3 1.8 %copy-start.14 = (bf16[512,512]{1,0:T(8,128)(2,1)}, bf16[512,512]{1,0:T(8,128)(2,1)S(1)}, u32[]{:S(2)}) copy-start(bf16[512,512]{1,0:T(8,128)(2,1)S(1)} %collective-permute-done.14.refs_1_) | copy-start | bytes 1572868
  65.3 7.2 %collective-permute-start.15 = (bf16[4,80,256]{2,1,0:T(8,128)(2,1)S(1)}, bf16[4,80,256]{2,1,0:T(8,128)(2,1)S(1)}, u32[]{:S(2)}, u32[]{:S(2)}) collective-permute-start(bf16[4,80,256]{2,1,0:T(8,128)(2,1)S(1)} %get-tuple-element.138), channel_id=1, source_target_pairs={{0,4},{4,0},{8,12},{12,8},{16,20},{20,16},{24,28},{28,24},{1,5},{5... | collective-permute-start | bytes 491528 | tf_op jit(solution)/shard_map/ppermute | solution.py:52
  67.2 5.4 %collective-permute-start.16 = (bf16[2,512,512]{2,1,0:T(8,128)(2,1)S(1)}, bf16[2,512,512]{2,1,0:T(8,128)(2,1)S(1)}, u32[]{:S(2)}, u32[]{:S(2)}) collective-permute-start(bf16[2,512,512]{2,1,0:T(8,128)(2,1)S(1)} %get-tuple-element.146), channel_id=1, source_target_pairs={{0,1},{1,0},{2,3},{3,2},{4,5},{5,4},{6,7},{7,6},{8,9},{9,8},{10,11... | collective-permute-start | bytes 3145736 | tf_op jit(solution)/shard_map/ppermute | solution.py:52
  67.3 9.6 %collective-permute-start.20 = (bf16[64,384]{1,0:T(8,128)(2,1)S(1)}, bf16[64,384]{1,0:T(8,128)(2,1)S(1)}, u32[]{:S(2)}, u32[]{:S(2)}) collective-permute-start(bf16[64,384]{1,0:T(8,128)(2,1)S(1)} %get-tuple-element.157), channel_id=1, source_target_pairs={{0,16},{4,20},{8,24},{12,28},{16,0},{20,4},{24,8},{28,12},{1,17},{... | collective-permute-start | bytes 147464 | tf_op jit(solution)/shard_map/ppermute | solution.py:52
  71.0 8.6 %collective-permute-start.21 = (bf16[64,384]{1,0:T(8,128)(2,1)S(1)}, bf16[64,384]{1,0:T(8,128)(2,1)S(1)}, u32[]{:S(2)}, u32[]{:S(2)}) collective-permute-start(bf16[64,384]{1,0:T(8,128)(2,1)S(1)} %get-tuple-element.158), channel_id=1, source_target_pairs={{0,8},{4,12},{8,0},{12,4},{16,24},{20,28},{24,16},{28,20},{1,9},{5... | collective-permute-start | bytes 147464 | tf_op jit(solution)/shard_map/ppermute | solution.py:52
  72.4 7.2 %collective-permute-start.22 = (bf16[64,384]{1,0:T(8,128)(2,1)S(1)}, bf16[64,384]{1,0:T(8,128)(2,1)S(1)}, u32[]{:S(2)}, u32[]{:S(2)}) collective-permute-start(bf16[64,384]{1,0:T(8,128)(2,1)S(1)} %get-tuple-element.159), channel_id=1, source_target_pairs={{0,24},{4,28},{8,16},{12,20},{16,8},{20,12},{24,0},{28,4},{1,25},{... | collective-permute-start | bytes 147464 | tf_op jit(solution)/shard_map/ppermute | solution.py:52
  72.6 9.1 %collective-permute-start.17 = (bf16[80,256]{1,0:T(8,128)(2,1)S(1)}, bf16[80,256]{1,0:T(8,128)(2,1)S(1)}, u32[]{:S(2)}, u32[]{:S(2)}) collective-permute-start(bf16[80,256]{1,0:T(8,128)(2,1)S(1)} %get-tuple-element.147), channel_id=1, source_target_pairs={{0,16},{4,20},{8,24},{12,28},{16,0},{20,4},{24,8},{28,12},{1,17},{... | collective-permute-start | bytes 122888 | tf_op jit(solution)/shard_map/ppermute | solution.py:52
  74.8 6.9 %collective-permute-start.18 = (bf16[80,256]{1,0:T(8,128)(2,1)S(1)}, bf16[80,256]{1,0:T(8,128)(2,1)S(1)}, u32[]{:S(2)}, u32[]{:S(2)}) collective-permute-start(bf16[80,256]{1,0:T(8,128)(2,1)S(1)} %get-tuple-element.148), channel_id=1, source_target_pairs={{0,8},{4,12},{8,0},{12,4},{16,24},{20,28},{24,16},{28,20},{1,9},{5... | collective-permute-start | bytes 122888 | tf_op jit(solution)/shard_map/ppermute | solution.py:52
  76.9 5.8 %collective-permute-start.19 = (bf16[80,256]{1,0:T(8,128)(2,1)S(1)}, bf16[80,256]{1,0:T(8,128)(2,1)S(1)}, u32[]{:S(2)}, u32[]{:S(2)}) collective-permute-start(bf16[80,256]{1,0:T(8,128)(2,1)S(1)} %get-tuple-element.149), channel_id=1, source_target_pairs={{0,24},{4,28},{8,16},{12,20},{16,8},{20,12},{24,0},{28,4},{1,25},{... | collective-permute-start | bytes 122888 | tf_op jit(solution)/shard_map/ppermute | solution.py:52
  80.5 13.8 %collective-permute-start.23 = (bf16[512,512]{1,0:T(8,128)(2,1)}, bf16[512,512]{1,0:T(8,128)(2,1)}, u32[]{:S(2)}, u32[]{:S(2)}) collective-permute-start(bf16[512,512]{1,0:T(8,128)(2,1)} %get-tuple-element.163), channel_id=1, source_target_pairs={{0,2},{1,3},{2,0},{3,1},{4,6},{5,7},{6,4},{7,5},{8,10},{9,11},{10,... | collective-permute-start | bytes 1572872 | tf_op jit(solution)/shard_map/ppermute | solution.py:52
  83.5 14.6 %copy-start.2 = (f32[64,4,128]{2,1,0:T(4,128)S(1)}, f32[64,4,128]{2,1,0:T(4,128)}, u32[]{:S(2)}) copy-start(f32[64,4,128]{2,1,0:T(4,128)} %refs_0_.5) | copy-start | bytes 393220
  83.5 14.6 %copy-start.3 = (f32[64,4,128]{2,1,0:T(4,128)S(1)}, f32[64,4,128]{2,1,0:T(4,128)}, u32[]{:S(2)}) copy-start(f32[64,4,128]{2,1,0:T(4,128)} %refs_1_.1) | copy-start | bytes 393220
  83.5 14.6 %copy-start.4 = (f32[64,4,128]{2,1,0:T(4,128)S(1)}, f32[64,4,128]{2,1,0:T(4,128)}, u32[]{:S(2)}) copy-start(f32[64,4,128]{2,1,0:T(4,128)} %refs_2_.1) | copy-start | bytes 393220
  83.5 14.6 %copy-start.6 = (f32[8832]{0:T(1024)S(1)}, f32[8832]{0:T(1024)}, u32[]{:S(2)}) copy-start(f32[8832]{0:T(1024)} %param.24) | copy-start | bytes 105988
  83.5 14.6 %copy-start.7 = (f32[8832]{0:T(1024)S(1)}, f32[8832]{0:T(1024)}, u32[]{:S(2)}) copy-start(f32[8832]{0:T(1024)} %param.25) | copy-start | bytes 105988
  83.5 14.6 %copy-start.9 = (f32[128,64]{0,1:T(8,128)S(1)}, f32[128,64]{0,1:T(8,128)}, u32[]{:S(2)}) copy-start(f32[128,64]{0,1:T(8,128)} %param.18) | copy-start | bytes 98308
  83.5 14.6 %copy-start.10 = (f32[128,64]{0,1:T(8,128)S(1)}, f32[128,64]{0,1:T(8,128)}, u32[]{:S(2)}) copy-start(f32[128,64]{0,1:T(8,128)} %param.22) | copy-start | bytes 98308
  83.5 14.6 %copy-start.11 = (f32[128,64]{0,1:T(8,128)S(1)}, f32[128,64]{0,1:T(8,128)}, u32[]{:S(2)}) copy-start(f32[128,64]{0,1:T(8,128)} %param.23) | copy-start | bytes 98308
  83.5 14.6 %all-to-all-start = ((f32[32,8,128]{2,1,0:T(8,128)}), f32[32,8,128]{2,1,0:T(8,128)S(1)}, u32[]{:S(2)}, u32[]{:S(2)}) async-start(f32[32,8,128]{2,1,0:T(8,128)} %get-tuple-element.164), calls=%async_computation | async-start | bytes 262144 | tf_op jit(solution)/shard_map/all_to_all | solution.py:904
  87.1 1.0 %copy-start.15 = (bf16[512,512]{1,0:T(8,128)(2,1)S(1)}, bf16[512,512]{1,0:T(8,128)(2,1)}, u32[]{:S(2)}) copy-start(bf16[512,512]{1,0:T(8,128)(2,1)} %copy-done.14) | copy-start | bytes 1572868
  94.3 1.0 %copy-start.13 = (bf16[512,512]{1,0:T(8,128)(2,1)S(1)}, bf16[512,512]{1,0:T(8,128)(2,1)}, u32[]{:S(2)}) copy-start(bf16[512,512]{1,0:T(8,128)(2,1)} %cot_ref.1) | copy-start | bytes 1572868

commit v7 on v6

--- a/solution.py
+++ b/solution.py
@@ -111,13 +111,13 @@
     return [mine] + [swap(leaving[k - 1], "dp", k * low) for k in order]
 
 
-def fold_cores(keep, crossed):
+def fold_cores(keep, crossed, cuts=1):
     chips, rows, columns = keep.shape
     return call(
         functools.partial(rows_kernel, chips),
         "rows",
         [VMEM] * 2,
-        [((rows, columns), f32, VMEM)] + [((rows, columns), bf16, VMEM)] * (chips - 1),
+        [((rows, columns), f32, VMEM)] + [((rows // cuts, columns), bf16, VMEM)] * (cuts * (chips - 1)),
         [],
         0.1,
     )(keep, crossed)
@@ -316,22 +316,28 @@
     kx_ref, qs_ref, trow_ref, vt_ref, pos_ref, ss_ref, attn_ref = refs[:7]
     if first:
         attn_ref[:first] = before_ref[...]
-    for i in range(first, last):
-        queries = query_columns(qs_ref[i], trow_ref[i], heads)
-        scores = [dot(kx_ref[j], queries) for j in range(i + 1)]
-        weights = []
-        for j in range(i + 1):
-            h = masked(scores[j], pos_ref[i - j], ss_ref[:, i * TILE : (i + 1) * TILE], j, heads)
+    tiles = [(i, j) for i in range(first, last) for j in range(i + 1)]
+    scores, weights = {}, {}
+    for t in range(len(tiles) + 3):
+        if t < len(tiles):
+            i, j = tiles[t]
+            if j == 0:
+                queries = query_columns(qs_ref[i], trow_ref[i], heads)
+            scores[t] = dot(kx_ref[j], queries)
+        if 0 <= t - 1 < len(tiles):
+            i, j = tiles[t - 1]
+            h = masked(scores.pop(t - 1), pos_ref[i - j], ss_ref[:, i * TILE : (i + 1) * TILE], j, heads)
             w, slope = weights_and_slope(h)
-            weights.append(w.astype(bf16))
+            weights[t - 1] = w.astype(bf16)
             if kept:
-                at = (i * (i + 1) - first * (first + 1)) // 2 + j
-                refs[7][at] = weights[j]
-                refs[8][at] = slope.astype(bf16)
-        total = dot(vt_ref[0], weights[0])
-        for j in range(1, i + 1):
-            total = total + dot(vt_ref[j], weights[j])
-        attn_ref[i] = own_rows(total, heads)
+                refs[7][t - 1] = weights[t - 1]
+                refs[8][t - 1] = slope.astype(bf16)
+        if t >= 3:
+            i, j = tiles[t - 3]
+            more = dot(vt_ref[j], weights.pop(t - 3))
+            total = more if j == 0 else total + more
+            if i == j:
+                attn_ref[i] = own_rows(total, heads)
 
 
 def gate_kernel(n_head, *refs):
@@ -489,7 +495,7 @@
     def add(ref, at, value, first):
         ref[at] = value if first else ref[at] + value
 
-    for t in range(len(tiles) + 2):
+    for t in range(len(tiles) + 3):
         if t < len(tiles):
             i, j = tiles[t]
             if j == 0:
@@ -507,9 +513,9 @@
             ds = back * slope
             grads[t - 1] = ds.astype(bf16)
             add(posg_ref, i - j, sum(ds[:, g * TILE : (g + 1) * TILE] for g in range(heads)), i == nb - 1)
-        if t >= 2:
-            i, j = tiles[t - 2]
-            low = grads.pop(t - 2)
+        if t >= 3:
+            i, j = tiles[t - 3]
+            low = grads.pop(t - 3)
             if j == 0:
                 times = jnp.concatenate([kx_ref[i, :, :NTB]] * heads, axis=0)
                 q = jnp.concatenate([times, own_lanes(q_ref[i], heads)], axis=1)
@@ -588,7 +594,8 @@
     refs[-1][...] = total.astype(bf16)
 
 
-def finish_kernel(tokens_ref, cot_ref, mine_ref, *refs):
+def finish_kernel(part, *refs):
+    tokens_ref, cot_ref, mine_ref, *refs = refs[part:]
     x = tokens_ref[...].astype(f32)
     x = x - jnp.sum(x, axis=1, keepdims=True) / D
     scale = lax.rsqrt(jnp.sum(x * x, axis=1, keepdims=True) / D + norm_epsilon)
@@ -608,7 +615,10 @@
         if k == 0:
             mine_ref[...] = total
         else:
-            leaving[k - 1][...] = total.astype(bf16)
+            rows = leaving[0].shape[0]
+            cuts = total.shape[0] // rows
+            for c in range(cuts):
+                leaving[(k - 1) * cuts + c][...] = total[c * rows : (c + 1) * rows].astype(bf16)
 
 
 def collect_kernel(high, extra, *refs):
@@ -685,7 +695,7 @@
     update(lambda k: state[6 + k][...], put_small, small, rate_small, 0.0)
 
 
-def call(kernel, name, in_specs, outs, scratch, us, room=16):
+def call(kernel, name, in_specs, outs, scratch, us, room=16, **more):
     return pl.pallas_call(
         kernel,
         out_shape=[jax.ShapeDtypeStruct(shape, dtype) for shape, dtype, _ in outs],
@@ -695,6 +705,7 @@
         compiler_params=pltpu.CompilerParams(vmem_limit_bytes=room * 2**20 * max(1, lax.axis_size("head") // 4)),
         cost_estimate=pl.CostEstimate(flops=int(us * 1e9), bytes_accessed=int(us * 3e6), transcendentals=0),
         name=name,
+        **more,
     )
 
 
@@ -888,8 +899,9 @@
     (early,) = call(
         sum_kernel, "sum", [VMEM] * high, [((rows_here, 3 * width), f32, VMEM)], [], 14
     )(*early_blocks)
-    mine, *leaving = fold_cores(keep, after(crossed, late_blocks[0]))
-    arrived = [swap(leaving[k - 1], "head", 2 * k) for k in range(1, chips)]
+    mine, *leaving = fold_cores(keep, after(crossed, late_blocks[0]), 2)
+    half = here // 2
+    arrived = [[swap(leaving[2 * k - 2 + part], "head", 2 * k) for k in range(1, chips)] for part in range(2)]
     n_all = n_dp * n_head
     grads_shape = ((rows_here, 5 * width), f32)
     grads, message = call(
@@ -905,9 +917,21 @@
     (mixed,) = call(
         mix_kernel, "mix", [VMEM] * (2 + chips), [((here, D), bf16, VMEM)], [], 1
     )(tokens, small_rows, after(branch, message), *received)
-    (input_grad,) = call(
-        finish_kernel, "finish", [VMEM] * (2 + chips), [((here, D), f32, VMEM)], [], 1
-    )(tokens, cotangent, mine, *arrived)
+    input_grad = None
+    for part in range(2):
+        rows = pl.BlockSpec((half, D), lambda i, part=part: (part, 0))
+        alone = pl.BlockSpec((half, D), lambda i: (0, 0))
+        before = [] if part == 0 else [input_grad]
+        (input_grad,) = call(
+            functools.partial(finish_kernel, part),
+            "finish",
+            [pl.BlockSpec(memory_space=pl.ANY)] * len(before) + [rows] * 3 + [alone] * (chips - 1),
+            [((here, D), f32, rows)],
+            [],
+            1,
+            grid=(1,),
+            input_output_aliases={0: 0} if before else {},
+        )(*before, tokens, cotangent, mine, *arrived[part])
     heard = after(heard, input_grad)
     state = [proj_weight, proj_mean, proj_square, out_weight.T, out_mean.T, out_square.T]
     state += [x.reshape(-1, 128) for x in (small_params, small_mean, small_square)]

time: 100 us -> 97 us (0.970)
  waiting for transfers between devices: 19.4 us -> 16.4 us
  Pallas kernels: 42.8 us -> 41.6 us
    ppermute x24 -> x25, waiting for transfers between devices: 19.4 us -> 14.9 us  [swap(): return lax.ppermute(x, axis, [(i, i ^ k) for i in range(n)])]
    all_to_all x1, waiting for transfers between devices: 0.01 us -> 1.5 us  [shards(): heard = lax.all_to_all(message, ('dp', 'head'), 0, 0, tiled=True)]
    pallas_call x2, Pallas kernels: 8.87 us -> 7.87 us  [attend(): call(functools.partial(attend_kernel, heads, first, last, kept), 'attend'...]
    pallas_call x1 -> x2, Pallas kernels: 2.73 us -> 3.39 us  [shards(): call(functools.partial(finish_kernel, part), 'finish', [pl.BlockSpec(memo...]
    ppermute x24 -> x25, starting transfers between devices: 29.2 us -> 29.5 us  [swap(): return lax.ppermute(x, axis, [(i, i ^ k) for i in range(n)])]
    unnamed x36 -> x38, local copies, waits for them, and re-layouts: 3.81 us -> 4 us
  transfers between devices with their start and end apart: 25 -> 26, of which waited for: 8 -> 9; matrix products, arithmetic and copies ran while one was open for 0% -> 0% of each run, Pallas kernels for 38% -> 38%
where the time goes in v7:
time: 97 us; the launch traced here: 96.6 us
  Pallas kernels  41.6 us (43%)
  starting transfers between devices  33.5 us (35%)
  waiting for transfers between devices  16.4 us (17%)
  local copies, waits for them, and re-layouts  4 us (4%)
  between operations  1.15 us (1%)
    ppermute x25, starting transfers between devices, swap(): return lax.ppermute(x, axis, [(i, i ^ k) for i in range(n)])  29.5 us
    ppermute x25, waiting for transfers between devices, swap(): return lax.ppermute(x, axis, [(i, i ^ k) for i in range(n)])  14.9 us
    pallas_call x1, Pallas kernels, shards(): call(functools.partial(backward_kernel, heads, n_dp, extra, kept), 'backw...  10.6 us
    pallas_call x2, Pallas kernels, attend(): call(functools.partial(attend_kernel, heads, first, last, kept), 'attend'...  7.87 us
    pallas_call x1, Pallas kernels, shards(): call(functools.partial(values_kernel, heads, kept), 'values', [VMEM] * (l...  4.32 us
    unnamed x38, local copies, waits for them, and re-layouts  4 us
    all_to_all x1, starting transfers between devices, shards(): heard = lax.all_to_all(message, ('dp', 'head'), 0, 0, tiled=True)  3.98 us
    pallas_call x2, Pallas kernels, shards(): call(functools.partial(finish_kernel, part), 'finish', [pl.BlockSpec(memo...  3.39 us
  transfers between devices with their start and end apart: 26, of which 9 were waited for; matrix products, arithmetic and copies ran while one was open for 0% of the time, Pallas kernels for 38%

profile of v7, /device:TPU:0, one launch (start us, length us, event | category | flops | bytes accessed | tf_op | source)
XLA Modules:
  0.0 96.6 jit_solution(2012492811722498011)
XLA Ops:
  0.6 0.0 copy-start.2
  0.7 0.9 copy-done.2
  1.6 0.8 copy-done.9
  2.3 0.3 cast.1.refs_0_
  2.6 0.0 copy-start
  2.7 4.1 %collective-permute-start.5 = (bf16[64,640]{1,0:T(8,128)(2,1)S(1)}, bf16[64,640]{1,0:T(8,128)(2,1)S(1)}, u32[]{:S(2)}, u32[]{:S(2)}) collective-permute-start(bf16[64,640]{1,0:T(8,128)(2,1)S(1)} %cast.1.refs_0_), channel_id=1, source_target_pairs={{0,16},{4,20},{8,24},{12,28},{16,0},{20,4},{24,8},{28,12},{1,17},{... | collective-permute-start | bytes 245768 | tf_op jit(solution)/shard_map/ppermute | solution.py:52
  6.8 1.5 %collective-permute-start.3 = (bf16[512,512]{1,0:T(8,128)(2,1)}, bf16[512,512]{1,0:T(8,128)(2,1)S(1)}, u32[]{:S(2)}, u32[]{:S(2)}) collective-permute-start(bf16[512,512]{1,0:T(8,128)(2,1)} %refs_1_.4), channel_id=1, source_target_pairs={{0,2},{1,3},{2,0},{3,1},{4,6},{5,7},{6,4},{7,5},{8,10},{9,11},{10,... | collective-permute-start | bytes 1572872 | tf_op jit(solution)/shard_map/ppermute | solution.py:52
  8.3 2.7 %collective-permute-done.5.refs_1_ = bf16[64,640]{1,0:T(8,128)(2,1)S(1)} collective-permute-done((bf16[64,640]{1,0:T(8,128)(2,1)S(1)}, bf16[64,640]{1,0:T(8,128)(2,1)S(1)}, u32[]{:S(2)}, u32[]{:S(2)}) %collective-permute-start.5) | collective-permute-done | bytes 81952 | tf_op jit(solution)/shard_map/ppermute | solution.py:52
  11.0 0.8 collective-permute-start.6
  11.8 0.5 collective-permute-start
  12.3 1.5 %collective-permute-start.1 = (bf16[512,512]{1,0:T(8,128)(2,1)S(1)}, bf16[512,512]{1,0:T(8,128)(2,1)S(1)}, u32[]{:S(2)}, u32[]{:S(2)}) collective-permute-start(bf16[512,512]{1,0:T(8,128)(2,1)S(1)} %copy-done.1), channel_id=1, source_target_pairs={{0,2},{1,3},{2,0},{3,1},{4,6},{5,7},{6,4},{7,5},{8,10},{9,11},{10,... | collective-permute-start | bytes 1572872 | tf_op jit(solution)/shard_map/ppermute | solution.py:52
  13.8 2.6 %collective-permute-done.6.refs_2_ = bf16[128,640]{1,0:T(8,128)(2,1)S(1)} collective-permute-done((bf16[128,640]{1,0:T(8,128)(2,1)S(1)}, bf16[128,640]{1,0:T(8,128)(2,1)S(1)}, u32[]{:S(2)}, u32[]{:S(2)}) %collective-permute-start.6) | collective-permute-done | bytes 163872 | tf_op jit(solution)/shard_map/ppermute | solution.py:52
  16.4 1.8 %collective-permute-start.7 = (bf16[256,640]{1,0:T(8,128)(2,1)S(1)}, bf16[256,640]{1,0:T(8,128)(2,1)S(1)}, u32[]{:S(2)}, u32[]{:S(2)}) collective-permute-start(bf16[256,640]{1,0:T(8,128)(2,1)S(1)} %join.4), channel_id=1, source_target_pairs={{0,4},{4,0},{8,12},{12,8},{16,20},{20,16},{24,28},{28,24},{1,5},{5... | collective-permute-start | bytes 983048 | tf_op jit(solution)/shard_map/ppermute | solution.py:52
  18.2 3.6 %collective-permute-done.3.refs_2_ = bf16[512,512]{1,0:T(8,128)(2,1)S(1)} collective-permute-done((bf16[512,512]{1,0:T(8,128)(2,1)}, bf16[512,512]{1,0:T(8,128)(2,1)S(1)}, u32[]{:S(2)}, u32[]{:S(2)}) %collective-permute-start.3) | collective-permute-done | bytes 524320 | tf_op jit(solution)/shard_map/ppermute | solution.py:52
  21.8 2.5 %prepare.1 = (f32[8,256,256]{2,1,0:T(8,128)S(1)}, bf16[8,256,128]{2,1,0:T(8,128)(2,1)S(1)}, bf16[8,128,256]{2,1,0:T(8,128)(2,1)S(1)}, bf16[8,128,256]{2,1,0:T(8,128)(2,1)S(1)}) custom-call(s32[1,2048]{1,0:T(1,128)S(1)} %bitcast.26, f32[69,128]{1,0:T(8,128)S(1)} %bitcast.17), custom_call_target="tpu_custom_call" | custom-call | flops 5000000000 | bytes 15000000 | tf_op jit(solution)/shard_map/prepare/pallas_call | solution.py:760
  24.4 1.3 %normalize.1.refs_0_.refs_5_.refs_11_.refs_8_.refs_4_ = bf16[8,256,512]{2,1,0:T(8,128)(2,1)S(1)} custom-call(bf16[512,512]{1,0:T(8,128)(2,1)S(1)} %copy-done, bf16[512,512]{1,0:T(8,128)(2,1)S(1)} %collective-permute-done.2.refs_1_, bf16[512,512]{1,0:T(8,128)(2,1)S(1)} %collective-permute-done.3.refs_2_, bf16[512,512]{1,0:T(8,128)(2,1)S(1)} %collective-permute-done.4.refs_3_), custom_call_target="tpu_custom_call" | custom-call | flops 1000000000 | bytes 3000000 | tf_op jit(solution)/shard_map/normalize/pallas_call | solution.py:783
  25.7 0.3 assemble.1.refs_1_.refs_6_.wt_ref
  26.0 0.0 copy-start.18
  26.0 1.8 %project.1 = (bf16[8,384,256]{2,1,0:T(8,128)(2,1)S(1)}, bf16[8,256,256]{2,1,0:T(8,128)(2,1)S(1)}, bf16[8,256,256]{2,1,0:T(8,128)(2,1)S(1)}, bf16[8,128,256]{2,1,...) custom-call(bf16[8,256,512]{2,1,0:T(8,128)(2,1)S(1)} %normalize.1.re, ...), custom_call_target="tpu_custom_call" | custom-call | flops 5000000000 | bytes 15000000 | tf_op jit(solution)/shard_map/project/pallas_call | solution.py:793
  27.9 4.5 %attend.2 = (f32[6,128,256]{2,1,0:T(8,128)S(1)}, bf16[21,256,512]{2,1,0:T(8,128)(2,1)S(1)}, bf16[21,256,512]{2,1,0:T(8,128)(2,1)S(1)}) custom-call(bf16[8,256,256]{2,1,0:T(8,128)(2,1)S(1)} %get-tuple-element.106.refs_0_.refs_1_.refs_2_, bf16[8,128,256]{2,1,0:T(8,128)(2,1)S(1)} %get-tuple-element.107.refs_1_.refs_2_, ...), custom_call_target="tpu_custom_call" | custom-call | flops 8000000000 | bytes 24000000 | tf_op jit(solution)/shard_map/attend/pallas_call | solution.py:806
  32.4 0.6 collective-permute-start.8
  32.9 3.4 %attend.3 = (f32[8,128,256]{2,1,0:T(8,128)S(1)}, bf16[15,256,512]{2,1,0:T(8,128)(2,1)S(1)}, bf16[15,256,512]{2,1,0:T(8,128)(2,1)S(1)}) custom-call(f32[6,128,256]{2,1,0:T(8,128)S(1)} %get-tuple-element.113.refs_0_, bf16[8,256,256]{2,1,0:T(8,128)(2,1)S(1)} %get-tuple-element.106.refs_0_.refs_1_.refs_2_, ...), custom_call_target="tpu_custom_call" | custom-call | flops 8000000000 | bytes 24000000 | tf_op jit(solution)/shard_map/attend/pallas_call | solution.py:806
  36.3 1.6 %gate.1 = (f32[8,128,256]{2,1,0:T(8,128)S(1)}, f32[8,128,256]{2,1,0:T(8,128)S(1)}, f32[8,4,256]{2,1,0:T(4,128)S(1)}, f32[1,512]{1,0:T(1,128)S(1)}) custom-call(bf16[512,512]{1,0:T(8,128)(2,1)S(1)} %copy-done.1, bf16[512,512]{1,0:T(8,128)(2,1)S(1)} %collective-permute-done.refs_1_.refs_5_, bf16[512,512]{1,0:T(8,128)(2,1)S(1)} %collective-permute-done.1.refs_2_.refs_6_, ...), custom_call_target="tpu_custom_call" | custom-call | flops 5000000000 | bytes 15000000 | tf_op jit(solution)/shard_map/gate/pallas_call | solution.py:823
  38.0 1.7 %collective-permute-start.10 = (f32[8,4,256]{2,1,0:T(4,128)S(1)}, f32[8,4,256]{2,1,0:T(4,128)S(1)}, u32[]{:S(2)}, u32[]{:S(2)}) collective-permute-start(f32[8,4,256]{2,1,0:T(4,128)S(1)} %get-tuple-element.115.refs_0_), channel_id=1, source_target_pairs={{0,2},{1,3},{2,0},{3,1},{4,6},{5,7},{6,4},{7,5},{8,10},{9,11},{10,... | collective-permute-start | bytes 98312 | tf_op jit(solution)/shard_map/ppermute | solution.py:52
  39.7 0.6 collective-permute-start.9
  40.4 1.8 %collective-permute-done.10.refs_2_ = f32[8,4,256]{2,1,0:T(4,128)S(1)} collective-permute-done((f32[8,4,256]{2,1,0:T(4,128)S(1)}, f32[8,4,256]{2,1,0:T(4,128)S(1)}, u32[]{:S(2)}, u32[]{:S(2)}) %collective-permute-start.10) | collective-permute-done | bytes 32800 | tf_op jit(solution)/shard_map/ppermute | solution.py:52
  42.1 1.2 %collective-permute-done.11.refs_3_ = f32[8,4,256]{2,1,0:T(4,128)S(1)} collective-permute-done((f32[8,4,256]{2,1,0:T(4,128)S(1)}, f32[8,4,256]{2,1,0:T(4,128)S(1)}, u32[]{:S(2)}, u32[]{:S(2)}) %collective-permute-start.11) | collective-permute-done | bytes 32800 | tf_op jit(solution)/shard_map/ppermute | solution.py:52
  43.3 0.8 branch.1
  44.1 0.1 collective-permute-start.12
  44.2 1.3 %middle.1 = (bf16[8,256,128]{2,1,0:T(8,128)(2,1)S(1)}, bf16[8,128,256]{2,1,0:T(8,128)(2,1)S(1)}, bf16[8,256,128]{2,1,0:T(8,128)(2,1)S(1)}, f32[256,512]{1,0:T(8,128)S(1)}) custom-call(f32[8,4,256]{2,1,0:T(4,128)S(1)} %get-tuple-element.115.refs_0_, f32[8,4,256]{2,1,0:T(4,128)S(1)} %collective-permute-done.9.refs_1_, ...), custom_call_target="tpu_custom_call" | custom-call | flops 6000000000 | bytes 18000000 | tf_op jit(solution)/shard_map/middle/pallas_call | solution.py:839
  45.5 1.3 %collective-permute-done.12.crossed_ref = bf16[2,512,512]{2,1,0:T(8,128)(2,1)S(1)} collective-permute-done((bf16[2,512,512]{2,1,0:T(8,128)(2,1)S(1)}, bf16[2,512,512]{2,1,0:T(8,128)(2,1)S(1)}, u32[]{:S(2)}, u32[]{:S(2)}) %collective-permute-start.12) | collective-permute-done | bytes 1048608 | tf_op jit(solution)/shard_map/ppermute | solution.py:52
  46.9 0.2 rows.2
  47.1 0.7 collective-permute-start.14
  47.8 4.3 %values.1 = (bf16[8,256,128]{2,1,0:T(8,128)(2,1)S(1)}, bf16[4,64,384]{2,1,0:T(8,128)(2,1)S(1)}, bf16[4,64,384]{2,1,0:T(8,128)(2,1)S(1)}) custom-call(bf16[21,256,512]{2,1,0:T(8,128)(2,1)S(1)} %get-tuple-element.132.refs_0_, bf16[15,256,512]{2,1,0:T(8,128)(2,1)S(1)} %get-tuple-element.133.refs_1_, bf16[8,256,128]{2,1,0:T(8,128)(2,1)S(1)} %get-tuple-element.134.refs_2_, ...), custom_call_target="tpu_custom_call" | custom-call | flops 12000000000 | bytes 36000000 | tf_op jit(solution)/shard_map/values/pallas_call | solution.py:855
  52.1 1.6 %collective-permute-start.13 = (bf16[4,64,384]{2,1,0:T(8,128)(2,1)S(1)}, bf16[4,64,384]{2,1,0:T(8,128)(2,1)S(1)}, u32[]{:S(2)}, u32[]{:S(2)}) collective-permute-start(bf16[4,64,384]{2,1,0:T(8,128)(2,1)S(1)} %get-tuple-element.136), channel_id=1, source_target_pairs={{0,4},{4,0},{8,12},{12,8},{16,20},{20,16},{24,28},{28,24},{1,5},{5... | collective-permute-start | bytes 589832 | tf_op jit(solution)/shard_map/ppermute | solution.py:52
  53.7 10.6 %backward.1 = (bf16[8,256,256]{2,1,0:T(8,128)(2,1)S(1)}, bf16[4,80,256]{2,1,0:T(8,128)(2,1)S(1)}, bf16[4,80,256]{2,1,0:T(8,128)(2,1)S(1)}) custom-call(bf16[21,256,512]{2,1,0:T(8,128)(2,1)S(1)} %get-tuple-element.120.refs_0_, bf16[15,256,512]{2,1,0:T(8,128)(2,1)S(1)} %get-tuple-element.121.refs_1_, ...), custom_call_target="tpu_custom_call" | custom-call | flops 2000000000 | bytes 6000000 | tf_op jit(solution)/shard_map/backward/pallas_call | solution.py:868
  64.4 0.5 collective-permute-start.15
  64.9 1.3 %input_rows.1 = (bf16[2,512,512]{2,1,0:T(8,128)(2,1)S(1)}, bf16[2,512,512]{2,1,0:T(8,128)(2,1)S(1)}) custom-call(bf16[8,256,256]{2,1,0:T(8,128)(2,1)S(1)} %get-tuple-element.144.gp_ref, bf16[8,256,128]{2,1,0:T(8,128)(2,1)S(1)} %get-tuple-element.145.gun_ref, bf16[8,256,128]{2,1,0:T(8,128)(2,1)S(1)} %get-tuple-element.146.gpv_ref, ...), custom_call_target="tpu_custom_call" | custom-call | flops 4000000000 | bytes 12000000 | tf_op jit(solution)/shard_map/input_rows/pallas_call | solution.py:888
  66.2 0.1 collective-permute-start.16
  66.3 0.1 fold.3
  66.4 3.6 %collective-permute-start.20 = (bf16[64,384]{1,0:T(8,128)(2,1)S(1)}, bf16[64,384]{1,0:T(8,128)(2,1)S(1)}, u32[]{:S(2)}, u32[]{:S(2)}) collective-permute-start(bf16[64,384]{1,0:T(8,128)(2,1)S(1)} %get-tuple-element.158), channel_id=1, source_target_pairs={{0,16},{4,20},{8,24},{12,28},{16,0},{20,4},{24,8},{28,12},{1,17},{... | collective-permute-start | bytes 147464 | tf_op jit(solution)/shard_map/ppermute | solution.py:52
  70.0 1.4 %collective-permute-start.21 = (bf16[64,384]{1,0:T(8,128)(2,1)S(1)}, bf16[64,384]{1,0:T(8,128)(2,1)S(1)}, u32[]{:S(2)}, u32[]{:S(2)}) collective-permute-start(bf16[64,384]{1,0:T(8,128)(2,1)S(1)} %get-tuple-element.159), channel_id=1, source_target_pairs={{0,8},{4,12},{8,0},{12,4},{16,24},{20,28},{24,16},{28,20},{1,9},{5... | collective-permute-start | bytes 147464 | tf_op jit(solution)/shard_map/ppermute | solution.py:52
  71.4 0.1 collective-permute-start.22
  71.6 2.3 %collective-permute-start.17 = (bf16[80,256]{1,0:T(8,128)(2,1)S(1)}, bf16[80,256]{1,0:T(8,128)(2,1)S(1)}, u32[]{:S(2)}, u32[]{:S(2)}) collective-permute-start(bf16[80,256]{1,0:T(8,128)(2,1)S(1)} %get-tuple-element.148), channel_id=1, source_target_pairs={{0,16},{4,20},{8,24},{12,28},{16,0},{20,4},{24,8},{28,12},{1,17},{... | collective-permute-start | bytes 122888 | tf_op jit(solution)/shard_map/ppermute | solution.py:52
  73.9 2.1 %collective-permute-start.18 = (bf16[80,256]{1,0:T(8,128)(2,1)S(1)}, bf16[80,256]{1,0:T(8,128)(2,1)S(1)}, u32[]{:S(2)}, u32[]{:S(2)}) collective-permute-start(bf16[80,256]{1,0:T(8,128)(2,1)S(1)} %get-tuple-element.149), channel_id=1, source_target_pairs={{0,8},{4,12},{8,0},{12,4},{16,24},{20,28},{24,16},{28,20},{1,9},{5... | collective-permute-start | bytes 122888 | tf_op jit(solution)/shard_map/ppermute | solution.py:52
  75.9 1.7 %collective-permute-start.19 = (bf16[80,256]{1,0:T(8,128)(2,1)S(1)}, bf16[80,256]{1,0:T(8,128)(2,1)S(1)}, u32[]{:S(2)}, u32[]{:S(2)}) collective-permute-start(bf16[80,256]{1,0:T(8,128)(2,1)S(1)} %get-tuple-element.150), channel_id=1, source_target_pairs={{0,24},{4,28},{8,16},{12,20},{16,8},{20,12},{24,0},{28,4},{1,25},{... | collective-permute-start | bytes 122888 | tf_op jit(solution)/shard_map/ppermute | solution.py:52
  77.6 0.1 collective-permute-done.22.refs_3_
  77.7 0.2 rows.3
  78.0 2.1 %collective-permute-start.23 = (bf16[256,512]{1,0:T(8,128)(2,1)S(1)}, bf16[256,512]{1,0:T(8,128)(2,1)}, u32[]{:S(2)}, u32[]{:S(2)}) collective-permute-start(bf16[256,512]{1,0:T(8,128)(2,1)S(1)} %get-tuple-element.164), channel_id=1, source_target_pairs={{0,2},{1,3},{2,0},{3,1},{4,6},{5,7},{6,4},{7,5},{8,10},{9,11},{10,... | collective-permute-start | bytes 786440 | tf_op jit(solution)/shard_map/ppermute | solution.py:52
  80.1 0.1 collective-permute-start.24
  80.2 1.6 %collective-permute-done.19.refs_3_ = bf16[80,256]{1,0:T(8,128)(2,1)S(1)} collective-permute-done((bf16[80,256]{1,0:T(8,128)(2,1)S(1)}, bf16[80,256]{1,0:T(8,128)(2,1)S(1)}, u32[]{:S(2)}, u32[]{:S(2)}) %collective-permute-start.19) | collective-permute-done | bytes 40992 | tf_op jit(solution)/shard_map/ppermute | solution.py:52
  81.7 0.8 collect.1
  82.5 4.0 %all-to-all-start = ((f32[32,8,128]{2,1,0:T(8,128)}), f32[32,8,128]{2,1,0:T(8,128)S(1)}, u32[]{:S(2)}, u32[]{:S(2)}) async-start(f32[32,8,128]{2,1,0:T(8,128)} %get-tuple-element.166), calls=%async_computation | async-start | bytes 262144 | tf_op jit(solution)/shard_map/all_to_all | solution.py:916
  86.5 0.0 copy-start.14
  86.5 1.2 %copy-done.14 = f32[512,512]{1,0:T(8,128)S(1)} copy-done((f32[512,512]{1,0:T(8,128)S(1)}, f32[512,512]{1,0:T(8,128)}, u32[]{:S(2)}) %copy-start.14) | copy-done | bytes 1048600
  87.7 1.0 %copy-done.16 = bf16[512,512]{1,0:T(8,128)(2,1)S(1)} copy-done((bf16[512,512]{1,0:T(8,128)(2,1)S(1)}, bf16[512,512]{1,0:T(8,128)(2,1)}, u32[]{:S(2)}) %copy-start.16) | copy-done | bytes 524312
  88.8 1.0 %mix.1 = bf16[512,512]{1,0:T(8,128)(2,1)} custom-call(bf16[512,512]{1,0:T(8,128)(2,1)S(1)} %copy-done, f32[69,128]{1,0:T(8,128)S(1)} %bitcast.18, f32[512,512]{1,0:T(8,128)S(1)} %copy-done.14, bf16[512,512]{1,0:T(8,128)(2,1)S(1)} %copy-done.16), custom_call_target="tpu_custom_call" | custom-call | flops 1000000000 | bytes 3000000 | tf_op jit(solution)/shard_map/mix/pallas_call | solution.py:917
  89.8 0.0 copy-start.8
  89.8 0.0 copy-start.10
  89.8 2.2 %finish.2.refs_0_ = f32[512,512]{1,0:T(8,128)} custom-call(bf16[512,512]{1,0:T(8,128)(2,1)S(1)} %copy-done, bf16[512,512]{1,0:T(8,128)(2,1)S(1)} %copy-done.1, f32[512,512]{1,0:T(8,128)S(1)} %get-tuple-element.169.refs_2_.refs_3_, bf16[256,512]{1,0:T(8,128)(2,1)} %collective-permute-done.23.refs_3_), custom_call_target="tpu_custom_call" | custom-call | flops 1000000000 | bytes 3000000 | tf_op jit(solution)/shard_map/finish/pallas_call | solution.py:925
  92.1 0.0 collective-permute-done.24.refs_4_
  92.1 1.2 %finish.3 = f32[512,512]{1,0:T(8,128)} custom-call(f32[512,512]{1,0:T(8,128)} %finish.2.refs_0_, bf16[512,512]{1,0:T(8,128)(2,1)S(1)} %copy-done, bf16[512,512]{1,0:T(8,128)(2,1)S(1)} %copy-done.1, f32[512,512]{1,0:T(8,128)S(1)} %get-tuple-element.169.refs_2_.refs_3_, ...), custom_call_target="tpu_custom_call", output_to_operand_aliasing={{}: (0, {})} | custom-call | flops 1000000000 | bytes 3000000 | tf_op jit(solution)/shard_map/finish/pallas_call | solution.py:925
  93.2 1.5 %all-to-all-done.heard_ref = f32[32,8,128]{2,1,0:T(8,128)S(1)} async-done(((f32[32,8,128]{2,1,0:T(8,128)}), f32[32,8,128]{2,1,0:T(8,128)S(1)}, u32[]{:S(2)}, u32[]{:S(2)}) %all-to-all-start) | async-done | bytes 131104 | tf_op jit(solution)/shard_map/all_to_all | solution.py:916
  94.8 1.7 %update.1 = (f32[64,4,128]{2,1,0:T(4,128)}, f32[64,128]{1,0:T(8,128)}, f32[69,128]{1,0:T(8,128)}, f32[1,1]{1,0:T(1,128)}, f32[64,4,128]{2,1,0:T(4,128)}, /*index...) custom-call(f32[32,8,128]{2,1,0:T(8,128)S(1)} %all-to-all-done.heard, ...), custom_call_target="tpu_custom_call" | custom-call | flops 100000000 | bytes 300000 | tf_op jit(solution)/shard_map/update/pallas_call | solution.py:940
  (52 shorter events, 0.3 us)
Async XLA Ops:
  0.6 0.9 copy-start.2
  1.6 0.8 copy-start.9
  2.6 9.2 %copy-start = (bf16[512,512]{1,0:T(8,128)(2,1)S(1)}, bf16[512,512]{1,0:T(8,128)(2,1)}, u32[]{:S(2)}) copy-start(bf16[512,512]{1,0:T(8,128)(2,1)} %refs_1_.4) | copy-start | bytes 1572868
  2.7 9.2 %copy-start.1 = (bf16[512,512]{1,0:T(8,128)(2,1)S(1)}, bf16[512,512]{1,0:T(8,128)(2,1)}, u32[]{:S(2)}) copy-start(bf16[512,512]{1,0:T(8,128)(2,1)} %refs_2_.2) | copy-start | bytes 1572868
  2.7 8.3 %collective-permute-start.5 = (bf16[64,640]{1,0:T(8,128)(2,1)S(1)}, bf16[64,640]{1,0:T(8,128)(2,1)S(1)}, u32[]{:S(2)}, u32[]{:S(2)}) collective-permute-start(bf16[64,640]{1,0:T(8,128)(2,1)S(1)} %cast.1.refs_0_), channel_id=1, source_target_pairs={{0,16},{4,20},{8,24},{12,28},{16,0},{20,4},{24,8},{28,12},{1,17},{... | collective-permute-start | bytes 245768 | tf_op jit(solution)/shard_map/ppermute | solution.py:52
  6.8 15.1 %collective-permute-start.3 = (bf16[512,512]{1,0:T(8,128)(2,1)}, bf16[512,512]{1,0:T(8,128)(2,1)S(1)}, u32[]{:S(2)}, u32[]{:S(2)}) collective-permute-start(bf16[512,512]{1,0:T(8,128)(2,1)} %refs_1_.4), channel_id=1, source_target_pairs={{0,2},{1,3},{2,0},{3,1},{4,6},{5,7},{6,4},{7,5},{8,10},{9,11},{10,... | collective-permute-start | bytes 1572872 | tf_op jit(solution)/shard_map/ppermute | solution.py:52
  11.0 10.8 %copy-start.6 = (f32[8832]{0:T(1024)S(1)}, f32[8832]{0:T(1024)}, u32[]{:S(2)}) copy-start(f32[8832]{0:T(1024)} %param.19) | copy-start | bytes 105988
  11.0 10.8 %copy-start.17 = (s32[2048]{0:T(1024)S(1)}, s32[2048]{0:T(1024)}, u32[]{:S(2)}) copy-start(s32[2048]{0:T(1024)} %param.16) | copy-start | bytes 24580
  11.0 5.4 %collective-permute-start.6 = (bf16[128,640]{1,0:T(8,128)(2,1)S(1)}, bf16[128,640]{1,0:T(8,128)(2,1)S(1)}, u32[]{:S(2)}, u32[]{:S(2)}) collective-permute-start(bf16[128,640]{1,0:T(8,128)(2,1)S(1)} %join.3), channel_id=1, source_target_pairs={{0,8},{4,12},{8,0},{12,4},{16,24},{20,28},{24,16},{28,20},{1,9},{5... | collective-permute-start | bytes 491528 | tf_op jit(solution)/shard_map/ppermute | solution.py:52
  11.8 12.6 %collective-permute-start.2 = (bf16[512,512]{1,0:T(8,128)(2,1)S(1)}, bf16[512,512]{1,0:T(8,128)(2,1)S(1)}, u32[]{:S(2)}, u32[]{:S(2)}) collective-permute-start(bf16[512,512]{1,0:T(8,128)(2,1)S(1)} %copy-done), channel_id=1, source_target_pairs={{0,1},{1,0},{2,3},{3,2},{4,5},{5,4},{6,7},{7,6},{8,9},{9,8},{10,11... | collective-permute-start | bytes 1572872 | tf_op jit(solution)/shard_map/ppermute | solution.py:52
  11.8 24.5 %collective-permute-start = (bf16[512,512]{1,0:T(8,128)(2,1)S(1)}, bf16[512,512]{1,0:T(8,128)(2,1)S(1)}, u32[]{:S(2)}, u32[]{:S(2)}) collective-permute-start(bf16[512,512]{1,0:T(8,128)(2,1)S(1)} %copy-done.1), channel_id=1, source_target_pairs={{0,1},{1,0},{2,3},{3,2},{4,5},{5,4},{6,7},{7,6},{8,9},{9,8},{10,11... | collective-permute-start | bytes 1572872 | tf_op jit(solution)/shard_map/ppermute | solution.py:52
  12.3 20.0 %collective-permute-start.1 = (bf16[512,512]{1,0:T(8,128)(2,1)S(1)}, bf16[512,512]{1,0:T(8,128)(2,1)S(1)}, u32[]{:S(2)}, u32[]{:S(2)}) collective-permute-start(bf16[512,512]{1,0:T(8,128)(2,1)S(1)} %copy-done.1), channel_id=1, source_target_pairs={{0,2},{1,3},{2,0},{3,1},{4,6},{5,7},{6,4},{7,5},{8,10},{9,11},{10,... | collective-permute-start | bytes 1572872 | tf_op jit(solution)/shard_map/ppermute | solution.py:52
  16.4 7.9 %collective-permute-start.7 = (bf16[256,640]{1,0:T(8,128)(2,1)S(1)}, bf16[256,640]{1,0:T(8,128)(2,1)S(1)}, u32[]{:S(2)}, u32[]{:S(2)}) collective-permute-start(bf16[256,640]{1,0:T(8,128)(2,1)S(1)} %join.4), channel_id=1, source_target_pairs={{0,4},{4,0},{8,12},{12,8},{16,20},{20,16},{24,28},{28,24},{1,5},{5... | collective-permute-start | bytes 983048 | tf_op jit(solution)/shard_map/ppermute | solution.py:52
  21.8 2.6 %collective-permute-start.4 = (bf16[512,512]{1,0:T(8,128)(2,1)S(1)}, bf16[512,512]{1,0:T(8,128)(2,1)S(1)}, u32[]{:S(2)}, u32[]{:S(2)}) collective-permute-start(bf16[512,512]{1,0:T(8,128)(2,1)S(1)} %collective-permute-done.3.refs_2_), channel_id=1, source_target_pairs={{0,1},{1,0},{2,3},{3,2},{4,5},{5,4},{6,7},{7,6},{8,9},{9,8},{10,11... | collective-permute-start | bytes 1572872 | tf_op jit(solution)/shard_map/ppermute | solution.py:52
  26.0 1.8 %copy-start.18 = (s32[2048]{0:T(1024)S(1)}, s32[2048]{0:T(1024)}, u32[]{:S(2)}) copy-start(s32[2048]{0:T(1024)} %param.15) | copy-start | bytes 24580
  32.4 4.0 %collective-permute-start.8 = (bf16[512,512]{1,0:T(8,128)(2,1)S(1)}, bf16[512,512]{1,0:T(8,128)(2,1)S(1)}, u32[]{:S(2)}, u32[]{:S(2)}) collective-permute-start(bf16[512,512]{1,0:T(8,128)(2,1)S(1)} %collective-permute-done.1.refs_2_.refs_6_), channel_id=1, source_target_pairs={{0,1},{1,0},{2,3},{3,2},{4,5},{5,4},{6,7},{7,6},{8,9},{9,8},{10,11... | collective-permute-start | bytes 1572872 | tf_op jit(solution)/shard_map/ppermute | solution.py:52
  38.0 4.2 %collective-permute-start.10 = (f32[8,4,256]{2,1,0:T(4,128)S(1)}, f32[8,4,256]{2,1,0:T(4,128)S(1)}, u32[]{:S(2)}, u32[]{:S(2)}) collective-permute-start(f32[8,4,256]{2,1,0:T(4,128)S(1)} %get-tuple-element.115.refs_0_), channel_id=1, source_target_pairs={{0,2},{1,3},{2,0},{3,1},{4,6},{5,7},{6,4},{7,5},{8,10},{9,11},{10,... | collective-permute-start | bytes 98312 | tf_op jit(solution)/shard_map/ppermute | solution.py:52
  39.7 3.6 %collective-permute-start.11 = (f32[8,4,256]{2,1,0:T(4,128)S(1)}, f32[8,4,256]{2,1,0:T(4,128)S(1)}, u32[]{:S(2)}, u32[]{:S(2)}) collective-permute-start(f32[8,4,256]{2,1,0:T(4,128)S(1)} %get-tuple-element.115.refs_0_), channel_id=1, source_target_pairs={{0,3},{1,2},{2,1},{3,0},{4,7},{5,6},{6,5},{7,4},{8,11},{9,10},{10,... | collective-permute-start | bytes 98312 | tf_op jit(solution)/shard_map/ppermute | solution.py:52
  39.7 3.6 %collective-permute-start.9 = (f32[8,4,256]{2,1,0:T(4,128)S(1)}, f32[8,4,256]{2,1,0:T(4,128)S(1)}, u32[]{:S(2)}, u32[]{:S(2)}) collective-permute-start(f32[8,4,256]{2,1,0:T(4,128)S(1)} %get-tuple-element.115.refs_0_), channel_id=1, source_target_pairs={{0,1},{1,0},{2,3},{3,2},{4,5},{5,4},{6,7},{7,6},{8,9},{9,8},{10,11... | collective-permute-start | bytes 98312 | tf_op jit(solution)/shard_map/ppermute | solution.py:52
  44.1 2.7 %collective-permute-start.12 = (bf16[2,512,512]{2,1,0:T(8,128)(2,1)S(1)}, bf16[2,512,512]{2,1,0:T(8,128)(2,1)S(1)}, u32[]{:S(2)}, u32[]{:S(2)}) collective-permute-start(bf16[2,512,512]{2,1,0:T(8,128)(2,1)S(1)} %get-tuple-element.118), channel_id=1, source_target_pairs={{0,1},{1,0},{2,3},{3,2},{4,5},{5,4},{6,7},{7,6},{8,9},{9,8},{10,11... | collective-permute-start | bytes 3145736 | tf_op jit(solution)/shard_map/ppermute | solution.py:52
  47.1 5.0 %copy-start.13 = (f32[512,512]{1,0:T(8,128)}, f32[512,512]{1,0:T(8,128)S(1)}, u32[]{:S(2)}) copy-start(f32[512,512]{1,0:T(8,128)S(1)} %get-tuple-element.167.refs_0_) | copy-start | bytes 3145732
  47.1 17.3 %collective-permute-start.14 = (bf16[512,512]{1,0:T(8,128)(2,1)S(1)}, bf16[512,512]{1,0:T(8,128)(2,1)S(1)}, u32[]{:S(2)}, u32[]{:S(2)}) collective-permute-start(bf16[512,512]{1,0:T(8,128)(2,1)S(1)} %get-tuple-element.137), channel_id=1, source_target_pairs={{0,2},{1,3},{2,0},{3,1},{4,6},{5,7},{6,4},{7,5},{8,10},{9,11},{10,... | collective-permute-start | bytes 1572872 | tf_op jit(solution)/shard_map/ppermute | solution.py:52
  52.1 12.2 %collective-permute-start.13 = (bf16[4,64,384]{2,1,0:T(8,128)(2,1)S(1)}, bf16[4,64,384]{2,1,0:T(8,128)(2,1)S(1)}, u32[]{:S(2)}, u32[]{:S(2)}) collective-permute-start(bf16[4,64,384]{2,1,0:T(8,128)(2,1)S(1)} %get-tuple-element.136), channel_id=1, source_target_pairs={{0,4},{4,0},{8,12},{12,8},{16,20},{20,16},{24,28},{28,24},{1,5},{5... | collective-permute-start | bytes 589832 | tf_op jit(solution)/shard_map/ppermute | solution.py:52
  64.4 1.8 %copy-start.15 = (bf16[512,512]{1,0:T(8,128)(2,1)}, bf16[512,512]{1,0:T(8,128)(2,1)S(1)}, u32[]{:S(2)}) copy-start(bf16[512,512]{1,0:T(8,128)(2,1)S(1)} %collective-permute-done.14.refs_1_) | copy-start | bytes 1572868
  64.4 7.2 %collective-permute-start.15 = (bf16[4,80,256]{2,1,0:T(8,128)(2,1)S(1)}, bf16[4,80,256]{2,1,0:T(8,128)(2,1)S(1)}, u32[]{:S(2)}, u32[]{:S(2)}) collective-permute-start(bf16[4,80,256]{2,1,0:T(8,128)(2,1)S(1)} %get-tuple-element.139), channel_id=1, source_target_pairs={{0,4},{4,0},{8,12},{12,8},{16,20},{20,16},{24,28},{28,24},{1,5},{5... | collective-permute-start | bytes 491528 | tf_op jit(solution)/shard_map/ppermute | solution.py:52
  66.2 5.4 %collective-permute-start.16 = (bf16[2,512,512]{2,1,0:T(8,128)(2,1)S(1)}, bf16[2,512,512]{2,1,0:T(8,128)(2,1)S(1)}, u32[]{:S(2)}, u32[]{:S(2)}) collective-permute-start(bf16[2,512,512]{2,1,0:T(8,128)(2,1)S(1)} %get-tuple-element.147), channel_id=1, source_target_pairs={{0,1},{1,0},{2,3},{3,2},{4,5},{5,4},{6,7},{7,6},{8,9},{9,8},{10,11... | collective-permute-start | bytes 3145736 | tf_op jit(solution)/shard_map/ppermute | solution.py:52
  66.4 9.6 %collective-permute-start.20 = (bf16[64,384]{1,0:T(8,128)(2,1)S(1)}, bf16[64,384]{1,0:T(8,128)(2,1)S(1)}, u32[]{:S(2)}, u32[]{:S(2)}) collective-permute-start(bf16[64,384]{1,0:T(8,128)(2,1)S(1)} %get-tuple-element.158), channel_id=1, source_target_pairs={{0,16},{4,20},{8,24},{12,28},{16,0},{20,4},{24,8},{28,12},{1,17},{... | collective-permute-start | bytes 147464 | tf_op jit(solution)/shard_map/ppermute | solution.py:52
  70.0 7.6 %collective-permute-start.21 = (bf16[64,384]{1,0:T(8,128)(2,1)S(1)}, bf16[64,384]{1,0:T(8,128)(2,1)S(1)}, u32[]{:S(2)}, u32[]{:S(2)}) collective-permute-start(bf16[64,384]{1,0:T(8,128)(2,1)S(1)} %get-tuple-element.159), channel_id=1, source_target_pairs={{0,8},{4,12},{8,0},{12,4},{16,24},{20,28},{24,16},{28,20},{1,9},{5... | collective-permute-start | bytes 147464 | tf_op jit(solution)/shard_map/ppermute | solution.py:52
  71.4 6.3 %collective-permute-start.22 = (bf16[64,384]{1,0:T(8,128)(2,1)S(1)}, bf16[64,384]{1,0:T(8,128)(2,1)S(1)}, u32[]{:S(2)}, u32[]{:S(2)}) collective-permute-start(bf16[64,384]{1,0:T(8,128)(2,1)S(1)} %get-tuple-element.160), channel_id=1, source_target_pairs={{0,24},{4,28},{8,16},{12,20},{16,8},{20,12},{24,0},{28,4},{1,25},{... | collective-permute-start | bytes 147464 | tf_op jit(solution)/shard_map/ppermute | solution.py:52
  71.6 8.6 %collective-permute-start.17 = (bf16[80,256]{1,0:T(8,128)(2,1)S(1)}, bf16[80,256]{1,0:T(8,128)(2,1)S(1)}, u32[]{:S(2)}, u32[]{:S(2)}) collective-permute-start(bf16[80,256]{1,0:T(8,128)(2,1)S(1)} %get-tuple-element.148), channel_id=1, source_target_pairs={{0,16},{4,20},{8,24},{12,28},{16,0},{20,4},{24,8},{28,12},{1,17},{... | collective-permute-start | bytes 122888 | tf_op jit(solution)/shard_map/ppermute | solution.py:52
  73.9 6.3 %collective-permute-start.18 = (bf16[80,256]{1,0:T(8,128)(2,1)S(1)}, bf16[80,256]{1,0:T(8,128)(2,1)S(1)}, u32[]{:S(2)}, u32[]{:S(2)}) collective-permute-start(bf16[80,256]{1,0:T(8,128)(2,1)S(1)} %get-tuple-element.149), channel_id=1, source_target_pairs={{0,8},{4,12},{8,0},{12,4},{16,24},{20,28},{24,16},{28,20},{1,9},{5... | collective-permute-start | bytes 122888 | tf_op jit(solution)/shard_map/ppermute | solution.py:52
  75.9 5.8 %collective-permute-start.19 = (bf16[80,256]{1,0:T(8,128)(2,1)S(1)}, bf16[80,256]{1,0:T(8,128)(2,1)S(1)}, u32[]{:S(2)}, u32[]{:S(2)}) collective-permute-start(bf16[80,256]{1,0:T(8,128)(2,1)S(1)} %get-tuple-element.150), channel_id=1, source_target_pairs={{0,24},{4,28},{8,16},{12,20},{16,8},{20,12},{24,0},{28,4},{1,25},{... | collective-permute-start | bytes 122888 | tf_op jit(solution)/shard_map/ppermute | solution.py:52
  78.0 11.8 %collective-permute-start.23 = (bf16[256,512]{1,0:T(8,128)(2,1)S(1)}, bf16[256,512]{1,0:T(8,128)(2,1)}, u32[]{:S(2)}, u32[]{:S(2)}) collective-permute-start(bf16[256,512]{1,0:T(8,128)(2,1)S(1)} %get-tuple-element.164), channel_id=1, source_target_pairs={{0,2},{1,3},{2,0},{3,1},{4,6},{5,7},{6,4},{7,5},{8,10},{9,11},{10,... | collective-permute-start | bytes 786440 | tf_op jit(solution)/shard_map/ppermute | solution.py:52
  80.1 12.0 %collective-permute-start.24 = (bf16[256,512]{1,0:T(8,128)(2,1)S(1)}, bf16[256,512]{1,0:T(8,128)(2,1)S(1)}, u32[]{:S(2)}, u32[]{:S(2)}) collective-permute-start(bf16[256,512]{1,0:T(8,128)(2,1)S(1)} %get-tuple-element.165), channel_id=1, source_target_pairs={{0,2},{1,3},{2,0},{3,1},{4,6},{5,7},{6,4},{7,5},{8,10},{9,11},{10,... | collective-permute-start | bytes 786440 | tf_op jit(solution)/shard_map/ppermute | solution.py:52
  82.5 12.2 %all-to-all-start = ((f32[32,8,128]{2,1,0:T(8,128)}), f32[32,8,128]{2,1,0:T(8,128)S(1)}, u32[]{:S(2)}, u32[]{:S(2)}) async-start(f32[32,8,128]{2,1,0:T(8,128)} %get-tuple-element.166), calls=%async_computation | async-start | bytes 262144 | tf_op jit(solution)/shard_map/all_to_all | solution.py:916
  86.5 1.2 %copy-start.14 = (f32[512,512]{1,0:T(8,128)S(1)}, f32[512,512]{1,0:T(8,128)}, u32[]{:S(2)}) copy-start(f32[512,512]{1,0:T(8,128)} %copy-done.13) | copy-start | bytes 3145732
  87.7 1.0 %copy-start.16 = (bf16[512,512]{1,0:T(8,128)(2,1)S(1)}, bf16[512,512]{1,0:T(8,128)(2,1)}, u32[]{:S(2)}) copy-start(bf16[512,512]{1,0:T(8,128)(2,1)} %copy-done.15) | copy-start | bytes 1572868
  89.8 5.0 %copy-start.3 = (f32[64,4,128]{2,1,0:T(4,128)S(1)}, f32[64,4,128]{2,1,0:T(4,128)}, u32[]{:S(2)}) copy-start(f32[64,4,128]{2,1,0:T(4,128)} %refs_0_.7) | copy-start | bytes 393220
  89.8 5.0 %copy-start.4 = (f32[64,4,128]{2,1,0:T(4,128)S(1)}, f32[64,4,128]{2,1,0:T(4,128)}, u32[]{:S(2)}) copy-start(f32[64,4,128]{2,1,0:T(4,128)} %refs_1_.5) | copy-start | bytes 393220
  89.8 5.0 %copy-start.5 = (f32[64,4,128]{2,1,0:T(4,128)S(1)}, f32[64,4,128]{2,1,0:T(4,128)}, u32[]{:S(2)}) copy-start(f32[64,4,128]{2,1,0:T(4,128)} %refs_2_.3) | copy-start | bytes 393220
  89.8 5.0 %copy-start.7 = (f32[8832]{0:T(1024)S(1)}, f32[8832]{0:T(1024)}, u32[]{:S(2)}) copy-start(f32[8832]{0:T(1024)} %param.24) | copy-start | bytes 105988
  89.8 5.0 %copy-start.8 = (f32[8832]{0:T(1024)S(1)}, f32[8832]{0:T(1024)}, u32[]{:S(2)}) copy-start(f32[8832]{0:T(1024)} %param.25) | copy-start | bytes 105988
  89.8 5.0 %copy-start.10 = (f32[128,64]{0,1:T(8,128)S(1)}, f32[128,64]{0,1:T(8,128)}, u32[]{:S(2)}) copy-start(f32[128,64]{0,1:T(8,128)} %param.18) | copy-start | bytes 98308
  89.8 5.0 %copy-start.11 = (f32[128,64]{0,1:T(8,128)S(1)}, f32[128,64]{0,1:T(8,128)}, u32[]{:S(2)}) copy-start(f32[128,64]{0,1:T(8,128)} %param.22) | copy-start | bytes 98308
  89.8 5.0 %copy-start.12 = (f32[128,64]{0,1:T(8,128)S(1)}, f32[128,64]{0,1:T(8,128)}, u32[]{:S(2)}) copy-start(f32[128,64]{0,1:T(8,128)} %param.23) | copy-start | bytes 98308

commit v8 on v7

--- a/solution.py
+++ b/solution.py
@@ -72,20 +72,21 @@
     return lax.optimization_barrier((x,) + others)[0]
 
 
-def gather_dp(x):
+def gather_dp(x, behind):
     n = lax.axis_size("dp")
-    arrays, offsets, operands = [x], [[0]], []
+    arrays, offsets = [x], [[0]]
     k = n // 2
     while k:
         operand = join(arrays) if len(arrays) > 1 else x
-        operands.append(operand)
+        if k == 1:
+            operand = after(operand, behind)
         arrays.append(swap(operand, "dp", k))
         offsets.append([o ^ k for group in offsets for o in group])
         k //= 2
-    return arrays, offsets, operands
-
-
-def join(arrays, us=2):
+    return arrays, offsets
+
+
+def join(arrays, us=0.1):
     shape = (sum(x.shape[0] for x in arrays), arrays[0].shape[1])
     return call(join_kernel, "join", [VMEM] * len(arrays), [(shape, arrays[0].dtype, VMEM)], [], us)(*arrays)[0]
 
@@ -245,10 +246,13 @@
         at += ref.shape[0]
 
 
-def normalize_kernel(*refs):
-    x_pieces, xn_ref = refs[:-1], refs[-1]
-    per = x_pieces[0].shape[0] // TILE
-    for k, piece in enumerate(x_pieces):
+def normalize_kernel(which, *refs):
+    before = refs[: len(refs) - len(which) - 1]
+    pieces, xn_ref = refs[len(before) : -1], refs[-1]
+    per = pieces[0].shape[0] // TILE
+    for ref in before:
+        xn_ref[...] = ref[...]
+    for k, piece in zip(which, pieces):
         for r in range(per):
             x = piece[r * TILE : (r + 1) * TILE, :].astype(f32)
             x = x - jnp.sum(x, axis=1, keepdims=True) / D
@@ -633,8 +637,7 @@
     message = jnp.concatenate(
         [
             total[rows : rows + extra, :128] + total[rows + extra : rows + 2 * extra, :128],
-            jnp.zeros((7 - extra, 128), f32),
-            jnp.broadcast_to(squares, (1, 128)),
+            jnp.broadcast_to(squares, (message_ref.shape[1] - extra, 128)),
         ],
         axis=0,
     )
@@ -649,9 +652,10 @@
     width = grad_out_ref.shape[1]
     lead, pos_rows, used = D // 128, POS // 128, (D + group) // 128
     grad_small_ref[...] = jnp.zeros_like(grad_small_ref)
-    squares = heard_ref[0, 7:8, :]
+    last = heard_ref.shape[1] - 1
+    squares = heard_ref[0, last:, :]
     for k in range(1, n_all):
-        squares = squares + heard_ref[k, 7:8, :]
+        squares = squares + heard_ref[k, last:, :]
     for p in range(n_all // n_head):
         rows = heard_ref[p * n_head, :extra, :]
         for h in range(1, n_head):
@@ -702,7 +706,7 @@
         in_specs=in_specs,
         out_specs=[spec for _, _, spec in outs],
         scratch_shapes=scratch,
-        compiler_params=pltpu.CompilerParams(vmem_limit_bytes=room * 2**20 * max(1, lax.axis_size("head") // 4)),
+        compiler_params=pltpu.CompilerParams(vmem_limit_bytes=min(60, room * max(1, lax.axis_size("head") // 4)) * 2**20),
         cost_estimate=pl.CostEstimate(flops=int(us * 1e9), bytes_accessed=int(us * 3e6), transcendentals=0),
         name=name,
         **more,
@@ -750,13 +754,10 @@
         ],
         1,
     )(proj_weight, out_weight.T)
-    x_pieces = gather_cores(tokens, gather_chips(after(tokens, weights)))
-    w_pieces, offsets, operands = gather_dp(weights)
-    cot_chips = gather_chips(after(cotangent, weights))
+    x_chips = gather_chips(after(tokens, weights))
     starts = seq_start.reshape(1, group)
+    times = time_bucket.reshape(1, group)
     small_rows = small_params.reshape(-1, 128)
-    times = time_bucket.reshape(1, group)
-
     pos, oh, oht, trow = call(
         prepare_kernel,
         "prepare",
@@ -768,8 +769,8 @@
             ((nb, NTB, TILE), bf16, VMEM),
         ],
         [],
-        5,
-    )(after(times, operands[1]), small_rows)
+        2,
+    )(after(times, weights), small_rows)
 
     items = [
         ((nb, 3 * width, TILE), bf16),
@@ -780,15 +781,31 @@
         ((nb, TILE, width), bf16),
         ((nb, width, TILE), bf16),
     ]
-    (xn,) = call(normalize_kernel, "normalize", [VMEM] * n_head, [((nb, TILE, D), bf16, VMEM)], [], 1)(*x_pieces)
-    w_pieces[-1] = after(join(w_pieces[-1:], 4), xn)
+    w_pieces, offsets = gather_dp(weights, pos)
+    cot_chips = gather_chips(after(cotangent, weights))
+
+    x_pieces = gather_cores(tokens, x_chips)
+    near = [0, 1] + list(range(2, n_head, 2))
+    far = list(range(3, n_head, 2))
+    xn = []
+    for which in (near, far):
+        xn = call(
+            functools.partial(normalize_kernel, which),
+            "normalize",
+            [VMEM] * (len(xn) + len(which)),
+            [((nb, TILE, D), bf16, VMEM)],
+            [],
+            0.1,
+        )(*xn, *[x_pieces[k] for k in which])
+    (xn,) = xn
+    w_pieces[-1] = after(join(w_pieces[-1:], 6), xn)
     (wt,) = call(
         functools.partial(assemble_kernel, offsets),
         "assemble",
         [VMEM] * len(w_pieces),
         [((5 * width, D), bf16, VMEM)],
         [pltpu.VMEM((D, 5 * width), bf16)],
-        5,
+        0.5,
     )(*w_pieces)
     dsilu, kx, kxt, qs, q, v, vt = call(
         functools.partial(project_kernel, heads),
@@ -796,7 +813,7 @@
         [VMEM] * 4,
         [item + (VMEM,) for item in items],
         [],
-        5,
+        1,
     )(xn, wt, oh, oht)
 
     kept = nb * (nb + 1) // 2 * heads <= KEPT_TILES
@@ -809,7 +826,7 @@
             [VMEM] * (len(before) + 6),
             [((last, width, TILE), f32, VMEM)] + [((count, TILE, heads * TILE), bf16, VMEM)] * (2 * kept),
             [],
-            8,
+            8 if before else 0.5,
         )(*before, kx, qs, trow, vt, pos, starts)
 
     split = nb - nb // 4
@@ -908,7 +925,7 @@
         functools.partial(collect_kernel, high, extra),
         "collect",
         [VMEM] * (high + 1),
-        [grads_shape + (VMEM,), ((n_all, 8, 128), f32, VMEM)],
+        [grads_shape + (VMEM,), ((n_all, 4 if extra < 4 else 8, 128), f32, VMEM)],
         [],
         10,
     )(*late_blocks, early)

time: 97 us -> 95.2 us (0.981)
  starting transfers between devices: 33.5 us -> 31.8 us
  Pallas kernels: 41.6 us -> 42.8 us
  local copies, waits for them, and re-layouts: 4 us -> 2.95 us
    all_to_all x1, waiting for transfers between devices: 1.5 us -> 0.01 us  [shards(): heard = lax.all_to_all(message, ('dp', 'head'), 0, 0, tiled=True)]
    ppermute x25, waiting for transfers between devices: 14.9 us -> 16.3 us  [swap(): return lax.ppermute(x, axis, [(i, i ^ k) for i in range(n)])]
    ppermute x25, starting transfers between devices: 29.5 us -> 28.2 us  [swap(): return lax.ppermute(x, axis, [(i, i ^ k) for i in range(n)])]
    unnamed x38 -> x34, local copies, waits for them, and re-layouts: 4 us -> 2.95 us
  transfers between devices with their start and end apart: 26 -> 26, of which waited for: 9 -> 11; matrix products, arithmetic and copies ran while one was open for 0% -> 0% of each run, Pallas kernels for 38% -> 40%
where the time goes in v8:
time: 95.2 us; the launch traced here: 94.9 us
  Pallas kernels  42.8 us (45%)
  starting transfers between devices  31.8 us (33%)
  waiting for transfers between devices  16.3 us (17%)
  local copies, waits for them, and re-layouts  2.95 us (3%)
  between operations  1.1 us (1%)
    ppermute x25, starting transfers between devices, swap(): return lax.ppermute(x, axis, [(i, i ^ k) for i in range(n)])  28.2 us
    ppermute x25, waiting for transfers between devices, swap(): return lax.ppermute(x, axis, [(i, i ^ k) for i in range(n)])  16.3 us
    pallas_call x1, Pallas kernels, shards(): call(functools.partial(backward_kernel, heads, n_dp, extra, kept), 'backw...  10.6 us
    pallas_call x2, Pallas kernels, attend(): call(functools.partial(attend_kernel, heads, first, last, kept), 'attend'...  8.23 us
    pallas_call x1, Pallas kernels, shards(): call(functools.partial(values_kernel, heads, kept), 'values', [VMEM] * (l...  4.31 us
    all_to_all x1, starting transfers between devices, shards(): heard = lax.all_to_all(message, ('dp', 'head'), 0, 0, tiled=True)  3.55 us
    pallas_call x2, Pallas kernels, shards(): call(functools.partial(finish_kernel, part), 'finish', [pl.BlockSpec(memo...  3.39 us
    unnamed x34, local copies, waits for them, and re-layouts  2.95 us
  transfers between devices with their start and end apart: 26, of which 11 were waited for; matrix products, arithmetic and copies ran while one was open for 0% of the time, Pallas kernels for 40%

profile of v8, /device:TPU:0, one launch (start us, length us, event | category | flops | bytes accessed | tf_op | source)
XLA Modules:
  0.0 94.9 jit_solution(2925004006978375443)
XLA Ops:
  0.6 0.0 copy-start.2
  0.7 0.9 copy-done.2
  1.6 0.8 copy-done.9
  2.3 0.3 cast.1.refs_0_
  2.7 4.1 %collective-permute-start.5 = (bf16[64,640]{1,0:T(8,128)(2,1)S(1)}, bf16[64,640]{1,0:T(8,128)(2,1)S(1)}, u32[]{:S(2)}, u32[]{:S(2)}) collective-permute-start(bf16[64,640]{1,0:T(8,128)(2,1)S(1)} %cast.1.refs_0_), channel_id=1, source_target_pairs={{0,16},{4,20},{8,24},{12,28},{16,0},{20,4},{24,8},{28,12},{1,17},{... | collective-permute-start | bytes 245768 | tf_op jit(solution)/shard_map/ppermute | solution.py:52
  6.8 1.5 %collective-permute-start.3 = (bf16[512,512]{1,0:T(8,128)(2,1)}, bf16[512,512]{1,0:T(8,128)(2,1)S(1)}, u32[]{:S(2)}, u32[]{:S(2)}) collective-permute-start(bf16[512,512]{1,0:T(8,128)(2,1)} %refs_1_.4), channel_id=1, source_target_pairs={{0,2},{1,3},{2,0},{3,1},{4,6},{5,7},{6,4},{7,5},{8,10},{9,11},{10,... | collective-permute-start | bytes 1572872 | tf_op jit(solution)/shard_map/ppermute | solution.py:52
  8.3 2.7 %collective-permute-done.5.refs_1_ = bf16[64,640]{1,0:T(8,128)(2,1)S(1)} collective-permute-done((bf16[64,640]{1,0:T(8,128)(2,1)S(1)}, bf16[64,640]{1,0:T(8,128)(2,1)S(1)}, u32[]{:S(2)}, u32[]{:S(2)}) %collective-permute-start.5) | collective-permute-done | bytes 81952 | tf_op jit(solution)/shard_map/ppermute | solution.py:52
  11.0 0.8 collective-permute-start.6
  11.8 2.5 %prepare.1 = (f32[8,256,256]{2,1,0:T(8,128)S(1)}, bf16[8,256,128]{2,1,0:T(8,128)(2,1)S(1)}, bf16[8,128,256]{2,1,0:T(8,128)(2,1)S(1)}, bf16[8,128,256]{2,1,0:T(8,128)(2,1)S(1)}) custom-call(s32[1,2048]{1,0:T(1,128)S(1)} %bitcast.28, f32[69,128]{1,0:T(8,128)S(1)} %bitcast.17), custom_call_target="tpu_custom_call" | custom-call | flops 2000000000 | bytes 6000000 | tf_op jit(solution)/shard_map/prepare/pallas_call | solution.py:761
  14.3 2.1 %collective-permute-done.6.refs_2_ = bf16[128,640]{1,0:T(8,128)(2,1)S(1)} collective-permute-done((bf16[128,640]{1,0:T(8,128)(2,1)S(1)}, bf16[128,640]{1,0:T(8,128)(2,1)S(1)}, u32[]{:S(2)}, u32[]{:S(2)}) %collective-permute-start.6) | collective-permute-done | bytes 163872 | tf_op jit(solution)/shard_map/ppermute | solution.py:52
  16.4 1.8 %collective-permute-start.7 = (bf16[256,640]{1,0:T(8,128)(2,1)S(1)}, bf16[256,640]{1,0:T(8,128)(2,1)S(1)}, u32[]{:S(2)}, u32[]{:S(2)}) collective-permute-start(bf16[256,640]{1,0:T(8,128)(2,1)S(1)} %join.4), channel_id=1, source_target_pairs={{0,4},{4,0},{8,12},{12,8},{16,20},{20,16},{24,28},{28,24},{1,5},{5... | collective-permute-start | bytes 983048 | tf_op jit(solution)/shard_map/ppermute | solution.py:52
  18.2 1.5 %collective-permute-start.1 = (bf16[512,512]{1,0:T(8,128)(2,1)S(1)}, bf16[512,512]{1,0:T(8,128)(2,1)S(1)}, u32[]{:S(2)}, u32[]{:S(2)}) collective-permute-start(bf16[512,512]{1,0:T(8,128)(2,1)S(1)} %copy-done.1), channel_id=1, source_target_pairs={{0,2},{1,3},{2,0},{3,1},{4,6},{5,7},{6,4},{7,5},{8,10},{9,11},{10,... | collective-permute-start | bytes 1572872 | tf_op jit(solution)/shard_map/ppermute | solution.py:52
  19.7 1.7 %collective-permute-done.3.refs_2_ = bf16[512,512]{1,0:T(8,128)(2,1)S(1)} collective-permute-done((bf16[512,512]{1,0:T(8,128)(2,1)}, bf16[512,512]{1,0:T(8,128)(2,1)S(1)}, u32[]{:S(2)}, u32[]{:S(2)}) %collective-permute-start.3) | collective-permute-done | bytes 524320 | tf_op jit(solution)/shard_map/ppermute | solution.py:52
  21.3 1.0 %normalize.2.refs_0_ = bf16[8,256,512]{2,1,0:T(8,128)(2,1)S(1)} custom-call(bf16[512,512]{1,0:T(8,128)(2,1)S(1)} %copy-done, bf16[512,512]{1,0:T(8,128)(2,1)S(1)} %collective-permute-done.2.refs_1_, bf16[512,512]{1,0:T(8,128)(2,1)S(1)} %collective-permute-done.3.refs_2_), custom_call_target="tpu_custom_call" | custom-call | flops 100000000 | bytes 300000 | tf_op jit(solution)/shard_map/normalize/pallas_call | solution.py:792
  22.3 1.8 %collective-permute-done.7.refs_0_ = bf16[256,640]{1,0:T(8,128)(2,1)S(1)} collective-permute-done((bf16[256,640]{1,0:T(8,128)(2,1)S(1)}, bf16[256,640]{1,0:T(8,128)(2,1)S(1)}, u32[]{:S(2)}, u32[]{:S(2)}) %collective-permute-start.7) | collective-permute-done | bytes 327712 | tf_op jit(solution)/shard_map/ppermute | solution.py:52
  24.1 0.4 normalize.3.refs_0_.refs_5_.refs_11_.refs_8_.refs_4_
  24.5 0.0 copy-start.13
  24.5 0.3 assemble.1.refs_1_.refs_6_.wt_ref
  24.8 1.8 %project.1 = (bf16[8,384,256]{2,1,0:T(8,128)(2,1)S(1)}, bf16[8,256,256]{2,1,0:T(8,128)(2,1)S(1)}, bf16[8,256,256]{2,1,0:T(8,128)(2,1)S(1)}, bf16[8,128,256]{2,1,...) custom-call(bf16[8,256,512]{2,1,0:T(8,128)(2,1)S(1)} %normalize.3.re, ...), custom_call_target="tpu_custom_call" | custom-call | flops 1000000000 | bytes 3000000 | tf_op jit(solution)/shard_map/project/pallas_call | solution.py:810
  26.7 4.7 %attend.2 = (f32[6,128,256]{2,1,0:T(8,128)S(1)}, bf16[21,256,512]{2,1,0:T(8,128)(2,1)S(1)}, bf16[21,256,512]{2,1,0:T(8,128)(2,1)S(1)}) custom-call(bf16[8,256,256]{2,1,0:T(8,128)(2,1)S(1)} %get-tuple-element.109.refs_0_.refs_1_.refs_2_, bf16[8,128,256]{2,1,0:T(8,128)(2,1)S(1)} %get-tuple-element.110.refs_1_.refs_2_, ...), custom_call_target="tpu_custom_call" | custom-call | flops 500000000 | bytes 1500000 | tf_op jit(solution)/shard_map/attend/pallas_call | solution.py:823
  31.4 1.2 %collective-permute-done.1.refs_2_.refs_6_ = bf16[512,512]{1,0:T(8,128)(2,1)S(1)} collective-permute-done((bf16[512,512]{1,0:T(8,128)(2,1)S(1)}, bf16[512,512]{1,0:T(8,128)(2,1)S(1)}, u32[]{:S(2)}, u32[]{:S(2)}) %collective-permute-start.1) | collective-permute-done | bytes 524320 | tf_op jit(solution)/shard_map/ppermute | solution.py:52
  32.6 3.5 %attend.3 = (f32[8,128,256]{2,1,0:T(8,128)S(1)}, bf16[15,256,512]{2,1,0:T(8,128)(2,1)S(1)}, bf16[15,256,512]{2,1,0:T(8,128)(2,1)S(1)}) custom-call(f32[6,128,256]{2,1,0:T(8,128)S(1)} %get-tuple-element.115.refs_0_, bf16[8,256,256]{2,1,0:T(8,128)(2,1)S(1)} %get-tuple-element.109.refs_0_.refs_1_.refs_2_, ...), custom_call_target="tpu_custom_call" | custom-call | flops 8000000000 | bytes 24000000 | tf_op jit(solution)/shard_map/attend/pallas_call | solution.py:823
  36.1 1.8 %gate.1 = (f32[8,128,256]{2,1,0:T(8,128)S(1)}, f32[8,128,256]{2,1,0:T(8,128)S(1)}, f32[8,4,256]{2,1,0:T(4,128)S(1)}, f32[1,512]{1,0:T(1,128)S(1)}) custom-call(bf16[512,512]{1,0:T(8,128)(2,1)S(1)} %copy-done.1, bf16[512,512]{1,0:T(8,128)(2,1)S(1)} %collective-permute-done.refs_1_.refs_5_, bf16[512,512]{1,0:T(8,128)(2,1)S(1)} %collective-permute-done.1.refs_2_.refs_6_, ...), custom_call_target="tpu_custom_call" | custom-call | flops 5000000000 | bytes 15000000 | tf_op jit(solution)/shard_map/gate/pallas_call | solution.py:840
  37.9 1.6 %collective-permute-start.10 = (f32[8,4,256]{2,1,0:T(4,128)S(1)}, f32[8,4,256]{2,1,0:T(4,128)S(1)}, u32[]{:S(2)}, u32[]{:S(2)}) collective-permute-start(f32[8,4,256]{2,1,0:T(4,128)S(1)} %get-tuple-element.117.refs_0_), channel_id=1, source_target_pairs={{0,2},{1,3},{2,0},{3,1},{4,6},{5,7},{6,4},{7,5},{8,10},{9,11},{10,... | collective-permute-start | bytes 98312 | tf_op jit(solution)/shard_map/ppermute | solution.py:52
  39.5 0.4 collective-permute-start.11
  39.8 0.3 collective-permute-start.9
  40.1 1.8 %collective-permute-done.10.refs_2_ = f32[8,4,256]{2,1,0:T(4,128)S(1)} collective-permute-done((f32[8,4,256]{2,1,0:T(4,128)S(1)}, f32[8,4,256]{2,1,0:T(4,128)S(1)}, u32[]{:S(2)}, u32[]{:S(2)}) %collective-permute-start.10) | collective-permute-done | bytes 32800 | tf_op jit(solution)/shard_map/ppermute | solution.py:52
  41.9 0.9 collective-permute-done.11.refs_3_
  42.8 0.8 branch.1
  43.7 0.3 collective-permute-start.12
  44.0 1.3 %middle.1 = (bf16[8,256,128]{2,1,0:T(8,128)(2,1)S(1)}, bf16[8,128,256]{2,1,0:T(8,128)(2,1)S(1)}, bf16[8,256,128]{2,1,0:T(8,128)(2,1)S(1)}, f32[256,512]{1,0:T(8,128)S(1)}) custom-call(f32[8,4,256]{2,1,0:T(4,128)S(1)} %get-tuple-element.117.refs_0_, f32[8,4,256]{2,1,0:T(4,128)S(1)} %collective-permute-done.9.refs_1_, ...), custom_call_target="tpu_custom_call" | custom-call | flops 6000000000 | bytes 18000000 | tf_op jit(solution)/shard_map/middle/pallas_call | solution.py:856
  45.2 1.1 %collective-permute-done.12.crossed_ref = bf16[2,512,512]{2,1,0:T(8,128)(2,1)S(1)} collective-permute-done((bf16[2,512,512]{2,1,0:T(8,128)(2,1)S(1)}, bf16[2,512,512]{2,1,0:T(8,128)(2,1)S(1)}, u32[]{:S(2)}, u32[]{:S(2)}) %collective-permute-start.12) | collective-permute-done | bytes 1048608 | tf_op jit(solution)/shard_map/ppermute | solution.py:52
  46.4 0.2 rows.2
  46.6 0.0 copy-start.14
  46.6 1.0 %collective-permute-start.14 = (bf16[512,512]{1,0:T(8,128)(2,1)S(1)}, bf16[512,512]{1,0:T(8,128)(2,1)S(1)}, u32[]{:S(2)}, u32[]{:S(2)}) collective-permute-start(bf16[512,512]{1,0:T(8,128)(2,1)S(1)} %get-tuple-element.139), channel_id=1, source_target_pairs={{0,2},{1,3},{2,0},{3,1},{4,6},{5,7},{6,4},{7,5},{8,10},{9,11},{10,... | collective-permute-start | bytes 1572872 | tf_op jit(solution)/shard_map/ppermute | solution.py:52
  47.6 4.3 %values.1 = (bf16[8,256,128]{2,1,0:T(8,128)(2,1)S(1)}, bf16[4,64,384]{2,1,0:T(8,128)(2,1)S(1)}, bf16[4,64,384]{2,1,0:T(8,128)(2,1)S(1)}) custom-call(bf16[21,256,512]{2,1,0:T(8,128)(2,1)S(1)} %get-tuple-element.134.refs_0_, bf16[15,256,512]{2,1,0:T(8,128)(2,1)S(1)} %get-tuple-element.135.refs_1_, bf16[8,256,128]{2,1,0:T(8,128)(2,1)S(1)} %get-tuple-element.136.refs_2_, ...), custom_call_target="tpu_custom_call" | custom-call | flops 12000000000 | bytes 36000000 | tf_op jit(solution)/shard_map/values/pallas_call | solution.py:872
  51.9 1.6 %collective-permute-start.13 = (bf16[4,64,384]{2,1,0:T(8,128)(2,1)S(1)}, bf16[4,64,384]{2,1,0:T(8,128)(2,1)S(1)}, u32[]{:S(2)}, u32[]{:S(2)}) collective-permute-start(bf16[4,64,384]{2,1,0:T(8,128)(2,1)S(1)} %get-tuple-element.138), channel_id=1, source_target_pairs={{0,4},{4,0},{8,12},{12,8},{16,20},{20,16},{24,28},{28,24},{1,5},{5... | collective-permute-start | bytes 589832 | tf_op jit(solution)/shard_map/ppermute | solution.py:52
  53.5 10.6 %backward.1 = (bf16[8,256,256]{2,1,0:T(8,128)(2,1)S(1)}, bf16[4,80,256]{2,1,0:T(8,128)(2,1)S(1)}, bf16[4,80,256]{2,1,0:T(8,128)(2,1)S(1)}) custom-call(bf16[21,256,512]{2,1,0:T(8,128)(2,1)S(1)} %get-tuple-element.122.refs_0_, bf16[15,256,512]{2,1,0:T(8,128)(2,1)S(1)} %get-tuple-element.123.refs_1_, ...), custom_call_target="tpu_custom_call" | custom-call | flops 2000000000 | bytes 6000000 | tf_op jit(solution)/shard_map/backward/pallas_call | solution.py:885
  64.1 0.6 collective-permute-start.15
  64.7 1.3 %input_rows.1 = (bf16[2,512,512]{2,1,0:T(8,128)(2,1)S(1)}, bf16[2,512,512]{2,1,0:T(8,128)(2,1)S(1)}) custom-call(bf16[8,256,256]{2,1,0:T(8,128)(2,1)S(1)} %get-tuple-element.146.gp_ref, bf16[8,256,128]{2,1,0:T(8,128)(2,1)S(1)} %get-tuple-element.147.gun_ref, bf16[8,256,128]{2,1,0:T(8,128)(2,1)S(1)} %get-tuple-element.148.gpv_ref, ...), custom_call_target="tpu_custom_call" | custom-call | flops 4000000000 | bytes 12000000 | tf_op jit(solution)/shard_map/input_rows/pallas_call | solution.py:905
  66.0 0.1 collective-permute-start.16
  66.0 0.1 fold.3
  66.1 3.3 %collective-permute-start.20 = (bf16[64,384]{1,0:T(8,128)(2,1)S(1)}, bf16[64,384]{1,0:T(8,128)(2,1)S(1)}, u32[]{:S(2)}, u32[]{:S(2)}) collective-permute-start(bf16[64,384]{1,0:T(8,128)(2,1)S(1)} %get-tuple-element.160), channel_id=1, source_target_pairs={{0,16},{4,20},{8,24},{12,28},{16,0},{20,4},{24,8},{28,12},{1,17},{... | collective-permute-start | bytes 147464 | tf_op jit(solution)/shard_map/ppermute | solution.py:52
  69.4 1.4 %collective-permute-start.21 = (bf16[64,384]{1,0:T(8,128)(2,1)S(1)}, bf16[64,384]{1,0:T(8,128)(2,1)S(1)}, u32[]{:S(2)}, u32[]{:S(2)}) collective-permute-start(bf16[64,384]{1,0:T(8,128)(2,1)S(1)} %get-tuple-element.161), channel_id=1, source_target_pairs={{0,8},{4,12},{8,0},{12,4},{16,24},{20,28},{24,16},{28,20},{1,9},{5... | collective-permute-start | bytes 147464 | tf_op jit(solution)/shard_map/ppermute | solution.py:52
  70.9 0.1 collective-permute-start.22
  71.0 2.2 %collective-permute-start.17 = (bf16[80,256]{1,0:T(8,128)(2,1)S(1)}, bf16[80,256]{1,0:T(8,128)(2,1)S(1)}, u32[]{:S(2)}, u32[]{:S(2)}) collective-permute-start(bf16[80,256]{1,0:T(8,128)(2,1)S(1)} %get-tuple-element.150), channel_id=1, source_target_pairs={{0,16},{4,20},{8,24},{12,28},{16,0},{20,4},{24,8},{28,12},{1,17},{... | collective-permute-start | bytes 122888 | tf_op jit(solution)/shard_map/ppermute | solution.py:52
  73.3 2.1 %collective-permute-start.18 = (bf16[80,256]{1,0:T(8,128)(2,1)S(1)}, bf16[80,256]{1,0:T(8,128)(2,1)S(1)}, u32[]{:S(2)}, u32[]{:S(2)}) collective-permute-start(bf16[80,256]{1,0:T(8,128)(2,1)S(1)} %get-tuple-element.151), channel_id=1, source_target_pairs={{0,8},{4,12},{8,0},{12,4},{16,24},{20,28},{24,16},{28,20},{1,9},{5... | collective-permute-start | bytes 122888 | tf_op jit(solution)/shard_map/ppermute | solution.py:52
  75.4 1.7 %collective-permute-start.19 = (bf16[80,256]{1,0:T(8,128)(2,1)S(1)}, bf16[80,256]{1,0:T(8,128)(2,1)S(1)}, u32[]{:S(2)}, u32[]{:S(2)}) collective-permute-start(bf16[80,256]{1,0:T(8,128)(2,1)S(1)} %get-tuple-element.152), channel_id=1, source_target_pairs={{0,24},{4,28},{8,16},{12,20},{16,8},{20,12},{24,0},{28,4},{1,25},{... | collective-permute-start | bytes 122888 | tf_op jit(solution)/shard_map/ppermute | solution.py:52
  77.0 0.1 collective-permute-done.22.refs_3_
  77.2 0.9 rows.3
  78.0 1.1 %collective-permute-start.23 = (bf16[256,512]{1,0:T(8,128)(2,1)S(1)}, bf16[256,512]{1,0:T(8,128)(2,1)}, u32[]{:S(2)}, u32[]{:S(2)}) collective-permute-start(bf16[256,512]{1,0:T(8,128)(2,1)S(1)} %get-tuple-element.166), channel_id=1, source_target_pairs={{0,2},{1,3},{2,0},{3,1},{4,6},{5,7},{6,4},{7,5},{8,10},{9,11},{10,... | collective-permute-start | bytes 786440 | tf_op jit(solution)/shard_map/ppermute | solution.py:52
  79.2 0.9 collective-permute-start.24
  80.1 1.1 %collective-permute-done.19.refs_3_ = bf16[80,256]{1,0:T(8,128)(2,1)S(1)} collective-permute-done((bf16[80,256]{1,0:T(8,128)(2,1)S(1)}, bf16[80,256]{1,0:T(8,128)(2,1)S(1)}, u32[]{:S(2)}, u32[]{:S(2)}) %collective-permute-start.19) | collective-permute-done | bytes 40992 | tf_op jit(solution)/shard_map/ppermute | solution.py:52
  81.2 0.8 collect.1
  81.9 3.5 %all-to-all-start = ((f32[32,4,128]{2,1,0:T(4,128)}), f32[32,4,128]{2,1,0:T(4,128)S(1)}, u32[]{:S(2)}, u32[]{:S(2)}) async-start(f32[32,4,128]{2,1,0:T(4,128)} %get-tuple-element.168), calls=%async_computation | async-start | bytes 131072 | tf_op jit(solution)/shard_map/all_to_all | solution.py:933
  85.5 0.0 copy-start.15
  85.5 1.2 %copy-done.15 = f32[512,512]{1,0:T(8,128)S(1)} copy-done((f32[512,512]{1,0:T(8,128)S(1)}, f32[512,512]{1,0:T(8,128)}, u32[]{:S(2)}) %copy-start.15) | copy-done | bytes 1048600
  86.7 1.0 %mix.1 = bf16[512,512]{1,0:T(8,128)(2,1)} custom-call(bf16[512,512]{1,0:T(8,128)(2,1)S(1)} %copy-done, f32[69,128]{1,0:T(8,128)S(1)} %bitcast.18, f32[512,512]{1,0:T(8,128)S(1)} %copy-done.15, bf16[512,512]{1,0:T(8,128)(2,1)S(1)} %collective-permute-done.14.refs_1_), custom_call_target="tpu_custom_call" | custom-call | flops 1000000000 | bytes 3000000 | tf_op jit(solution)/shard_map/mix/pallas_call | solution.py:934
  87.7 0.0 copy-start.8
  87.8 0.0 copy-start.10
  87.8 2.2 %finish.2.refs_0_ = f32[512,512]{1,0:T(8,128)} custom-call(bf16[512,512]{1,0:T(8,128)(2,1)S(1)} %copy-done, bf16[512,512]{1,0:T(8,128)(2,1)S(1)} %copy-done.1, f32[512,512]{1,0:T(8,128)S(1)} %get-tuple-element.171.refs_2_.refs_3_, bf16[256,512]{1,0:T(8,128)(2,1)} %collective-permute-done.23.refs_3_), custom_call_target="tpu_custom_call" | custom-call | flops 1000000000 | bytes 3000000 | tf_op jit(solution)/shard_map/finish/pallas_call | solution.py:942
  90.0 1.8 %collective-permute-done.24.refs_4_ = bf16[256,512]{1,0:T(8,128)(2,1)S(1)} collective-permute-done((bf16[256,512]{1,0:T(8,128)(2,1)}, bf16[256,512]{1,0:T(8,128)(2,1)S(1)}, u32[]{:S(2)}, u32[]{:S(2)}) %collective-permute-start.24) | collective-permute-done | bytes 262176 | tf_op jit(solution)/shard_map/ppermute | solution.py:52
  91.9 1.2 %finish.3 = f32[512,512]{1,0:T(8,128)} custom-call(f32[512,512]{1,0:T(8,128)} %finish.2.refs_0_, bf16[512,512]{1,0:T(8,128)(2,1)S(1)} %copy-done, bf16[512,512]{1,0:T(8,128)(2,1)S(1)} %copy-done.1, f32[512,512]{1,0:T(8,128)S(1)} %get-tuple-element.171.refs_2_.refs_3_, ...), custom_call_target="tpu_custom_call", output_to_operand_aliasing={{}: (0, {})} | custom-call | flops 1000000000 | bytes 3000000 | tf_op jit(solution)/shard_map/finish/pallas_call | solution.py:942
  93.1 1.7 %update.1 = (f32[64,4,128]{2,1,0:T(4,128)}, f32[64,128]{1,0:T(8,128)}, f32[69,128]{1,0:T(8,128)}, f32[1,1]{1,0:T(1,128)}, f32[64,4,128]{2,1,0:T(4,128)}, /*index...) custom-call(f32[32,4,128]{2,1,0:T(4,128)S(1)} %all-to-all-done.heard, ...), custom_call_target="tpu_custom_call" | custom-call | flops 100000000 | bytes 300000 | tf_op jit(solution)/shard_map/update/pallas_call | solution.py:957
  (49 shorter events, 0.2 us)
Async XLA Ops:
  0.6 0.9 copy-start.2
  1.6 0.8 copy-start.9
  2.3 9.5 %copy-start.6 = (f32[8832]{0:T(1024)S(1)}, f32[8832]{0:T(1024)}, u32[]{:S(2)}) copy-start(f32[8832]{0:T(1024)} %param.19) | copy-start | bytes 105988
  2.3 9.5 %copy-start.16 = (s32[2048]{0:T(1024)S(1)}, s32[2048]{0:T(1024)}, u32[]{:S(2)}) copy-start(s32[2048]{0:T(1024)} %param.16) | copy-start | bytes 24580
  2.7 8.3 %collective-permute-start.5 = (bf16[64,640]{1,0:T(8,128)(2,1)S(1)}, bf16[64,640]{1,0:T(8,128)(2,1)S(1)}, u32[]{:S(2)}, u32[]{:S(2)}) collective-permute-start(bf16[64,640]{1,0:T(8,128)(2,1)S(1)} %cast.1.refs_0_), channel_id=1, source_target_pairs={{0,16},{4,20},{8,24},{12,28},{16,0},{20,4},{24,8},{28,12},{1,17},{... | collective-permute-start | bytes 245768 | tf_op jit(solution)/shard_map/ppermute | solution.py:52
  6.8 14.6 %collective-permute-start.2 = (bf16[512,512]{1,0:T(8,128)(2,1)}, bf16[512,512]{1,0:T(8,128)(2,1)S(1)}, u32[]{:S(2)}, u32[]{:S(2)}) collective-permute-start(bf16[512,512]{1,0:T(8,128)(2,1)} %refs_1_.4), channel_id=1, source_target_pairs={{0,1},{1,0},{2,3},{3,2},{4,5},{5,4},{6,7},{7,6},{8,9},{9,8},{10,11... | collective-permute-start | bytes 1572872 | tf_op jit(solution)/shard_map/ppermute | solution.py:52
  6.8 14.5 %collective-permute-start.3 = (bf16[512,512]{1,0:T(8,128)(2,1)}, bf16[512,512]{1,0:T(8,128)(2,1)S(1)}, u32[]{:S(2)}, u32[]{:S(2)}) collective-permute-start(bf16[512,512]{1,0:T(8,128)(2,1)} %refs_1_.4), channel_id=1, source_target_pairs={{0,2},{1,3},{2,0},{3,1},{4,6},{5,7},{6,4},{7,5},{8,10},{9,11},{10,... | collective-permute-start | bytes 1572872 | tf_op jit(solution)/shard_map/ppermute | solution.py:52
  11.0 5.4 %collective-permute-start.6 = (bf16[128,640]{1,0:T(8,128)(2,1)S(1)}, bf16[128,640]{1,0:T(8,128)(2,1)S(1)}, u32[]{:S(2)}, u32[]{:S(2)}) collective-permute-start(bf16[128,640]{1,0:T(8,128)(2,1)S(1)} %join.3), channel_id=1, source_target_pairs={{0,8},{4,12},{8,0},{12,4},{16,24},{20,28},{24,16},{28,20},{1,9},{5... | collective-permute-start | bytes 491528 | tf_op jit(solution)/shard_map/ppermute | solution.py:52
  11.8 6.4 %copy-start.1 = (bf16[512,512]{1,0:T(8,128)(2,1)S(1)}, bf16[512,512]{1,0:T(8,128)(2,1)}, u32[]{:S(2)}) copy-start(bf16[512,512]{1,0:T(8,128)(2,1)} %refs_2_.2) | copy-start | bytes 1572868
  11.8 9.5 %copy-start = (bf16[512,512]{1,0:T(8,128)(2,1)S(1)}, bf16[512,512]{1,0:T(8,128)(2,1)}, u32[]{:S(2)}) copy-start(bf16[512,512]{1,0:T(8,128)(2,1)} %refs_1_.4) | copy-start | bytes 1572868
  16.4 7.7 %collective-permute-start.7 = (bf16[256,640]{1,0:T(8,128)(2,1)S(1)}, bf16[256,640]{1,0:T(8,128)(2,1)S(1)}, u32[]{:S(2)}, u32[]{:S(2)}) collective-permute-start(bf16[256,640]{1,0:T(8,128)(2,1)S(1)} %join.4), channel_id=1, source_target_pairs={{0,4},{4,0},{8,12},{12,8},{16,20},{20,16},{24,28},{28,24},{1,5},{5... | collective-permute-start | bytes 983048 | tf_op jit(solution)/shard_map/ppermute | solution.py:52
  18.2 17.9 %collective-permute-start = (bf16[512,512]{1,0:T(8,128)(2,1)S(1)}, bf16[512,512]{1,0:T(8,128)(2,1)S(1)}, u32[]{:S(2)}, u32[]{:S(2)}) collective-permute-start(bf16[512,512]{1,0:T(8,128)(2,1)S(1)} %copy-done.1), channel_id=1, source_target_pairs={{0,1},{1,0},{2,3},{3,2},{4,5},{5,4},{6,7},{7,6},{8,9},{9,8},{10,11... | collective-permute-start | bytes 1572872 | tf_op jit(solution)/shard_map/ppermute | solution.py:52
  18.2 14.4 %collective-permute-start.1 = (bf16[512,512]{1,0:T(8,128)(2,1)S(1)}, bf16[512,512]{1,0:T(8,128)(2,1)S(1)}, u32[]{:S(2)}, u32[]{:S(2)}) collective-permute-start(bf16[512,512]{1,0:T(8,128)(2,1)S(1)} %copy-done.1), channel_id=1, source_target_pairs={{0,2},{1,3},{2,0},{3,1},{4,6},{5,7},{6,4},{7,5},{8,10},{9,11},{10,... | collective-permute-start | bytes 1572872 | tf_op jit(solution)/shard_map/ppermute | solution.py:52
  21.3 2.8 %collective-permute-start.4 = (bf16[512,512]{1,0:T(8,128)(2,1)S(1)}, bf16[512,512]{1,0:T(8,128)(2,1)S(1)}, u32[]{:S(2)}, u32[]{:S(2)}) collective-permute-start(bf16[512,512]{1,0:T(8,128)(2,1)S(1)} %collective-permute-done.3.refs_2_), channel_id=1, source_target_pairs={{0,1},{1,0},{2,3},{3,2},{4,5},{5,4},{6,7},{7,6},{8,9},{9,8},{10,11... | collective-permute-start | bytes 1572872 | tf_op jit(solution)/shard_map/ppermute | solution.py:52
  24.5 2.2 %copy-start.13 = (s32[2048]{0:T(1024)S(1)}, s32[2048]{0:T(1024)}, u32[]{:S(2)}) copy-start(s32[2048]{0:T(1024)} %param.15) | copy-start | bytes 24580
  32.6 3.5 %collective-permute-start.8 = (bf16[512,512]{1,0:T(8,128)(2,1)S(1)}, bf16[512,512]{1,0:T(8,128)(2,1)S(1)}, u32[]{:S(2)}, u32[]{:S(2)}) collective-permute-start(bf16[512,512]{1,0:T(8,128)(2,1)S(1)} %collective-permute-done.1.refs_2_.refs_6_), channel_id=1, source_target_pairs={{0,1},{1,0},{2,3},{3,2},{4,5},{5,4},{6,7},{7,6},{8,9},{9,8},{10,11... | collective-permute-start | bytes 1572872 | tf_op jit(solution)/shard_map/ppermute | solution.py:52
  37.9 4.0 %collective-permute-start.10 = (f32[8,4,256]{2,1,0:T(4,128)S(1)}, f32[8,4,256]{2,1,0:T(4,128)S(1)}, u32[]{:S(2)}, u32[]{:S(2)}) collective-permute-start(f32[8,4,256]{2,1,0:T(4,128)S(1)} %get-tuple-element.117.refs_0_), channel_id=1, source_target_pairs={{0,2},{1,3},{2,0},{3,1},{4,6},{5,7},{6,4},{7,5},{8,10},{9,11},{10,... | collective-permute-start | bytes 98312 | tf_op jit(solution)/shard_map/ppermute | solution.py:52
  39.5 3.3 %collective-permute-start.11 = (f32[8,4,256]{2,1,0:T(4,128)S(1)}, f32[8,4,256]{2,1,0:T(4,128)S(1)}, u32[]{:S(2)}, u32[]{:S(2)}) collective-permute-start(f32[8,4,256]{2,1,0:T(4,128)S(1)} %get-tuple-element.117.refs_0_), channel_id=1, source_target_pairs={{0,3},{1,2},{2,1},{3,0},{4,7},{5,6},{6,5},{7,4},{8,11},{9,10},{10,... | collective-permute-start | bytes 98312 | tf_op jit(solution)/shard_map/ppermute | solution.py:52
  39.8 3.0 %collective-permute-start.9 = (f32[8,4,256]{2,1,0:T(4,128)S(1)}, f32[8,4,256]{2,1,0:T(4,128)S(1)}, u32[]{:S(2)}, u32[]{:S(2)}) collective-permute-start(f32[8,4,256]{2,1,0:T(4,128)S(1)} %get-tuple-element.117.refs_0_), channel_id=1, source_target_pairs={{0,1},{1,0},{2,3},{3,2},{4,5},{5,4},{6,7},{7,6},{8,9},{9,8},{10,11... | collective-permute-start | bytes 98312 | tf_op jit(solution)/shard_map/ppermute | solution.py:52
  43.7 2.7 %collective-permute-start.12 = (bf16[2,512,512]{2,1,0:T(8,128)(2,1)S(1)}, bf16[2,512,512]{2,1,0:T(8,128)(2,1)S(1)}, u32[]{:S(2)}, u32[]{:S(2)}) collective-permute-start(bf16[2,512,512]{2,1,0:T(8,128)(2,1)S(1)} %get-tuple-element.120), channel_id=1, source_target_pairs={{0,1},{1,0},{2,3},{3,2},{4,5},{5,4},{6,7},{7,6},{8,9},{9,8},{10,11... | collective-permute-start | bytes 3145736 | tf_op jit(solution)/shard_map/ppermute | solution.py:52
  46.6 5.3 %copy-start.14 = (f32[512,512]{1,0:T(8,128)}, f32[512,512]{1,0:T(8,128)S(1)}, u32[]{:S(2)}) copy-start(f32[512,512]{1,0:T(8,128)S(1)} %get-tuple-element.169.refs_0_) | copy-start | bytes 3145732
  46.6 17.5 %collective-permute-start.14 = (bf16[512,512]{1,0:T(8,128)(2,1)S(1)}, bf16[512,512]{1,0:T(8,128)(2,1)S(1)}, u32[]{:S(2)}, u32[]{:S(2)}) collective-permute-start(bf16[512,512]{1,0:T(8,128)(2,1)S(1)} %get-tuple-element.139), channel_id=1, source_target_pairs={{0,2},{1,3},{2,0},{3,1},{4,6},{5,7},{6,4},{7,5},{8,10},{9,11},{10,... | collective-permute-start | bytes 1572872 | tf_op jit(solution)/shard_map/ppermute | solution.py:52
  51.9 12.2 %collective-permute-start.13 = (bf16[4,64,384]{2,1,0:T(8,128)(2,1)S(1)}, bf16[4,64,384]{2,1,0:T(8,128)(2,1)S(1)}, u32[]{:S(2)}, u32[]{:S(2)}) collective-permute-start(bf16[4,64,384]{2,1,0:T(8,128)(2,1)S(1)} %get-tuple-element.138), channel_id=1, source_target_pairs={{0,4},{4,0},{8,12},{12,8},{16,20},{20,16},{24,28},{28,24},{1,5},{5... | collective-permute-start | bytes 589832 | tf_op jit(solution)/shard_map/ppermute | solution.py:52
  64.1 6.9 %collective-permute-start.15 = (bf16[4,80,256]{2,1,0:T(8,128)(2,1)S(1)}, bf16[4,80,256]{2,1,0:T(8,128)(2,1)S(1)}, u32[]{:S(2)}, u32[]{:S(2)}) collective-permute-start(bf16[4,80,256]{2,1,0:T(8,128)(2,1)S(1)} %get-tuple-element.141), channel_id=1, source_target_pairs={{0,4},{4,0},{8,12},{12,8},{16,20},{20,16},{24,28},{28,24},{1,5},{5... | collective-permute-start | bytes 491528 | tf_op jit(solution)/shard_map/ppermute | solution.py:52
  66.0 5.1 %collective-permute-start.16 = (bf16[2,512,512]{2,1,0:T(8,128)(2,1)S(1)}, bf16[2,512,512]{2,1,0:T(8,128)(2,1)S(1)}, u32[]{:S(2)}, u32[]{:S(2)}) collective-permute-start(bf16[2,512,512]{2,1,0:T(8,128)(2,1)S(1)} %get-tuple-element.149), channel_id=1, source_target_pairs={{0,1},{1,0},{2,3},{3,2},{4,5},{5,4},{6,7},{7,6},{8,9},{9,8},{10,11... | collective-permute-start | bytes 3145736 | tf_op jit(solution)/shard_map/ppermute | solution.py:52
  66.1 9.3 %collective-permute-start.20 = (bf16[64,384]{1,0:T(8,128)(2,1)S(1)}, bf16[64,384]{1,0:T(8,128)(2,1)S(1)}, u32[]{:S(2)}, u32[]{:S(2)}) collective-permute-start(bf16[64,384]{1,0:T(8,128)(2,1)S(1)} %get-tuple-element.160), channel_id=1, source_target_pairs={{0,16},{4,20},{8,24},{12,28},{16,0},{20,4},{24,8},{28,12},{1,17},{... | collective-permute-start | bytes 147464 | tf_op jit(solution)/shard_map/ppermute | solution.py:52
  69.4 7.6 %collective-permute-start.21 = (bf16[64,384]{1,0:T(8,128)(2,1)S(1)}, bf16[64,384]{1,0:T(8,128)(2,1)S(1)}, u32[]{:S(2)}, u32[]{:S(2)}) collective-permute-start(bf16[64,384]{1,0:T(8,128)(2,1)S(1)} %get-tuple-element.161), channel_id=1, source_target_pairs={{0,8},{4,12},{8,0},{12,4},{16,24},{20,28},{24,16},{28,20},{1,9},{5... | collective-permute-start | bytes 147464 | tf_op jit(solution)/shard_map/ppermute | solution.py:52
  70.9 6.3 %collective-permute-start.22 = (bf16[64,384]{1,0:T(8,128)(2,1)S(1)}, bf16[64,384]{1,0:T(8,128)(2,1)S(1)}, u32[]{:S(2)}, u32[]{:S(2)}) collective-permute-start(bf16[64,384]{1,0:T(8,128)(2,1)S(1)} %get-tuple-element.162), channel_id=1, source_target_pairs={{0,24},{4,28},{8,16},{12,20},{16,8},{20,12},{24,0},{28,4},{1,25},{... | collective-permute-start | bytes 147464 | tf_op jit(solution)/shard_map/ppermute | solution.py:52
  71.0 9.0 %collective-permute-start.17 = (bf16[80,256]{1,0:T(8,128)(2,1)S(1)}, bf16[80,256]{1,0:T(8,128)(2,1)S(1)}, u32[]{:S(2)}, u32[]{:S(2)}) collective-permute-start(bf16[80,256]{1,0:T(8,128)(2,1)S(1)} %get-tuple-element.150), channel_id=1, source_target_pairs={{0,16},{4,20},{8,24},{12,28},{16,0},{20,4},{24,8},{28,12},{1,17},{... | collective-permute-start | bytes 122888 | tf_op jit(solution)/shard_map/ppermute | solution.py:52
  73.3 6.8 %collective-permute-start.18 = (bf16[80,256]{1,0:T(8,128)(2,1)S(1)}, bf16[80,256]{1,0:T(8,128)(2,1)S(1)}, u32[]{:S(2)}, u32[]{:S(2)}) collective-permute-start(bf16[80,256]{1,0:T(8,128)(2,1)S(1)} %get-tuple-element.151), channel_id=1, source_target_pairs={{0,8},{4,12},{8,0},{12,4},{16,24},{20,28},{24,16},{28,20},{1,9},{5... | collective-permute-start | bytes 122888 | tf_op jit(solution)/shard_map/ppermute | solution.py:52
  75.4 5.8 %collective-permute-start.19 = (bf16[80,256]{1,0:T(8,128)(2,1)S(1)}, bf16[80,256]{1,0:T(8,128)(2,1)S(1)}, u32[]{:S(2)}, u32[]{:S(2)}) collective-permute-start(bf16[80,256]{1,0:T(8,128)(2,1)S(1)} %get-tuple-element.152), channel_id=1, source_target_pairs={{0,24},{4,28},{8,16},{12,20},{16,8},{20,12},{24,0},{28,4},{1,25},{... | collective-permute-start | bytes 122888 | tf_op jit(solution)/shard_map/ppermute | solution.py:52
  78.0 9.7 %collective-permute-start.23 = (bf16[256,512]{1,0:T(8,128)(2,1)S(1)}, bf16[256,512]{1,0:T(8,128)(2,1)}, u32[]{:S(2)}, u32[]{:S(2)}) collective-permute-start(bf16[256,512]{1,0:T(8,128)(2,1)S(1)} %get-tuple-element.166), channel_id=1, source_target_pairs={{0,2},{1,3},{2,0},{3,1},{4,6},{5,7},{6,4},{7,5},{8,10},{9,11},{10,... | collective-permute-start | bytes 786440 | tf_op jit(solution)/shard_map/ppermute | solution.py:52
  79.2 12.7 %collective-permute-start.24 = (bf16[256,512]{1,0:T(8,128)(2,1)}, bf16[256,512]{1,0:T(8,128)(2,1)S(1)}, u32[]{:S(2)}, u32[]{:S(2)}) collective-permute-start(bf16[256,512]{1,0:T(8,128)(2,1)} %get-tuple-element.167), channel_id=1, source_target_pairs={{0,2},{1,3},{2,0},{3,1},{4,6},{5,7},{6,4},{7,5},{8,10},{9,11},{10,... | collective-permute-start | bytes 786440 | tf_op jit(solution)/shard_map/ppermute | solution.py:52
  81.9 11.1 %all-to-all-start = ((f32[32,4,128]{2,1,0:T(4,128)}), f32[32,4,128]{2,1,0:T(4,128)S(1)}, u32[]{:S(2)}, u32[]{:S(2)}) async-start(f32[32,4,128]{2,1,0:T(4,128)} %get-tuple-element.168), calls=%async_computation | async-start | bytes 131072 | tf_op jit(solution)/shard_map/all_to_all | solution.py:933
  85.5 1.2 %copy-start.15 = (f32[512,512]{1,0:T(8,128)S(1)}, f32[512,512]{1,0:T(8,128)}, u32[]{:S(2)}) copy-start(f32[512,512]{1,0:T(8,128)} %copy-done.14) | copy-start | bytes 3145732
  87.7 5.3 %copy-start.3 = (f32[64,4,128]{2,1,0:T(4,128)S(1)}, f32[64,4,128]{2,1,0:T(4,128)}, u32[]{:S(2)}) copy-start(f32[64,4,128]{2,1,0:T(4,128)} %refs_0_.7) | copy-start | bytes 393220
  87.7 5.3 %copy-start.4 = (f32[64,4,128]{2,1,0:T(4,128)S(1)}, f32[64,4,128]{2,1,0:T(4,128)}, u32[]{:S(2)}) copy-start(f32[64,4,128]{2,1,0:T(4,128)} %refs_1_.5) | copy-start | bytes 393220
  87.7 5.3 %copy-start.5 = (f32[64,4,128]{2,1,0:T(4,128)S(1)}, f32[64,4,128]{2,1,0:T(4,128)}, u32[]{:S(2)}) copy-start(f32[64,4,128]{2,1,0:T(4,128)} %refs_2_.3) | copy-start | bytes 393220
  87.7 5.3 %copy-start.7 = (f32[8832]{0:T(1024)S(1)}, f32[8832]{0:T(1024)}, u32[]{:S(2)}) copy-start(f32[8832]{0:T(1024)} %param.24) | copy-start | bytes 105988
  87.7 5.3 %copy-start.8 = (f32[8832]{0:T(1024)S(1)}, f32[8832]{0:T(1024)}, u32[]{:S(2)}) copy-start(f32[8832]{0:T(1024)} %param.25) | copy-start | bytes 105988
  87.8 5.3 %copy-start.10 = (f32[128,64]{0,1:T(8,128)S(1)}, f32[128,64]{0,1:T(8,128)}, u32[]{:S(2)}) copy-start(f32[128,64]{0,1:T(8,128)} %param.18) | copy-start | bytes 98308
  87.8 5.3 %copy-start.11 = (f32[128,64]{0,1:T(8,128)S(1)}, f32[128,64]{0,1:T(8,128)}, u32[]{:S(2)}) copy-start(f32[128,64]{0,1:T(8,128)} %param.22) | copy-start | bytes 98308
  87.8 5.3 %copy-start.12 = (f32[128,64]{0,1:T(8,128)S(1)}, f32[128,64]{0,1:T(8,128)}, u32[]{:S(2)}) copy-start(f32[128,64]{0,1:T(8,128)} %param.23) | copy-start | bytes 98308

commit v9 on v8

--- a/solution.py
+++ b/solution.py
@@ -108,8 +108,7 @@
         us,
     )(own, *received)
     leaving = after_all(leaving, *behind)
-    order = sorted(range(1, high), key=lambda k: k != high // 2)
-    return [mine] + [swap(leaving[k - 1], "dp", k * low) for k in order]
+    return [mine] + [swap(leaving[k - 1], "dp", k * low) for k in reversed(range(1, high))]
 
 
 def fold_cores(keep, crossed, cuts=1):

time: 95.2 us -> 94.4 us (level)
    ppermute x25, starting transfers between devices: 28.2 us -> 26.7 us  [swap(): return lax.ppermute(x, axis, [(i, i ^ k) for i in range(n)])]
  transfers between devices with their start and end apart: 26 -> 26, of which waited for: 11 -> 12; matrix products, arithmetic and copies ran while one was open for 0% -> 0% of each run, Pallas kernels for 40% -> 40%
where the time goes in v9:
time: 94.4 us; the launch traced here: 94.1 us
  Pallas kernels  42.8 us (45%)
  starting transfers between devices  31 us (33%)
  waiting for transfers between devices  16.3 us (17%)
  local copies, waits for them, and re-layouts  2.95 us (3%)
  between operations  1.09 us (1%)
    ppermute x25, starting transfers between devices, swap(): return lax.ppermute(x, axis, [(i, i ^ k) for i in range(n)])  26.7 us
    ppermute x25, waiting for transfers between devices, swap(): return lax.ppermute(x, axis, [(i, i ^ k) for i in range(n)])  15.6 us
    pallas_call x1, Pallas kernels, shards(): call(functools.partial(backward_kernel, heads, n_dp, extra, kept), 'backw...  10.6 us
    pallas_call x2, Pallas kernels, attend(): call(functools.partial(attend_kernel, heads, first, last, kept), 'attend'...  8.23 us
    all_to_all x1, starting transfers between devices, shards(): heard = lax.all_to_all(message, ('dp', 'head'), 0, 0, tiled=True)  4.33 us
    pallas_call x1, Pallas kernels, shards(): call(functools.partial(values_kernel, heads, kept), 'values', [VMEM] * (l...  4.31 us
    pallas_call x2, Pallas kernels, shards(): call(functools.partial(finish_kernel, part), 'finish', [pl.BlockSpec(memo...  3.39 us
    unnamed x34, local copies, waits for them, and re-layouts  2.95 us
  transfers between devices with their start and end apart: 26, of which 12 were waited for; matrix products, arithmetic and copies ran while one was open for 0% of the time, Pallas kernels for 40%

profile of v9, /device:TPU:0, one launch (start us, length us, event | category | flops | bytes accessed | tf_op | source)
XLA Modules:
  0.0 94.1 jit_solution(14834142733504810570)
XLA Ops:
  0.6 0.0 copy-start.2
  0.7 0.9 copy-done.2
  1.6 0.8 copy-done.9
  2.3 0.3 cast.1.refs_0_
  2.7 4.1 %collective-permute-start.5 = (bf16[64,640]{1,0:T(8,128)(2,1)S(1)}, bf16[64,640]{1,0:T(8,128)(2,1)S(1)}, u32[]{:S(2)}, u32[]{:S(2)}) collective-permute-start(bf16[64,640]{1,0:T(8,128)(2,1)S(1)} %cast.1.refs_0_), channel_id=1, source_target_pairs={{0,16},{4,20},{8,24},{12,28},{16,0},{20,4},{24,8},{28,12},{1,17},{... | collective-permute-start | bytes 245768 | tf_op jit(solution)/shard_map/ppermute | solution.py:52
  6.8 1.5 %collective-permute-start.3 = (bf16[512,512]{1,0:T(8,128)(2,1)}, bf16[512,512]{1,0:T(8,128)(2,1)S(1)}, u32[]{:S(2)}, u32[]{:S(2)}) collective-permute-start(bf16[512,512]{1,0:T(8,128)(2,1)} %refs_1_.4), channel_id=1, source_target_pairs={{0,2},{1,3},{2,0},{3,1},{4,6},{5,7},{6,4},{7,5},{8,10},{9,11},{10,... | collective-permute-start | bytes 1572872 | tf_op jit(solution)/shard_map/ppermute | solution.py:52
  8.3 2.7 %collective-permute-done.5.refs_1_ = bf16[64,640]{1,0:T(8,128)(2,1)S(1)} collective-permute-done((bf16[64,640]{1,0:T(8,128)(2,1)S(1)}, bf16[64,640]{1,0:T(8,128)(2,1)S(1)}, u32[]{:S(2)}, u32[]{:S(2)}) %collective-permute-start.5) | collective-permute-done | bytes 81952 | tf_op jit(solution)/shard_map/ppermute | solution.py:52
  11.0 0.8 collective-permute-start.6
  11.8 2.5 %prepare.1 = (f32[8,256,256]{2,1,0:T(8,128)S(1)}, bf16[8,256,128]{2,1,0:T(8,128)(2,1)S(1)}, bf16[8,128,256]{2,1,0:T(8,128)(2,1)S(1)}, bf16[8,128,256]{2,1,0:T(8,128)(2,1)S(1)}) custom-call(s32[1,2048]{1,0:T(1,128)S(1)} %bitcast.28, f32[69,128]{1,0:T(8,128)S(1)} %bitcast.17), custom_call_target="tpu_custom_call" | custom-call | flops 2000000000 | bytes 6000000 | tf_op jit(solution)/shard_map/prepare/pallas_call | solution.py:760
  14.3 2.1 %collective-permute-done.6.refs_2_ = bf16[128,640]{1,0:T(8,128)(2,1)S(1)} collective-permute-done((bf16[128,640]{1,0:T(8,128)(2,1)S(1)}, bf16[128,640]{1,0:T(8,128)(2,1)S(1)}, u32[]{:S(2)}, u32[]{:S(2)}) %collective-permute-start.6) | collective-permute-done | bytes 163872 | tf_op jit(solution)/shard_map/ppermute | solution.py:52
  16.4 1.8 %collective-permute-start.7 = (bf16[256,640]{1,0:T(8,128)(2,1)S(1)}, bf16[256,640]{1,0:T(8,128)(2,1)S(1)}, u32[]{:S(2)}, u32[]{:S(2)}) collective-permute-start(bf16[256,640]{1,0:T(8,128)(2,1)S(1)} %join.4), channel_id=1, source_target_pairs={{0,4},{4,0},{8,12},{12,8},{16,20},{20,16},{24,28},{28,24},{1,5},{5... | collective-permute-start | bytes 983048 | tf_op jit(solution)/shard_map/ppermute | solution.py:52
  18.2 1.5 %collective-permute-start.1 = (bf16[512,512]{1,0:T(8,128)(2,1)S(1)}, bf16[512,512]{1,0:T(8,128)(2,1)S(1)}, u32[]{:S(2)}, u32[]{:S(2)}) collective-permute-start(bf16[512,512]{1,0:T(8,128)(2,1)S(1)} %copy-done.1), channel_id=1, source_target_pairs={{0,2},{1,3},{2,0},{3,1},{4,6},{5,7},{6,4},{7,5},{8,10},{9,11},{10,... | collective-permute-start | bytes 1572872 | tf_op jit(solution)/shard_map/ppermute | solution.py:52
  19.7 1.7 %collective-permute-done.3.refs_2_ = bf16[512,512]{1,0:T(8,128)(2,1)S(1)} collective-permute-done((bf16[512,512]{1,0:T(8,128)(2,1)}, bf16[512,512]{1,0:T(8,128)(2,1)S(1)}, u32[]{:S(2)}, u32[]{:S(2)}) %collective-permute-start.3) | collective-permute-done | bytes 524320 | tf_op jit(solution)/shard_map/ppermute | solution.py:52
  21.3 1.0 %normalize.2.refs_0_ = bf16[8,256,512]{2,1,0:T(8,128)(2,1)S(1)} custom-call(bf16[512,512]{1,0:T(8,128)(2,1)S(1)} %copy-done, bf16[512,512]{1,0:T(8,128)(2,1)S(1)} %collective-permute-done.2.refs_1_, bf16[512,512]{1,0:T(8,128)(2,1)S(1)} %collective-permute-done.3.refs_2_), custom_call_target="tpu_custom_call" | custom-call | flops 100000000 | bytes 300000 | tf_op jit(solution)/shard_map/normalize/pallas_call | solution.py:791
  22.3 1.8 %collective-permute-done.7.refs_0_ = bf16[256,640]{1,0:T(8,128)(2,1)S(1)} collective-permute-done((bf16[256,640]{1,0:T(8,128)(2,1)S(1)}, bf16[256,640]{1,0:T(8,128)(2,1)S(1)}, u32[]{:S(2)}, u32[]{:S(2)}) %collective-permute-start.7) | collective-permute-done | bytes 327712 | tf_op jit(solution)/shard_map/ppermute | solution.py:52
  24.1 0.4 normalize.3.refs_0_.refs_5_.refs_11_.refs_8_.refs_4_
  24.5 0.0 copy-start.13
  24.5 0.3 assemble.1.refs_1_.refs_6_.wt_ref
  24.8 1.8 %project.1 = (bf16[8,384,256]{2,1,0:T(8,128)(2,1)S(1)}, bf16[8,256,256]{2,1,0:T(8,128)(2,1)S(1)}, bf16[8,256,256]{2,1,0:T(8,128)(2,1)S(1)}, bf16[8,128,256]{2,1,...) custom-call(bf16[8,256,512]{2,1,0:T(8,128)(2,1)S(1)} %normalize.3.re, ...), custom_call_target="tpu_custom_call" | custom-call | flops 1000000000 | bytes 3000000 | tf_op jit(solution)/shard_map/project/pallas_call | solution.py:809
  26.7 4.7 %attend.2 = (f32[6,128,256]{2,1,0:T(8,128)S(1)}, bf16[21,256,512]{2,1,0:T(8,128)(2,1)S(1)}, bf16[21,256,512]{2,1,0:T(8,128)(2,1)S(1)}) custom-call(bf16[8,256,256]{2,1,0:T(8,128)(2,1)S(1)} %get-tuple-element.109.refs_0_.refs_1_.refs_2_, bf16[8,128,256]{2,1,0:T(8,128)(2,1)S(1)} %get-tuple-element.110.refs_1_.refs_2_, ...), custom_call_target="tpu_custom_call" | custom-call | flops 500000000 | bytes 1500000 | tf_op jit(solution)/shard_map/attend/pallas_call | solution.py:822
  31.4 1.2 %collective-permute-done.1.refs_2_.refs_6_ = bf16[512,512]{1,0:T(8,128)(2,1)S(1)} collective-permute-done((bf16[512,512]{1,0:T(8,128)(2,1)S(1)}, bf16[512,512]{1,0:T(8,128)(2,1)S(1)}, u32[]{:S(2)}, u32[]{:S(2)}) %collective-permute-start.1) | collective-permute-done | bytes 524320 | tf_op jit(solution)/shard_map/ppermute | solution.py:52
  32.6 3.5 %attend.3 = (f32[8,128,256]{2,1,0:T(8,128)S(1)}, bf16[15,256,512]{2,1,0:T(8,128)(2,1)S(1)}, bf16[15,256,512]{2,1,0:T(8,128)(2,1)S(1)}) custom-call(f32[6,128,256]{2,1,0:T(8,128)S(1)} %get-tuple-element.115.refs_0_, bf16[8,256,256]{2,1,0:T(8,128)(2,1)S(1)} %get-tuple-element.109.refs_0_.refs_1_.refs_2_, ...), custom_call_target="tpu_custom_call" | custom-call | flops 8000000000 | bytes 24000000 | tf_op jit(solution)/shard_map/attend/pallas_call | solution.py:822
  36.1 1.8 %gate.1 = (f32[8,128,256]{2,1,0:T(8,128)S(1)}, f32[8,128,256]{2,1,0:T(8,128)S(1)}, f32[8,4,256]{2,1,0:T(4,128)S(1)}, f32[1,512]{1,0:T(1,128)S(1)}) custom-call(bf16[512,512]{1,0:T(8,128)(2,1)S(1)} %copy-done.1, bf16[512,512]{1,0:T(8,128)(2,1)S(1)} %collective-permute-done.refs_1_.refs_5_, bf16[512,512]{1,0:T(8,128)(2,1)S(1)} %collective-permute-done.1.refs_2_.refs_6_, ...), custom_call_target="tpu_custom_call" | custom-call | flops 5000000000 | bytes 15000000 | tf_op jit(solution)/shard_map/gate/pallas_call | solution.py:839
  37.9 1.6 %collective-permute-start.10 = (f32[8,4,256]{2,1,0:T(4,128)S(1)}, f32[8,4,256]{2,1,0:T(4,128)S(1)}, u32[]{:S(2)}, u32[]{:S(2)}) collective-permute-start(f32[8,4,256]{2,1,0:T(4,128)S(1)} %get-tuple-element.117.refs_0_), channel_id=1, source_target_pairs={{0,2},{1,3},{2,0},{3,1},{4,6},{5,7},{6,4},{7,5},{8,10},{9,11},{10,... | collective-permute-start | bytes 98312 | tf_op jit(solution)/shard_map/ppermute | solution.py:52
  39.5 0.4 collective-permute-start.11
  39.8 0.3 collective-permute-start.9
  40.1 1.8 %collective-permute-done.10.refs_2_ = f32[8,4,256]{2,1,0:T(4,128)S(1)} collective-permute-done((f32[8,4,256]{2,1,0:T(4,128)S(1)}, f32[8,4,256]{2,1,0:T(4,128)S(1)}, u32[]{:S(2)}, u32[]{:S(2)}) %collective-permute-start.10) | collective-permute-done | bytes 32800 | tf_op jit(solution)/shard_map/ppermute | solution.py:52
  41.9 0.9 collective-permute-done.11.refs_3_
  42.8 0.8 branch.1
  43.7 0.3 collective-permute-start.12
  44.0 1.3 %middle.1 = (bf16[8,256,128]{2,1,0:T(8,128)(2,1)S(1)}, bf16[8,128,256]{2,1,0:T(8,128)(2,1)S(1)}, bf16[8,256,128]{2,1,0:T(8,128)(2,1)S(1)}, f32[256,512]{1,0:T(8,128)S(1)}) custom-call(f32[8,4,256]{2,1,0:T(4,128)S(1)} %get-tuple-element.117.refs_0_, f32[8,4,256]{2,1,0:T(4,128)S(1)} %collective-permute-done.9.refs_1_, ...), custom_call_target="tpu_custom_call" | custom-call | flops 6000000000 | bytes 18000000 | tf_op jit(solution)/shard_map/middle/pallas_call | solution.py:855
  45.2 1.1 %collective-permute-done.12.crossed_ref = bf16[2,512,512]{2,1,0:T(8,128)(2,1)S(1)} collective-permute-done((bf16[2,512,512]{2,1,0:T(8,128)(2,1)S(1)}, bf16[2,512,512]{2,1,0:T(8,128)(2,1)S(1)}, u32[]{:S(2)}, u32[]{:S(2)}) %collective-permute-start.12) | collective-permute-done | bytes 1048608 | tf_op jit(solution)/shard_map/ppermute | solution.py:52
  46.4 0.2 rows.2
  46.6 0.0 copy-start.14
  46.6 1.0 %collective-permute-start.14 = (bf16[512,512]{1,0:T(8,128)(2,1)S(1)}, bf16[512,512]{1,0:T(8,128)(2,1)S(1)}, u32[]{:S(2)}, u32[]{:S(2)}) collective-permute-start(bf16[512,512]{1,0:T(8,128)(2,1)S(1)} %get-tuple-element.139), channel_id=1, source_target_pairs={{0,2},{1,3},{2,0},{3,1},{4,6},{5,7},{6,4},{7,5},{8,10},{9,11},{10,... | collective-permute-start | bytes 1572872 | tf_op jit(solution)/shard_map/ppermute | solution.py:52
  47.6 4.3 %values.1 = (bf16[8,256,128]{2,1,0:T(8,128)(2,1)S(1)}, bf16[4,64,384]{2,1,0:T(8,128)(2,1)S(1)}, bf16[4,64,384]{2,1,0:T(8,128)(2,1)S(1)}) custom-call(bf16[21,256,512]{2,1,0:T(8,128)(2,1)S(1)} %get-tuple-element.134.refs_0_, bf16[15,256,512]{2,1,0:T(8,128)(2,1)S(1)} %get-tuple-element.135.refs_1_, bf16[8,256,128]{2,1,0:T(8,128)(2,1)S(1)} %get-tuple-element.136.refs_2_, ...), custom_call_target="tpu_custom_call" | custom-call | flops 12000000000 | bytes 36000000 | tf_op jit(solution)/shard_map/values/pallas_call | solution.py:871
  51.9 1.6 %collective-permute-start.13 = (bf16[4,64,384]{2,1,0:T(8,128)(2,1)S(1)}, bf16[4,64,384]{2,1,0:T(8,128)(2,1)S(1)}, u32[]{:S(2)}, u32[]{:S(2)}) collective-permute-start(bf16[4,64,384]{2,1,0:T(8,128)(2,1)S(1)} %get-tuple-element.138), channel_id=1, source_target_pairs={{0,4},{4,0},{8,12},{12,8},{16,20},{20,16},{24,28},{28,24},{1,5},{5... | collective-permute-start | bytes 589832 | tf_op jit(solution)/shard_map/ppermute | solution.py:52
  53.5 10.6 %backward.1 = (bf16[8,256,256]{2,1,0:T(8,128)(2,1)S(1)}, bf16[4,80,256]{2,1,0:T(8,128)(2,1)S(1)}, bf16[4,80,256]{2,1,0:T(8,128)(2,1)S(1)}) custom-call(bf16[21,256,512]{2,1,0:T(8,128)(2,1)S(1)} %get-tuple-element.122.refs_0_, bf16[15,256,512]{2,1,0:T(8,128)(2,1)S(1)} %get-tuple-element.123.refs_1_, ...), custom_call_target="tpu_custom_call" | custom-call | flops 2000000000 | bytes 6000000 | tf_op jit(solution)/shard_map/backward/pallas_call | solution.py:884
  64.1 0.6 collective-permute-start.15
  64.7 1.3 %input_rows.1 = (bf16[2,512,512]{2,1,0:T(8,128)(2,1)S(1)}, bf16[2,512,512]{2,1,0:T(8,128)(2,1)S(1)}) custom-call(bf16[8,256,256]{2,1,0:T(8,128)(2,1)S(1)} %get-tuple-element.146.gp_ref, bf16[8,256,128]{2,1,0:T(8,128)(2,1)S(1)} %get-tuple-element.147.gun_ref, bf16[8,256,128]{2,1,0:T(8,128)(2,1)S(1)} %get-tuple-element.148.gpv_ref, ...), custom_call_target="tpu_custom_call" | custom-call | flops 4000000000 | bytes 12000000 | tf_op jit(solution)/shard_map/input_rows/pallas_call | solution.py:904
  66.0 0.1 collective-permute-start.16
  66.0 0.1 fold.3
  66.1 4.2 %collective-permute-start.20 = (bf16[64,384]{1,0:T(8,128)(2,1)S(1)}, bf16[64,384]{1,0:T(8,128)(2,1)S(1)}, u32[]{:S(2)}, u32[]{:S(2)}) collective-permute-start(bf16[64,384]{1,0:T(8,128)(2,1)S(1)} %get-tuple-element.160), channel_id=1, source_target_pairs={{0,24},{4,28},{8,16},{12,20},{16,8},{20,12},{24,0},{28,4},{1,25},{... | collective-permute-start | bytes 147464 | tf_op jit(solution)/shard_map/ppermute | solution.py:52
  70.3 0.6 collective-permute-start.22
  71.0 3.8 %collective-permute-start.17 = (bf16[80,256]{1,0:T(8,128)(2,1)S(1)}, bf16[80,256]{1,0:T(8,128)(2,1)S(1)}, u32[]{:S(2)}, u32[]{:S(2)}) collective-permute-start(bf16[80,256]{1,0:T(8,128)(2,1)S(1)} %get-tuple-element.150), channel_id=1, source_target_pairs={{0,24},{4,28},{8,16},{12,20},{16,8},{20,12},{24,0},{28,4},{1,25},{... | collective-permute-start | bytes 122888 | tf_op jit(solution)/shard_map/ppermute | solution.py:52
  74.8 0.6 collective-permute-start.19
  75.5 0.8 collective-permute-done.21.refs_2_
  76.3 0.9 rows.3
  77.2 1.1 %collective-permute-start.23 = (bf16[256,512]{1,0:T(8,128)(2,1)S(1)}, bf16[256,512]{1,0:T(8,128)(2,1)}, u32[]{:S(2)}, u32[]{:S(2)}) collective-permute-start(bf16[256,512]{1,0:T(8,128)(2,1)S(1)} %get-tuple-element.166), channel_id=1, source_target_pairs={{0,2},{1,3},{2,0},{3,1},{4,6},{5,7},{6,4},{7,5},{8,10},{9,11},{10,... | collective-permute-start | bytes 786440 | tf_op jit(solution)/shard_map/ppermute | solution.py:52
  78.3 0.9 collective-permute-start.24
  79.2 0.5 collective-permute-done.18.refs_2_
  79.7 0.8 collect.1
  80.5 4.3 %all-to-all-start = ((f32[32,4,128]{2,1,0:T(4,128)}), f32[32,4,128]{2,1,0:T(4,128)S(1)}, u32[]{:S(2)}, u32[]{:S(2)}) async-start(f32[32,4,128]{2,1,0:T(4,128)} %get-tuple-element.168), calls=%async_computation | async-start | bytes 131072 | tf_op jit(solution)/shard_map/all_to_all | solution.py:932
  84.8 0.0 copy-start.15
  84.8 1.2 %copy-done.15 = f32[512,512]{1,0:T(8,128)S(1)} copy-done((f32[512,512]{1,0:T(8,128)S(1)}, f32[512,512]{1,0:T(8,128)}, u32[]{:S(2)}) %copy-start.15) | copy-done | bytes 1048600
  86.0 1.0 %mix.1 = bf16[512,512]{1,0:T(8,128)(2,1)} custom-call(bf16[512,512]{1,0:T(8,128)(2,1)S(1)} %copy-done, f32[69,128]{1,0:T(8,128)S(1)} %bitcast.18, f32[512,512]{1,0:T(8,128)S(1)} %copy-done.15, bf16[512,512]{1,0:T(8,128)(2,1)S(1)} %collective-permute-done.14.refs_1_), custom_call_target="tpu_custom_call" | custom-call | flops 1000000000 | bytes 3000000 | tf_op jit(solution)/shard_map/mix/pallas_call | solution.py:933
  87.1 0.0 copy-start.7
  87.1 0.0 copy-start.10
  87.1 0.0 copy-start.11
  87.1 2.2 %finish.2.refs_0_ = f32[512,512]{1,0:T(8,128)} custom-call(bf16[512,512]{1,0:T(8,128)(2,1)S(1)} %copy-done, bf16[512,512]{1,0:T(8,128)(2,1)S(1)} %copy-done.1, f32[512,512]{1,0:T(8,128)S(1)} %get-tuple-element.171.refs_2_.refs_3_, bf16[256,512]{1,0:T(8,128)(2,1)} %collective-permute-done.23.refs_3_), custom_call_target="tpu_custom_call" | custom-call | flops 1000000000 | bytes 3000000 | tf_op jit(solution)/shard_map/finish/pallas_call | solution.py:941
  89.3 1.1 %collective-permute-done.24.refs_4_ = bf16[256,512]{1,0:T(8,128)(2,1)S(1)} collective-permute-done((bf16[256,512]{1,0:T(8,128)(2,1)}, bf16[256,512]{1,0:T(8,128)(2,1)S(1)}, u32[]{:S(2)}, u32[]{:S(2)}) %collective-permute-start.24) | collective-permute-done | bytes 262176 | tf_op jit(solution)/shard_map/ppermute | solution.py:52
  90.4 1.2 %finish.3 = f32[512,512]{1,0:T(8,128)} custom-call(f32[512,512]{1,0:T(8,128)} %finish.2.refs_0_, bf16[512,512]{1,0:T(8,128)(2,1)S(1)} %copy-done, bf16[512,512]{1,0:T(8,128)(2,1)S(1)} %copy-done.1, f32[512,512]{1,0:T(8,128)S(1)} %get-tuple-element.171.refs_2_.refs_3_, ...), custom_call_target="tpu_custom_call", output_to_operand_aliasing={{}: (0, {})} | custom-call | flops 1000000000 | bytes 3000000 | tf_op jit(solution)/shard_map/finish/pallas_call | solution.py:941
  91.6 0.6 all-to-all-done.heard_ref
  92.3 1.7 %update.1 = (f32[64,4,128]{2,1,0:T(4,128)}, f32[64,128]{1,0:T(8,128)}, f32[69,128]{1,0:T(8,128)}, f32[1,1]{1,0:T(1,128)}, f32[64,4,128]{2,1,0:T(4,128)}, /*index...) custom-call(f32[32,4,128]{2,1,0:T(4,128)S(1)} %all-to-all-done.heard, ...), custom_call_target="tpu_custom_call" | custom-call | flops 100000000 | bytes 300000 | tf_op jit(solution)/shard_map/update/pallas_call | solution.py:956
  (49 shorter events, 0.2 us)
Async XLA Ops:
  0.6 0.9 copy-start.2
  1.6 0.8 copy-start.9
  2.3 9.5 %copy-start.6 = (f32[8832]{0:T(1024)S(1)}, f32[8832]{0:T(1024)}, u32[]{:S(2)}) copy-start(f32[8832]{0:T(1024)} %param.19) | copy-start | bytes 105988
  2.3 9.5 %copy-start.16 = (s32[2048]{0:T(1024)S(1)}, s32[2048]{0:T(1024)}, u32[]{:S(2)}) copy-start(s32[2048]{0:T(1024)} %param.16) | copy-start | bytes 24580
  2.7 8.3 %collective-permute-start.5 = (bf16[64,640]{1,0:T(8,128)(2,1)S(1)}, bf16[64,640]{1,0:T(8,128)(2,1)S(1)}, u32[]{:S(2)}, u32[]{:S(2)}) collective-permute-start(bf16[64,640]{1,0:T(8,128)(2,1)S(1)} %cast.1.refs_0_), channel_id=1, source_target_pairs={{0,16},{4,20},{8,24},{12,28},{16,0},{20,4},{24,8},{28,12},{1,17},{... | collective-permute-start | bytes 245768 | tf_op jit(solution)/shard_map/ppermute | solution.py:52
  6.8 14.6 %collective-permute-start.2 = (bf16[512,512]{1,0:T(8,128)(2,1)}, bf16[512,512]{1,0:T(8,128)(2,1)S(1)}, u32[]{:S(2)}, u32[]{:S(2)}) collective-permute-start(bf16[512,512]{1,0:T(8,128)(2,1)} %refs_1_.4), channel_id=1, source_target_pairs={{0,1},{1,0},{2,3},{3,2},{4,5},{5,4},{6,7},{7,6},{8,9},{9,8},{10,11... | collective-permute-start | bytes 1572872 | tf_op jit(solution)/shard_map/ppermute | solution.py:52
  6.8 14.5 %collective-permute-start.3 = (bf16[512,512]{1,0:T(8,128)(2,1)}, bf16[512,512]{1,0:T(8,128)(2,1)S(1)}, u32[]{:S(2)}, u32[]{:S(2)}) collective-permute-start(bf16[512,512]{1,0:T(8,128)(2,1)} %refs_1_.4), channel_id=1, source_target_pairs={{0,2},{1,3},{2,0},{3,1},{4,6},{5,7},{6,4},{7,5},{8,10},{9,11},{10,... | collective-permute-start | bytes 1572872 | tf_op jit(solution)/shard_map/ppermute | solution.py:52
  11.0 5.4 %collective-permute-start.6 = (bf16[128,640]{1,0:T(8,128)(2,1)S(1)}, bf16[128,640]{1,0:T(8,128)(2,1)S(1)}, u32[]{:S(2)}, u32[]{:S(2)}) collective-permute-start(bf16[128,640]{1,0:T(8,128)(2,1)S(1)} %join.3), channel_id=1, source_target_pairs={{0,8},{4,12},{8,0},{12,4},{16,24},{20,28},{24,16},{28,20},{1,9},{5... | collective-permute-start | bytes 491528 | tf_op jit(solution)/shard_map/ppermute | solution.py:52
  11.8 6.4 %copy-start.1 = (bf16[512,512]{1,0:T(8,128)(2,1)S(1)}, bf16[512,512]{1,0:T(8,128)(2,1)}, u32[]{:S(2)}) copy-start(bf16[512,512]{1,0:T(8,128)(2,1)} %refs_2_.2) | copy-start | bytes 1572868
  11.8 9.5 %copy-start = (bf16[512,512]{1,0:T(8,128)(2,1)S(1)}, bf16[512,512]{1,0:T(8,128)(2,1)}, u32[]{:S(2)}) copy-start(bf16[512,512]{1,0:T(8,128)(2,1)} %refs_1_.4) | copy-start | bytes 1572868
  16.4 7.7 %collective-permute-start.7 = (bf16[256,640]{1,0:T(8,128)(2,1)S(1)}, bf16[256,640]{1,0:T(8,128)(2,1)S(1)}, u32[]{:S(2)}, u32[]{:S(2)}) collective-permute-start(bf16[256,640]{1,0:T(8,128)(2,1)S(1)} %join.4), channel_id=1, source_target_pairs={{0,4},{4,0},{8,12},{12,8},{16,20},{20,16},{24,28},{28,24},{1,5},{5... | collective-permute-start | bytes 983048 | tf_op jit(solution)/shard_map/ppermute | solution.py:52
  18.2 17.9 %collective-permute-start = (bf16[512,512]{1,0:T(8,128)(2,1)S(1)}, bf16[512,512]{1,0:T(8,128)(2,1)S(1)}, u32[]{:S(2)}, u32[]{:S(2)}) collective-permute-start(bf16[512,512]{1,0:T(8,128)(2,1)S(1)} %copy-done.1), channel_id=1, source_target_pairs={{0,1},{1,0},{2,3},{3,2},{4,5},{5,4},{6,7},{7,6},{8,9},{9,8},{10,11... | collective-permute-start | bytes 1572872 | tf_op jit(solution)/shard_map/ppermute | solution.py:52
  18.2 14.4 %collective-permute-start.1 = (bf16[512,512]{1,0:T(8,128)(2,1)S(1)}, bf16[512,512]{1,0:T(8,128)(2,1)S(1)}, u32[]{:S(2)}, u32[]{:S(2)}) collective-permute-start(bf16[512,512]{1,0:T(8,128)(2,1)S(1)} %copy-done.1), channel_id=1, source_target_pairs={{0,2},{1,3},{2,0},{3,1},{4,6},{5,7},{6,4},{7,5},{8,10},{9,11},{10,... | collective-permute-start | bytes 1572872 | tf_op jit(solution)/shard_map/ppermute | solution.py:52
  21.3 2.8 %collective-permute-start.4 = (bf16[512,512]{1,0:T(8,128)(2,1)S(1)}, bf16[512,512]{1,0:T(8,128)(2,1)S(1)}, u32[]{:S(2)}, u32[]{:S(2)}) collective-permute-start(bf16[512,512]{1,0:T(8,128)(2,1)S(1)} %collective-permute-done.3.refs_2_), channel_id=1, source_target_pairs={{0,1},{1,0},{2,3},{3,2},{4,5},{5,4},{6,7},{7,6},{8,9},{9,8},{10,11... | collective-permute-start | bytes 1572872 | tf_op jit(solution)/shard_map/ppermute | solution.py:52
  24.5 2.2 %copy-start.13 = (s32[2048]{0:T(1024)S(1)}, s32[2048]{0:T(1024)}, u32[]{:S(2)}) copy-start(s32[2048]{0:T(1024)} %param.15) | copy-start | bytes 24580
  32.6 3.5 %collective-permute-start.8 = (bf16[512,512]{1,0:T(8,128)(2,1)S(1)}, bf16[512,512]{1,0:T(8,128)(2,1)S(1)}, u32[]{:S(2)}, u32[]{:S(2)}) collective-permute-start(bf16[512,512]{1,0:T(8,128)(2,1)S(1)} %collective-permute-done.1.refs_2_.refs_6_), channel_id=1, source_target_pairs={{0,1},{1,0},{2,3},{3,2},{4,5},{5,4},{6,7},{7,6},{8,9},{9,8},{10,11... | collective-permute-start | bytes 1572872 | tf_op jit(solution)/shard_map/ppermute | solution.py:52
  37.9 4.0 %collective-permute-start.10 = (f32[8,4,256]{2,1,0:T(4,128)S(1)}, f32[8,4,256]{2,1,0:T(4,128)S(1)}, u32[]{:S(2)}, u32[]{:S(2)}) collective-permute-start(f32[8,4,256]{2,1,0:T(4,128)S(1)} %get-tuple-element.117.refs_0_), channel_id=1, source_target_pairs={{0,2},{1,3},{2,0},{3,1},{4,6},{5,7},{6,4},{7,5},{8,10},{9,11},{10,... | collective-permute-start | bytes 98312 | tf_op jit(solution)/shard_map/ppermute | solution.py:52
  39.5 3.3 %collective-permute-start.11 = (f32[8,4,256]{2,1,0:T(4,128)S(1)}, f32[8,4,256]{2,1,0:T(4,128)S(1)}, u32[]{:S(2)}, u32[]{:S(2)}) collective-permute-start(f32[8,4,256]{2,1,0:T(4,128)S(1)} %get-tuple-element.117.refs_0_), channel_id=1, source_target_pairs={{0,3},{1,2},{2,1},{3,0},{4,7},{5,6},{6,5},{7,4},{8,11},{9,10},{10,... | collective-permute-start | bytes 98312 | tf_op jit(solution)/shard_map/ppermute | solution.py:52
  39.8 3.0 %collective-permute-start.9 = (f32[8,4,256]{2,1,0:T(4,128)S(1)}, f32[8,4,256]{2,1,0:T(4,128)S(1)}, u32[]{:S(2)}, u32[]{:S(2)}) collective-permute-start(f32[8,4,256]{2,1,0:T(4,128)S(1)} %get-tuple-element.117.refs_0_), channel_id=1, source_target_pairs={{0,1},{1,0},{2,3},{3,2},{4,5},{5,4},{6,7},{7,6},{8,9},{9,8},{10,11... | collective-permute-start | bytes 98312 | tf_op jit(solution)/shard_map/ppermute | solution.py:52
  43.7 2.7 %collective-permute-start.12 = (bf16[2,512,512]{2,1,0:T(8,128)(2,1)S(1)}, bf16[2,512,512]{2,1,0:T(8,128)(2,1)S(1)}, u32[]{:S(2)}, u32[]{:S(2)}) collective-permute-start(bf16[2,512,512]{2,1,0:T(8,128)(2,1)S(1)} %get-tuple-element.120), channel_id=1, source_target_pairs={{0,1},{1,0},{2,3},{3,2},{4,5},{5,4},{6,7},{7,6},{8,9},{9,8},{10,11... | collective-permute-start | bytes 3145736 | tf_op jit(solution)/shard_map/ppermute | solution.py:52
  46.6 5.3 %copy-start.14 = (f32[512,512]{1,0:T(8,128)}, f32[512,512]{1,0:T(8,128)S(1)}, u32[]{:S(2)}) copy-start(f32[512,512]{1,0:T(8,128)S(1)} %get-tuple-element.169.refs_0_) | copy-start | bytes 3145732
  46.6 17.5 %collective-permute-start.14 = (bf16[512,512]{1,0:T(8,128)(2,1)S(1)}, bf16[512,512]{1,0:T(8,128)(2,1)S(1)}, u32[]{:S(2)}, u32[]{:S(2)}) collective-permute-start(bf16[512,512]{1,0:T(8,128)(2,1)S(1)} %get-tuple-element.139), channel_id=1, source_target_pairs={{0,2},{1,3},{2,0},{3,1},{4,6},{5,7},{6,4},{7,5},{8,10},{9,11},{10,... | collective-permute-start | bytes 1572872 | tf_op jit(solution)/shard_map/ppermute | solution.py:52
  51.9 12.2 %collective-permute-start.13 = (bf16[4,64,384]{2,1,0:T(8,128)(2,1)S(1)}, bf16[4,64,384]{2,1,0:T(8,128)(2,1)S(1)}, u32[]{:S(2)}, u32[]{:S(2)}) collective-permute-start(bf16[4,64,384]{2,1,0:T(8,128)(2,1)S(1)} %get-tuple-element.138), channel_id=1, source_target_pairs={{0,4},{4,0},{8,12},{12,8},{16,20},{20,16},{24,28},{28,24},{1,5},{5... | collective-permute-start | bytes 589832 | tf_op jit(solution)/shard_map/ppermute | solution.py:52
  64.1 6.8 %collective-permute-start.15 = (bf16[4,80,256]{2,1,0:T(8,128)(2,1)S(1)}, bf16[4,80,256]{2,1,0:T(8,128)(2,1)S(1)}, u32[]{:S(2)}, u32[]{:S(2)}) collective-permute-start(bf16[4,80,256]{2,1,0:T(8,128)(2,1)S(1)} %get-tuple-element.141), channel_id=1, source_target_pairs={{0,4},{4,0},{8,12},{12,8},{16,20},{20,16},{24,28},{28,24},{1,5},{5... | collective-permute-start | bytes 491528 | tf_op jit(solution)/shard_map/ppermute | solution.py:52
  66.0 5.0 %collective-permute-start.16 = (bf16[2,512,512]{2,1,0:T(8,128)(2,1)S(1)}, bf16[2,512,512]{2,1,0:T(8,128)(2,1)S(1)}, u32[]{:S(2)}, u32[]{:S(2)}) collective-permute-start(bf16[2,512,512]{2,1,0:T(8,128)(2,1)S(1)} %get-tuple-element.149), channel_id=1, source_target_pairs={{0,1},{1,0},{2,3},{3,2},{4,5},{5,4},{6,7},{7,6},{8,9},{9,8},{10,11... | collective-permute-start | bytes 3145736 | tf_op jit(solution)/shard_map/ppermute | solution.py:52
  66.1 8.7 %collective-permute-start.20 = (bf16[64,384]{1,0:T(8,128)(2,1)S(1)}, bf16[64,384]{1,0:T(8,128)(2,1)S(1)}, u32[]{:S(2)}, u32[]{:S(2)}) collective-permute-start(bf16[64,384]{1,0:T(8,128)(2,1)S(1)} %get-tuple-element.160), channel_id=1, source_target_pairs={{0,24},{4,28},{8,16},{12,20},{16,8},{20,12},{24,0},{28,4},{1,25},{... | collective-permute-start | bytes 147464 | tf_op jit(solution)/shard_map/ppermute | solution.py:52
  70.3 6.0 %collective-permute-start.21 = (bf16[64,384]{1,0:T(8,128)(2,1)S(1)}, bf16[64,384]{1,0:T(8,128)(2,1)S(1)}, u32[]{:S(2)}, u32[]{:S(2)}) collective-permute-start(bf16[64,384]{1,0:T(8,128)(2,1)S(1)} %get-tuple-element.161), channel_id=1, source_target_pairs={{0,16},{4,20},{8,24},{12,28},{16,0},{20,4},{24,8},{28,12},{1,17},{... | collective-permute-start | bytes 147464 | tf_op jit(solution)/shard_map/ppermute | solution.py:52
  70.3 6.0 %collective-permute-start.22 = (bf16[64,384]{1,0:T(8,128)(2,1)S(1)}, bf16[64,384]{1,0:T(8,128)(2,1)S(1)}, u32[]{:S(2)}, u32[]{:S(2)}) collective-permute-start(bf16[64,384]{1,0:T(8,128)(2,1)S(1)} %get-tuple-element.162), channel_id=1, source_target_pairs={{0,8},{4,12},{8,0},{12,4},{16,24},{20,28},{24,16},{28,20},{1,9},{5... | collective-permute-start | bytes 147464 | tf_op jit(solution)/shard_map/ppermute | solution.py:52
  71.0 8.2 %collective-permute-start.17 = (bf16[80,256]{1,0:T(8,128)(2,1)S(1)}, bf16[80,256]{1,0:T(8,128)(2,1)S(1)}, u32[]{:S(2)}, u32[]{:S(2)}) collective-permute-start(bf16[80,256]{1,0:T(8,128)(2,1)S(1)} %get-tuple-element.150), channel_id=1, source_target_pairs={{0,24},{4,28},{8,16},{12,20},{16,8},{20,12},{24,0},{28,4},{1,25},{... | collective-permute-start | bytes 122888 | tf_op jit(solution)/shard_map/ppermute | solution.py:52
  74.8 4.9 %collective-permute-start.18 = (bf16[80,256]{1,0:T(8,128)(2,1)S(1)}, bf16[80,256]{1,0:T(8,128)(2,1)S(1)}, u32[]{:S(2)}, u32[]{:S(2)}) collective-permute-start(bf16[80,256]{1,0:T(8,128)(2,1)S(1)} %get-tuple-element.151), channel_id=1, source_target_pairs={{0,16},{4,20},{8,24},{12,28},{16,0},{20,4},{24,8},{28,12},{1,17},{... | collective-permute-start | bytes 122888 | tf_op jit(solution)/shard_map/ppermute | solution.py:52
  74.8 4.9 %collective-permute-start.19 = (bf16[80,256]{1,0:T(8,128)(2,1)S(1)}, bf16[80,256]{1,0:T(8,128)(2,1)S(1)}, u32[]{:S(2)}, u32[]{:S(2)}) collective-permute-start(bf16[80,256]{1,0:T(8,128)(2,1)S(1)} %get-tuple-element.152), channel_id=1, source_target_pairs={{0,8},{4,12},{8,0},{12,4},{16,24},{20,28},{24,16},{28,20},{1,9},{5... | collective-permute-start | bytes 122888 | tf_op jit(solution)/shard_map/ppermute | solution.py:52
  77.2 9.9 %collective-permute-start.23 = (bf16[256,512]{1,0:T(8,128)(2,1)S(1)}, bf16[256,512]{1,0:T(8,128)(2,1)}, u32[]{:S(2)}, u32[]{:S(2)}) collective-permute-start(bf16[256,512]{1,0:T(8,128)(2,1)S(1)} %get-tuple-element.166), channel_id=1, source_target_pairs={{0,2},{1,3},{2,0},{3,1},{4,6},{5,7},{6,4},{7,5},{8,10},{9,11},{10,... | collective-permute-start | bytes 786440 | tf_op jit(solution)/shard_map/ppermute | solution.py:52
  78.3 12.1 %collective-permute-start.24 = (bf16[256,512]{1,0:T(8,128)(2,1)}, bf16[256,512]{1,0:T(8,128)(2,1)S(1)}, u32[]{:S(2)}, u32[]{:S(2)}) collective-permute-start(bf16[256,512]{1,0:T(8,128)(2,1)} %get-tuple-element.167), channel_id=1, source_target_pairs={{0,2},{1,3},{2,0},{3,1},{4,6},{5,7},{6,4},{7,5},{8,10},{9,11},{10,... | collective-permute-start | bytes 786440 | tf_op jit(solution)/shard_map/ppermute | solution.py:52
  80.5 11.7 %all-to-all-start = ((f32[32,4,128]{2,1,0:T(4,128)}), f32[32,4,128]{2,1,0:T(4,128)S(1)}, u32[]{:S(2)}, u32[]{:S(2)}) async-start(f32[32,4,128]{2,1,0:T(4,128)} %get-tuple-element.168), calls=%async_computation | async-start | bytes 131072 | tf_op jit(solution)/shard_map/all_to_all | solution.py:932
  84.8 1.2 %copy-start.15 = (f32[512,512]{1,0:T(8,128)S(1)}, f32[512,512]{1,0:T(8,128)}, u32[]{:S(2)}) copy-start(f32[512,512]{1,0:T(8,128)} %copy-done.14) | copy-start | bytes 3145732
  87.0 5.2 %copy-start.3 = (f32[64,4,128]{2,1,0:T(4,128)S(1)}, f32[64,4,128]{2,1,0:T(4,128)}, u32[]{:S(2)}) copy-start(f32[64,4,128]{2,1,0:T(4,128)} %refs_0_.7) | copy-start | bytes 393220
  87.0 5.2 %copy-start.4 = (f32[64,4,128]{2,1,0:T(4,128)S(1)}, f32[64,4,128]{2,1,0:T(4,128)}, u32[]{:S(2)}) copy-start(f32[64,4,128]{2,1,0:T(4,128)} %refs_1_.5) | copy-start | bytes 393220
  87.0 5.2 %copy-start.5 = (f32[64,4,128]{2,1,0:T(4,128)S(1)}, f32[64,4,128]{2,1,0:T(4,128)}, u32[]{:S(2)}) copy-start(f32[64,4,128]{2,1,0:T(4,128)} %refs_2_.3) | copy-start | bytes 393220
  87.1 5.2 %copy-start.7 = (f32[8832]{0:T(1024)S(1)}, f32[8832]{0:T(1024)}, u32[]{:S(2)}) copy-start(f32[8832]{0:T(1024)} %param.24) | copy-start | bytes 105988
  87.1 5.2 %copy-start.8 = (f32[8832]{0:T(1024)S(1)}, f32[8832]{0:T(1024)}, u32[]{:S(2)}) copy-start(f32[8832]{0:T(1024)} %param.25) | copy-start | bytes 105988
  87.1 5.2 %copy-start.10 = (f32[128,64]{0,1:T(8,128)S(1)}, f32[128,64]{0,1:T(8,128)}, u32[]{:S(2)}) copy-start(f32[128,64]{0,1:T(8,128)} %param.18) | copy-start | bytes 98308
  87.1 5.2 %copy-start.11 = (f32[128,64]{0,1:T(8,128)S(1)}, f32[128,64]{0,1:T(8,128)}, u32[]{:S(2)}) copy-start(f32[128,64]{0,1:T(8,128)} %param.22) | copy-start | bytes 98308
  87.1 5.2 %copy-start.12 = (f32[128,64]{0,1:T(8,128)S(1)}, f32[128,64]{0,1:T(8,128)}, u32[]{:S(2)}) copy-start(f32[128,64]{0,1:T(8,128)} %param.23) | copy-start | bytes 98308

commit v10 on v9

--- a/solution.py
+++ b/solution.py
@@ -828,7 +828,7 @@
             8 if before else 0.5,
         )(*before, kx, qs, trow, vt, pos, starts)
 
-    split = nb - nb // 4
+    split = nb - nb // 8
     attn, *kept_first = attend(0, split)
     cot_chips = after_all(cot_chips, attn)
     attn, *kept_last = attend(split, nb, after(attn, *cot_chips))

time: 94.4 us -> 94.4 us (level)
  starting transfers between devices: 31 us -> 32.1 us
    ppermute x25, starting transfers between devices: 26.7 us -> 27.8 us  [swap(): return lax.ppermute(x, axis, [(i, i ^ k) for i in range(n)])]
  transfers between devices with their start and end apart: 26 -> 26, of which waited for: 12 -> 11; matrix products, arithmetic and copies ran while one was open for 0% -> 0% of each run, Pallas kernels for 40% -> 40%
where the time goes in v10:
time: 94.4 us; the launch traced here: 94.1 us
  Pallas kernels  42.5 us (45%)
  starting transfers between devices  32.1 us (34%)
  waiting for transfers between devices  15.4 us (16%)
  local copies, waits for them, and re-layouts  3 us (3%)
  between operations  1.1 us (1%)
    ppermute x25, starting transfers between devices, swap(): return lax.ppermute(x, axis, [(i, i ^ k) for i in range(n)])  27.8 us
    ppermute x25, waiting for transfers between devices, swap(): return lax.ppermute(x, axis, [(i, i ^ k) for i in range(n)])  14.7 us
    pallas_call x1, Pallas kernels, shards(): call(functools.partial(backward_kernel, heads, n_dp, extra, kept), 'backw...  10.7 us
    pallas_call x2, Pallas kernels, attend(): call(functools.partial(attend_kernel, heads, first, last, kept), 'attend'...  8.26 us
    all_to_all x1, starting transfers between devices, shards(): heard = lax.all_to_all(message, ('dp', 'head'), 0, 0, tiled=True)  4.33 us
    pallas_call x1, Pallas kernels, shards(): call(functools.partial(values_kernel, heads, kept), 'values', [VMEM] * (l...  4.29 us
    pallas_call x2, Pallas kernels, shards(): call(functools.partial(finish_kernel, part), 'finish', [pl.BlockSpec(memo...  3.29 us
    unnamed x34, local copies, waits for them, and re-layouts  3 us
  transfers between devices with their start and end apart: 26, of which 11 were waited for; matrix products, arithmetic and copies ran while one was open for 0% of the time, Pallas kernels for 40%

profile of v10, /device:TPU:0, one launch (start us, length us, event | category | flops | bytes accessed | tf_op | source)
XLA Modules:
  0.0 94.1 jit_solution(2364312840926382895)
XLA Ops:
  0.7 0.0 copy-start.2
  0.7 1.0 %copy-done.2 = f32[64,4,128]{2,1,0:T(4,128)S(1)} copy-done((f32[64,4,128]{2,1,0:T(4,128)S(1)}, f32[64,4,128]{2,1,0:T(4,128)}, u32[]{:S(2)}) %copy-start.2) | copy-done | bytes 131096
  1.6 0.8 copy-done.9
  2.4 0.3 cast.1.refs_0_
  2.7 4.1 %collective-permute-start.5 = (bf16[64,640]{1,0:T(8,128)(2,1)S(1)}, bf16[64,640]{1,0:T(8,128)(2,1)S(1)}, u32[]{:S(2)}, u32[]{:S(2)}) collective-permute-start(bf16[64,640]{1,0:T(8,128)(2,1)S(1)} %cast.1.refs_0_), channel_id=1, source_target_pairs={{0,16},{4,20},{8,24},{12,28},{16,0},{20,4},{24,8},{28,12},{1,17},{... | collective-permute-start | bytes 245768 | tf_op jit(solution)/shard_map/ppermute | solution.py:52
  6.8 1.5 %collective-permute-start.3 = (bf16[512,512]{1,0:T(8,128)(2,1)S(1)}, bf16[512,512]{1,0:T(8,128)(2,1)S(1)}, u32[]{:S(2)}, u32[]{:S(2)}) collective-permute-start(bf16[512,512]{1,0:T(8,128)(2,1)S(1)} %copy-done), channel_id=1, source_target_pairs={{0,2},{1,3},{2,0},{3,1},{4,6},{5,7},{6,4},{7,5},{8,10},{9,11},{10,... | collective-permute-start | bytes 1572872 | tf_op jit(solution)/shard_map/ppermute | solution.py:52
  8.3 2.7 %collective-permute-done.5.refs_1_ = bf16[64,640]{1,0:T(8,128)(2,1)S(1)} collective-permute-done((bf16[64,640]{1,0:T(8,128)(2,1)S(1)}, bf16[64,640]{1,0:T(8,128)(2,1)S(1)}, u32[]{:S(2)}, u32[]{:S(2)}) %collective-permute-start.5) | collective-permute-done | bytes 81952 | tf_op jit(solution)/shard_map/ppermute | solution.py:52
  11.1 0.8 collective-permute-start.6
  11.9 2.5 %prepare.1 = (f32[8,256,256]{2,1,0:T(8,128)S(1)}, bf16[8,256,128]{2,1,0:T(8,128)(2,1)S(1)}, bf16[8,128,256]{2,1,0:T(8,128)(2,1)S(1)}, bf16[8,128,256]{2,1,0:T(8,128)(2,1)S(1)}) custom-call(s32[1,2048]{1,0:T(1,128)S(1)} %bitcast.28, f32[69,128]{1,0:T(8,128)S(1)} %bitcast.17), custom_call_target="tpu_custom_call" | custom-call | flops 2000000000 | bytes 6000000 | tf_op jit(solution)/shard_map/prepare/pallas_call | solution.py:760
  14.3 2.1 %collective-permute-done.6.refs_2_ = bf16[128,640]{1,0:T(8,128)(2,1)S(1)} collective-permute-done((bf16[128,640]{1,0:T(8,128)(2,1)S(1)}, bf16[128,640]{1,0:T(8,128)(2,1)S(1)}, u32[]{:S(2)}, u32[]{:S(2)}) %collective-permute-start.6) | collective-permute-done | bytes 163872 | tf_op jit(solution)/shard_map/ppermute | solution.py:52
  16.5 1.8 %collective-permute-start.7 = (bf16[256,640]{1,0:T(8,128)(2,1)S(1)}, bf16[256,640]{1,0:T(8,128)(2,1)S(1)}, u32[]{:S(2)}, u32[]{:S(2)}) collective-permute-start(bf16[256,640]{1,0:T(8,128)(2,1)S(1)} %join.4), channel_id=1, source_target_pairs={{0,4},{4,0},{8,12},{12,8},{16,20},{20,16},{24,28},{28,24},{1,5},{5... | collective-permute-start | bytes 983048 | tf_op jit(solution)/shard_map/ppermute | solution.py:52
  18.2 1.5 %collective-permute-start.1 = (bf16[512,512]{1,0:T(8,128)(2,1)S(1)}, bf16[512,512]{1,0:T(8,128)(2,1)S(1)}, u32[]{:S(2)}, u32[]{:S(2)}) collective-permute-start(bf16[512,512]{1,0:T(8,128)(2,1)S(1)} %copy-done.1), channel_id=1, source_target_pairs={{0,2},{1,3},{2,0},{3,1},{4,6},{5,7},{6,4},{7,5},{8,10},{9,11},{10,... | collective-permute-start | bytes 1572872 | tf_op jit(solution)/shard_map/ppermute | solution.py:52
  19.7 1.4 %collective-permute-done.3.refs_2_ = bf16[512,512]{1,0:T(8,128)(2,1)S(1)} collective-permute-done((bf16[512,512]{1,0:T(8,128)(2,1)S(1)}, bf16[512,512]{1,0:T(8,128)(2,1)S(1)}, u32[]{:S(2)}, u32[]{:S(2)}) %collective-permute-start.3) | collective-permute-done | bytes 524320 | tf_op jit(solution)/shard_map/ppermute | solution.py:52
  21.2 1.0 %normalize.2.refs_0_ = bf16[8,256,512]{2,1,0:T(8,128)(2,1)S(1)} custom-call(bf16[512,512]{1,0:T(8,128)(2,1)S(1)} %copy-done, bf16[512,512]{1,0:T(8,128)(2,1)S(1)} %collective-permute-done.2.refs_1_, bf16[512,512]{1,0:T(8,128)(2,1)S(1)} %collective-permute-done.3.refs_2_), custom_call_target="tpu_custom_call" | custom-call | flops 100000000 | bytes 300000 | tf_op jit(solution)/shard_map/normalize/pallas_call | solution.py:791
  22.2 2.0 %collective-permute-done.7.refs_0_ = bf16[256,640]{1,0:T(8,128)(2,1)S(1)} collective-permute-done((bf16[256,640]{1,0:T(8,128)(2,1)S(1)}, bf16[256,640]{1,0:T(8,128)(2,1)S(1)}, u32[]{:S(2)}, u32[]{:S(2)}) %collective-permute-start.7) | collective-permute-done | bytes 327712 | tf_op jit(solution)/shard_map/ppermute | solution.py:52
  24.2 0.4 normalize.3.refs_0_.refs_5_.refs_11_.refs_8_.refs_4_
  24.6 0.3 assemble.1.refs_1_.refs_6_.wt_ref
  24.9 0.0 copy-start.13
  24.9 1.8 %project.1 = (bf16[8,384,256]{2,1,0:T(8,128)(2,1)S(1)}, bf16[8,256,256]{2,1,0:T(8,128)(2,1)S(1)}, bf16[8,256,256]{2,1,0:T(8,128)(2,1)S(1)}, bf16[8,128,256]{2,1,...) custom-call(bf16[8,256,512]{2,1,0:T(8,128)(2,1)S(1)} %normalize.3.re, ...), custom_call_target="tpu_custom_call" | custom-call | flops 1000000000 | bytes 3000000 | tf_op jit(solution)/shard_map/project/pallas_call | solution.py:809
  26.7 6.2 %attend.2 = (f32[7,128,256]{2,1,0:T(8,128)S(1)}, bf16[28,256,512]{2,1,0:T(8,128)(2,1)S(1)}, bf16[28,256,512]{2,1,0:T(8,128)(2,1)S(1)}) custom-call(bf16[8,256,256]{2,1,0:T(8,128)(2,1)S(1)} %get-tuple-element.109.refs_0_.refs_1_.refs_2_, bf16[8,128,256]{2,1,0:T(8,128)(2,1)S(1)} %get-tuple-element.110.refs_1_.refs_2_, ...), custom_call_target="tpu_custom_call" | custom-call | flops 500000000 | bytes 1500000 | tf_op jit(solution)/shard_map/attend/pallas_call | solution.py:822
  32.9 0.1 collective-permute-start.8
  33.0 2.1 %attend.3 = (f32[8,128,256]{2,1,0:T(8,128)S(1)}, bf16[8,256,512]{2,1,0:T(8,128)(2,1)S(1)}, bf16[8,256,512]{2,1,0:T(8,128)(2,1)S(1)}) custom-call(f32[7,128,256]{2,1,0:T(8,128)S(1)} %get-tuple-element.115.refs_0_, bf16[8,256,256]{2,1,0:T(8,128)(2,1)S(1)} %get-tuple-element.109.refs_0_.refs_1_.refs_2_, ...), custom_call_target="tpu_custom_call" | custom-call | flops 8000000000 | bytes 24000000 | tf_op jit(solution)/shard_map/attend/pallas_call | solution.py:822
  35.1 1.7 %gate.1 = (f32[8,128,256]{2,1,0:T(8,128)S(1)}, f32[8,128,256]{2,1,0:T(8,128)S(1)}, f32[8,4,256]{2,1,0:T(4,128)S(1)}, f32[1,512]{1,0:T(1,128)S(1)}) custom-call(bf16[512,512]{1,0:T(8,128)(2,1)S(1)} %copy-done.1, bf16[512,512]{1,0:T(8,128)(2,1)S(1)} %collective-permute-done.refs_1_.refs_5_, bf16[512,512]{1,0:T(8,128)(2,1)S(1)} %collective-permute-done.1.refs_2_.refs_6_, ...), custom_call_target="tpu_custom_call" | custom-call | flops 5000000000 | bytes 15000000 | tf_op jit(solution)/shard_map/gate/pallas_call | solution.py:839
  36.8 1.5 %collective-permute-start.10 = (f32[8,4,256]{2,1,0:T(4,128)S(1)}, f32[8,4,256]{2,1,0:T(4,128)S(1)}, u32[]{:S(2)}, u32[]{:S(2)}) collective-permute-start(f32[8,4,256]{2,1,0:T(4,128)S(1)} %get-tuple-element.117.refs_0_), channel_id=1, source_target_pairs={{0,2},{1,3},{2,0},{3,1},{4,6},{5,7},{6,4},{7,5},{8,10},{9,11},{10,... | collective-permute-start | bytes 98312 | tf_op jit(solution)/shard_map/ppermute | solution.py:52
  38.4 0.4 collective-permute-start.11
  38.7 0.3 collective-permute-start.9
  39.1 1.8 %collective-permute-done.10.refs_2_ = f32[8,4,256]{2,1,0:T(4,128)S(1)} collective-permute-done((f32[8,4,256]{2,1,0:T(4,128)S(1)}, f32[8,4,256]{2,1,0:T(4,128)S(1)}, u32[]{:S(2)}, u32[]{:S(2)}) %collective-permute-start.10) | collective-permute-done | bytes 32800 | tf_op jit(solution)/shard_map/ppermute | solution.py:52
  40.8 0.9 collective-permute-done.11.refs_3_
  41.7 0.8 branch.1
  42.5 0.3 collective-permute-start.12
  42.8 1.2 %middle.1 = (bf16[8,256,128]{2,1,0:T(8,128)(2,1)S(1)}, bf16[8,128,256]{2,1,0:T(8,128)(2,1)S(1)}, bf16[8,256,128]{2,1,0:T(8,128)(2,1)S(1)}, f32[256,512]{1,0:T(8,128)S(1)}) custom-call(f32[8,4,256]{2,1,0:T(4,128)S(1)} %get-tuple-element.117.refs_0_, f32[8,4,256]{2,1,0:T(4,128)S(1)} %collective-permute-done.9.refs_1_, ...), custom_call_target="tpu_custom_call" | custom-call | flops 6000000000 | bytes 18000000 | tf_op jit(solution)/shard_map/middle/pallas_call | solution.py:855
  44.0 1.3 %collective-permute-done.12.crossed_ref = bf16[2,512,512]{2,1,0:T(8,128)(2,1)S(1)} collective-permute-done((bf16[2,512,512]{2,1,0:T(8,128)(2,1)S(1)}, bf16[2,512,512]{2,1,0:T(8,128)(2,1)S(1)}, u32[]{:S(2)}, u32[]{:S(2)}) %collective-permute-start.12) | collective-permute-done | bytes 1048608 | tf_op jit(solution)/shard_map/ppermute | solution.py:52
  45.3 0.2 rows.2
  45.5 0.0 copy-start.14
  45.5 1.0 %collective-permute-start.14 = (bf16[512,512]{1,0:T(8,128)(2,1)S(1)}, bf16[512,512]{1,0:T(8,128)(2,1)S(1)}, u32[]{:S(2)}, u32[]{:S(2)}) collective-permute-start(bf16[512,512]{1,0:T(8,128)(2,1)S(1)} %get-tuple-element.139), channel_id=1, source_target_pairs={{0,2},{1,3},{2,0},{3,1},{4,6},{5,7},{6,4},{7,5},{8,10},{9,11},{10,... | collective-permute-start | bytes 1572872 | tf_op jit(solution)/shard_map/ppermute | solution.py:52
  46.5 4.3 %values.1 = (bf16[8,256,128]{2,1,0:T(8,128)(2,1)S(1)}, bf16[4,64,384]{2,1,0:T(8,128)(2,1)S(1)}, bf16[4,64,384]{2,1,0:T(8,128)(2,1)S(1)}) custom-call(bf16[28,256,512]{2,1,0:T(8,128)(2,1)S(1)} %get-tuple-element.134.refs_0_, bf16[8,256,512]{2,1,0:T(8,128)(2,1)S(1)} %get-tuple-element.135.refs_1_, bf16[8,256,128]{2,1,0:T(8,128)(2,1)S(1)} %get-tuple-element.136.refs_2_, ...), custom_call_target="tpu_custom_call" | custom-call | flops 12000000000 | bytes 36000000 | tf_op jit(solution)/shard_map/values/pallas_call | solution.py:871
  50.8 1.6 %collective-permute-start.13 = (bf16[4,64,384]{2,1,0:T(8,128)(2,1)S(1)}, bf16[4,64,384]{2,1,0:T(8,128)(2,1)S(1)}, u32[]{:S(2)}, u32[]{:S(2)}) collective-permute-start(bf16[4,64,384]{2,1,0:T(8,128)(2,1)S(1)} %get-tuple-element.138), channel_id=1, source_target_pairs={{0,4},{4,0},{8,12},{12,8},{16,20},{20,16},{24,28},{28,24},{1,5},{5... | collective-permute-start | bytes 589832 | tf_op jit(solution)/shard_map/ppermute | solution.py:52
  52.4 10.7 %backward.1 = (bf16[8,256,256]{2,1,0:T(8,128)(2,1)S(1)}, bf16[4,80,256]{2,1,0:T(8,128)(2,1)S(1)}, bf16[4,80,256]{2,1,0:T(8,128)(2,1)S(1)}) custom-call(bf16[28,256,512]{2,1,0:T(8,128)(2,1)S(1)} %get-tuple-element.122.refs_0_, bf16[8,256,512]{2,1,0:T(8,128)(2,1)S(1)} %get-tuple-element.123.refs_1_, ...), custom_call_target="tpu_custom_call" | custom-call | flops 2000000000 | bytes 6000000 | tf_op jit(solution)/shard_map/backward/pallas_call | solution.py:884
  63.1 0.6 collective-permute-start.15
  63.6 1.2 %input_rows.1 = (bf16[2,512,512]{2,1,0:T(8,128)(2,1)S(1)}, bf16[2,512,512]{2,1,0:T(8,128)(2,1)S(1)}) custom-call(bf16[8,256,256]{2,1,0:T(8,128)(2,1)S(1)} %get-tuple-element.146.gp_ref, bf16[8,256,128]{2,1,0:T(8,128)(2,1)S(1)} %get-tuple-element.147.gun_ref, bf16[8,256,128]{2,1,0:T(8,128)(2,1)S(1)} %get-tuple-element.148.gpv_ref, ...), custom_call_target="tpu_custom_call" | custom-call | flops 4000000000 | bytes 12000000 | tf_op jit(solution)/shard_map/input_rows/pallas_call | solution.py:904
  64.9 0.1 collective-permute-start.16
  65.0 0.1 fold.3
  65.0 5.3 %collective-permute-start.20 = (bf16[64,384]{1,0:T(8,128)(2,1)S(1)}, bf16[64,384]{1,0:T(8,128)(2,1)S(1)}, u32[]{:S(2)}, u32[]{:S(2)}) collective-permute-start(bf16[64,384]{1,0:T(8,128)(2,1)S(1)} %get-tuple-element.160), channel_id=1, source_target_pairs={{0,24},{4,28},{8,16},{12,20},{16,8},{20,12},{24,0},{28,4},{1,25},{... | collective-permute-start | bytes 147464 | tf_op jit(solution)/shard_map/ppermute | solution.py:52
  70.3 0.6 collective-permute-start.22
  71.0 3.8 %collective-permute-start.17 = (bf16[80,256]{1,0:T(8,128)(2,1)S(1)}, bf16[80,256]{1,0:T(8,128)(2,1)S(1)}, u32[]{:S(2)}, u32[]{:S(2)}) collective-permute-start(bf16[80,256]{1,0:T(8,128)(2,1)S(1)} %get-tuple-element.150), channel_id=1, source_target_pairs={{0,24},{4,28},{8,16},{12,20},{16,8},{20,12},{24,0},{28,4},{1,25},{... | collective-permute-start | bytes 122888 | tf_op jit(solution)/shard_map/ppermute | solution.py:52
  74.8 0.6 collective-permute-start.19
  75.4 0.8 collective-permute-done.21.refs_2_
  76.3 0.9 rows.3
  77.1 1.1 %collective-permute-start.23 = (bf16[256,512]{1,0:T(8,128)(2,1)S(1)}, bf16[256,512]{1,0:T(8,128)(2,1)}, u32[]{:S(2)}, u32[]{:S(2)}) collective-permute-start(bf16[256,512]{1,0:T(8,128)(2,1)S(1)} %get-tuple-element.166), channel_id=1, source_target_pairs={{0,2},{1,3},{2,0},{3,1},{4,6},{5,7},{6,4},{7,5},{8,10},{9,11},{10,... | collective-permute-start | bytes 786440 | tf_op jit(solution)/shard_map/ppermute | solution.py:52
  78.3 0.9 collective-permute-start.24
  79.2 0.5 collective-permute-done.18.refs_2_
  79.7 0.8 collect.1
  80.5 4.3 %all-to-all-start = ((f32[32,4,128]{2,1,0:T(4,128)}), f32[32,4,128]{2,1,0:T(4,128)S(1)}, u32[]{:S(2)}, u32[]{:S(2)}) async-start(f32[32,4,128]{2,1,0:T(4,128)} %get-tuple-element.168), calls=%async_computation | async-start | bytes 131072 | tf_op jit(solution)/shard_map/all_to_all | solution.py:932
  84.8 0.0 copy-start.15
  84.8 1.2 %copy-done.15 = f32[512,512]{1,0:T(8,128)S(1)} copy-done((f32[512,512]{1,0:T(8,128)S(1)}, f32[512,512]{1,0:T(8,128)}, u32[]{:S(2)}) %copy-start.15) | copy-done | bytes 1048600
  86.0 1.0 %mix.1 = bf16[512,512]{1,0:T(8,128)(2,1)} custom-call(bf16[512,512]{1,0:T(8,128)(2,1)S(1)} %copy-done, f32[69,128]{1,0:T(8,128)S(1)} %bitcast.18, f32[512,512]{1,0:T(8,128)S(1)} %copy-done.15, bf16[512,512]{1,0:T(8,128)(2,1)S(1)} %collective-permute-done.14.refs_1_), custom_call_target="tpu_custom_call" | custom-call | flops 1000000000 | bytes 3000000 | tf_op jit(solution)/shard_map/mix/pallas_call | solution.py:933
  87.0 2.1 %finish.2.refs_0_ = f32[512,512]{1,0:T(8,128)} custom-call(bf16[512,512]{1,0:T(8,128)(2,1)S(1)} %copy-done, bf16[512,512]{1,0:T(8,128)(2,1)S(1)} %copy-done.1, f32[512,512]{1,0:T(8,128)S(1)} %get-tuple-element.171.refs_2_.refs_3_, bf16[256,512]{1,0:T(8,128)(2,1)} %collective-permute-done.23.refs_3_), custom_call_target="tpu_custom_call" | custom-call | flops 1000000000 | bytes 3000000 | tf_op jit(solution)/shard_map/finish/pallas_call | solution.py:941
  89.2 0.0 copy-start.8
  89.2 0.0 copy-start.10
  89.2 0.0 copy-start.11
  89.2 1.2 %collective-permute-done.24.refs_4_ = bf16[256,512]{1,0:T(8,128)(2,1)S(1)} collective-permute-done((bf16[256,512]{1,0:T(8,128)(2,1)}, bf16[256,512]{1,0:T(8,128)(2,1)S(1)}, u32[]{:S(2)}, u32[]{:S(2)}) %collective-permute-start.24) | collective-permute-done | bytes 262176 | tf_op jit(solution)/shard_map/ppermute | solution.py:52
  90.4 1.2 %finish.3 = f32[512,512]{1,0:T(8,128)} custom-call(f32[512,512]{1,0:T(8,128)} %finish.2.refs_0_, bf16[512,512]{1,0:T(8,128)(2,1)S(1)} %copy-done, bf16[512,512]{1,0:T(8,128)(2,1)S(1)} %copy-done.1, f32[512,512]{1,0:T(8,128)S(1)} %get-tuple-element.171.refs_2_.refs_3_, ...), custom_call_target="tpu_custom_call", output_to_operand_aliasing={{}: (0, {})} | custom-call | flops 1000000000 | bytes 3000000 | tf_op jit(solution)/shard_map/finish/pallas_call | solution.py:941
  91.6 0.6 all-to-all-done.heard_ref
  92.3 1.7 %update.1 = (f32[64,4,128]{2,1,0:T(4,128)}, f32[64,128]{1,0:T(8,128)}, f32[69,128]{1,0:T(8,128)}, f32[1,1]{1,0:T(1,128)}, f32[64,4,128]{2,1,0:T(4,128)}, /*index...) custom-call(f32[32,4,128]{2,1,0:T(4,128)S(1)} %all-to-all-done.heard, ...), custom_call_target="tpu_custom_call" | custom-call | flops 100000000 | bytes 300000 | tf_op jit(solution)/shard_map/update/pallas_call | solution.py:956
  (49 shorter events, 0.2 us)
Async XLA Ops:
  0.6 6.2 %copy-start = (bf16[512,512]{1,0:T(8,128)(2,1)S(1)}, bf16[512,512]{1,0:T(8,128)(2,1)}, u32[]{:S(2)}) copy-start(bf16[512,512]{1,0:T(8,128)(2,1)} %refs_1_.4) | copy-start | bytes 1572868
  0.7 1.0 %copy-start.2 = (f32[64,4,128]{2,1,0:T(4,128)S(1)}, f32[64,4,128]{2,1,0:T(4,128)}, u32[]{:S(2)}) copy-start(f32[64,4,128]{2,1,0:T(4,128)} %refs_0_.7) | copy-start | bytes 393220
  1.6 0.8 copy-start.9
  2.4 9.5 %copy-start.6 = (f32[8832]{0:T(1024)S(1)}, f32[8832]{0:T(1024)}, u32[]{:S(2)}) copy-start(f32[8832]{0:T(1024)} %param.19) | copy-start | bytes 105988
  2.4 9.5 %copy-start.16 = (s32[2048]{0:T(1024)S(1)}, s32[2048]{0:T(1024)}, u32[]{:S(2)}) copy-start(s32[2048]{0:T(1024)} %param.16) | copy-start | bytes 24580
  2.7 8.3 %collective-permute-start.5 = (bf16[64,640]{1,0:T(8,128)(2,1)S(1)}, bf16[64,640]{1,0:T(8,128)(2,1)S(1)}, u32[]{:S(2)}, u32[]{:S(2)}) collective-permute-start(bf16[64,640]{1,0:T(8,128)(2,1)S(1)} %cast.1.refs_0_), channel_id=1, source_target_pairs={{0,16},{4,20},{8,24},{12,28},{16,0},{20,4},{24,8},{28,12},{1,17},{... | collective-permute-start | bytes 245768 | tf_op jit(solution)/shard_map/ppermute | solution.py:52
  6.8 14.3 %collective-permute-start.2 = (bf16[512,512]{1,0:T(8,128)(2,1)S(1)}, bf16[512,512]{1,0:T(8,128)(2,1)S(1)}, u32[]{:S(2)}, u32[]{:S(2)}) collective-permute-start(bf16[512,512]{1,0:T(8,128)(2,1)S(1)} %copy-done), channel_id=1, source_target_pairs={{0,1},{1,0},{2,3},{3,2},{4,5},{5,4},{6,7},{7,6},{8,9},{9,8},{10,11... | collective-permute-start | bytes 1572872 | tf_op jit(solution)/shard_map/ppermute | solution.py:52
  6.8 14.3 %collective-permute-start.3 = (bf16[512,512]{1,0:T(8,128)(2,1)S(1)}, bf16[512,512]{1,0:T(8,128)(2,1)S(1)}, u32[]{:S(2)}, u32[]{:S(2)}) collective-permute-start(bf16[512,512]{1,0:T(8,128)(2,1)S(1)} %copy-done), channel_id=1, source_target_pairs={{0,2},{1,3},{2,0},{3,1},{4,6},{5,7},{6,4},{7,5},{8,10},{9,11},{10,... | collective-permute-start | bytes 1572872 | tf_op jit(solution)/shard_map/ppermute | solution.py:52
  11.1 5.4 %collective-permute-start.6 = (bf16[128,640]{1,0:T(8,128)(2,1)S(1)}, bf16[128,640]{1,0:T(8,128)(2,1)S(1)}, u32[]{:S(2)}, u32[]{:S(2)}) collective-permute-start(bf16[128,640]{1,0:T(8,128)(2,1)S(1)} %join.3), channel_id=1, source_target_pairs={{0,8},{4,12},{8,0},{12,4},{16,24},{20,28},{24,16},{28,20},{1,9},{5... | collective-permute-start | bytes 491528 | tf_op jit(solution)/shard_map/ppermute | solution.py:52
  11.8 6.4 %copy-start.1 = (bf16[512,512]{1,0:T(8,128)(2,1)S(1)}, bf16[512,512]{1,0:T(8,128)(2,1)}, u32[]{:S(2)}) copy-start(bf16[512,512]{1,0:T(8,128)(2,1)} %refs_2_.2) | copy-start | bytes 1572868
  16.5 7.7 %collective-permute-start.7 = (bf16[256,640]{1,0:T(8,128)(2,1)S(1)}, bf16[256,640]{1,0:T(8,128)(2,1)S(1)}, u32[]{:S(2)}, u32[]{:S(2)}) collective-permute-start(bf16[256,640]{1,0:T(8,128)(2,1)S(1)} %join.4), channel_id=1, source_target_pairs={{0,4},{4,0},{8,12},{12,8},{16,20},{20,16},{24,28},{28,24},{1,5},{5... | collective-permute-start | bytes 983048 | tf_op jit(solution)/shard_map/ppermute | solution.py:52
  18.2 16.9 %collective-permute-start = (bf16[512,512]{1,0:T(8,128)(2,1)S(1)}, bf16[512,512]{1,0:T(8,128)(2,1)S(1)}, u32[]{:S(2)}, u32[]{:S(2)}) collective-permute-start(bf16[512,512]{1,0:T(8,128)(2,1)S(1)} %copy-done.1), channel_id=1, source_target_pairs={{0,1},{1,0},{2,3},{3,2},{4,5},{5,4},{6,7},{7,6},{8,9},{9,8},{10,11... | collective-permute-start | bytes 1572872 | tf_op jit(solution)/shard_map/ppermute | solution.py:52
  18.2 14.7 %collective-permute-start.1 = (bf16[512,512]{1,0:T(8,128)(2,1)S(1)}, bf16[512,512]{1,0:T(8,128)(2,1)S(1)}, u32[]{:S(2)}, u32[]{:S(2)}) collective-permute-start(bf16[512,512]{1,0:T(8,128)(2,1)S(1)} %copy-done.1), channel_id=1, source_target_pairs={{0,2},{1,3},{2,0},{3,1},{4,6},{5,7},{6,4},{7,5},{8,10},{9,11},{10,... | collective-permute-start | bytes 1572872 | tf_op jit(solution)/shard_map/ppermute | solution.py:52
  21.2 3.0 %collective-permute-start.4 = (bf16[512,512]{1,0:T(8,128)(2,1)S(1)}, bf16[512,512]{1,0:T(8,128)(2,1)S(1)}, u32[]{:S(2)}, u32[]{:S(2)}) collective-permute-start(bf16[512,512]{1,0:T(8,128)(2,1)S(1)} %collective-permute-done.3.refs_2_), channel_id=1, source_target_pairs={{0,1},{1,0},{2,3},{3,2},{4,5},{5,4},{6,7},{7,6},{8,9},{9,8},{10,11... | collective-permute-start | bytes 1572872 | tf_op jit(solution)/shard_map/ppermute | solution.py:52
  24.9 1.8 %copy-start.13 = (s32[2048]{0:T(1024)S(1)}, s32[2048]{0:T(1024)}, u32[]{:S(2)}) copy-start(s32[2048]{0:T(1024)} %param.15) | copy-start | bytes 24580
  32.9 2.2 %collective-permute-start.8 = (bf16[512,512]{1,0:T(8,128)(2,1)S(1)}, bf16[512,512]{1,0:T(8,128)(2,1)S(1)}, u32[]{:S(2)}, u32[]{:S(2)}) collective-permute-start(bf16[512,512]{1,0:T(8,128)(2,1)S(1)} %collective-permute-done.1.refs_2_.refs_6_), channel_id=1, source_target_pairs={{0,1},{1,0},{2,3},{3,2},{4,5},{5,4},{6,7},{7,6},{8,9},{9,8},{10,11... | collective-permute-start | bytes 1572872 | tf_op jit(solution)/shard_map/ppermute | solution.py:52
  36.8 4.0 %collective-permute-start.10 = (f32[8,4,256]{2,1,0:T(4,128)S(1)}, f32[8,4,256]{2,1,0:T(4,128)S(1)}, u32[]{:S(2)}, u32[]{:S(2)}) collective-permute-start(f32[8,4,256]{2,1,0:T(4,128)S(1)} %get-tuple-element.117.refs_0_), channel_id=1, source_target_pairs={{0,2},{1,3},{2,0},{3,1},{4,6},{5,7},{6,4},{7,5},{8,10},{9,11},{10,... | collective-permute-start | bytes 98312 | tf_op jit(solution)/shard_map/ppermute | solution.py:52
  38.4 3.3 %collective-permute-start.11 = (f32[8,4,256]{2,1,0:T(4,128)S(1)}, f32[8,4,256]{2,1,0:T(4,128)S(1)}, u32[]{:S(2)}, u32[]{:S(2)}) collective-permute-start(f32[8,4,256]{2,1,0:T(4,128)S(1)} %get-tuple-element.117.refs_0_), channel_id=1, source_target_pairs={{0,3},{1,2},{2,1},{3,0},{4,7},{5,6},{6,5},{7,4},{8,11},{9,10},{10,... | collective-permute-start | bytes 98312 | tf_op jit(solution)/shard_map/ppermute | solution.py:52
  38.7 3.0 %collective-permute-start.9 = (f32[8,4,256]{2,1,0:T(4,128)S(1)}, f32[8,4,256]{2,1,0:T(4,128)S(1)}, u32[]{:S(2)}, u32[]{:S(2)}) collective-permute-start(f32[8,4,256]{2,1,0:T(4,128)S(1)} %get-tuple-element.117.refs_0_), channel_id=1, source_target_pairs={{0,1},{1,0},{2,3},{3,2},{4,5},{5,4},{6,7},{7,6},{8,9},{9,8},{10,11... | collective-permute-start | bytes 98312 | tf_op jit(solution)/shard_map/ppermute | solution.py:52
  42.5 2.7 %collective-permute-start.12 = (bf16[2,512,512]{2,1,0:T(8,128)(2,1)S(1)}, bf16[2,512,512]{2,1,0:T(8,128)(2,1)S(1)}, u32[]{:S(2)}, u32[]{:S(2)}) collective-permute-start(bf16[2,512,512]{2,1,0:T(8,128)(2,1)S(1)} %get-tuple-element.120), channel_id=1, source_target_pairs={{0,1},{1,0},{2,3},{3,2},{4,5},{5,4},{6,7},{7,6},{8,9},{9,8},{10,11... | collective-permute-start | bytes 3145736 | tf_op jit(solution)/shard_map/ppermute | solution.py:52
  45.5 5.3 %copy-start.14 = (f32[512,512]{1,0:T(8,128)}, f32[512,512]{1,0:T(8,128)S(1)}, u32[]{:S(2)}) copy-start(f32[512,512]{1,0:T(8,128)S(1)} %get-tuple-element.169.refs_0_) | copy-start | bytes 3145732
  45.5 17.5 %collective-permute-start.14 = (bf16[512,512]{1,0:T(8,128)(2,1)S(1)}, bf16[512,512]{1,0:T(8,128)(2,1)S(1)}, u32[]{:S(2)}, u32[]{:S(2)}) collective-permute-start(bf16[512,512]{1,0:T(8,128)(2,1)S(1)} %get-tuple-element.139), channel_id=1, source_target_pairs={{0,2},{1,3},{2,0},{3,1},{4,6},{5,7},{6,4},{7,5},{8,10},{9,11},{10,... | collective-permute-start | bytes 1572872 | tf_op jit(solution)/shard_map/ppermute | solution.py:52
  50.8 12.3 %collective-permute-start.13 = (bf16[4,64,384]{2,1,0:T(8,128)(2,1)S(1)}, bf16[4,64,384]{2,1,0:T(8,128)(2,1)S(1)}, u32[]{:S(2)}, u32[]{:S(2)}) collective-permute-start(bf16[4,64,384]{2,1,0:T(8,128)(2,1)S(1)} %get-tuple-element.138), channel_id=1, source_target_pairs={{0,4},{4,0},{8,12},{12,8},{16,20},{20,16},{24,28},{28,24},{1,5},{5... | collective-permute-start | bytes 589832 | tf_op jit(solution)/shard_map/ppermute | solution.py:52
  63.1 7.9 %collective-permute-start.15 = (bf16[4,80,256]{2,1,0:T(8,128)(2,1)S(1)}, bf16[4,80,256]{2,1,0:T(8,128)(2,1)S(1)}, u32[]{:S(2)}, u32[]{:S(2)}) collective-permute-start(bf16[4,80,256]{2,1,0:T(8,128)(2,1)S(1)} %get-tuple-element.141), channel_id=1, source_target_pairs={{0,4},{4,0},{8,12},{12,8},{16,20},{20,16},{24,28},{28,24},{1,5},{5... | collective-permute-start | bytes 491528 | tf_op jit(solution)/shard_map/ppermute | solution.py:52
  64.9 6.1 %collective-permute-start.16 = (bf16[2,512,512]{2,1,0:T(8,128)(2,1)S(1)}, bf16[2,512,512]{2,1,0:T(8,128)(2,1)S(1)}, u32[]{:S(2)}, u32[]{:S(2)}) collective-permute-start(bf16[2,512,512]{2,1,0:T(8,128)(2,1)S(1)} %get-tuple-element.149), channel_id=1, source_target_pairs={{0,1},{1,0},{2,3},{3,2},{4,5},{5,4},{6,7},{7,6},{8,9},{9,8},{10,11... | collective-permute-start | bytes 3145736 | tf_op jit(solution)/shard_map/ppermute | solution.py:52
  65.0 9.8 %collective-permute-start.20 = (bf16[64,384]{1,0:T(8,128)(2,1)S(1)}, bf16[64,384]{1,0:T(8,128)(2,1)S(1)}, u32[]{:S(2)}, u32[]{:S(2)}) collective-permute-start(bf16[64,384]{1,0:T(8,128)(2,1)S(1)} %get-tuple-element.160), channel_id=1, source_target_pairs={{0,24},{4,28},{8,16},{12,20},{16,8},{20,12},{24,0},{28,4},{1,25},{... | collective-permute-start | bytes 147464 | tf_op jit(solution)/shard_map/ppermute | solution.py:52
  70.3 6.0 %collective-permute-start.21 = (bf16[64,384]{1,0:T(8,128)(2,1)S(1)}, bf16[64,384]{1,0:T(8,128)(2,1)S(1)}, u32[]{:S(2)}, u32[]{:S(2)}) collective-permute-start(bf16[64,384]{1,0:T(8,128)(2,1)S(1)} %get-tuple-element.161), channel_id=1, source_target_pairs={{0,16},{4,20},{8,24},{12,28},{16,0},{20,4},{24,8},{28,12},{1,17},{... | collective-permute-start | bytes 147464 | tf_op jit(solution)/shard_map/ppermute | solution.py:52
  70.3 6.0 %collective-permute-start.22 = (bf16[64,384]{1,0:T(8,128)(2,1)S(1)}, bf16[64,384]{1,0:T(8,128)(2,1)S(1)}, u32[]{:S(2)}, u32[]{:S(2)}) collective-permute-start(bf16[64,384]{1,0:T(8,128)(2,1)S(1)} %get-tuple-element.162), channel_id=1, source_target_pairs={{0,8},{4,12},{8,0},{12,4},{16,24},{20,28},{24,16},{28,20},{1,9},{5... | collective-permute-start | bytes 147464 | tf_op jit(solution)/shard_map/ppermute | solution.py:52
  71.0 8.2 %collective-permute-start.17 = (bf16[80,256]{1,0:T(8,128)(2,1)S(1)}, bf16[80,256]{1,0:T(8,128)(2,1)S(1)}, u32[]{:S(2)}, u32[]{:S(2)}) collective-permute-start(bf16[80,256]{1,0:T(8,128)(2,1)S(1)} %get-tuple-element.150), channel_id=1, source_target_pairs={{0,24},{4,28},{8,16},{12,20},{16,8},{20,12},{24,0},{28,4},{1,25},{... | collective-permute-start | bytes 122888 | tf_op jit(solution)/shard_map/ppermute | solution.py:52
  74.8 4.9 %collective-permute-start.18 = (bf16[80,256]{1,0:T(8,128)(2,1)S(1)}, bf16[80,256]{1,0:T(8,128)(2,1)S(1)}, u32[]{:S(2)}, u32[]{:S(2)}) collective-permute-start(bf16[80,256]{1,0:T(8,128)(2,1)S(1)} %get-tuple-element.151), channel_id=1, source_target_pairs={{0,16},{4,20},{8,24},{12,28},{16,0},{20,4},{24,8},{28,12},{1,17},{... | collective-permute-start | bytes 122888 | tf_op jit(solution)/shard_map/ppermute | solution.py:52
  74.8 4.9 %collective-permute-start.19 = (bf16[80,256]{1,0:T(8,128)(2,1)S(1)}, bf16[80,256]{1,0:T(8,128)(2,1)S(1)}, u32[]{:S(2)}, u32[]{:S(2)}) collective-permute-start(bf16[80,256]{1,0:T(8,128)(2,1)S(1)} %get-tuple-element.152), channel_id=1, source_target_pairs={{0,8},{4,12},{8,0},{12,4},{16,24},{20,28},{24,16},{28,20},{1,9},{5... | collective-permute-start | bytes 122888 | tf_op jit(solution)/shard_map/ppermute | solution.py:52
  77.1 9.9 %collective-permute-start.23 = (bf16[256,512]{1,0:T(8,128)(2,1)S(1)}, bf16[256,512]{1,0:T(8,128)(2,1)}, u32[]{:S(2)}, u32[]{:S(2)}) collective-permute-start(bf16[256,512]{1,0:T(8,128)(2,1)S(1)} %get-tuple-element.166), channel_id=1, source_target_pairs={{0,2},{1,3},{2,0},{3,1},{4,6},{5,7},{6,4},{7,5},{8,10},{9,11},{10,... | collective-permute-start | bytes 786440 | tf_op jit(solution)/shard_map/ppermute | solution.py:52
  78.3 12.1 %collective-permute-start.24 = (bf16[256,512]{1,0:T(8,128)(2,1)}, bf16[256,512]{1,0:T(8,128)(2,1)S(1)}, u32[]{:S(2)}, u32[]{:S(2)}) collective-permute-start(bf16[256,512]{1,0:T(8,128)(2,1)} %get-tuple-element.167), channel_id=1, source_target_pairs={{0,2},{1,3},{2,0},{3,1},{4,6},{5,7},{6,4},{7,5},{8,10},{9,11},{10,... | collective-permute-start | bytes 786440 | tf_op jit(solution)/shard_map/ppermute | solution.py:52
  80.5 11.7 %all-to-all-start = ((f32[32,4,128]{2,1,0:T(4,128)}), f32[32,4,128]{2,1,0:T(4,128)S(1)}, u32[]{:S(2)}, u32[]{:S(2)}) async-start(f32[32,4,128]{2,1,0:T(4,128)} %get-tuple-element.168), calls=%async_computation | async-start | bytes 131072 | tf_op jit(solution)/shard_map/all_to_all | solution.py:932
  84.8 1.2 %copy-start.15 = (f32[512,512]{1,0:T(8,128)S(1)}, f32[512,512]{1,0:T(8,128)}, u32[]{:S(2)}) copy-start(f32[512,512]{1,0:T(8,128)} %copy-done.14) | copy-start | bytes 3145732
  89.1 3.1 %copy-start.3 = (f32[64,4,128]{2,1,0:T(4,128)S(1)}, f32[64,4,128]{2,1,0:T(4,128)}, u32[]{:S(2)}) copy-start(f32[64,4,128]{2,1,0:T(4,128)} %refs_0_.7) | copy-start | bytes 393220
  89.1 3.1 %copy-start.4 = (f32[64,4,128]{2,1,0:T(4,128)S(1)}, f32[64,4,128]{2,1,0:T(4,128)}, u32[]{:S(2)}) copy-start(f32[64,4,128]{2,1,0:T(4,128)} %refs_1_.5) | copy-start | bytes 393220
  89.1 3.1 %copy-start.5 = (f32[64,4,128]{2,1,0:T(4,128)S(1)}, f32[64,4,128]{2,1,0:T(4,128)}, u32[]{:S(2)}) copy-start(f32[64,4,128]{2,1,0:T(4,128)} %refs_2_.3) | copy-start | bytes 393220
  89.1 3.1 %copy-start.7 = (f32[8832]{0:T(1024)S(1)}, f32[8832]{0:T(1024)}, u32[]{:S(2)}) copy-start(f32[8832]{0:T(1024)} %param.24) | copy-start | bytes 105988
  89.2 3.1 %copy-start.8 = (f32[8832]{0:T(1024)S(1)}, f32[8832]{0:T(1024)}, u32[]{:S(2)}) copy-start(f32[8832]{0:T(1024)} %param.25) | copy-start | bytes 105988
  89.2 3.1 %copy-start.10 = (f32[128,64]{0,1:T(8,128)S(1)}, f32[128,64]{0,1:T(8,128)}, u32[]{:S(2)}) copy-start(f32[128,64]{0,1:T(8,128)} %param.18) | copy-start | bytes 98308
  89.2 3.1 %copy-start.11 = (f32[128,64]{0,1:T(8,128)S(1)}, f32[128,64]{0,1:T(8,128)}, u32[]{:S(2)}) copy-start(f32[128,64]{0,1:T(8,128)} %param.22) | copy-start | bytes 98308
  89.2 3.1 %copy-start.12 = (f32[128,64]{0,1:T(8,128)S(1)}, f32[128,64]{0,1:T(8,128)}, u32[]{:S(2)}) copy-start(f32[128,64]{0,1:T(8,128)} %param.23) | copy-start | bytes 98308

commit v11 on v9

--- a/solution.py
+++ b/solution.py
@@ -387,9 +387,9 @@
 
 
 def branch_kernel(n_head, *refs):
-    stats, (attn_ref, p_ref, wt_ref, keep, send) = refs[:n_head], refs[n_head:]
+    stats, (attn_ref, p_ref, wt_ref), branches = refs[:n_head], refs[n_head : n_head + 3], refs[n_head + 3 :]
     width = attn_ref.shape[1]
-    per = keep.shape[1] // TILE
+    per = branches[0].shape[0] // TILE
     for k in range(n_head):
         device = lax.axis_index("head") ^ k
         for r in range(per):
@@ -397,9 +397,13 @@
             normed = standardized(i, n_head, stats, attn_ref)[0]
             p = p_ref[i]
             gated = (normed * (p * (0.5 + 0.5 * jnp.tanh(0.5 * p)))).astype(bf16)
-            (keep, send)[k % 2][device // 2, r * TILE : (r + 1) * TILE] = dot(
+            branches[k][r * TILE : (r + 1) * TILE, :] = dot(
                 flip(gated).astype(bf16), wt_ref[4 * width :]
             ).astype(bf16)
+
+
+def pair_kernel(keep_ref, crossed_ref, out_ref):
+    out_ref[...] = (keep_ref[...].astype(f32) + crossed_ref[...].astype(f32)).astype(bf16)
 
 
 def middle_kernel(n_head, *refs):
@@ -847,11 +851,11 @@
 
     stats = [stat] + [swap(stat, "head", k) for k in range(1, n_head)]
     chips = n_head // 2
-    split_shape = ((chips, here, D), bf16, VMEM)
-    keep, send = call(
-        functools.partial(branch_kernel, n_head), "branch", [VMEM] * (n_head + 3), [split_shape] * 2, [], 1
+    share = ((here, D), bf16, VMEM)
+    branches = call(
+        functools.partial(branch_kernel, n_head), "branch", [VMEM] * (n_head + 3), [share] * n_head, [], 1
     )(*stats, attn, p_gate, wt)
-    crossed = swap(send, "head", 1)
+    crossed = [swap(branches[2 * k + 1], "head", 1) for k in range(chips)]
     da, dat, gun, wg_sum = call(
         functools.partial(middle_kernel, n_head),
         "middle",
@@ -865,8 +869,11 @@
         [],
         6,
     )(*stats, *cot_pieces, attn, p_gate, gg, xn)
-    branch, *leaving = fold_cores(keep, crossed)
-    received = [swap(sent, "head", 2 * (k + 1)) for k, sent in enumerate(leaving)]
+    received = [
+        swap(call(pair_kernel, "pair", [VMEM] * 2, [share], [], 0.1)(branches[2 * k], crossed[k])[0], "head", 2 * k)
+        for k in range(1, chips)
+    ]
+    branch = (branches[0], crossed[0])
     held = kept_weights if kept else (kx, qs, trow, pos, starts)
     gpv, *early_parts = call(
         functools.partial(values_kernel, heads, kept),
@@ -931,8 +938,8 @@
     message = after(message, *leaving)
     heard = lax.all_to_all(message, ("dp", "head"), 0, 0, tiled=True)
     (mixed,) = call(
-        mix_kernel, "mix", [VMEM] * (2 + chips), [((here, D), bf16, VMEM)], [], 1
-    )(tokens, small_rows, after(branch, message), *received)
+        mix_kernel, "mix", [VMEM] * (3 + chips), [((here, D), bf16, VMEM)], [], 1
+    )(tokens, small_rows, after(branch[0], message), branch[1], *received)
     input_grad = None
     for part in range(2):
         rows = pl.BlockSpec((half, D), lambda i, part=part: (part, 0))

time: 94.4 us -> 95.5 us (1.012)
  waiting for transfers between devices: 16.3 us -> 14.3 us
  local copies, waits for them, and re-layouts: 2.95 us -> 4.59 us
  Pallas kernels: 42.8 us -> 43.8 us
    unnamed x34 -> x38, local copies, waits for them, and re-layouts: 2.95 us -> 4.59 us
    ppermute x25 -> x26, waiting for transfers between devices: 15.6 us -> 14.3 us  [swap(): return lax.ppermute(x, axis, [(i, i ^ k) for i in range(n)])]
    pallas_call x1 -> x2, Pallas kernels: 0.99 us -> 2.25 us  [the longest x1 2.12 us: shards(): call(mix_kernel, 'mix', [VMEM] * (3 + chips), [((here, D), bf16, VMEM)],...]
    ppermute x25 -> x26, starting transfers between devices: 26.7 us -> 27.7 us  [swap(): return lax.ppermute(x, axis, [(i, i ^ k) for i in range(n)])]
  transfers between devices with their start and end apart: 26 -> 27, of which waited for: 12 -> 10; matrix products, arithmetic and copies ran while one was open for 0% -> 0% of each run, Pallas kernels for 40% -> 41%
where the time goes in v11:
time: 95.5 us; the launch traced here: 95.1 us
  Pallas kernels  43.8 us (46%)
  starting transfers between devices  31.4 us (33%)
  waiting for transfers between devices  14.3 us (15%)
  local copies, waits for them, and re-layouts  4.59 us (5%)
  between operations  1.1 us (1%)
    ppermute x26, starting transfers between devices, swap(): return lax.ppermute(x, axis, [(i, i ^ k) for i in range(n)])  27.7 us
    ppermute x26, waiting for transfers between devices, swap(): return lax.ppermute(x, axis, [(i, i ^ k) for i in range(n)])  14.3 us
    pallas_call x1, Pallas kernels, shards(): call(functools.partial(backward_kernel, heads, n_dp, extra, kept), 'backw...  10.6 us
    pallas_call x2, Pallas kernels, attend(): call(functools.partial(attend_kernel, heads, first, last, kept), 'attend'...  8.23 us
    unnamed x38, local copies, waits for them, and re-layouts  4.59 us
    pallas_call x1, Pallas kernels, shards(): call(functools.partial(values_kernel, heads, kept), 'values', [VMEM] * (l...  4.32 us
    all_to_all x1, starting transfers between devices, shards(): heard = lax.all_to_all(message, ('dp', 'head'), 0, 0, tiled=True)  3.64 us
    pallas_call x2, Pallas kernels, shards(): call(functools.partial(finish_kernel, part), 'finish', [pl.BlockSpec(memo...  3.39 us
  transfers between devices with their start and end apart: 27, of which 10 were waited for; matrix products, arithmetic and copies ran while one was open for 0% of the time, Pallas kernels for 41%

profile of v11, /device:TPU:0, one launch (start us, length us, event | category | flops | bytes accessed | tf_op | source)
XLA Modules:
  0.0 95.1 jit_solution(6078318299225475842)
XLA Ops:
  0.6 0.0 copy-start.2
  0.7 0.9 copy-done.2
  1.6 0.8 copy-done.9
  2.3 0.3 cast.1.refs_0_
  2.7 4.1 %collective-permute-start.5 = (bf16[64,640]{1,0:T(8,128)(2,1)S(1)}, bf16[64,640]{1,0:T(8,128)(2,1)S(1)}, u32[]{:S(2)}, u32[]{:S(2)}) collective-permute-start(bf16[64,640]{1,0:T(8,128)(2,1)S(1)} %cast.1.refs_0_), channel_id=1, source_target_pairs={{0,16},{4,20},{8,24},{12,28},{16,0},{20,4},{24,8},{28,12},{1,17},{... | collective-permute-start | bytes 245768 | tf_op jit(solution)/shard_map/ppermute | solution.py:52
  6.8 1.5 %collective-permute-start.3 = (bf16[512,512]{1,0:T(8,128)(2,1)}, bf16[512,512]{1,0:T(8,128)(2,1)S(1)}, u32[]{:S(2)}, u32[]{:S(2)}) collective-permute-start(bf16[512,512]{1,0:T(8,128)(2,1)} %refs_1_.4), channel_id=1, source_target_pairs={{0,2},{1,3},{2,0},{3,1},{4,6},{5,7},{6,4},{7,5},{8,10},{9,11},{10,... | collective-permute-start | bytes 1572872 | tf_op jit(solution)/shard_map/ppermute | solution.py:52
  8.3 2.7 %collective-permute-done.5.refs_1_ = bf16[64,640]{1,0:T(8,128)(2,1)S(1)} collective-permute-done((bf16[64,640]{1,0:T(8,128)(2,1)S(1)}, bf16[64,640]{1,0:T(8,128)(2,1)S(1)}, u32[]{:S(2)}, u32[]{:S(2)}) %collective-permute-start.5) | collective-permute-done | bytes 81952 | tf_op jit(solution)/shard_map/ppermute | solution.py:52
  11.0 0.8 collective-permute-start.6
  11.8 2.5 %prepare.1 = (f32[8,256,256]{2,1,0:T(8,128)S(1)}, bf16[8,256,128]{2,1,0:T(8,128)(2,1)S(1)}, bf16[8,128,256]{2,1,0:T(8,128)(2,1)S(1)}, bf16[8,128,256]{2,1,0:T(8,128)(2,1)S(1)}) custom-call(s32[1,2048]{1,0:T(1,128)S(1)} %bitcast.28, f32[69,128]{1,0:T(8,128)S(1)} %bitcast.17), custom_call_target="tpu_custom_call" | custom-call | flops 2000000000 | bytes 6000000 | tf_op jit(solution)/shard_map/prepare/pallas_call | solution.py:764
  14.3 2.1 %collective-permute-done.6.refs_2_ = bf16[128,640]{1,0:T(8,128)(2,1)S(1)} collective-permute-done((bf16[128,640]{1,0:T(8,128)(2,1)S(1)}, bf16[128,640]{1,0:T(8,128)(2,1)S(1)}, u32[]{:S(2)}, u32[]{:S(2)}) %collective-permute-start.6) | collective-permute-done | bytes 163872 | tf_op jit(solution)/shard_map/ppermute | solution.py:52
  16.4 1.8 %collective-permute-start.7 = (bf16[256,640]{1,0:T(8,128)(2,1)S(1)}, bf16[256,640]{1,0:T(8,128)(2,1)S(1)}, u32[]{:S(2)}, u32[]{:S(2)}) collective-permute-start(bf16[256,640]{1,0:T(8,128)(2,1)S(1)} %join.4), channel_id=1, source_target_pairs={{0,4},{4,0},{8,12},{12,8},{16,20},{20,16},{24,28},{28,24},{1,5},{5... | collective-permute-start | bytes 983048 | tf_op jit(solution)/shard_map/ppermute | solution.py:52
  18.2 1.5 %collective-permute-start.1 = (bf16[512,512]{1,0:T(8,128)(2,1)S(1)}, bf16[512,512]{1,0:T(8,128)(2,1)S(1)}, u32[]{:S(2)}, u32[]{:S(2)}) collective-permute-start(bf16[512,512]{1,0:T(8,128)(2,1)S(1)} %copy-done.1), channel_id=1, source_target_pairs={{0,2},{1,3},{2,0},{3,1},{4,6},{5,7},{6,4},{7,5},{8,10},{9,11},{10,... | collective-permute-start | bytes 1572872 | tf_op jit(solution)/shard_map/ppermute | solution.py:52
  19.7 1.7 %collective-permute-done.3.refs_2_ = bf16[512,512]{1,0:T(8,128)(2,1)S(1)} collective-permute-done((bf16[512,512]{1,0:T(8,128)(2,1)}, bf16[512,512]{1,0:T(8,128)(2,1)S(1)}, u32[]{:S(2)}, u32[]{:S(2)}) %collective-permute-start.3) | collective-permute-done | bytes 524320 | tf_op jit(solution)/shard_map/ppermute | solution.py:52
  21.3 1.0 %normalize.2.refs_0_ = bf16[8,256,512]{2,1,0:T(8,128)(2,1)S(1)} custom-call(bf16[512,512]{1,0:T(8,128)(2,1)S(1)} %copy-done, bf16[512,512]{1,0:T(8,128)(2,1)S(1)} %collective-permute-done.2.refs_1_, bf16[512,512]{1,0:T(8,128)(2,1)S(1)} %collective-permute-done.3.refs_2_), custom_call_target="tpu_custom_call" | custom-call | flops 100000000 | bytes 300000 | tf_op jit(solution)/shard_map/normalize/pallas_call | solution.py:795
  22.3 1.8 %collective-permute-done.7.refs_0_ = bf16[256,640]{1,0:T(8,128)(2,1)S(1)} collective-permute-done((bf16[256,640]{1,0:T(8,128)(2,1)S(1)}, bf16[256,640]{1,0:T(8,128)(2,1)S(1)}, u32[]{:S(2)}, u32[]{:S(2)}) %collective-permute-start.7) | collective-permute-done | bytes 327712 | tf_op jit(solution)/shard_map/ppermute | solution.py:52
  24.1 0.4 normalize.3.refs_0_.refs_5_.refs_11_.refs_8_.refs_4_
  24.5 0.0 copy-start.13
  24.5 0.3 assemble.1.refs_1_.refs_6_.wt_ref
  24.8 1.8 %project.1 = (bf16[8,384,256]{2,1,0:T(8,128)(2,1)S(1)}, bf16[8,256,256]{2,1,0:T(8,128)(2,1)S(1)}, bf16[8,256,256]{2,1,0:T(8,128)(2,1)S(1)}, bf16[8,128,256]{2,1,...) custom-call(bf16[8,256,512]{2,1,0:T(8,128)(2,1)S(1)} %normalize.3.re, ...), custom_call_target="tpu_custom_call" | custom-call | flops 1000000000 | bytes 3000000 | tf_op jit(solution)/shard_map/project/pallas_call | solution.py:813
  26.7 4.7 %attend.2 = (f32[6,128,256]{2,1,0:T(8,128)S(1)}, bf16[21,256,512]{2,1,0:T(8,128)(2,1)S(1)}, bf16[21,256,512]{2,1,0:T(8,128)(2,1)S(1)}) custom-call(bf16[8,256,256]{2,1,0:T(8,128)(2,1)S(1)} %get-tuple-element.109.refs_0_.refs_1_.refs_2_, bf16[8,128,256]{2,1,0:T(8,128)(2,1)S(1)} %get-tuple-element.110.refs_1_.refs_2_, ...), custom_call_target="tpu_custom_call" | custom-call | flops 500000000 | bytes 1500000 | tf_op jit(solution)/shard_map/attend/pallas_call | solution.py:826
  31.4 1.2 %collective-permute-done.1.refs_2_.refs_6_ = bf16[512,512]{1,0:T(8,128)(2,1)S(1)} collective-permute-done((bf16[512,512]{1,0:T(8,128)(2,1)S(1)}, bf16[512,512]{1,0:T(8,128)(2,1)S(1)}, u32[]{:S(2)}, u32[]{:S(2)}) %collective-permute-start.1) | collective-permute-done | bytes 524320 | tf_op jit(solution)/shard_map/ppermute | solution.py:52
  32.6 3.5 %attend.3 = (f32[8,128,256]{2,1,0:T(8,128)S(1)}, bf16[15,256,512]{2,1,0:T(8,128)(2,1)S(1)}, bf16[15,256,512]{2,1,0:T(8,128)(2,1)S(1)}) custom-call(f32[6,128,256]{2,1,0:T(8,128)S(1)} %get-tuple-element.115.refs_0_, bf16[8,256,256]{2,1,0:T(8,128)(2,1)S(1)} %get-tuple-element.109.refs_0_.refs_1_.refs_2_, ...), custom_call_target="tpu_custom_call" | custom-call | flops 8000000000 | bytes 24000000 | tf_op jit(solution)/shard_map/attend/pallas_call | solution.py:826
  36.1 1.8 %gate.1 = (f32[8,128,256]{2,1,0:T(8,128)S(1)}, f32[8,128,256]{2,1,0:T(8,128)S(1)}, f32[8,4,256]{2,1,0:T(4,128)S(1)}, f32[1,512]{1,0:T(1,128)S(1)}) custom-call(bf16[512,512]{1,0:T(8,128)(2,1)S(1)} %copy-done.1, bf16[512,512]{1,0:T(8,128)(2,1)S(1)} %collective-permute-done.refs_1_.refs_5_, bf16[512,512]{1,0:T(8,128)(2,1)S(1)} %collective-permute-done.1.refs_2_.refs_6_, ...), custom_call_target="tpu_custom_call" | custom-call | flops 5000000000 | bytes 15000000 | tf_op jit(solution)/shard_map/gate/pallas_call | solution.py:843
  37.9 1.7 %collective-permute-start.11 = (f32[8,4,256]{2,1,0:T(4,128)S(1)}, f32[8,4,256]{2,1,0:T(4,128)S(1)}, u32[]{:S(2)}, u32[]{:S(2)}) collective-permute-start(f32[8,4,256]{2,1,0:T(4,128)S(1)} %get-tuple-element.117.refs_0_), channel_id=1, source_target_pairs={{0,3},{1,2},{2,1},{3,0},{4,7},{5,6},{6,5},{7,4},{8,11},{9,10},{10,... | collective-permute-start | bytes 98312 | tf_op jit(solution)/shard_map/ppermute | solution.py:52
  39.6 0.5 collective-permute-start.10
  40.1 1.2 %collective-permute-done.11.refs_3_ = f32[8,4,256]{2,1,0:T(4,128)S(1)} collective-permute-done((f32[8,4,256]{2,1,0:T(4,128)S(1)}, f32[8,4,256]{2,1,0:T(4,128)S(1)}, u32[]{:S(2)}, u32[]{:S(2)}) %collective-permute-start.11) | collective-permute-done | bytes 32800 | tf_op jit(solution)/shard_map/ppermute | solution.py:52
  41.3 2.2 %collective-permute-done.10.refs_2_ = f32[8,4,256]{2,1,0:T(4,128)S(1)} collective-permute-done((f32[8,4,256]{2,1,0:T(4,128)S(1)}, f32[8,4,256]{2,1,0:T(4,128)S(1)}, u32[]{:S(2)}, u32[]{:S(2)}) %collective-permute-start.10) | collective-permute-done | bytes 32800 | tf_op jit(solution)/shard_map/ppermute | solution.py:52
  43.5 0.8 branch.1
  44.3 0.0 copy-start.17
  44.4 0.8 copy-done.17
  45.1 1.3 %middle.1 = (bf16[8,256,128]{2,1,0:T(8,128)(2,1)S(1)}, bf16[8,128,256]{2,1,0:T(8,128)(2,1)S(1)}, bf16[8,256,128]{2,1,0:T(8,128)(2,1)S(1)}, f32[256,512]{1,0:T(8,128)S(1)}) custom-call(f32[8,4,256]{2,1,0:T(4,128)S(1)} %get-tuple-element.117.refs_0_, f32[8,4,256]{2,1,0:T(4,128)S(1)} %collective-permute-done.9.refs_1_, ...), custom_call_target="tpu_custom_call" | custom-call | flops 6000000000 | bytes 18000000 | tf_op jit(solution)/shard_map/middle/pallas_call | solution.py:859
  46.4 0.6 collective-permute-done.13.crossed_ref
  47.0 0.1 pair.1
  47.2 0.6 collective-permute-start.14
  47.8 4.3 %values.1 = (bf16[8,256,128]{2,1,0:T(8,128)(2,1)S(1)}, bf16[4,64,384]{2,1,0:T(8,128)(2,1)S(1)}, bf16[4,64,384]{2,1,0:T(8,128)(2,1)S(1)}) custom-call(bf16[21,256,512]{2,1,0:T(8,128)(2,1)S(1)} %get-tuple-element.132.refs_0_, bf16[15,256,512]{2,1,0:T(8,128)(2,1)S(1)} %get-tuple-element.133.refs_1_, bf16[8,256,128]{2,1,0:T(8,128)(2,1)S(1)} %get-tuple-element.134.refs_2_, ...), custom_call_target="tpu_custom_call" | custom-call | flops 12000000000 | bytes 36000000 | tf_op jit(solution)/shard_map/values/pallas_call | solution.py:878
  52.1 1.6 %collective-permute-start.12 = (bf16[4,64,384]{2,1,0:T(8,128)(2,1)S(1)}, bf16[4,64,384]{2,1,0:T(8,128)(2,1)S(1)}, u32[]{:S(2)}, u32[]{:S(2)}) collective-permute-start(bf16[4,64,384]{2,1,0:T(8,128)(2,1)S(1)} %get-tuple-element.136), channel_id=1, source_target_pairs={{0,4},{4,0},{8,12},{12,8},{16,20},{20,16},{24,28},{28,24},{1,5},{5... | collective-permute-start | bytes 589832 | tf_op jit(solution)/shard_map/ppermute | solution.py:52
  53.7 10.6 %backward.1 = (bf16[8,256,256]{2,1,0:T(8,128)(2,1)S(1)}, bf16[4,80,256]{2,1,0:T(8,128)(2,1)S(1)}, bf16[4,80,256]{2,1,0:T(8,128)(2,1)S(1)}) custom-call(bf16[21,256,512]{2,1,0:T(8,128)(2,1)S(1)} %get-tuple-element.120.refs_0_, bf16[15,256,512]{2,1,0:T(8,128)(2,1)S(1)} %get-tuple-element.121.refs_1_, ...), custom_call_target="tpu_custom_call" | custom-call | flops 2000000000 | bytes 6000000 | tf_op jit(solution)/shard_map/backward/pallas_call | solution.py:891
  64.3 0.0 copy-start.14
  64.3 0.6 collective-permute-start.15
  64.9 1.3 %input_rows.1 = (bf16[2,512,512]{2,1,0:T(8,128)(2,1)S(1)}, bf16[2,512,512]{2,1,0:T(8,128)(2,1)S(1)}) custom-call(bf16[8,256,256]{2,1,0:T(8,128)(2,1)S(1)} %get-tuple-element.145.gp_ref, bf16[8,256,128]{2,1,0:T(8,128)(2,1)S(1)} %get-tuple-element.146.gun_ref, bf16[8,256,128]{2,1,0:T(8,128)(2,1)S(1)} %get-tuple-element.147.gpv_ref, ...), custom_call_target="tpu_custom_call" | custom-call | flops 4000000000 | bytes 12000000 | tf_op jit(solution)/shard_map/input_rows/pallas_call | solution.py:911
  66.2 0.3 collective-permute-start.16
  66.5 4.2 %collective-permute-start.20 = (bf16[64,384]{1,0:T(8,128)(2,1)S(1)}, bf16[64,384]{1,0:T(8,128)(2,1)S(1)}, u32[]{:S(2)}, u32[]{:S(2)}) collective-permute-start(bf16[64,384]{1,0:T(8,128)(2,1)S(1)} %get-tuple-element.159), channel_id=1, source_target_pairs={{0,24},{4,28},{8,16},{12,20},{16,8},{20,12},{24,0},{28,4},{1,25},{... | collective-permute-start | bytes 147464 | tf_op jit(solution)/shard_map/ppermute | solution.py:52
  70.7 0.3 collective-permute-done.15.refs_1_
  71.0 1.6 %collective-permute-start.22 = (bf16[64,384]{1,0:T(8,128)(2,1)S(1)}, bf16[64,384]{1,0:T(8,128)(2,1)S(1)}, u32[]{:S(2)}, u32[]{:S(2)}) collective-permute-start(bf16[64,384]{1,0:T(8,128)(2,1)S(1)} %get-tuple-element.161), channel_id=1, source_target_pairs={{0,8},{4,12},{8,0},{12,4},{16,24},{20,28},{24,16},{28,20},{1,9},{5... | collective-permute-start | bytes 147464 | tf_op jit(solution)/shard_map/ppermute | solution.py:52
  72.6 3.2 %collective-permute-start.17 = (bf16[80,256]{1,0:T(8,128)(2,1)S(1)}, bf16[80,256]{1,0:T(8,128)(2,1)S(1)}, u32[]{:S(2)}, u32[]{:S(2)}) collective-permute-start(bf16[80,256]{1,0:T(8,128)(2,1)S(1)} %get-tuple-element.149), channel_id=1, source_target_pairs={{0,24},{4,28},{8,16},{12,20},{16,8},{20,12},{24,0},{28,4},{1,25},{... | collective-permute-start | bytes 122888 | tf_op jit(solution)/shard_map/ppermute | solution.py:52
  75.8 0.0 collective-permute-start.18
  75.9 1.8 %collective-permute-start.19 = (bf16[80,256]{1,0:T(8,128)(2,1)S(1)}, bf16[80,256]{1,0:T(8,128)(2,1)S(1)}, u32[]{:S(2)}, u32[]{:S(2)}) collective-permute-start(bf16[80,256]{1,0:T(8,128)(2,1)S(1)} %get-tuple-element.151), channel_id=1, source_target_pairs={{0,8},{4,12},{8,0},{12,4},{16,24},{20,28},{24,16},{28,20},{1,9},{5... | collective-permute-start | bytes 122888 | tf_op jit(solution)/shard_map/ppermute | solution.py:52
  77.7 0.9 rows.1
  78.6 1.5 %collective-permute-start.24 = (bf16[256,512]{1,0:T(8,128)(2,1)S(1)}, bf16[256,512]{1,0:T(8,128)(2,1)}, u32[]{:S(2)}, u32[]{:S(2)}) collective-permute-start(bf16[256,512]{1,0:T(8,128)(2,1)S(1)} %get-tuple-element.165), channel_id=1, source_target_pairs={{0,2},{1,3},{2,0},{3,1},{4,6},{5,7},{6,4},{7,5},{8,10},{9,11},{10,... | collective-permute-start | bytes 786440 | tf_op jit(solution)/shard_map/ppermute | solution.py:52
  80.1 0.5 collective-permute-start.25
  80.6 0.5 collective-permute-done.18.refs_2_
  81.2 0.8 collect.1
  81.9 3.6 %all-to-all-start = ((f32[32,4,128]{2,1,0:T(4,128)}), f32[32,4,128]{2,1,0:T(4,128)S(1)}, u32[]{:S(2)}, u32[]{:S(2)}) async-start(f32[32,4,128]{2,1,0:T(4,128)} %get-tuple-element.167), calls=%async_computation | async-start | bytes 131072 | tf_op jit(solution)/shard_map/all_to_all | solution.py:939
  85.6 0.0 copy-start.15
  85.6 1.0 %copy-done.15 = bf16[512,512]{1,0:T(8,128)(2,1)S(1)} copy-done((bf16[512,512]{1,0:T(8,128)(2,1)S(1)}, bf16[512,512]{1,0:T(8,128)(2,1)}, u32[]{:S(2)}) %copy-start.15) | copy-done | bytes 524312
  86.6 1.0 %copy-done.18 = bf16[512,512]{1,0:T(8,128)(2,1)S(1)} copy-done((bf16[512,512]{1,0:T(8,128)(2,1)S(1)}, bf16[512,512]{1,0:T(8,128)(2,1)}, u32[]{:S(2)}) %copy-start.18) | copy-done | bytes 524312
  87.7 2.1 %mix.1 = bf16[512,512]{1,0:T(8,128)(2,1)} custom-call(bf16[512,512]{1,0:T(8,128)(2,1)S(1)} %copy-done, f32[69,128]{1,0:T(8,128)S(1)} %bitcast.18, bf16[512,512]{1,0:T(8,128)(2,1)S(1)} %copy-done.18, bf16[512,512]{1,0:T(8,128)(2,1)} %collective-permute-done.23.refs_1_, bf16[512,512]{1,0:T(8,128)(2,1)S(1)} %copy-done.15), custom_call_target="tpu_custom_call" | custom-call | flops 1000000000 | bytes 3000000 | tf_op jit(solution)/shard_map/mix/pallas_call | solution.py:940
  89.8 0.0 copy-start.7
  89.8 0.0 copy-start.8
  89.8 0.0 copy-start.10
  89.8 0.0 copy-start.11
  89.9 2.2 %finish.2.refs_0_ = f32[512,512]{1,0:T(8,128)} custom-call(bf16[512,512]{1,0:T(8,128)(2,1)S(1)} %copy-done, bf16[512,512]{1,0:T(8,128)(2,1)S(1)} %copy-done.1, f32[512,512]{1,0:T(8,128)S(1)} %get-tuple-element.171.refs_2_.refs_3_, bf16[256,512]{1,0:T(8,128)(2,1)} %collective-permute-done.24.refs_3_), custom_call_target="tpu_custom_call" | custom-call | flops 1000000000 | bytes 3000000 | tf_op jit(solution)/shard_map/finish/pallas_call | solution.py:948
  92.1 1.2 %finish.3 = f32[512,512]{1,0:T(8,128)} custom-call(f32[512,512]{1,0:T(8,128)} %finish.2.refs_0_, bf16[512,512]{1,0:T(8,128)(2,1)S(1)} %copy-done, bf16[512,512]{1,0:T(8,128)(2,1)S(1)} %copy-done.1, f32[512,512]{1,0:T(8,128)S(1)} %get-tuple-element.171.refs_2_.refs_3_, ...), custom_call_target="tpu_custom_call", output_to_operand_aliasing={{}: (0, {})} | custom-call | flops 1000000000 | bytes 3000000 | tf_op jit(solution)/shard_map/finish/pallas_call | solution.py:948
  93.3 1.7 %update.1 = (f32[64,4,128]{2,1,0:T(4,128)}, f32[64,128]{1,0:T(8,128)}, f32[69,128]{1,0:T(8,128)}, f32[1,1]{1,0:T(1,128)}, f32[64,4,128]{2,1,0:T(4,128)}, /*index...) custom-call(f32[32,4,128]{2,1,0:T(4,128)S(1)} %all-to-all-done.heard, ...), custom_call_target="tpu_custom_call" | custom-call | flops 100000000 | bytes 300000 | tf_op jit(solution)/shard_map/update/pallas_call | solution.py:963
  (55 shorter events, 0.3 us)
Async XLA Ops:
  0.6 0.9 copy-start.2
  1.6 0.8 copy-start.9
  2.3 9.5 %copy-start.6 = (f32[8832]{0:T(1024)S(1)}, f32[8832]{0:T(1024)}, u32[]{:S(2)}) copy-start(f32[8832]{0:T(1024)} %param.19) | copy-start | bytes 105988
  2.3 9.5 %copy-start.16 = (s32[2048]{0:T(1024)S(1)}, s32[2048]{0:T(1024)}, u32[]{:S(2)}) copy-start(s32[2048]{0:T(1024)} %param.16) | copy-start | bytes 24580
  2.7 8.3 %collective-permute-start.5 = (bf16[64,640]{1,0:T(8,128)(2,1)S(1)}, bf16[64,640]{1,0:T(8,128)(2,1)S(1)}, u32[]{:S(2)}, u32[]{:S(2)}) collective-permute-start(bf16[64,640]{1,0:T(8,128)(2,1)S(1)} %cast.1.refs_0_), channel_id=1, source_target_pairs={{0,16},{4,20},{8,24},{12,28},{16,0},{20,4},{24,8},{28,12},{1,17},{... | collective-permute-start | bytes 245768 | tf_op jit(solution)/shard_map/ppermute | solution.py:52
  6.8 14.6 %collective-permute-start.2 = (bf16[512,512]{1,0:T(8,128)(2,1)}, bf16[512,512]{1,0:T(8,128)(2,1)S(1)}, u32[]{:S(2)}, u32[]{:S(2)}) collective-permute-start(bf16[512,512]{1,0:T(8,128)(2,1)} %refs_1_.4), channel_id=1, source_target_pairs={{0,1},{1,0},{2,3},{3,2},{4,5},{5,4},{6,7},{7,6},{8,9},{9,8},{10,11... | collective-permute-start | bytes 1572872 | tf_op jit(solution)/shard_map/ppermute | solution.py:52
  6.8 14.5 %collective-permute-start.3 = (bf16[512,512]{1,0:T(8,128)(2,1)}, bf16[512,512]{1,0:T(8,128)(2,1)S(1)}, u32[]{:S(2)}, u32[]{:S(2)}) collective-permute-start(bf16[512,512]{1,0:T(8,128)(2,1)} %refs_1_.4), channel_id=1, source_target_pairs={{0,2},{1,3},{2,0},{3,1},{4,6},{5,7},{6,4},{7,5},{8,10},{9,11},{10,... | collective-permute-start | bytes 1572872 | tf_op jit(solution)/shard_map/ppermute | solution.py:52
  11.0 5.4 %collective-permute-start.6 = (bf16[128,640]{1,0:T(8,128)(2,1)S(1)}, bf16[128,640]{1,0:T(8,128)(2,1)S(1)}, u32[]{:S(2)}, u32[]{:S(2)}) collective-permute-start(bf16[128,640]{1,0:T(8,128)(2,1)S(1)} %join.3), channel_id=1, source_target_pairs={{0,8},{4,12},{8,0},{12,4},{16,24},{20,28},{24,16},{28,20},{1,9},{5... | collective-permute-start | bytes 491528 | tf_op jit(solution)/shard_map/ppermute | solution.py:52
  11.8 6.4 %copy-start.1 = (bf16[512,512]{1,0:T(8,128)(2,1)S(1)}, bf16[512,512]{1,0:T(8,128)(2,1)}, u32[]{:S(2)}) copy-start(bf16[512,512]{1,0:T(8,128)(2,1)} %refs_2_.2) | copy-start | bytes 1572868
  11.8 9.5 %copy-start = (bf16[512,512]{1,0:T(8,128)(2,1)S(1)}, bf16[512,512]{1,0:T(8,128)(2,1)}, u32[]{:S(2)}) copy-start(bf16[512,512]{1,0:T(8,128)(2,1)} %refs_1_.4) | copy-start | bytes 1572868
  16.4 7.7 %collective-permute-start.7 = (bf16[256,640]{1,0:T(8,128)(2,1)S(1)}, bf16[256,640]{1,0:T(8,128)(2,1)S(1)}, u32[]{:S(2)}, u32[]{:S(2)}) collective-permute-start(bf16[256,640]{1,0:T(8,128)(2,1)S(1)} %join.4), channel_id=1, source_target_pairs={{0,4},{4,0},{8,12},{12,8},{16,20},{20,16},{24,28},{28,24},{1,5},{5... | collective-permute-start | bytes 983048 | tf_op jit(solution)/shard_map/ppermute | solution.py:52
  18.2 17.9 %collective-permute-start = (bf16[512,512]{1,0:T(8,128)(2,1)S(1)}, bf16[512,512]{1,0:T(8,128)(2,1)S(1)}, u32[]{:S(2)}, u32[]{:S(2)}) collective-permute-start(bf16[512,512]{1,0:T(8,128)(2,1)S(1)} %copy-done.1), channel_id=1, source_target_pairs={{0,1},{1,0},{2,3},{3,2},{4,5},{5,4},{6,7},{7,6},{8,9},{9,8},{10,11... | collective-permute-start | bytes 1572872 | tf_op jit(solution)/shard_map/ppermute | solution.py:52
  18.2 14.4 %collective-permute-start.1 = (bf16[512,512]{1,0:T(8,128)(2,1)S(1)}, bf16[512,512]{1,0:T(8,128)(2,1)S(1)}, u32[]{:S(2)}, u32[]{:S(2)}) collective-permute-start(bf16[512,512]{1,0:T(8,128)(2,1)S(1)} %copy-done.1), channel_id=1, source_target_pairs={{0,2},{1,3},{2,0},{3,1},{4,6},{5,7},{6,4},{7,5},{8,10},{9,11},{10,... | collective-permute-start | bytes 1572872 | tf_op jit(solution)/shard_map/ppermute | solution.py:52
  21.3 2.8 %collective-permute-start.4 = (bf16[512,512]{1,0:T(8,128)(2,1)S(1)}, bf16[512,512]{1,0:T(8,128)(2,1)S(1)}, u32[]{:S(2)}, u32[]{:S(2)}) collective-permute-start(bf16[512,512]{1,0:T(8,128)(2,1)S(1)} %collective-permute-done.3.refs_2_), channel_id=1, source_target_pairs={{0,1},{1,0},{2,3},{3,2},{4,5},{5,4},{6,7},{7,6},{8,9},{9,8},{10,11... | collective-permute-start | bytes 1572872 | tf_op jit(solution)/shard_map/ppermute | solution.py:52
  24.5 2.2 %copy-start.13 = (s32[2048]{0:T(1024)S(1)}, s32[2048]{0:T(1024)}, u32[]{:S(2)}) copy-start(s32[2048]{0:T(1024)} %param.15) | copy-start | bytes 24580
  32.6 3.5 %collective-permute-start.8 = (bf16[512,512]{1,0:T(8,128)(2,1)S(1)}, bf16[512,512]{1,0:T(8,128)(2,1)S(1)}, u32[]{:S(2)}, u32[]{:S(2)}) collective-permute-start(bf16[512,512]{1,0:T(8,128)(2,1)S(1)} %collective-permute-done.1.refs_2_.refs_6_), channel_id=1, source_target_pairs={{0,1},{1,0},{2,3},{3,2},{4,5},{5,4},{6,7},{7,6},{8,9},{9,8},{10,11... | collective-permute-start | bytes 1572872 | tf_op jit(solution)/shard_map/ppermute | solution.py:52
  37.9 3.4 %collective-permute-start.11 = (f32[8,4,256]{2,1,0:T(4,128)S(1)}, f32[8,4,256]{2,1,0:T(4,128)S(1)}, u32[]{:S(2)}, u32[]{:S(2)}) collective-permute-start(f32[8,4,256]{2,1,0:T(4,128)S(1)} %get-tuple-element.117.refs_0_), channel_id=1, source_target_pairs={{0,3},{1,2},{2,1},{3,0},{4,7},{5,6},{6,5},{7,4},{8,11},{9,10},{10,... | collective-permute-start | bytes 98312 | tf_op jit(solution)/shard_map/ppermute | solution.py:52
  39.6 3.9 %collective-permute-start.10 = (f32[8,4,256]{2,1,0:T(4,128)S(1)}, f32[8,4,256]{2,1,0:T(4,128)S(1)}, u32[]{:S(2)}, u32[]{:S(2)}) collective-permute-start(f32[8,4,256]{2,1,0:T(4,128)S(1)} %get-tuple-element.117.refs_0_), channel_id=1, source_target_pairs={{0,2},{1,3},{2,0},{3,1},{4,6},{5,7},{6,4},{7,5},{8,10},{9,11},{10,... | collective-permute-start | bytes 98312 | tf_op jit(solution)/shard_map/ppermute | solution.py:52
  40.1 3.4 %collective-permute-start.9 = (f32[8,4,256]{2,1,0:T(4,128)S(1)}, f32[8,4,256]{2,1,0:T(4,128)S(1)}, u32[]{:S(2)}, u32[]{:S(2)}) collective-permute-start(f32[8,4,256]{2,1,0:T(4,128)S(1)} %get-tuple-element.117.refs_0_), channel_id=1, source_target_pairs={{0,1},{1,0},{2,3},{3,2},{4,5},{5,4},{6,7},{7,6},{8,9},{9,8},{10,11... | collective-permute-start | bytes 98312 | tf_op jit(solution)/shard_map/ppermute | solution.py:52
  44.3 0.8 copy-start.17
  45.1 1.9 %collective-permute-start.13 = (bf16[512,512]{1,0:T(8,128)(2,1)S(1)}, bf16[512,512]{1,0:T(8,128)(2,1)S(1)}, u32[]{:S(2)}, u32[]{:S(2)}) collective-permute-start(bf16[512,512]{1,0:T(8,128)(2,1)S(1)} %get-tuple-element.138), channel_id=1, source_target_pairs={{0,1},{1,0},{2,3},{3,2},{4,5},{5,4},{6,7},{7,6},{8,9},{9,8},{10,11... | collective-permute-start | bytes 1572872 | tf_op jit(solution)/shard_map/ppermute | solution.py:52
  47.2 17.1 %collective-permute-start.14 = (bf16[512,512]{1,0:T(8,128)(2,1)S(1)}, bf16[512,512]{1,0:T(8,128)(2,1)S(1)}, u32[]{:S(2)}, u32[]{:S(2)}) collective-permute-start(bf16[512,512]{1,0:T(8,128)(2,1)S(1)} %pair.1), channel_id=1, source_target_pairs={{0,2},{1,3},{2,0},{3,1},{4,6},{5,7},{6,4},{7,5},{8,10},{9,11},{10,... | collective-permute-start | bytes 1572872 | tf_op jit(solution)/shard_map/ppermute | solution.py:52
  52.1 12.2 %collective-permute-start.12 = (bf16[4,64,384]{2,1,0:T(8,128)(2,1)S(1)}, bf16[4,64,384]{2,1,0:T(8,128)(2,1)S(1)}, u32[]{:S(2)}, u32[]{:S(2)}) collective-permute-start(bf16[4,64,384]{2,1,0:T(8,128)(2,1)S(1)} %get-tuple-element.136), channel_id=1, source_target_pairs={{0,4},{4,0},{8,12},{12,8},{16,20},{20,16},{24,28},{28,24},{1,5},{5... | collective-permute-start | bytes 589832 | tf_op jit(solution)/shard_map/ppermute | solution.py:52
  53.7 31.9 %collective-permute-start.23 = (bf16[512,512]{1,0:T(8,128)(2,1)S(1)}, bf16[512,512]{1,0:T(8,128)(2,1)}, u32[]{:S(2)}, u32[]{:S(2)}) collective-permute-start(bf16[512,512]{1,0:T(8,128)(2,1)S(1)} %get-tuple-element.169), channel_id=1, source_target_pairs={{0,1},{1,0},{2,3},{3,2},{4,5},{5,4},{6,7},{7,6},{8,9},{9,8},{10,11... | collective-permute-start | bytes 1572872 | tf_op jit(solution)/shard_map/ppermute | solution.py:52
  64.3 1.9 %copy-start.14 = (bf16[512,512]{1,0:T(8,128)(2,1)}, bf16[512,512]{1,0:T(8,128)(2,1)S(1)}, u32[]{:S(2)}) copy-start(bf16[512,512]{1,0:T(8,128)(2,1)S(1)} %collective-permute-done.14.refs_2_) | copy-start | bytes 1572868
  64.3 6.7 %collective-permute-start.15 = (bf16[4,80,256]{2,1,0:T(8,128)(2,1)S(1)}, bf16[4,80,256]{2,1,0:T(8,128)(2,1)S(1)}, u32[]{:S(2)}, u32[]{:S(2)}) collective-permute-start(bf16[4,80,256]{2,1,0:T(8,128)(2,1)S(1)} %get-tuple-element.140), channel_id=1, source_target_pairs={{0,4},{4,0},{8,12},{12,8},{16,20},{20,16},{24,28},{28,24},{1,5},{5... | collective-permute-start | bytes 491528 | tf_op jit(solution)/shard_map/ppermute | solution.py:52
  66.2 6.5 %collective-permute-start.16 = (bf16[2,512,512]{2,1,0:T(8,128)(2,1)S(1)}, bf16[2,512,512]{2,1,0:T(8,128)(2,1)S(1)}, u32[]{:S(2)}, u32[]{:S(2)}) collective-permute-start(bf16[2,512,512]{2,1,0:T(8,128)(2,1)S(1)} %get-tuple-element.148), channel_id=1, source_target_pairs={{0,1},{1,0},{2,3},{3,2},{4,5},{5,4},{6,7},{7,6},{8,9},{9,8},{10,11... | collective-permute-start | bytes 3145736 | tf_op jit(solution)/shard_map/ppermute | solution.py:52
  66.5 9.3 %collective-permute-start.20 = (bf16[64,384]{1,0:T(8,128)(2,1)S(1)}, bf16[64,384]{1,0:T(8,128)(2,1)S(1)}, u32[]{:S(2)}, u32[]{:S(2)}) collective-permute-start(bf16[64,384]{1,0:T(8,128)(2,1)S(1)} %get-tuple-element.159), channel_id=1, source_target_pairs={{0,24},{4,28},{8,16},{12,20},{16,8},{20,12},{24,0},{28,4},{1,25},{... | collective-permute-start | bytes 147464 | tf_op jit(solution)/shard_map/ppermute | solution.py:52
  70.7 5.2 %collective-permute-start.21 = (bf16[64,384]{1,0:T(8,128)(2,1)S(1)}, bf16[64,384]{1,0:T(8,128)(2,1)S(1)}, u32[]{:S(2)}, u32[]{:S(2)}) collective-permute-start(bf16[64,384]{1,0:T(8,128)(2,1)S(1)} %get-tuple-element.160), channel_id=1, source_target_pairs={{0,16},{4,20},{8,24},{12,28},{16,0},{20,4},{24,8},{28,12},{1,17},{... | collective-permute-start | bytes 147464 | tf_op jit(solution)/shard_map/ppermute | solution.py:52
  71.0 6.7 %collective-permute-start.22 = (bf16[64,384]{1,0:T(8,128)(2,1)S(1)}, bf16[64,384]{1,0:T(8,128)(2,1)S(1)}, u32[]{:S(2)}, u32[]{:S(2)}) collective-permute-start(bf16[64,384]{1,0:T(8,128)(2,1)S(1)} %get-tuple-element.161), channel_id=1, source_target_pairs={{0,8},{4,12},{8,0},{12,4},{16,24},{20,28},{24,16},{28,20},{1,9},{5... | collective-permute-start | bytes 147464 | tf_op jit(solution)/shard_map/ppermute | solution.py:52
  72.6 7.4 %collective-permute-start.17 = (bf16[80,256]{1,0:T(8,128)(2,1)S(1)}, bf16[80,256]{1,0:T(8,128)(2,1)S(1)}, u32[]{:S(2)}, u32[]{:S(2)}) collective-permute-start(bf16[80,256]{1,0:T(8,128)(2,1)S(1)} %get-tuple-element.149), channel_id=1, source_target_pairs={{0,24},{4,28},{8,16},{12,20},{16,8},{20,12},{24,0},{28,4},{1,25},{... | collective-permute-start | bytes 122888 | tf_op jit(solution)/shard_map/ppermute | solution.py:52
  75.8 5.3 %collective-permute-start.18 = (bf16[80,256]{1,0:T(8,128)(2,1)S(1)}, bf16[80,256]{1,0:T(8,128)(2,1)S(1)}, u32[]{:S(2)}, u32[]{:S(2)}) collective-permute-start(bf16[80,256]{1,0:T(8,128)(2,1)S(1)} %get-tuple-element.150), channel_id=1, source_target_pairs={{0,16},{4,20},{8,24},{12,28},{16,0},{20,4},{24,8},{28,12},{1,17},{... | collective-permute-start | bytes 122888 | tf_op jit(solution)/shard_map/ppermute | solution.py:52
  75.9 5.3 %collective-permute-start.19 = (bf16[80,256]{1,0:T(8,128)(2,1)S(1)}, bf16[80,256]{1,0:T(8,128)(2,1)S(1)}, u32[]{:S(2)}, u32[]{:S(2)}) collective-permute-start(bf16[80,256]{1,0:T(8,128)(2,1)S(1)} %get-tuple-element.151), channel_id=1, source_target_pairs={{0,8},{4,12},{8,0},{12,4},{16,24},{20,28},{24,16},{28,20},{1,9},{5... | collective-permute-start | bytes 122888 | tf_op jit(solution)/shard_map/ppermute | solution.py:52
  78.6 11.2 %collective-permute-start.24 = (bf16[256,512]{1,0:T(8,128)(2,1)S(1)}, bf16[256,512]{1,0:T(8,128)(2,1)}, u32[]{:S(2)}, u32[]{:S(2)}) collective-permute-start(bf16[256,512]{1,0:T(8,128)(2,1)S(1)} %get-tuple-element.165), channel_id=1, source_target_pairs={{0,2},{1,3},{2,0},{3,1},{4,6},{5,7},{6,4},{7,5},{8,10},{9,11},{10,... | collective-permute-start | bytes 786440 | tf_op jit(solution)/shard_map/ppermute | solution.py:52
  80.1 12.0 %collective-permute-start.25 = (bf16[256,512]{1,0:T(8,128)(2,1)}, bf16[256,512]{1,0:T(8,128)(2,1)S(1)}, u32[]{:S(2)}, u32[]{:S(2)}) collective-permute-start(bf16[256,512]{1,0:T(8,128)(2,1)} %get-tuple-element.166), channel_id=1, source_target_pairs={{0,2},{1,3},{2,0},{3,1},{4,6},{5,7},{6,4},{7,5},{8,10},{9,11},{10,... | collective-permute-start | bytes 786440 | tf_op jit(solution)/shard_map/ppermute | solution.py:52
  81.9 11.3 %all-to-all-start = ((f32[32,4,128]{2,1,0:T(4,128)}), f32[32,4,128]{2,1,0:T(4,128)S(1)}, u32[]{:S(2)}, u32[]{:S(2)}) async-start(f32[32,4,128]{2,1,0:T(4,128)} %get-tuple-element.167), calls=%async_computation | async-start | bytes 131072 | tf_op jit(solution)/shard_map/all_to_all | solution.py:939
  85.6 1.0 %copy-start.15 = (bf16[512,512]{1,0:T(8,128)(2,1)S(1)}, bf16[512,512]{1,0:T(8,128)(2,1)}, u32[]{:S(2)}) copy-start(bf16[512,512]{1,0:T(8,128)(2,1)} %copy-done.14) | copy-start | bytes 1572868
  86.6 1.0 %copy-start.18 = (bf16[512,512]{1,0:T(8,128)(2,1)S(1)}, bf16[512,512]{1,0:T(8,128)(2,1)}, u32[]{:S(2)}) copy-start(bf16[512,512]{1,0:T(8,128)(2,1)} %copy-done.17) | copy-start | bytes 1572868
  89.8 3.5 %copy-start.3 = (f32[64,4,128]{2,1,0:T(4,128)S(1)}, f32[64,4,128]{2,1,0:T(4,128)}, u32[]{:S(2)}) copy-start(f32[64,4,128]{2,1,0:T(4,128)} %refs_0_.7) | copy-start | bytes 393220
  89.8 3.5 %copy-start.4 = (f32[64,4,128]{2,1,0:T(4,128)S(1)}, f32[64,4,128]{2,1,0:T(4,128)}, u32[]{:S(2)}) copy-start(f32[64,4,128]{2,1,0:T(4,128)} %refs_1_.5) | copy-start | bytes 393220
  89.8 3.5 %copy-start.5 = (f32[64,4,128]{2,1,0:T(4,128)S(1)}, f32[64,4,128]{2,1,0:T(4,128)}, u32[]{:S(2)}) copy-start(f32[64,4,128]{2,1,0:T(4,128)} %refs_2_.3) | copy-start | bytes 393220
  89.8 3.5 %copy-start.7 = (f32[8832]{0:T(1024)S(1)}, f32[8832]{0:T(1024)}, u32[]{:S(2)}) copy-start(f32[8832]{0:T(1024)} %param.24) | copy-start | bytes 105988
  89.8 3.5 %copy-start.8 = (f32[8832]{0:T(1024)S(1)}, f32[8832]{0:T(1024)}, u32[]{:S(2)}) copy-start(f32[8832]{0:T(1024)} %param.25) | copy-start | bytes 105988
  89.8 3.5 %copy-start.10 = (f32[128,64]{0,1:T(8,128)S(1)}, f32[128,64]{0,1:T(8,128)}, u32[]{:S(2)}) copy-start(f32[128,64]{0,1:T(8,128)} %param.18) | copy-start | bytes 98308
  89.8 3.5 %copy-start.11 = (f32[128,64]{0,1:T(8,128)S(1)}, f32[128,64]{0,1:T(8,128)}, u32[]{:S(2)}) copy-start(f32[128,64]{0,1:T(8,128)} %param.22) | copy-start | bytes 98308
  89.8 3.5 %copy-start.12 = (f32[128,64]{0,1:T(8,128)S(1)}, f32[128,64]{0,1:T(8,128)}, u32[]{:S(2)}) copy-start(f32[128,64]{0,1:T(8,128)} %param.23) | copy-start | bytes 98308

commit v12 on v11

--- a/solution.py
+++ b/solution.py
@@ -16,7 +16,7 @@
 STEP = 10
 TILE = 256
 NEG = -1e9
-ROOM = 16
+ROOM = 14
 KEPT_TILES = 72
 VALUES = 12
 BACKWARD = 2
@@ -702,7 +702,7 @@
     update(lambda k: state[6 + k][...], put_small, small, rate_small, 0.0)
 
 
-def call(kernel, name, in_specs, outs, scratch, us, room=16, **more):
+def call(kernel, name, in_specs, outs, scratch, us, room=14, **more):
     return pl.pallas_call(
         kernel,
         out_shape=[jax.ShapeDtypeStruct(shape, dtype) for shape, dtype, _ in outs],

time: 95.5 us -> 95.5 us (level)
  no operation moved by 1% of the time
where the time goes in v12:
time: 95.5 us; the launch traced here: 95.1 us
  Pallas kernels  43.8 us (46%)
  starting transfers between devices  31.4 us (33%)
  waiting for transfers between devices  14.3 us (15%)
  local copies, waits for them, and re-layouts  4.59 us (5%)
  between operations  1.1 us (1%)
    ppermute x26, starting transfers between devices, swap(): return lax.ppermute(x, axis, [(i, i ^ k) for i in range(n)])  27.7 us
    ppermute x26, waiting for transfers between devices, swap(): return lax.ppermute(x, axis, [(i, i ^ k) for i in range(n)])  14.3 us
    pallas_call x1, Pallas kernels, shards(): call(functools.partial(backward_kernel, heads, n_dp, extra, kept), 'backw...  10.6 us
    pallas_call x2, Pallas kernels, attend(): call(functools.partial(attend_kernel, heads, first, last, kept), 'attend'...  8.23 us
    unnamed x38, local copies, waits for them, and re-layouts  4.59 us
    pallas_call x1, Pallas kernels, shards(): call(functools.partial(values_kernel, heads, kept), 'values', [VMEM] * (l...  4.32 us
    all_to_all x1, starting transfers between devices, shards(): heard = lax.all_to_all(message, ('dp', 'head'), 0, 0, tiled=True)  3.64 us
    pallas_call x2, Pallas kernels, shards(): call(functools.partial(finish_kernel, part), 'finish', [pl.BlockSpec(memo...  3.39 us
  transfers between devices with their start and end apart: 27, of which 10 were waited for; matrix products, arithmetic and copies ran while one was open for 0% of the time, Pallas kernels for 41%

profile of v12, /device:TPU:0, one launch (start us, length us, event | category | flops | bytes accessed | tf_op | source)
XLA Modules:
  0.0 95.1 jit_solution(12408969440935685144)
XLA Ops:
  0.6 0.0 copy-start.2
  0.7 0.9 copy-done.2
  1.6 0.8 copy-done.9
  2.3 0.3 cast.1.refs_0_
  2.7 4.1 %collective-permute-start.5 = (bf16[64,640]{1,0:T(8,128)(2,1)S(1)}, bf16[64,640]{1,0:T(8,128)(2,1)S(1)}, u32[]{:S(2)}, u32[]{:S(2)}) collective-permute-start(bf16[64,640]{1,0:T(8,128)(2,1)S(1)} %cast.1.refs_0_), channel_id=1, source_target_pairs={{0,16},{4,20},{8,24},{12,28},{16,0},{20,4},{24,8},{28,12},{1,17},{... | collective-permute-start | bytes 245768 | tf_op jit(solution)/shard_map/ppermute | solution.py:52
  6.8 1.5 %collective-permute-start.3 = (bf16[512,512]{1,0:T(8,128)(2,1)}, bf16[512,512]{1,0:T(8,128)(2,1)S(1)}, u32[]{:S(2)}, u32[]{:S(2)}) collective-permute-start(bf16[512,512]{1,0:T(8,128)(2,1)} %refs_1_.4), channel_id=1, source_target_pairs={{0,2},{1,3},{2,0},{3,1},{4,6},{5,7},{6,4},{7,5},{8,10},{9,11},{10,... | collective-permute-start | bytes 1572872 | tf_op jit(solution)/shard_map/ppermute | solution.py:52
  8.3 2.7 %collective-permute-done.5.refs_1_ = bf16[64,640]{1,0:T(8,128)(2,1)S(1)} collective-permute-done((bf16[64,640]{1,0:T(8,128)(2,1)S(1)}, bf16[64,640]{1,0:T(8,128)(2,1)S(1)}, u32[]{:S(2)}, u32[]{:S(2)}) %collective-permute-start.5) | collective-permute-done | bytes 81952 | tf_op jit(solution)/shard_map/ppermute | solution.py:52
  11.0 0.8 collective-permute-start.6
  11.8 2.5 %prepare.1 = (f32[8,256,256]{2,1,0:T(8,128)S(1)}, bf16[8,256,128]{2,1,0:T(8,128)(2,1)S(1)}, bf16[8,128,256]{2,1,0:T(8,128)(2,1)S(1)}, bf16[8,128,256]{2,1,0:T(8,128)(2,1)S(1)}) custom-call(s32[1,2048]{1,0:T(1,128)S(1)} %bitcast.28, f32[69,128]{1,0:T(8,128)S(1)} %bitcast.17), custom_call_target="tpu_custom_call" | custom-call | flops 2000000000 | bytes 6000000 | tf_op jit(solution)/shard_map/prepare/pallas_call | solution.py:764
  14.3 2.1 %collective-permute-done.6.refs_2_ = bf16[128,640]{1,0:T(8,128)(2,1)S(1)} collective-permute-done((bf16[128,640]{1,0:T(8,128)(2,1)S(1)}, bf16[128,640]{1,0:T(8,128)(2,1)S(1)}, u32[]{:S(2)}, u32[]{:S(2)}) %collective-permute-start.6) | collective-permute-done | bytes 163872 | tf_op jit(solution)/shard_map/ppermute | solution.py:52
  16.4 1.8 %collective-permute-start.7 = (bf16[256,640]{1,0:T(8,128)(2,1)S(1)}, bf16[256,640]{1,0:T(8,128)(2,1)S(1)}, u32[]{:S(2)}, u32[]{:S(2)}) collective-permute-start(bf16[256,640]{1,0:T(8,128)(2,1)S(1)} %join.4), channel_id=1, source_target_pairs={{0,4},{4,0},{8,12},{12,8},{16,20},{20,16},{24,28},{28,24},{1,5},{5... | collective-permute-start | bytes 983048 | tf_op jit(solution)/shard_map/ppermute | solution.py:52
  18.2 1.5 %collective-permute-start.1 = (bf16[512,512]{1,0:T(8,128)(2,1)S(1)}, bf16[512,512]{1,0:T(8,128)(2,1)S(1)}, u32[]{:S(2)}, u32[]{:S(2)}) collective-permute-start(bf16[512,512]{1,0:T(8,128)(2,1)S(1)} %copy-done.1), channel_id=1, source_target_pairs={{0,2},{1,3},{2,0},{3,1},{4,6},{5,7},{6,4},{7,5},{8,10},{9,11},{10,... | collective-permute-start | bytes 1572872 | tf_op jit(solution)/shard_map/ppermute | solution.py:52
  19.7 1.7 %collective-permute-done.3.refs_2_ = bf16[512,512]{1,0:T(8,128)(2,1)S(1)} collective-permute-done((bf16[512,512]{1,0:T(8,128)(2,1)}, bf16[512,512]{1,0:T(8,128)(2,1)S(1)}, u32[]{:S(2)}, u32[]{:S(2)}) %collective-permute-start.3) | collective-permute-done | bytes 524320 | tf_op jit(solution)/shard_map/ppermute | solution.py:52
  21.3 1.0 %normalize.2.refs_0_ = bf16[8,256,512]{2,1,0:T(8,128)(2,1)S(1)} custom-call(bf16[512,512]{1,0:T(8,128)(2,1)S(1)} %copy-done, bf16[512,512]{1,0:T(8,128)(2,1)S(1)} %collective-permute-done.2.refs_1_, bf16[512,512]{1,0:T(8,128)(2,1)S(1)} %collective-permute-done.3.refs_2_), custom_call_target="tpu_custom_call" | custom-call | flops 100000000 | bytes 300000 | tf_op jit(solution)/shard_map/normalize/pallas_call | solution.py:795
  22.3 1.8 %collective-permute-done.7.refs_0_ = bf16[256,640]{1,0:T(8,128)(2,1)S(1)} collective-permute-done((bf16[256,640]{1,0:T(8,128)(2,1)S(1)}, bf16[256,640]{1,0:T(8,128)(2,1)S(1)}, u32[]{:S(2)}, u32[]{:S(2)}) %collective-permute-start.7) | collective-permute-done | bytes 327712 | tf_op jit(solution)/shard_map/ppermute | solution.py:52
  24.1 0.4 normalize.3.refs_0_.refs_5_.refs_11_.refs_8_.refs_4_
  24.5 0.0 copy-start.13
  24.5 0.3 assemble.1.refs_1_.refs_6_.wt_ref
  24.8 1.8 %project.1 = (bf16[8,384,256]{2,1,0:T(8,128)(2,1)S(1)}, bf16[8,256,256]{2,1,0:T(8,128)(2,1)S(1)}, bf16[8,256,256]{2,1,0:T(8,128)(2,1)S(1)}, bf16[8,128,256]{2,1,...) custom-call(bf16[8,256,512]{2,1,0:T(8,128)(2,1)S(1)} %normalize.3.re, ...), custom_call_target="tpu_custom_call" | custom-call | flops 1000000000 | bytes 3000000 | tf_op jit(solution)/shard_map/project/pallas_call | solution.py:813
  26.7 4.7 %attend.2 = (f32[6,128,256]{2,1,0:T(8,128)S(1)}, bf16[21,256,512]{2,1,0:T(8,128)(2,1)S(1)}, bf16[21,256,512]{2,1,0:T(8,128)(2,1)S(1)}) custom-call(bf16[8,256,256]{2,1,0:T(8,128)(2,1)S(1)} %get-tuple-element.109.refs_0_.refs_1_.refs_2_, bf16[8,128,256]{2,1,0:T(8,128)(2,1)S(1)} %get-tuple-element.110.refs_1_.refs_2_, ...), custom_call_target="tpu_custom_call" | custom-call | flops 500000000 | bytes 1500000 | tf_op jit(solution)/shard_map/attend/pallas_call | solution.py:826
  31.4 1.2 %collective-permute-done.1.refs_2_.refs_6_ = bf16[512,512]{1,0:T(8,128)(2,1)S(1)} collective-permute-done((bf16[512,512]{1,0:T(8,128)(2,1)S(1)}, bf16[512,512]{1,0:T(8,128)(2,1)S(1)}, u32[]{:S(2)}, u32[]{:S(2)}) %collective-permute-start.1) | collective-permute-done | bytes 524320 | tf_op jit(solution)/shard_map/ppermute | solution.py:52
  32.6 3.5 %attend.3 = (f32[8,128,256]{2,1,0:T(8,128)S(1)}, bf16[15,256,512]{2,1,0:T(8,128)(2,1)S(1)}, bf16[15,256,512]{2,1,0:T(8,128)(2,1)S(1)}) custom-call(f32[6,128,256]{2,1,0:T(8,128)S(1)} %get-tuple-element.115.refs_0_, bf16[8,256,256]{2,1,0:T(8,128)(2,1)S(1)} %get-tuple-element.109.refs_0_.refs_1_.refs_2_, ...), custom_call_target="tpu_custom_call" | custom-call | flops 8000000000 | bytes 24000000 | tf_op jit(solution)/shard_map/attend/pallas_call | solution.py:826
  36.1 1.8 %gate.1 = (f32[8,128,256]{2,1,0:T(8,128)S(1)}, f32[8,128,256]{2,1,0:T(8,128)S(1)}, f32[8,4,256]{2,1,0:T(4,128)S(1)}, f32[1,512]{1,0:T(1,128)S(1)}) custom-call(bf16[512,512]{1,0:T(8,128)(2,1)S(1)} %copy-done.1, bf16[512,512]{1,0:T(8,128)(2,1)S(1)} %collective-permute-done.refs_1_.refs_5_, bf16[512,512]{1,0:T(8,128)(2,1)S(1)} %collective-permute-done.1.refs_2_.refs_6_, ...), custom_call_target="tpu_custom_call" | custom-call | flops 5000000000 | bytes 15000000 | tf_op jit(solution)/shard_map/gate/pallas_call | solution.py:843
  37.9 1.7 %collective-permute-start.11 = (f32[8,4,256]{2,1,0:T(4,128)S(1)}, f32[8,4,256]{2,1,0:T(4,128)S(1)}, u32[]{:S(2)}, u32[]{:S(2)}) collective-permute-start(f32[8,4,256]{2,1,0:T(4,128)S(1)} %get-tuple-element.117.refs_0_), channel_id=1, source_target_pairs={{0,3},{1,2},{2,1},{3,0},{4,7},{5,6},{6,5},{7,4},{8,11},{9,10},{10,... | collective-permute-start | bytes 98312 | tf_op jit(solution)/shard_map/ppermute | solution.py:52
  39.6 0.5 collective-permute-start.10
  40.1 1.2 %collective-permute-done.11.refs_3_ = f32[8,4,256]{2,1,0:T(4,128)S(1)} collective-permute-done((f32[8,4,256]{2,1,0:T(4,128)S(1)}, f32[8,4,256]{2,1,0:T(4,128)S(1)}, u32[]{:S(2)}, u32[]{:S(2)}) %collective-permute-start.11) | collective-permute-done | bytes 32800 | tf_op jit(solution)/shard_map/ppermute | solution.py:52
  41.3 2.2 %collective-permute-done.10.refs_2_ = f32[8,4,256]{2,1,0:T(4,128)S(1)} collective-permute-done((f32[8,4,256]{2,1,0:T(4,128)S(1)}, f32[8,4,256]{2,1,0:T(4,128)S(1)}, u32[]{:S(2)}, u32[]{:S(2)}) %collective-permute-start.10) | collective-permute-done | bytes 32800 | tf_op jit(solution)/shard_map/ppermute | solution.py:52
  43.5 0.8 branch.1
  44.3 0.0 copy-start.17
  44.4 0.8 copy-done.17
  45.1 1.3 %middle.1 = (bf16[8,256,128]{2,1,0:T(8,128)(2,1)S(1)}, bf16[8,128,256]{2,1,0:T(8,128)(2,1)S(1)}, bf16[8,256,128]{2,1,0:T(8,128)(2,1)S(1)}, f32[256,512]{1,0:T(8,128)S(1)}) custom-call(f32[8,4,256]{2,1,0:T(4,128)S(1)} %get-tuple-element.117.refs_0_, f32[8,4,256]{2,1,0:T(4,128)S(1)} %collective-permute-done.9.refs_1_, ...), custom_call_target="tpu_custom_call" | custom-call | flops 6000000000 | bytes 18000000 | tf_op jit(solution)/shard_map/middle/pallas_call | solution.py:859
  46.4 0.6 collective-permute-done.13.crossed_ref
  47.0 0.1 pair.1
  47.2 0.6 collective-permute-start.14
  47.8 4.3 %values.1 = (bf16[8,256,128]{2,1,0:T(8,128)(2,1)S(1)}, bf16[4,64,384]{2,1,0:T(8,128)(2,1)S(1)}, bf16[4,64,384]{2,1,0:T(8,128)(2,1)S(1)}) custom-call(bf16[21,256,512]{2,1,0:T(8,128)(2,1)S(1)} %get-tuple-element.132.refs_0_, bf16[15,256,512]{2,1,0:T(8,128)(2,1)S(1)} %get-tuple-element.133.refs_1_, bf16[8,256,128]{2,1,0:T(8,128)(2,1)S(1)} %get-tuple-element.134.refs_2_, ...), custom_call_target="tpu_custom_call" | custom-call | flops 12000000000 | bytes 36000000 | tf_op jit(solution)/shard_map/values/pallas_call | solution.py:878
  52.1 1.6 %collective-permute-start.12 = (bf16[4,64,384]{2,1,0:T(8,128)(2,1)S(1)}, bf16[4,64,384]{2,1,0:T(8,128)(2,1)S(1)}, u32[]{:S(2)}, u32[]{:S(2)}) collective-permute-start(bf16[4,64,384]{2,1,0:T(8,128)(2,1)S(1)} %get-tuple-element.136), channel_id=1, source_target_pairs={{0,4},{4,0},{8,12},{12,8},{16,20},{20,16},{24,28},{28,24},{1,5},{5... | collective-permute-start | bytes 589832 | tf_op jit(solution)/shard_map/ppermute | solution.py:52
  53.7 10.6 %backward.1 = (bf16[8,256,256]{2,1,0:T(8,128)(2,1)S(1)}, bf16[4,80,256]{2,1,0:T(8,128)(2,1)S(1)}, bf16[4,80,256]{2,1,0:T(8,128)(2,1)S(1)}) custom-call(bf16[21,256,512]{2,1,0:T(8,128)(2,1)S(1)} %get-tuple-element.120.refs_0_, bf16[15,256,512]{2,1,0:T(8,128)(2,1)S(1)} %get-tuple-element.121.refs_1_, ...), custom_call_target="tpu_custom_call" | custom-call | flops 2000000000 | bytes 6000000 | tf_op jit(solution)/shard_map/backward/pallas_call | solution.py:891
  64.3 0.0 copy-start.14
  64.3 0.6 collective-permute-start.15
  64.9 1.3 %input_rows.1 = (bf16[2,512,512]{2,1,0:T(8,128)(2,1)S(1)}, bf16[2,512,512]{2,1,0:T(8,128)(2,1)S(1)}) custom-call(bf16[8,256,256]{2,1,0:T(8,128)(2,1)S(1)} %get-tuple-element.145.gp_ref, bf16[8,256,128]{2,1,0:T(8,128)(2,1)S(1)} %get-tuple-element.146.gun_ref, bf16[8,256,128]{2,1,0:T(8,128)(2,1)S(1)} %get-tuple-element.147.gpv_ref, ...), custom_call_target="tpu_custom_call" | custom-call | flops 4000000000 | bytes 12000000 | tf_op jit(solution)/shard_map/input_rows/pallas_call | solution.py:911
  66.2 0.3 collective-permute-start.16
  66.5 4.2 %collective-permute-start.20 = (bf16[64,384]{1,0:T(8,128)(2,1)S(1)}, bf16[64,384]{1,0:T(8,128)(2,1)S(1)}, u32[]{:S(2)}, u32[]{:S(2)}) collective-permute-start(bf16[64,384]{1,0:T(8,128)(2,1)S(1)} %get-tuple-element.159), channel_id=1, source_target_pairs={{0,24},{4,28},{8,16},{12,20},{16,8},{20,12},{24,0},{28,4},{1,25},{... | collective-permute-start | bytes 147464 | tf_op jit(solution)/shard_map/ppermute | solution.py:52
  70.7 0.3 collective-permute-done.15.refs_1_
  71.0 1.6 %collective-permute-start.22 = (bf16[64,384]{1,0:T(8,128)(2,1)S(1)}, bf16[64,384]{1,0:T(8,128)(2,1)S(1)}, u32[]{:S(2)}, u32[]{:S(2)}) collective-permute-start(bf16[64,384]{1,0:T(8,128)(2,1)S(1)} %get-tuple-element.161), channel_id=1, source_target_pairs={{0,8},{4,12},{8,0},{12,4},{16,24},{20,28},{24,16},{28,20},{1,9},{5... | collective-permute-start | bytes 147464 | tf_op jit(solution)/shard_map/ppermute | solution.py:52
  72.6 3.2 %collective-permute-start.17 = (bf16[80,256]{1,0:T(8,128)(2,1)S(1)}, bf16[80,256]{1,0:T(8,128)(2,1)S(1)}, u32[]{:S(2)}, u32[]{:S(2)}) collective-permute-start(bf16[80,256]{1,0:T(8,128)(2,1)S(1)} %get-tuple-element.149), channel_id=1, source_target_pairs={{0,24},{4,28},{8,16},{12,20},{16,8},{20,12},{24,0},{28,4},{1,25},{... | collective-permute-start | bytes 122888 | tf_op jit(solution)/shard_map/ppermute | solution.py:52
  75.8 0.0 collective-permute-start.18
  75.9 1.8 %collective-permute-start.19 = (bf16[80,256]{1,0:T(8,128)(2,1)S(1)}, bf16[80,256]{1,0:T(8,128)(2,1)S(1)}, u32[]{:S(2)}, u32[]{:S(2)}) collective-permute-start(bf16[80,256]{1,0:T(8,128)(2,1)S(1)} %get-tuple-element.151), channel_id=1, source_target_pairs={{0,8},{4,12},{8,0},{12,4},{16,24},{20,28},{24,16},{28,20},{1,9},{5... | collective-permute-start | bytes 122888 | tf_op jit(solution)/shard_map/ppermute | solution.py:52
  77.7 0.9 rows.1
  78.6 1.5 %collective-permute-start.24 = (bf16[256,512]{1,0:T(8,128)(2,1)S(1)}, bf16[256,512]{1,0:T(8,128)(2,1)}, u32[]{:S(2)}, u32[]{:S(2)}) collective-permute-start(bf16[256,512]{1,0:T(8,128)(2,1)S(1)} %get-tuple-element.165), channel_id=1, source_target_pairs={{0,2},{1,3},{2,0},{3,1},{4,6},{5,7},{6,4},{7,5},{8,10},{9,11},{10,... | collective-permute-start | bytes 786440 | tf_op jit(solution)/shard_map/ppermute | solution.py:52
  80.1 0.5 collective-permute-start.25
  80.6 0.5 collective-permute-done.18.refs_2_
  81.2 0.8 collect.1
  81.9 3.6 %all-to-all-start = ((f32[32,4,128]{2,1,0:T(4,128)}), f32[32,4,128]{2,1,0:T(4,128)S(1)}, u32[]{:S(2)}, u32[]{:S(2)}) async-start(f32[32,4,128]{2,1,0:T(4,128)} %get-tuple-element.167), calls=%async_computation | async-start | bytes 131072 | tf_op jit(solution)/shard_map/all_to_all | solution.py:939
  85.6 0.0 copy-start.15
  85.6 1.0 %copy-done.15 = bf16[512,512]{1,0:T(8,128)(2,1)S(1)} copy-done((bf16[512,512]{1,0:T(8,128)(2,1)S(1)}, bf16[512,512]{1,0:T(8,128)(2,1)}, u32[]{:S(2)}) %copy-start.15) | copy-done | bytes 524312
  86.6 1.0 %copy-done.18 = bf16[512,512]{1,0:T(8,128)(2,1)S(1)} copy-done((bf16[512,512]{1,0:T(8,128)(2,1)S(1)}, bf16[512,512]{1,0:T(8,128)(2,1)}, u32[]{:S(2)}) %copy-start.18) | copy-done | bytes 524312
  87.7 2.1 %mix.1 = bf16[512,512]{1,0:T(8,128)(2,1)} custom-call(bf16[512,512]{1,0:T(8,128)(2,1)S(1)} %copy-done, f32[69,128]{1,0:T(8,128)S(1)} %bitcast.18, bf16[512,512]{1,0:T(8,128)(2,1)S(1)} %copy-done.18, bf16[512,512]{1,0:T(8,128)(2,1)} %collective-permute-done.23.refs_1_, bf16[512,512]{1,0:T(8,128)(2,1)S(1)} %copy-done.15), custom_call_target="tpu_custom_call" | custom-call | flops 1000000000 | bytes 3000000 | tf_op jit(solution)/shard_map/mix/pallas_call | solution.py:940
  89.8 0.0 copy-start.7
  89.8 0.0 copy-start.8
  89.8 0.0 copy-start.10
  89.8 0.0 copy-start.11
  89.9 2.2 %finish.2.refs_0_ = f32[512,512]{1,0:T(8,128)} custom-call(bf16[512,512]{1,0:T(8,128)(2,1)S(1)} %copy-done, bf16[512,512]{1,0:T(8,128)(2,1)S(1)} %copy-done.1, f32[512,512]{1,0:T(8,128)S(1)} %get-tuple-element.171.refs_2_.refs_3_, bf16[256,512]{1,0:T(8,128)(2,1)} %collective-permute-done.24.refs_3_), custom_call_target="tpu_custom_call" | custom-call | flops 1000000000 | bytes 3000000 | tf_op jit(solution)/shard_map/finish/pallas_call | solution.py:948
  92.1 1.2 %finish.3 = f32[512,512]{1,0:T(8,128)} custom-call(f32[512,512]{1,0:T(8,128)} %finish.2.refs_0_, bf16[512,512]{1,0:T(8,128)(2,1)S(1)} %copy-done, bf16[512,512]{1,0:T(8,128)(2,1)S(1)} %copy-done.1, f32[512,512]{1,0:T(8,128)S(1)} %get-tuple-element.171.refs_2_.refs_3_, ...), custom_call_target="tpu_custom_call", output_to_operand_aliasing={{}: (0, {})} | custom-call | flops 1000000000 | bytes 3000000 | tf_op jit(solution)/shard_map/finish/pallas_call | solution.py:948
  93.3 1.7 %update.1 = (f32[64,4,128]{2,1,0:T(4,128)}, f32[64,128]{1,0:T(8,128)}, f32[69,128]{1,0:T(8,128)}, f32[1,1]{1,0:T(1,128)}, f32[64,4,128]{2,1,0:T(4,128)}, /*index...) custom-call(f32[32,4,128]{2,1,0:T(4,128)S(1)} %all-to-all-done.heard, ...), custom_call_target="tpu_custom_call" | custom-call | flops 100000000 | bytes 300000 | tf_op jit(solution)/shard_map/update/pallas_call | solution.py:963
  (55 shorter events, 0.3 us)
Async XLA Ops:
  0.6 0.9 copy-start.2
  1.6 0.8 copy-start.9
  2.3 9.5 %copy-start.6 = (f32[8832]{0:T(1024)S(1)}, f32[8832]{0:T(1024)}, u32[]{:S(2)}) copy-start(f32[8832]{0:T(1024)} %param.19) | copy-start | bytes 105988
  2.3 9.5 %copy-start.16 = (s32[2048]{0:T(1024)S(1)}, s32[2048]{0:T(1024)}, u32[]{:S(2)}) copy-start(s32[2048]{0:T(1024)} %param.16) | copy-start | bytes 24580
  2.7 8.3 %collective-permute-start.5 = (bf16[64,640]{1,0:T(8,128)(2,1)S(1)}, bf16[64,640]{1,0:T(8,128)(2,1)S(1)}, u32[]{:S(2)}, u32[]{:S(2)}) collective-permute-start(bf16[64,640]{1,0:T(8,128)(2,1)S(1)} %cast.1.refs_0_), channel_id=1, source_target_pairs={{0,16},{4,20},{8,24},{12,28},{16,0},{20,4},{24,8},{28,12},{1,17},{... | collective-permute-start | bytes 245768 | tf_op jit(solution)/shard_map/ppermute | solution.py:52
  6.8 14.6 %collective-permute-start.2 = (bf16[512,512]{1,0:T(8,128)(2,1)}, bf16[512,512]{1,0:T(8,128)(2,1)S(1)}, u32[]{:S(2)}, u32[]{:S(2)}) collective-permute-start(bf16[512,512]{1,0:T(8,128)(2,1)} %refs_1_.4), channel_id=1, source_target_pairs={{0,1},{1,0},{2,3},{3,2},{4,5},{5,4},{6,7},{7,6},{8,9},{9,8},{10,11... | collective-permute-start | bytes 1572872 | tf_op jit(solution)/shard_map/ppermute | solution.py:52
  6.8 14.5 %collective-permute-start.3 = (bf16[512,512]{1,0:T(8,128)(2,1)}, bf16[512,512]{1,0:T(8,128)(2,1)S(1)}, u32[]{:S(2)}, u32[]{:S(2)}) collective-permute-start(bf16[512,512]{1,0:T(8,128)(2,1)} %refs_1_.4), channel_id=1, source_target_pairs={{0,2},{1,3},{2,0},{3,1},{4,6},{5,7},{6,4},{7,5},{8,10},{9,11},{10,... | collective-permute-start | bytes 1572872 | tf_op jit(solution)/shard_map/ppermute | solution.py:52
  11.0 5.4 %collective-permute-start.6 = (bf16[128,640]{1,0:T(8,128)(2,1)S(1)}, bf16[128,640]{1,0:T(8,128)(2,1)S(1)}, u32[]{:S(2)}, u32[]{:S(2)}) collective-permute-start(bf16[128,640]{1,0:T(8,128)(2,1)S(1)} %join.3), channel_id=1, source_target_pairs={{0,8},{4,12},{8,0},{12,4},{16,24},{20,28},{24,16},{28,20},{1,9},{5... | collective-permute-start | bytes 491528 | tf_op jit(solution)/shard_map/ppermute | solution.py:52
  11.8 6.4 %copy-start.1 = (bf16[512,512]{1,0:T(8,128)(2,1)S(1)}, bf16[512,512]{1,0:T(8,128)(2,1)}, u32[]{:S(2)}) copy-start(bf16[512,512]{1,0:T(8,128)(2,1)} %refs_2_.2) | copy-start | bytes 1572868
  11.8 9.5 %copy-start = (bf16[512,512]{1,0:T(8,128)(2,1)S(1)}, bf16[512,512]{1,0:T(8,128)(2,1)}, u32[]{:S(2)}) copy-start(bf16[512,512]{1,0:T(8,128)(2,1)} %refs_1_.4) | copy-start | bytes 1572868
  16.4 7.7 %collective-permute-start.7 = (bf16[256,640]{1,0:T(8,128)(2,1)S(1)}, bf16[256,640]{1,0:T(8,128)(2,1)S(1)}, u32[]{:S(2)}, u32[]{:S(2)}) collective-permute-start(bf16[256,640]{1,0:T(8,128)(2,1)S(1)} %join.4), channel_id=1, source_target_pairs={{0,4},{4,0},{8,12},{12,8},{16,20},{20,16},{24,28},{28,24},{1,5},{5... | collective-permute-start | bytes 983048 | tf_op jit(solution)/shard_map/ppermute | solution.py:52
  18.2 17.9 %collective-permute-start = (bf16[512,512]{1,0:T(8,128)(2,1)S(1)}, bf16[512,512]{1,0:T(8,128)(2,1)S(1)}, u32[]{:S(2)}, u32[]{:S(2)}) collective-permute-start(bf16[512,512]{1,0:T(8,128)(2,1)S(1)} %copy-done.1), channel_id=1, source_target_pairs={{0,1},{1,0},{2,3},{3,2},{4,5},{5,4},{6,7},{7,6},{8,9},{9,8},{10,11... | collective-permute-start | bytes 1572872 | tf_op jit(solution)/shard_map/ppermute | solution.py:52
  18.2 14.4 %collective-permute-start.1 = (bf16[512,512]{1,0:T(8,128)(2,1)S(1)}, bf16[512,512]{1,0:T(8,128)(2,1)S(1)}, u32[]{:S(2)}, u32[]{:S(2)}) collective-permute-start(bf16[512,512]{1,0:T(8,128)(2,1)S(1)} %copy-done.1), channel_id=1, source_target_pairs={{0,2},{1,3},{2,0},{3,1},{4,6},{5,7},{6,4},{7,5},{8,10},{9,11},{10,... | collective-permute-start | bytes 1572872 | tf_op jit(solution)/shard_map/ppermute | solution.py:52
  21.3 2.8 %collective-permute-start.4 = (bf16[512,512]{1,0:T(8,128)(2,1)S(1)}, bf16[512,512]{1,0:T(8,128)(2,1)S(1)}, u32[]{:S(2)}, u32[]{:S(2)}) collective-permute-start(bf16[512,512]{1,0:T(8,128)(2,1)S(1)} %collective-permute-done.3.refs_2_), channel_id=1, source_target_pairs={{0,1},{1,0},{2,3},{3,2},{4,5},{5,4},{6,7},{7,6},{8,9},{9,8},{10,11... | collective-permute-start | bytes 1572872 | tf_op jit(solution)/shard_map/ppermute | solution.py:52
  24.5 2.2 %copy-start.13 = (s32[2048]{0:T(1024)S(1)}, s32[2048]{0:T(1024)}, u32[]{:S(2)}) copy-start(s32[2048]{0:T(1024)} %param.15) | copy-start | bytes 24580
  32.6 3.5 %collective-permute-start.8 = (bf16[512,512]{1,0:T(8,128)(2,1)S(1)}, bf16[512,512]{1,0:T(8,128)(2,1)S(1)}, u32[]{:S(2)}, u32[]{:S(2)}) collective-permute-start(bf16[512,512]{1,0:T(8,128)(2,1)S(1)} %collective-permute-done.1.refs_2_.refs_6_), channel_id=1, source_target_pairs={{0,1},{1,0},{2,3},{3,2},{4,5},{5,4},{6,7},{7,6},{8,9},{9,8},{10,11... | collective-permute-start | bytes 1572872 | tf_op jit(solution)/shard_map/ppermute | solution.py:52
  37.9 3.4 %collective-permute-start.11 = (f32[8,4,256]{2,1,0:T(4,128)S(1)}, f32[8,4,256]{2,1,0:T(4,128)S(1)}, u32[]{:S(2)}, u32[]{:S(2)}) collective-permute-start(f32[8,4,256]{2,1,0:T(4,128)S(1)} %get-tuple-element.117.refs_0_), channel_id=1, source_target_pairs={{0,3},{1,2},{2,1},{3,0},{4,7},{5,6},{6,5},{7,4},{8,11},{9,10},{10,... | collective-permute-start | bytes 98312 | tf_op jit(solution)/shard_map/ppermute | solution.py:52
  39.6 3.9 %collective-permute-start.10 = (f32[8,4,256]{2,1,0:T(4,128)S(1)}, f32[8,4,256]{2,1,0:T(4,128)S(1)}, u32[]{:S(2)}, u32[]{:S(2)}) collective-permute-start(f32[8,4,256]{2,1,0:T(4,128)S(1)} %get-tuple-element.117.refs_0_), channel_id=1, source_target_pairs={{0,2},{1,3},{2,0},{3,1},{4,6},{5,7},{6,4},{7,5},{8,10},{9,11},{10,... | collective-permute-start | bytes 98312 | tf_op jit(solution)/shard_map/ppermute | solution.py:52
  40.1 3.4 %collective-permute-start.9 = (f32[8,4,256]{2,1,0:T(4,128)S(1)}, f32[8,4,256]{2,1,0:T(4,128)S(1)}, u32[]{:S(2)}, u32[]{:S(2)}) collective-permute-start(f32[8,4,256]{2,1,0:T(4,128)S(1)} %get-tuple-element.117.refs_0_), channel_id=1, source_target_pairs={{0,1},{1,0},{2,3},{3,2},{4,5},{5,4},{6,7},{7,6},{8,9},{9,8},{10,11... | collective-permute-start | bytes 98312 | tf_op jit(solution)/shard_map/ppermute | solution.py:52
  44.3 0.8 copy-start.17
  45.1 1.9 %collective-permute-start.13 = (bf16[512,512]{1,0:T(8,128)(2,1)S(1)}, bf16[512,512]{1,0:T(8,128)(2,1)S(1)}, u32[]{:S(2)}, u32[]{:S(2)}) collective-permute-start(bf16[512,512]{1,0:T(8,128)(2,1)S(1)} %get-tuple-element.138), channel_id=1, source_target_pairs={{0,1},{1,0},{2,3},{3,2},{4,5},{5,4},{6,7},{7,6},{8,9},{9,8},{10,11... | collective-permute-start | bytes 1572872 | tf_op jit(solution)/shard_map/ppermute | solution.py:52
  47.2 17.1 %collective-permute-start.14 = (bf16[512,512]{1,0:T(8,128)(2,1)S(1)}, bf16[512,512]{1,0:T(8,128)(2,1)S(1)}, u32[]{:S(2)}, u32[]{:S(2)}) collective-permute-start(bf16[512,512]{1,0:T(8,128)(2,1)S(1)} %pair.1), channel_id=1, source_target_pairs={{0,2},{1,3},{2,0},{3,1},{4,6},{5,7},{6,4},{7,5},{8,10},{9,11},{10,... | collective-permute-start | bytes 1572872 | tf_op jit(solution)/shard_map/ppermute | solution.py:52
  52.1 12.2 %collective-permute-start.12 = (bf16[4,64,384]{2,1,0:T(8,128)(2,1)S(1)}, bf16[4,64,384]{2,1,0:T(8,128)(2,1)S(1)}, u32[]{:S(2)}, u32[]{:S(2)}) collective-permute-start(bf16[4,64,384]{2,1,0:T(8,128)(2,1)S(1)} %get-tuple-element.136), channel_id=1, source_target_pairs={{0,4},{4,0},{8,12},{12,8},{16,20},{20,16},{24,28},{28,24},{1,5},{5... | collective-permute-start | bytes 589832 | tf_op jit(solution)/shard_map/ppermute | solution.py:52
  53.7 31.9 %collective-permute-start.23 = (bf16[512,512]{1,0:T(8,128)(2,1)S(1)}, bf16[512,512]{1,0:T(8,128)(2,1)}, u32[]{:S(2)}, u32[]{:S(2)}) collective-permute-start(bf16[512,512]{1,0:T(8,128)(2,1)S(1)} %get-tuple-element.169), channel_id=1, source_target_pairs={{0,1},{1,0},{2,3},{3,2},{4,5},{5,4},{6,7},{7,6},{8,9},{9,8},{10,11... | collective-permute-start | bytes 1572872 | tf_op jit(solution)/shard_map/ppermute | solution.py:52
  64.3 1.9 %copy-start.14 = (bf16[512,512]{1,0:T(8,128)(2,1)}, bf16[512,512]{1,0:T(8,128)(2,1)S(1)}, u32[]{:S(2)}) copy-start(bf16[512,512]{1,0:T(8,128)(2,1)S(1)} %collective-permute-done.14.refs_2_) | copy-start | bytes 1572868
  64.3 6.7 %collective-permute-start.15 = (bf16[4,80,256]{2,1,0:T(8,128)(2,1)S(1)}, bf16[4,80,256]{2,1,0:T(8,128)(2,1)S(1)}, u32[]{:S(2)}, u32[]{:S(2)}) collective-permute-start(bf16[4,80,256]{2,1,0:T(8,128)(2,1)S(1)} %get-tuple-element.140), channel_id=1, source_target_pairs={{0,4},{4,0},{8,12},{12,8},{16,20},{20,16},{24,28},{28,24},{1,5},{5... | collective-permute-start | bytes 491528 | tf_op jit(solution)/shard_map/ppermute | solution.py:52
  66.2 6.5 %collective-permute-start.16 = (bf16[2,512,512]{2,1,0:T(8,128)(2,1)S(1)}, bf16[2,512,512]{2,1,0:T(8,128)(2,1)S(1)}, u32[]{:S(2)}, u32[]{:S(2)}) collective-permute-start(bf16[2,512,512]{2,1,0:T(8,128)(2,1)S(1)} %get-tuple-element.148), channel_id=1, source_target_pairs={{0,1},{1,0},{2,3},{3,2},{4,5},{5,4},{6,7},{7,6},{8,9},{9,8},{10,11... | collective-permute-start | bytes 3145736 | tf_op jit(solution)/shard_map/ppermute | solution.py:52
  66.5 9.3 %collective-permute-start.20 = (bf16[64,384]{1,0:T(8,128)(2,1)S(1)}, bf16[64,384]{1,0:T(8,128)(2,1)S(1)}, u32[]{:S(2)}, u32[]{:S(2)}) collective-permute-start(bf16[64,384]{1,0:T(8,128)(2,1)S(1)} %get-tuple-element.159), channel_id=1, source_target_pairs={{0,24},{4,28},{8,16},{12,20},{16,8},{20,12},{24,0},{28,4},{1,25},{... | collective-permute-start | bytes 147464 | tf_op jit(solution)/shard_map/ppermute | solution.py:52
  70.7 5.2 %collective-permute-start.21 = (bf16[64,384]{1,0:T(8,128)(2,1)S(1)}, bf16[64,384]{1,0:T(8,128)(2,1)S(1)}, u32[]{:S(2)}, u32[]{:S(2)}) collective-permute-start(bf16[64,384]{1,0:T(8,128)(2,1)S(1)} %get-tuple-element.160), channel_id=1, source_target_pairs={{0,16},{4,20},{8,24},{12,28},{16,0},{20,4},{24,8},{28,12},{1,17},{... | collective-permute-start | bytes 147464 | tf_op jit(solution)/shard_map/ppermute | solution.py:52
  71.0 6.7 %collective-permute-start.22 = (bf16[64,384]{1,0:T(8,128)(2,1)S(1)}, bf16[64,384]{1,0:T(8,128)(2,1)S(1)}, u32[]{:S(2)}, u32[]{:S(2)}) collective-permute-start(bf16[64,384]{1,0:T(8,128)(2,1)S(1)} %get-tuple-element.161), channel_id=1, source_target_pairs={{0,8},{4,12},{8,0},{12,4},{16,24},{20,28},{24,16},{28,20},{1,9},{5... | collective-permute-start | bytes 147464 | tf_op jit(solution)/shard_map/ppermute | solution.py:52
  72.6 7.4 %collective-permute-start.17 = (bf16[80,256]{1,0:T(8,128)(2,1)S(1)}, bf16[80,256]{1,0:T(8,128)(2,1)S(1)}, u32[]{:S(2)}, u32[]{:S(2)}) collective-permute-start(bf16[80,256]{1,0:T(8,128)(2,1)S(1)} %get-tuple-element.149), channel_id=1, source_target_pairs={{0,24},{4,28},{8,16},{12,20},{16,8},{20,12},{24,0},{28,4},{1,25},{... | collective-permute-start | bytes 122888 | tf_op jit(solution)/shard_map/ppermute | solution.py:52
  75.8 5.3 %collective-permute-start.18 = (bf16[80,256]{1,0:T(8,128)(2,1)S(1)}, bf16[80,256]{1,0:T(8,128)(2,1)S(1)}, u32[]{:S(2)}, u32[]{:S(2)}) collective-permute-start(bf16[80,256]{1,0:T(8,128)(2,1)S(1)} %get-tuple-element.150), channel_id=1, source_target_pairs={{0,16},{4,20},{8,24},{12,28},{16,0},{20,4},{24,8},{28,12},{1,17},{... | collective-permute-start | bytes 122888 | tf_op jit(solution)/shard_map/ppermute | solution.py:52
  75.9 5.3 %collective-permute-start.19 = (bf16[80,256]{1,0:T(8,128)(2,1)S(1)}, bf16[80,256]{1,0:T(8,128)(2,1)S(1)}, u32[]{:S(2)}, u32[]{:S(2)}) collective-permute-start(bf16[80,256]{1,0:T(8,128)(2,1)S(1)} %get-tuple-element.151), channel_id=1, source_target_pairs={{0,8},{4,12},{8,0},{12,4},{16,24},{20,28},{24,16},{28,20},{1,9},{5... | collective-permute-start | bytes 122888 | tf_op jit(solution)/shard_map/ppermute | solution.py:52
  78.6 11.2 %collective-permute-start.24 = (bf16[256,512]{1,0:T(8,128)(2,1)S(1)}, bf16[256,512]{1,0:T(8,128)(2,1)}, u32[]{:S(2)}, u32[]{:S(2)}) collective-permute-start(bf16[256,512]{1,0:T(8,128)(2,1)S(1)} %get-tuple-element.165), channel_id=1, source_target_pairs={{0,2},{1,3},{2,0},{3,1},{4,6},{5,7},{6,4},{7,5},{8,10},{9,11},{10,... | collective-permute-start | bytes 786440 | tf_op jit(solution)/shard_map/ppermute | solution.py:52
  80.1 12.0 %collective-permute-start.25 = (bf16[256,512]{1,0:T(8,128)(2,1)}, bf16[256,512]{1,0:T(8,128)(2,1)S(1)}, u32[]{:S(2)}, u32[]{:S(2)}) collective-permute-start(bf16[256,512]{1,0:T(8,128)(2,1)} %get-tuple-element.166), channel_id=1, source_target_pairs={{0,2},{1,3},{2,0},{3,1},{4,6},{5,7},{6,4},{7,5},{8,10},{9,11},{10,... | collective-permute-start | bytes 786440 | tf_op jit(solution)/shard_map/ppermute | solution.py:52
  81.9 11.3 %all-to-all-start = ((f32[32,4,128]{2,1,0:T(4,128)}), f32[32,4,128]{2,1,0:T(4,128)S(1)}, u32[]{:S(2)}, u32[]{:S(2)}) async-start(f32[32,4,128]{2,1,0:T(4,128)} %get-tuple-element.167), calls=%async_computation | async-start | bytes 131072 | tf_op jit(solution)/shard_map/all_to_all | solution.py:939
  85.6 1.0 %copy-start.15 = (bf16[512,512]{1,0:T(8,128)(2,1)S(1)}, bf16[512,512]{1,0:T(8,128)(2,1)}, u32[]{:S(2)}) copy-start(bf16[512,512]{1,0:T(8,128)(2,1)} %copy-done.14) | copy-start | bytes 1572868
  86.6 1.0 %copy-start.18 = (bf16[512,512]{1,0:T(8,128)(2,1)S(1)}, bf16[512,512]{1,0:T(8,128)(2,1)}, u32[]{:S(2)}) copy-start(bf16[512,512]{1,0:T(8,128)(2,1)} %copy-done.17) | copy-start | bytes 1572868
  89.8 3.5 %copy-start.3 = (f32[64,4,128]{2,1,0:T(4,128)S(1)}, f32[64,4,128]{2,1,0:T(4,128)}, u32[]{:S(2)}) copy-start(f32[64,4,128]{2,1,0:T(4,128)} %refs_0_.7) | copy-start | bytes 393220
  89.8 3.5 %copy-start.4 = (f32[64,4,128]{2,1,0:T(4,128)S(1)}, f32[64,4,128]{2,1,0:T(4,128)}, u32[]{:S(2)}) copy-start(f32[64,4,128]{2,1,0:T(4,128)} %refs_1_.5) | copy-start | bytes 393220
  89.8 3.5 %copy-start.5 = (f32[64,4,128]{2,1,0:T(4,128)S(1)}, f32[64,4,128]{2,1,0:T(4,128)}, u32[]{:S(2)}) copy-start(f32[64,4,128]{2,1,0:T(4,128)} %refs_2_.3) | copy-start | bytes 393220
  89.8 3.5 %copy-start.7 = (f32[8832]{0:T(1024)S(1)}, f32[8832]{0:T(1024)}, u32[]{:S(2)}) copy-start(f32[8832]{0:T(1024)} %param.24) | copy-start | bytes 105988
  89.8 3.5 %copy-start.8 = (f32[8832]{0:T(1024)S(1)}, f32[8832]{0:T(1024)}, u32[]{:S(2)}) copy-start(f32[8832]{0:T(1024)} %param.25) | copy-start | bytes 105988
  89.8 3.5 %copy-start.10 = (f32[128,64]{0,1:T(8,128)S(1)}, f32[128,64]{0,1:T(8,128)}, u32[]{:S(2)}) copy-start(f32[128,64]{0,1:T(8,128)} %param.18) | copy-start | bytes 98308
  89.8 3.5 %copy-start.11 = (f32[128,64]{0,1:T(8,128)S(1)}, f32[128,64]{0,1:T(8,128)}, u32[]{:S(2)}) copy-start(f32[128,64]{0,1:T(8,128)} %param.22) | copy-start | bytes 98308
  89.8 3.5 %copy-start.12 = (f32[128,64]{0,1:T(8,128)S(1)}, f32[128,64]{0,1:T(8,128)}, u32[]{:S(2)}) copy-start(f32[128,64]{0,1:T(8,128)} %param.23) | copy-start | bytes 98308
